TPU v7x, 512 devices: a whole 4x8x8 slice. The times are simulated.
512 devices in a mesh: lat: 16 (over z_hi, x), lon: 32 (over z_lo, y, core).
Axes of the slice: x: 4, y: 8, z: 8 (z_hi: 4, z_lo: 2; z = z_hi * 2 + z_lo), core: 2. Of those that a mesh axis runs over, the one named last changes fastest.
Arguments:
- feats: bfloat16 [2, 128, 1024, 128], P(None, 'lat', 'lon'), may hold values from -41 to 41
- cond: bfloat16 [2, 128, 1024, 128], P(None, 'lat', 'lon'), may hold values from -6 to 6
- null_field: bfloat16 [128, 1024, 128], P('lat', 'lon'), may hold values from -6 to 6
- drop_flags: int32 [2, 128], replicated, may hold values from 0 to 1, as said below
- emb: float32 [2, 512], replicated, may hold values from -5 to 5
- style_weight: float32 [512, 128], replicated, may hold values from -0.044194173 to 0.044194173
- conv_weight: float32 [3, 3, 128, 128], replicated, may hold values from -0.1875 to 0.1875
- gamma: float32 [128], replicated, may hold values from 0.1 to 1.9
- beta: float32 [128], replicated, may hold values from -3 to 3
- cotangent: bfloat16 [2, 128, 1024, 128], P(None, 'lat', 'lon'), may hold values from -6 to 6
Outputs:
- block_out: bfloat16 [2, 128, 1024, 128], P(None, 'lat', 'lon')
- grad_feats: bfloat16 [2, 128, 1024, 128], P(None, 'lat', 'lon')
- grad_weight: float32 [3, 3, 128, 128], replicated
- grad_style: float32 [512, 128], replicated
- gamma_gradient: float32 [128], replicated
- grad_beta: float32 [128], replicated
Inputs may be any that keep to these rules, and one draw needn't show every extreme that they name: `drop_flags`: each sample drops exactly 64 of its channels.
All inputs are finite; a program needn't handle non-finite values.
Results may differ from a plain program's by a relative error of at most 0.0056.
Values may be sent and summed in bfloat16 or wider, within the bound.
No kernel may reach another device: no remote copies, remote signals or barrier semaphores. Data moves between devices by JAX's collectives and lax.ppermute only.
A program may use at most 64 MiB of HBM per device.

v0:
```python
import math

import jax
import jax.numpy as jnp
from jax import lax
from jax.sharding import PartitionSpec as P

GROUPS = 32


def padded_2(block, sides, width, periodic):
    for axis, dim in sides:
        count = lax.axis_size(axis)
        forward = [(i, i + 1) for i in range(count - 1)]
        if periodic:
            forward.append((count - 1, 0))
        backward = [(target, source) for source, target in forward]
        low = lax.ppermute(
            lax.slice_in_dim(block, block.shape[dim] - width, None, axis=dim), axis, forward
        )
        high = lax.ppermute(lax.slice_in_dim(block, 0, width, axis=dim), axis, backward)
        block = jnp.concatenate([low, block, high], axis=dim)
    return block


def modulate(conv_weight, style_weight, emb):
    style_scale = 1.0 + jnp.dot(emb, style_weight, precision=lax.Precision.HIGHEST)
    modded = conv_weight[None] * style_scale[:, None, None, :, None]
    demod = lax.rsqrt(jnp.sum(modded * modded, axis=(1, 2, 3)) + 1e-08)
    return modded * demod[:, None, None, None, :]


def extend(tile):
    widened = padded_2(tile, (("lon", 2),), 1, True)
    return padded_2(widened, (("lat", 1),), 1, False)


def apply_taps(padded, taps, tile_rows, tile_cols):
    total = jnp.zeros(padded.shape[:1] + (tile_rows, tile_cols, taps.shape[4]), jnp.float32)
    for row_tap in range(3):
        for col_tap in range(3):
            window = padded[:, row_tap : row_tap + tile_rows, col_tap : col_tap + tile_cols]
            total = total + jnp.einsum(
                "bhwi,bio->bhwo",
                window,
                taps[:, row_tap, col_tap],
                preferred_element_type=jnp.float32,
            )
    return total


def on_device(
    feats, cond, null_field, drop_flags, emb, style_weight, conv_weight, gamma, beta, cotangent
):
    samples, tile_rows, tile_cols, channels = feats.shape
    group_size = channels // GROUPS
    devices_all = lax.axis_size("lat") * lax.axis_size("lon")
    cells_per_group = tile_rows * tile_cols * devices_all * group_size
    scale_gradient = 1.0 / math.sqrt(samples * tile_rows * tile_cols * devices_all)

    def group_count_total(values):
        return jnp.sum(values, axis=(1, 2)).reshape(samples, GROUPS, group_size).sum(-1)

    def expand_groups(stat):
        return jnp.repeat(stat, group_size, axis=1)[:, None, None, :]

    dropped = drop_flags.astype(jnp.float32)[:, None, None, :]
    mixed = (
        feats.astype(jnp.float32)
        + dropped * null_field.astype(jnp.float32)[None]
        + (1.0 - dropped) * cond.astype(jnp.float32)
    ).astype(jnp.bfloat16)
    mixed32 = mixed.astype(jnp.float32)
    group_mean = lax.psum(group_count_total(mixed32), ("lat", "lon")) / cells_per_group
    centered_input = mixed32 - expand_groups(group_mean)
    group_var = (
        lax.psum(group_count_total(centered_input * centered_input), ("lat", "lon"))
        / cells_per_group
    )
    inverse_deviation = expand_groups(lax.rsqrt(group_var + 1e-05))
    normalized_input = centered_input * inverse_deviation
    preactivation = normalized_input * gamma + beta
    act = jax.nn.silu(preactivation).astype(jnp.bfloat16)
    w_eff32 = modulate(conv_weight, style_weight, emb)
    w_eff = w_eff32.astype(jnp.bfloat16)
    act_pad = extend(act)
    cot_pad = extend(cotangent)
    conv_out = apply_taps(act_pad, w_eff, tile_rows, tile_cols)
    block_out = (mixed32 + conv_out).astype(jnp.bfloat16)
    back_taps = jnp.swapaxes(w_eff[:, ::-1, ::-1], 3, 4)
    grad_act = apply_taps(cot_pad, back_taps, tile_rows, tile_cols)
    tap_rows = []
    for row_tap in range(3):
        tap_cols = []
        for col_tap in range(3):
            window = act_pad[:, row_tap : row_tap + tile_rows, col_tap : col_tap + tile_cols]
            tap_cols.append(
                jnp.einsum("bhwi,bhwo->bio", window, cotangent, preferred_element_type=jnp.float32)
            )
        tap_rows.append(jnp.stack(tap_cols, axis=1))
    local_eff = jnp.stack(tap_rows, axis=1)
    sig = jax.nn.sigmoid(preactivation)
    preactivation_gradient = grad_act * sig * (1.0 + preactivation * (1.0 - sig))
    gamma_partial = jnp.sum(preactivation_gradient * normalized_input, axis=(0, 1, 2))
    beta_part = jnp.sum(preactivation_gradient, axis=(0, 1, 2))
    normalized_gradient = preactivation_gradient * gamma
    product_mean_partial = group_count_total(normalized_gradient)
    squared_mean_partial = group_count_total(normalized_gradient * normalized_input)
    grad_eff, pmean_sum, qmean_sum, gamma_sum, beta_sum = lax.psum(
        (local_eff, product_mean_partial, squared_mean_partial, gamma_partial, beta_part),
        ("lat", "lon"),
    )
    _, pullback = jax.vjp(
        lambda weight, style: modulate(weight, style, emb), conv_weight, style_weight
    )
    weight_part, style_part = pullback(grad_eff)
    grad_weight = scale_gradient * weight_part
    grad_style = scale_gradient * style_part
    product_mean = pmean_sum / cells_per_group
    squared_mean = qmean_sum / cells_per_group
    mixed_gradient = inverse_deviation * (
        normalized_gradient
        - expand_groups(product_mean)
        - normalized_input * expand_groups(squared_mean)
    )
    grad_feats = (cotangent.astype(jnp.float32) + mixed_gradient).astype(jnp.bfloat16)
    return (
        block_out,
        grad_feats,
        grad_weight,
        grad_style,
        scale_gradient * gamma_sum,
        scale_gradient * beta_sum,
    )


def solution(mesh):
    placed = (
        P(None, "lat", "lon", None),
        P(None, "lat", "lon", None),
        P("lat", "lon", None),
        P(),
        P(),
        P(),
        P(),
        P(),
        P(),
        P(None, "lat", "lon", None),
    )
    return jax.shard_map(
        on_device,
        mesh=mesh,
        in_specs=placed,
        out_specs=(P(None, "lat", "lon", None), P(None, "lat", "lon", None), P(), P(), P(), P()),
        check_vma=False,
    )
```

profile of v0, /device:TPU:1, one launch (start us, length us, event | category | flops | bytes accessed | tf_op | source)
XLA Modules:
  0.0 623.9 jit_solution(7119591295118812241)
XLA Ops:
  7.2 0.7 broadcast_subtract_fusion
  8.0 0.7 convert_element_type.34
  8.7 0.8 convert_element_type.35
  9.5 1.1 convert_reduce_fusion
  10.8 106.1 %psum.49 = f32[2,32]{1,0:T(2,128)S(1)} all-reduce(f32[2,32]{1,0:T(2,128)S(1)} %reduce_sum.125), channel_id=1, replica_groups=mesh['lat'=16,'lon'=32] {'lat','lon'}, use_global_device_ids=true, to_apply=%region_2.0 | all-reduce | flops 64 | bytes 512 | tf_op jit(solution)/shard_map/psum | solution.py:74
  116.9 0.1 sub.35
  117.3 93.6 %psum.50 = f32[2,32]{1,0:T(2,128)S(1)} all-reduce(f32[2,32]{1,0:T(2,128)S(1)} %reduce_sum.145), channel_id=1, replica_groups=mesh['lat'=16,'lon'=32] {'lat','lon'}, use_global_device_ids=true, to_apply=%region_5.0 | all-reduce | flops 64 | bytes 512 | tf_op jit(solution)/shard_map/psum | solution.py:77
  210.9 0.1 mul.176
  211.1 0.8 fusion.34
  211.9 2.6 collective-permute-start.1
  214.5 3.2 collective-permute-start
  217.7 0.2 convolution_bitcast_fusion.5
  217.9 0.5 collective-permute-done
  218.5 3.7 collective-permute-start.2
  222.2 1.3 collective-permute-start.3
  223.5 0.2 convolution_bitcast_fusion.4
  223.7 0.2 convolution_bitcast_fusion.6
  224.0 2.7 collective-permute-done.3
  226.7 0.1 maximum_maximum_fusion
  226.8 0.2 convolution_bitcast_fusion.7
  227.1 0.2 convolution_bitcast_fusion.8
  227.3 0.2 convolution_bitcast_fusion.9
  227.5 0.2 convolution_bitcast_fusion.1
  227.8 0.2 convolution_bitcast_fusion.2
  228.0 0.2 convolution_bitcast_fusion.3
  228.3 1.2 pad_maximum_fusion
  229.5 7.5 %collective-permute-start.5 = (bf16[2,8,1,128]{3,2,1,0:T(2,128)(2,1)S(1)}, bf16[2,8,1,128]{3,2,1,0:T(2,128)(2,1)S(1)}, u32[]{:S(2)}, u32[]{:S(2)}) collective-permute-start(bf16[2,8,1,128]{3,2,1,0:T(2,128)(2,1)S(1)} %get-tuple-element.42), channel_id=1, source_target_pairs={{1,0},{2,1},{3,2},{4,3},{5,4},{6,5},{7,6},{8,7},{9,8},{10,9},{11,1... | collective-permute-start | bytes 12296 | tf_op jit(solution)/shard_map/ppermute | solution.py:21
  237.0 1.9 collective-permute-start.4
  238.9 1.1 collective-permute-done.4
  240.0 1.6 collective-permute-start.6
  241.7 1.3 collective-permute-start.7
  243.0 0.2 convolution_add_fusion.3
  243.3 3.0 collective-permute-done.7
  246.2 0.1 maximum_maximum_fusion.1
  246.3 259.3 %all-reduce.3.cloned.1.call-done = f32[2,3,3,128,128]{4,3,0,2,1:T(8,128)} async-done(((f32[2,3,3,128,128]{4,3,0,2,1:T(8,128)}), f32[2,3,3,128,128]{4,3,0,2,1:T(8,128)}) %all-reduce.3.cloned.1.call-update) | async-done | bytes 1179664 | tf_op jit(solution)/shard_map/psum | solution.py:109
  505.6 1.7 fusion.2
  507.3 0.6 multiply_reduce_fusion
  507.9 0.2 fusion.59
  508.1 0.2 fusion.62
  508.3 0.2 fusion.65
  508.4 0.9 fusion.76
  509.3 0.9 fusion.68
  510.2 0.9 fusion.71
  511.1 0.2 fusion.43
  511.3 0.2 fusion.45
  511.5 0.2 fusion.47
  511.7 0.2 convolution_bitcast_fusion
  511.9 0.2 fusion.53
  512.1 0.2 fusion.55
  512.3 0.2 fusion.49
  512.5 0.2 fusion.51
  512.7 1.1 fusion.41
  514.2 96.3 %all-reduce = (f32[2,32]{1,0:T(2,128)S(1)}, f32[2,32]{1,0:T(2,128)S(1)}, f32[128]{0:T(128)S(1)}, f32[128]{0:T(128)S(1)}) all-reduce(f32[2,32]{1,0:T(2,128)S(1)} %reduce_sum.150, f32[2,32]{1,0:T(2,128)S(1)} %reduce_sum.148, f32[128]{0:T(128)S(1)} %get-tuple-element.22, ...), channel_id=1, replica_groups=mesh['lat'=16,'lon'=32] {'lat','lon'}, use_global_device_ids=true, to_apply=%region_12.13 | all-reduce | flops 384 | bytes 3072 | tf_op jit(solution)/shard_map/psum | solution.py:109
  610.6 0.1 mul.193
  610.8 0.1 sub.39
  610.9 0.9 broadcast_multiply_fusion
  611.8 0.4 fusion.19
  612.2 0.8 copy.35
  613.1 0.5 broadcast_multiply_fusion.5
  613.6 0.5 broadcast_multiply_fusion.4
  614.1 1.7 fusion.40
  615.8 0.2 fusion.75
  616.0 0.2 fusion.9
  616.2 0.9 fusion.20
  (51 shorter events, 1.5 us)
Async XLA Ops:
  7.2 235.8 %copy-start = (f32[512,128]{1,0:T(8,128)S(1)}, f32[512,128]{1,0:T(8,128)}, u32[]{:S(2)}) copy-start(f32[512,128]{1,0:T(8,128)} %param.15) | copy-start | bytes 786436
  7.2 210.5 %copy-start.1 = (bf16[2,8,32,128]{3,2,1,0:T(8,128)(2,1)S(1)}, bf16[2,8,32,128]{3,2,1,0:T(8,128)(2,1)}, u32[]{:S(2)}) copy-start(bf16[2,8,32,128]{3,2,1,0:T(8,128)(2,1)} %param.19) | copy-start | bytes 393220
  7.2 498.4 %all-reduce.3.cloned.1.call-start = ((), (), s32[]{:S(2)}) async-start(), calls=%async_computation | async-start | bytes 2359296 | tf_op jit(solution)/shard_map/psum | solution.py:109
  211.9 6.1 collective-permute-start.1
  214.5 4.0 collective-permute-start
  218.5 5.5 collective-permute-start.2
  222.2 4.5 collective-permute-start.3
  229.4 13.6 %copy-start.7 = (f32[2,512]{1,0:T(2,128)S(1)}, f32[2,512]{1,0:T(2,128)}, u32[]{:S(2)}) copy-start(f32[2,512]{1,0:T(2,128)} %param.14) | copy-start | bytes 12292
  229.4 276.2 %copy-start.3 = (f32[3,3,128,128]{3,2,1,0:T(8,128)S(1)}, f32[3,3,128,128]{3,2,1,0:T(8,128)}, u32[]{:S(2)}) copy-start(f32[3,3,128,128]{3,2,1,0:T(8,128)} %param.16) | copy-start | bytes 1769476
  229.5 9.4 %collective-permute-start.5 = (bf16[2,8,1,128]{3,2,1,0:T(2,128)(2,1)S(1)}, bf16[2,8,1,128]{3,2,1,0:T(2,128)(2,1)S(1)}, u32[]{:S(2)}, u32[]{:S(2)}) collective-permute-start(bf16[2,8,1,128]{3,2,1,0:T(2,128)(2,1)S(1)} %get-tuple-element.42), channel_id=1, source_target_pairs={{1,0},{2,1},{3,2},{4,3},{5,4},{6,5},{7,6},{8,7},{9,8},{10,9},{11,1... | collective-permute-start | bytes 12296 | tf_op jit(solution)/shard_map/ppermute | solution.py:21
  237.0 3.1 collective-permute-start.4
  240.0 3.2 collective-permute-start.6
  241.7 4.5 collective-permute-start.7
  505.6 1.7 copy-start.2
  511.7 1.0 copy-start.8
  511.7 1.0 copy-start.9
  611.8 4.2 copy-start.4
  611.8 4.2 copy-start.5
  611.8 4.2 copy-start.6
Sparse Core Ops, SparseCore 0:
  229.6 275.9 all-reduce.2
where the time goes:
time: 625 us; the launch traced here: 624 us
  blocking collectives  296 us (47%)
  waiting for transfers between devices  267 us (43%)
  starting transfers between devices  23.1 us (4%)
  between operations  14.5 us (2%)
  other arithmetic  11.9 us (2%)
  matrix products  9.69 us (2%)
    psum x1, waiting for transfers between devices, on_device(): lax.psum((local_eff, product_mean_partial, squared_mean_partial, gamma_pa...  259 us
    psum x1, blocking collectives, on_device(): lax.psum(group_count_total(mixed32), ('lat', 'lon')) / cells_per_group  106 us
    psum x1, blocking collectives, on_device(): lax.psum((local_eff, product_mean_partial, squared_mean_partial, gamma_pa...  96.3 us
    psum x1, blocking collectives, on_device(): lax.psum(group_count_total(centered_input * centered_input), ('lat', 'lon'))  93.6 us
    ppermute x4, starting transfers between devices, padded_2(): lax.ppermute(lax.slice_in_dim(block, 0, width, axis=dim), axis, backward)  12.6 us
  transfers between devices with their start and end apart: 9, of which 5 were waited for; matrix products, arithmetic and copies ran while one was open for 0% of the time, Pallas kernels for 0%

commit v1 on v0

v1 whole, which is shorter than its diff:
```python
import math

import jax
import jax.numpy as jnp
from jax import lax
from jax.sharding import Mesh, PartitionSpec as P

GROUPS = 32
LAT = ("zh", "x")
LON = ("zl", "y", "c")
PLANE = ("x", "y")
COLUMN = ("zh", "zl")
F32 = jnp.float32
BF16 = jnp.bfloat16


def shift(block, axes, step, periodic):
    count = lax.axis_size(axes)
    pairs = [(i, i + step) for i in range(count)]
    if periodic:
        pairs = [(source, target % count) for source, target in pairs]
    else:
        pairs = [(source, target) for source, target in pairs if 0 <= target < count]
    return lax.ppermute(block, axes, pairs)


def extend(block, axes, dim, periodic):
    last = block.shape[dim] - 1
    low = shift(lax.slice_in_dim(block, last, last + 1, axis=dim), axes, 1, periodic)
    high = shift(lax.slice_in_dim(block, 0, 1, axis=dim), axes, -1, periodic)
    return jnp.concatenate([low, block, high], axis=dim)


def everyone(row, axes):
    count = lax.axis_size(axes)
    return lax.all_to_all(jnp.broadcast_to(row[None], (count,) + row.shape), axes, 0, 0)


def merge_moments(rows, count):
    mean = jnp.mean(rows[:, :1], axis=0)
    away = rows[:, :1] - mean
    spread = jnp.sum(rows[:, 1:] + count * away * away, axis=0)
    return jnp.concatenate([mean, spread], axis=0)


def two_terms(values):
    high = values.astype(BF16)
    return high, (values - high.astype(F32)).astype(BF16)


def apply_taps(padded, taps, tile_rows, tile_cols):
    total = jnp.zeros(padded.shape[:1] + (tile_rows, tile_cols, taps.shape[4]), F32)
    for row_tap in range(3):
        for col_tap in range(3):
            window = padded[:, row_tap : row_tap + tile_rows, col_tap : col_tap + tile_cols]
            total = total + jnp.einsum(
                "bhwi,bio->bhwo", window, taps[:, row_tap, col_tap], preferred_element_type=F32
            )
    return total


def on_device(
    feats, cond, null_field, drop_flags, emb, style_weight, conv_weight, gamma, beta, cotangent
):
    samples, tile_rows, tile_cols, channels = feats.shape
    group_size = channels // GROUPS
    lat_count, lon_count = lax.axis_size(LAT), lax.axis_size(LON)
    devices_all = lat_count * lon_count
    cells_local = tile_rows * tile_cols * group_size
    cells_per_group = cells_local * devices_all
    scale_gradient = 1.0 / math.sqrt(samples * tile_rows * tile_cols * devices_all)

    def group_total(values):
        return jnp.sum(values, axis=(1, 2)).reshape(samples, GROUPS, group_size).sum(-1)

    def expand(stat):
        return jnp.repeat(stat, group_size, axis=1)[:, None, None, :]

    dropped = drop_flags.astype(F32)[:, None, None, :]
    mixed = (
        feats.astype(F32)
        + dropped * null_field.astype(F32)[None]
        + (1.0 - dropped) * cond.astype(F32)
    ).astype(BF16)
    mixed32 = mixed.astype(F32)
    local_mean = group_total(mixed32) / cells_local
    away = mixed32 - expand(local_mean)
    local_spread = group_total(away * away)
    moments = jnp.stack([local_mean.reshape(-1), local_spread.reshape(-1)])
    moments = merge_moments(everyone(moments, LON), cells_local)
    moments = merge_moments(everyone(moments, LAT), cells_local * lon_count)
    group_mean = moments[0].reshape(samples, GROUPS)
    group_var = moments[1].reshape(samples, GROUPS) / cells_per_group

    both = jnp.stack([mixed, cotangent])
    both = extend(both, LON, 3, True)
    both = extend(both, LAT, 2, False)
    mixed_pad, cot_pad = both[0], both[1]

    style = 1.0 + jnp.dot(emb, style_weight, precision=lax.Precision.HIGHEST)
    power = jnp.sum(conv_weight * conv_weight, axis=(0, 1))
    demod = lax.rsqrt(jnp.dot(style * style, power, precision=lax.Precision.HIGHEST) + 1e-08)
    modded = conv_weight[None] * style[:, None, None, :, None]
    w_eff = (modded * demod[:, None, None, None, :]).astype(BF16)
    back_taps = jnp.swapaxes(w_eff[:, ::-1, ::-1], 3, 4)
    grad_act = apply_taps(cot_pad, back_taps, tile_rows, tile_cols)

    inverse_deviation = expand(lax.rsqrt(group_var + 1e-05))
    mean_all = expand(group_mean)

    def normalize(values):
        return (values.astype(F32) - mean_all) * inverse_deviation

    lat_at = lax.axis_index(LAT)
    row_at = jnp.arange(tile_rows + 2) + lat_at * tile_rows - 1
    inside = ((row_at >= 0) & (row_at < lat_count * tile_rows))[None, :, None, None]
    act_pad = jax.nn.silu(normalize(mixed_pad) * gamma + beta)
    act_pad = jnp.where(inside, act_pad, 0.0).astype(BF16)
    conv_out = apply_taps(act_pad, w_eff, tile_rows, tile_cols)
    block_out = (mixed32 + conv_out).astype(BF16)

    blocks = []
    for row_tap in range(3):
        for col_tap in range(3):
            window = act_pad[:, row_tap : row_tap + tile_rows, col_tap : col_tap + tile_cols]
            blocks.append(jnp.einsum("bhwi,bhwo->bio", window, cotangent, preferred_element_type=F32))
    local_eff = jnp.stack(blocks, axis=1)
    flat_weight = conv_weight.reshape((9, channels, channels))
    scaled = local_eff * demod[:, None, None, :]
    local_weight = jnp.sum(scaled * style[:, None, :, None], axis=0)
    local_style = jnp.sum(scaled * flat_weight[None], axis=(1, 3))
    local_demod = jnp.sum(local_eff * (flat_weight[None] * style[:, None, :, None]), axis=(1, 2))

    normalized = normalize(mixed)
    preactivation = normalized * gamma + beta
    sig = jax.nn.sigmoid(preactivation)
    grad_pre = grad_act * sig * (1.0 + preactivation * (1.0 - sig))
    local_gamma = jnp.sum(grad_pre * normalized, axis=(0, 1, 2))
    local_beta = jnp.sum(grad_pre, axis=(0, 1, 2))
    normalized_gradient = grad_pre * gamma
    local_p = group_total(normalized_gradient)
    local_q = group_total(normalized_gradient * normalized)

    small = jnp.concatenate(
        [
            local_demod.reshape(-1),
            local_style.reshape(-1),
            local_gamma,
            local_beta,
            local_p.reshape(-1),
            local_q.reshape(-1),
        ]
    )
    core_count, plane_count = lax.axis_size("c"), lax.axis_size(PLANE)
    parts = core_count * plane_count
    each = -(-small.shape[0] // parts)
    rows = 9 * channels // parts

    def pack(weight_rows, values):
        room = [(0, 0)] * (values.ndim - 1) + [(0, channels // 2 - each)]
        high, low = two_terms(values)
        extra = jnp.concatenate([jnp.pad(high, room), jnp.pad(low, room)], axis=-1)
        return jnp.concatenate([weight_rows.astype(BF16), extra[..., None, :]], axis=-2)

    def unpack(packed):
        wide = packed.astype(F32)
        half = channels // 2
        return wide[..., :rows, :], wide[..., rows, :each] + wide[..., rows, half : half + each]

    small_parts = jnp.pad(small, (0, each * parts - small.shape[0]))
    payload = pack(
        local_weight.reshape(core_count, plane_count, rows, channels),
        small_parts.reshape(core_count, plane_count, each),
    )
    for axes in ("c", PLANE, COLUMN):
        if axes == COLUMN:
            arrived = everyone(payload, axes)
        else:
            arrived = lax.all_to_all(payload, axes, 0, 0)
        weight_sum, small_sum = unpack(arrived)
        payload = pack(weight_sum.sum(0), small_sum.sum(0))
    payload = lax.all_gather(everyone(payload, PLANE), "c")
    weight_sum, small_sum = unpack(payload)
    weight_sum = weight_sum.reshape(3, 3, channels, channels)
    small_sum = small_sum.reshape(-1)
    cuts = [samples * channels, samples * channels, channels, channels, samples * GROUPS, samples * GROUPS]
    pieces, start = [], 0
    for cut in cuts:
        pieces.append(small_sum[start : start + cut])
        start += cut
    demod_sum = pieces[0].reshape(samples, channels) * demod * demod * demod
    style_sum = pieces[1].reshape(samples, channels)
    shrink = jnp.einsum("bi,bo->io", style * style, demod_sum, precision=lax.Precision.HIGHEST)
    grad_weight = scale_gradient * (weight_sum - shrink * conv_weight)
    grad_style_rows = style_sum - style * jnp.dot(
        demod_sum, power.T, precision=lax.Precision.HIGHEST
    )
    grad_style = scale_gradient * jnp.dot(emb.T, grad_style_rows, precision=lax.Precision.HIGHEST)
    product_mean = pieces[4].reshape(samples, GROUPS) / cells_per_group
    squared_mean = pieces[5].reshape(samples, GROUPS) / cells_per_group
    mixed_gradient = inverse_deviation * (
        normalized_gradient - expand(product_mean) - normalized * expand(squared_mean)
    )
    grad_feats = (cotangent.astype(F32) + mixed_gradient).astype(BF16)
    return (
        block_out,
        grad_feats,
        grad_weight,
        grad_style,
        scale_gradient * pieces[2],
        scale_gradient * pieces[3],
    )


def solution(mesh):
    parts = Mesh(mesh.devices.reshape(4, 4, 2, 8, 2), LAT + LON)
    tile = P(None, LAT, LON, None)
    placed = (tile, tile, P(LAT, LON, None), P(), P(), P(), P(), P(), P(), tile)
    return jax.shard_map(
        on_device,
        mesh=parts,
        in_specs=placed,
        out_specs=(tile, tile, P(), P(), P(), P()),
        check_vma=False,
    )
```

time: 625 us -> 124 us (0.20)
  blocking collectives: 296 us -> 12 us
  waiting for transfers between devices: 267 us -> 32.2 us
  starting transfers between devices: 23.1 us -> 50.4 us
  between operations: 14.5 us -> 1.37 us
    psum x3 -> x0, blocking collectives: 296 us -> none  [the longest x1 106 us: on_device(): lax.psum(group_count_total(mixed32), ('lat', 'lon')) / cells_per_group]
    psum x1 -> x0, waiting for transfers between devices: 259 us -> none  [on_device(): lax.psum((local_eff, product_mean_partial, squared_mean_partial, gamma_pa...]
    all_to_all x0 -> x5, starting transfers between devices: none -> 40.5 us  [the longest x4 33.7 us: everyone(): lax.all_to_all(jnp.broadcast_to(row[None], (count,) + row.shape), axes, 0...]
    all_to_all x0 -> x5, waiting for transfers between devices: none -> 29.9 us  [the longest x4 21.4 us: everyone(): lax.all_to_all(jnp.broadcast_to(row[None], (count,) + row.shape), axes, 0...]
    ppermute x8 -> x4, starting transfers between devices: 23.1 us -> 9.87 us  [shift(): return lax.ppermute(block, axes, pairs)]
    all_to_all x0 -> x1, blocking collectives: none -> 6.34 us  [on_device(): arrived = lax.all_to_all(payload, axes, 0, 0)]
  transfers between devices with their start and end apart: 9 -> 9, of which waited for: 5 -> 5; matrix products, arithmetic and copies ran while one was open for 0% -> 6% of each run, Pallas kernels for 0% -> 0%
where the time goes in v1:
time: 124 us; the launch traced here: 123 us
  starting transfers between devices  50.4 us (41%)
  waiting for transfers between devices  32.2 us (26%)
  blocking collectives  12 us (10%)
  other arithmetic  9.68 us (8%)
  matrix products  9.02 us (7%)
  local copies, waits for them, and re-layouts  8.28 us (7%)
  between operations  1.37 us (1%)
    all_to_all x4, starting transfers between devices, everyone(): lax.all_to_all(jnp.broadcast_to(row[None], (count,) + row.shape), axes, 0...  33.7 us
    all_to_all x4, waiting for transfers between devices, everyone(): lax.all_to_all(jnp.broadcast_to(row[None], (count,) + row.shape), axes, 0...  21.4 us
    ppermute x4, starting transfers between devices, shift(): return lax.ppermute(block, axes, pairs)  9.87 us
    all_to_all x1, waiting for transfers between devices, on_device(): arrived = lax.all_to_all(payload, axes, 0, 0)  8.48 us
    all_to_all x1, starting transfers between devices, on_device(): arrived = lax.all_to_all(payload, axes, 0, 0)  6.83 us
    all_to_all x1, blocking collectives, on_device(): arrived = lax.all_to_all(payload, axes, 0, 0)  6.34 us
    all_gather x1, blocking collectives, on_device(): payload = lax.all_gather(everyone(payload, PLANE), 'c')  5.71 us
    dot_general x18, matrix products, apply_taps(): jnp.einsum('bhwi,bio->bhwo', window, taps[:, row_tap, col_tap], preferred...  5.68 us
  transfers between devices with their start and end apart: 9, of which 5 were waited for; matrix products, arithmetic and copies ran while one was open for 6% of the time, Pallas kernels for 0%

profile of v1, /device:TPU:1, one launch (start us, length us, event | category | flops | bytes accessed | tf_op | source)
XLA Modules:
  0.0 123.0 jit_solution(13518912811032503174)
XLA Ops:
  0.7 0.8 broadcast_subtract_fusion
  1.4 0.7 convert_element_type.115
  2.1 0.8 convert_element_type.116
  3.0 1.1 convert_reduce_fusion
  4.9 0.7 reshape.191
  5.6 10.6 %all-to-all-start = ((f32[32,1,128]{2,1,0:T(1,128)}), f32[32,1,128]{2,1,0:T(1,128)S(1)}, u32[]{:S(2)}, u32[]{:S(2)}) async-start(f32[32,1,128]{2,1,0:T(1,128)} %reshape.191), calls=%async_computation | async-start | bytes 32768 | tf_op jit(solution)/shard_map/all_to_all | solution.py:36
  16.2 3.5 %collective-permute-start = (bf16[2,2,8,1,128]{4,3,2,1,0:T(2,128)(2,1)S(1)}, bf16[2,2,8,1,128]{4,3,2,1,0:T(2,128)(2,1)S(1)}, u32[]{:S(2)}, u32[]{:S(2)}) collective-permute-start(bf16[2,2,8,1,128]{4,3,2,1,0:T(2,128)(2,1)S(1)} %get-tuple-element.69), channel_id=1, source_target_pairs={{0,1},{1,2},{2,3},{3,4},{4,5},{5,6},{6,7},{7,8},{8,9},{9,10},{10,1... | collective-permute-start | bytes 24584 | tf_op jit(solution)/shard_map/ppermute | solution.py:24
  19.8 1.9 %collective-permute-start.1 = (bf16[2,2,8,1,128]{4,3,2,1,0:T(2,128)(2,1)S(1)}, bf16[2,2,8,1,128]{4,3,2,1,0:T(2,128)(2,1)S(1)}, u32[]{:S(2)}, u32[]{:S(2)}) collective-permute-start(bf16[2,2,8,1,128]{4,3,2,1,0:T(2,128)(2,1)S(1)} %get-tuple-element.70), channel_id=1, source_target_pairs={{0,31},{1,0},{2,1},{3,2},{4,3},{5,4},{6,5},{7,6},{8,7},{9,8},{10,9... | collective-permute-start | bytes 24584 | tf_op jit(solution)/shard_map/ppermute | solution.py:24
  21.8 0.2 convolution_add_fusion.17
  22.2 0.3 multiply_convert_fusion
  22.5 2.3 %collective-permute-done.1 = bf16[2,2,8,1,128]{4,3,2,1,0:T(2,128)(2,1)S(1)} collective-permute-done((bf16[2,2,8,1,128]{4,3,2,1,0:T(2,128)(2,1)S(1)}, bf16[2,2,8,1,128]{4,3,2,1,0:T(2,128)(2,1)S(1)}, u32[]{:S(2)}, u32[]{:S(2)}) %collective-permute-start.1) | collective-permute-done | bytes 8224 | tf_op jit(solution)/shard_map/ppermute | solution.py:24
  24.9 3.1 %collective-permute-start.2 = (bf16[2,2,1,34,128]{4,3,2,1,0:T(8,128)(2,1)S(1)}, bf16[2,2,1,34,128]{4,3,2,1,0:T(8,128)(2,1)S(1)}, u32[]{:S(2)}, u32[]{:S(2)}) collective-permute-start(bf16[2,2,1,34,128]{4,3,2,1,0:T(8,128)(2,1)S(1)} %get-tuple-element.67), channel_id=1, source_target_pairs={{0,32},{32,64},{64,96},{96,128},{128,160},{160,192},{192,224},{224... | collective-permute-start | bytes 104456 | tf_op jit(solution)/shard_map/ppermute | solution.py:24
  28.0 1.3 %collective-permute-start.3 = (bf16[2,2,1,34,128]{4,3,2,1,0:T(8,128)(2,1)S(1)}, bf16[2,2,1,34,128]{4,3,2,1,0:T(8,128)(2,1)S(1)}, u32[]{:S(2)}, u32[]{:S(2)}) collective-permute-start(bf16[2,2,1,34,128]{4,3,2,1,0:T(8,128)(2,1)S(1)} %get-tuple-element.68), channel_id=1, source_target_pairs={{32,0},{64,32},{96,64},{128,96},{160,128},{192,160},{224,192},{256... | collective-permute-start | bytes 104456 | tf_op jit(solution)/shard_map/ppermute | solution.py:24
  29.3 0.5 broadcast.157
  29.8 0.7 reduce.7
  30.7 0.7 reshape.193
  31.4 14.3 %all-to-all-start.1 = ((f32[16,1,128]{2,1,0:T(1,128)}), f32[16,1,128]{2,1,0:T(1,128)S(1)}, u32[]{:S(2)}, u32[]{:S(2)}) async-start(f32[16,1,128]{2,1,0:T(1,128)} %reshape.193), calls=%async_computation.1 | async-start | bytes 16384 | tf_op jit(solution)/shard_map/all_to_all | solution.py:36
  45.9 0.2 fusion.54
  46.1 0.2 convolution_add_fusion.7
  46.3 0.2 convolution_add_fusion.6
  46.5 0.2 convolution_add_fusion.5
  46.7 0.2 convolution_add_fusion.4
  46.9 0.2 convolution_add_fusion.3
  47.1 0.2 convolution_add_fusion.2
  47.3 0.9 convolution_add_fusion.1
  48.2 6.2 %all-to-all-done.1 = f32[16,1,128]{2,1,0:T(1,128)S(1)} async-done(((f32[16,1,128]{2,1,0:T(1,128)}), f32[16,1,128]{2,1,0:T(1,128)S(1)}, u32[]{:S(2)}, u32[]{:S(2)}) %all-to-all-start.1) | async-done | bytes 8224 | tf_op jit(solution)/shard_map/all_to_all | solution.py:36
  54.4 0.7 reduce.8
  55.8 0.2 fusion.25
  56.0 0.2 fusion.13
  56.3 0.2 fusion.12
  56.5 0.2 fusion.11
  56.7 0.2 fusion.10
  57.0 0.2 fusion.9
  57.2 0.2 fusion.8
  57.4 0.2 fusion.7
  57.7 0.2 fusion.6
  57.9 0.2 fusion.5
  58.1 0.4 multiply_reduce_fusion
  58.7 1.2 %fusion.41 = (f32[2,128]{1,0:T(2,128)S(1)}, f32[128]{0:T(128)S(1)}, f32[2,128]{1,0:T(2,128)S(1)}, f32[128]{0:T(128)S(1)}, f32[2,8,32,128]{3,2,1,0:T(8,128)S(1)}) fusion(bf16[2,8,32,128]{3,2,1,0:T(8,128)(2,1)S(1)} %get-tuple-element.66, f32[128]{0:T(128)S(1)} %copy-done.4, f32[2,128]{1,0:T(2,128)S(1)} %sub.96, f32[2,128]{1,0:T(2,128)S(1)} %mul.244, ...), kind=kOutput, calls=%fused_computation.85 | convolution fusion | flops 18152704 | bytes 858112 | tf_op jit(solution)/shard_map/bhwi,bio->bhwo/dot_general | solution.py:56
  61.0 6.3 %all_to_all.30 = bf16[2,32,19,128]{3,1,2,0:T(8,128)(2,1)S(1)} all-to-all(bf16[2,32,19,128]{3,1,2,0:T(8,128)(2,1)S(1)} %copy.134), channel_id=1, replica_groups=mesh['zh'=4,'x'=4,'zl'=2,'y'=8,'c'=2] {'c'}, dimensions={0} | all-to-all | bytes 622592 | tf_op jit(solution)/shard_map/all_to_all | solution.py:179
  67.8 0.7 copy.135
  68.6 6.8 %all-to-all-start.3 = ((bf16[32,19,128]{2,1,0:T(8,128)(2,1)}), bf16[32,19,128]{2,1,0:T(8,128)(2,1)S(1)}, u32[]{:S(2)}, u32[]{:S(2)}) async-start(bf16[32,19,128]{2,1,0:T(8,128)(2,1)} %copy.135), calls=%async_computation.3 | async-start | bytes 393216 | tf_op jit(solution)/shard_map/all_to_all | solution.py:179
  75.6 0.2 convolution_add_fusion.14
  75.8 0.2 convolution_add_fusion.13
  76.0 0.2 convolution_add_fusion.12
  76.1 0.2 convolution_add_fusion.11
  76.3 8.5 %all-to-all-done.3 = bf16[32,19,128]{2,1,0:T(8,128)(2,1)S(1)} async-done(((bf16[32,19,128]{2,1,0:T(8,128)(2,1)}), bf16[32,19,128]{2,1,0:T(8,128)(2,1)S(1)}, u32[]{:S(2)}, u32[]{:S(2)}) %all-to-all-start.3) | async-done | bytes 155680 | tf_op jit(solution)/shard_map/all_to_all | solution.py:179
  85.1 0.6 broadcast_in_dim.48
  85.7 3.3 %all-to-all-start.4 = ((bf16[8,19,128]{2,1,0:T(8,128)(2,1)}), bf16[8,19,128]{2,1,0:T(8,128)(2,1)S(1)}, u32[]{:S(2)}, u32[]{:S(2)}) async-start(bf16[8,19,128]{2,1,0:T(8,128)(2,1)} %broadcast_in_dim.48), calls=%async_computation.4 | async-start | bytes 98304 | tf_op jit(solution)/shard_map/all_to_all | solution.py:36
  89.1 0.2 convolution_add_fusion.10
  89.3 6.8 %all-to-all-done.4 = bf16[8,19,128]{2,1,0:T(8,128)(2,1)S(1)} async-done(((bf16[8,19,128]{2,1,0:T(8,128)(2,1)}), bf16[8,19,128]{2,1,0:T(8,128)(2,1)S(1)}, u32[]{:S(2)}, u32[]{:S(2)}) %all-to-all-start.4) | async-done | bytes 38944 | tf_op jit(solution)/shard_map/all_to_all | solution.py:36
  96.3 0.7 broadcast_in_dim.92
  97.0 5.5 %all-to-all-start.5 = ((bf16[32,19,128]{2,1,0:T(8,128)(2,1)}), bf16[32,19,128]{2,1,0:T(8,128)(2,1)S(1)}, u32[]{:S(2)}, u32[]{:S(2)}) async-start(bf16[32,19,128]{2,1,0:T(8,128)(2,1)} %broadcast_in_dim.92), calls=%async_computation.5 | async-start | bytes 393216 | tf_op jit(solution)/shard_map/all_to_all | solution.py:36
  102.6 0.8 fusion.4
  103.5 8.4 %all-to-all-done.5 = bf16[32,19,128]{2,1,0:T(8,128)(2,1)S(1)} async-done(((bf16[32,19,128]{2,1,0:T(8,128)(2,1)}), bf16[32,19,128]{2,1,0:T(8,128)(2,1)S(1)}, u32[]{:S(2)}, u32[]{:S(2)}) %all-to-all-start.5) | async-done | bytes 155680 | tf_op jit(solution)/shard_map/all_to_all | solution.py:36
  111.9 5.7 %all-gather = bf16[64,19,128]{2,0,1:T(8,128)(2,1)S(1)} all-gather(bf16[32,19,128]{2,0,1:T(8,128)(2,1)S(1)} %copy.138), channel_id=2, replica_groups=mesh['zh'=4,'x'=4,'zl'=2,'y'=8,'c'=2] {'c'}, dimensions={0}, use_global_device_ids=true | all-gather | bytes 466944 | tf_op jit(solution)/shard_map/all_gather | solution.py:182
  118.0 0.3 fusion.89
  118.2 0.2 fusion.15
  118.7 0.4 copy.139
  119.1 0.4 fusion.3
  119.6 0.8 copy.140
  120.8 0.5 slice_multiply_fusion.2
  121.3 0.9 subtract_multiply_fusion
  122.2 0.8 fusion.45
  (104 shorter events, 5.7 us)
Async XLA Ops:
  0.6 21.1 %copy-start = (f32[512,128]{1,0:T(8,128)S(1)}, f32[512,128]{1,0:T(8,128)}, u32[]{:S(2)}) copy-start(f32[512,128]{1,0:T(8,128)} %param.15) | copy-start | bytes 786436
  0.6 15.5 %copy-start.2 = (bf16[2,8,32,128]{3,2,1,0:T(8,128)(2,1)S(1)}, bf16[2,8,32,128]{3,2,1,0:T(8,128)(2,1)}, u32[]{:S(2)}) copy-start(bf16[2,8,32,128]{3,2,1,0:T(8,128)(2,1)} %param.19) | copy-start | bytes 393220
  0.7 21.0 %copy-start.1 = (f32[3,3,128,128]{3,2,1,0:T(8,128)S(1)}, f32[3,3,128,128]{3,2,1,0:T(8,128)}, u32[]{:S(2)}) copy-start(f32[3,3,128,128]{3,2,1,0:T(8,128)} %param.16) | copy-start | bytes 1769476
  0.7 21.1 %copy-start.3 = (f32[2,512]{1,0:T(2,128)S(1)}, f32[2,512]{1,0:T(2,128)}, u32[]{:S(2)}) copy-start(f32[2,512]{1,0:T(2,128)} %param.14) | copy-start | bytes 12292
  5.6 23.7 %all-to-all-start = ((f32[32,1,128]{2,1,0:T(1,128)}), f32[32,1,128]{2,1,0:T(1,128)S(1)}, u32[]{:S(2)}, u32[]{:S(2)}) async-start(f32[32,1,128]{2,1,0:T(1,128)} %reshape.191), calls=%async_computation | async-start | bytes 32768 | tf_op jit(solution)/shard_map/all_to_all | solution.py:36
  16.2 6.3 %collective-permute-start = (bf16[2,2,8,1,128]{4,3,2,1,0:T(2,128)(2,1)S(1)}, bf16[2,2,8,1,128]{4,3,2,1,0:T(2,128)(2,1)S(1)}, u32[]{:S(2)}, u32[]{:S(2)}) collective-permute-start(bf16[2,2,8,1,128]{4,3,2,1,0:T(2,128)(2,1)S(1)} %get-tuple-element.69), channel_id=1, source_target_pairs={{0,1},{1,2},{2,3},{3,4},{4,5},{5,6},{6,7},{7,8},{8,9},{9,10},{10,1... | collective-permute-start | bytes 24584 | tf_op jit(solution)/shard_map/ppermute | solution.py:24
  19.8 5.1 %collective-permute-start.1 = (bf16[2,2,8,1,128]{4,3,2,1,0:T(2,128)(2,1)S(1)}, bf16[2,2,8,1,128]{4,3,2,1,0:T(2,128)(2,1)S(1)}, u32[]{:S(2)}, u32[]{:S(2)}) collective-permute-start(bf16[2,2,8,1,128]{4,3,2,1,0:T(2,128)(2,1)S(1)} %get-tuple-element.70), channel_id=1, source_target_pairs={{0,31},{1,0},{2,1},{3,2},{4,3},{5,4},{6,5},{7,6},{8,7},{9,8},{10,9... | collective-permute-start | bytes 24584 | tf_op jit(solution)/shard_map/ppermute | solution.py:24
  24.9 20.8 %collective-permute-start.2 = (bf16[2,2,1,34,128]{4,3,2,1,0:T(8,128)(2,1)S(1)}, bf16[2,2,1,34,128]{4,3,2,1,0:T(8,128)(2,1)S(1)}, u32[]{:S(2)}, u32[]{:S(2)}) collective-permute-start(bf16[2,2,1,34,128]{4,3,2,1,0:T(8,128)(2,1)S(1)} %get-tuple-element.67), channel_id=1, source_target_pairs={{0,32},{32,64},{64,96},{96,128},{128,160},{160,192},{192,224},{224... | collective-permute-start | bytes 104456 | tf_op jit(solution)/shard_map/ppermute | solution.py:24
  28.0 17.7 %collective-permute-start.3 = (bf16[2,2,1,34,128]{4,3,2,1,0:T(8,128)(2,1)S(1)}, bf16[2,2,1,34,128]{4,3,2,1,0:T(8,128)(2,1)S(1)}, u32[]{:S(2)}, u32[]{:S(2)}) collective-permute-start(bf16[2,2,1,34,128]{4,3,2,1,0:T(8,128)(2,1)S(1)} %get-tuple-element.68), channel_id=1, source_target_pairs={{32,0},{64,32},{96,64},{128,96},{160,128},{192,160},{224,192},{256... | collective-permute-start | bytes 104456 | tf_op jit(solution)/shard_map/ppermute | solution.py:24
  31.4 23.0 %all-to-all-start.1 = ((f32[16,1,128]{2,1,0:T(1,128)}), f32[16,1,128]{2,1,0:T(1,128)S(1)}, u32[]{:S(2)}, u32[]{:S(2)}) async-start(f32[16,1,128]{2,1,0:T(1,128)} %reshape.193), calls=%async_computation.1 | async-start | bytes 16384 | tf_op jit(solution)/shard_map/all_to_all | solution.py:36
  46.9 8.9 %copy-start.4 = (f32[128]{0:T(128)S(1)}, f32[128]{0:T(128)}, u32[]{:S(2)}) copy-start(f32[128]{0:T(128)} %param.17) | copy-start | bytes 1540
  46.9 8.9 %copy-start.5 = (f32[128]{0:T(128)S(1)}, f32[128]{0:T(128)}, u32[]{:S(2)}) copy-start(f32[128]{0:T(128)} %param.18) | copy-start | bytes 1540
  68.6 16.2 %all-to-all-start.3 = ((bf16[32,19,128]{2,1,0:T(8,128)(2,1)}), bf16[32,19,128]{2,1,0:T(8,128)(2,1)S(1)}, u32[]{:S(2)}, u32[]{:S(2)}) async-start(bf16[32,19,128]{2,1,0:T(8,128)(2,1)} %copy.135), calls=%async_computation.3 | async-start | bytes 393216 | tf_op jit(solution)/shard_map/all_to_all | solution.py:179
  85.7 10.3 %all-to-all-start.4 = ((bf16[8,19,128]{2,1,0:T(8,128)(2,1)}), bf16[8,19,128]{2,1,0:T(8,128)(2,1)S(1)}, u32[]{:S(2)}, u32[]{:S(2)}) async-start(bf16[8,19,128]{2,1,0:T(8,128)(2,1)} %broadcast_in_dim.48), calls=%async_computation.4 | async-start | bytes 98304 | tf_op jit(solution)/shard_map/all_to_all | solution.py:36
  97.0 14.9 %all-to-all-start.5 = ((bf16[32,19,128]{2,1,0:T(8,128)(2,1)}), bf16[32,19,128]{2,1,0:T(8,128)(2,1)S(1)}, u32[]{:S(2)}, u32[]{:S(2)}) async-start(bf16[32,19,128]{2,1,0:T(8,128)(2,1)} %broadcast_in_dim.92), calls=%async_computation.5 | async-start | bytes 393216 | tf_op jit(solution)/shard_map/all_to_all | solution.py:36

commit v2 on v1

v2 whole, which is shorter than its diff:
```python
import functools
import math

import jax
import jax.numpy as jnp
from jax import lax
from jax.experimental import pallas as pl
from jax.experimental.pallas import tpu as pltpu
from jax.sharding import Mesh, PartitionSpec as P

GROUPS = 32
LAT = ("zh", "x")
LON = ("zl", "y", "c")
NEAR = ("zl", "y")
F32 = jnp.float32
BF16 = jnp.bfloat16
TILE = 8
SHARDS = 32
SLOT = 40
LANES = 128


def shift(block, axes, step, periodic):
    count = lax.axis_size(axes)
    pairs = [(i, i + step) for i in range(count)]
    if periodic:
        pairs = [(source, target % count) for source, target in pairs]
    else:
        pairs = [(source, target) for source, target in pairs if 0 <= target < count]
    return lax.ppermute(block, axes, pairs)


def extend(block, axes, dim, periodic):
    last = block.shape[dim] - 1
    low = shift(lax.slice_in_dim(block, last, last + 1, axis=dim), axes, 1, periodic)
    high = shift(lax.slice_in_dim(block, 0, 1, axis=dim), axes, -1, periodic)
    return jnp.concatenate([low, block, high], axis=dim)


def exchange(block, axes):
    return lax.all_to_all(block, axes, 0, 0)


def everyone(block, axes):
    return exchange(jnp.broadcast_to(block[None], (lax.axis_size(axes),) + block.shape), axes)


def call(body, outputs, scratch=()):
    return pl.pallas_call(
        body,
        out_shape=outputs,
        scratch_shapes=list(scratch),
        compiler_params=pltpu.CompilerParams(vmem_limit_bytes=48 * 1024 * 1024),
    )


def array(shape, dtype=F32):
    return jax.ShapeDtypeStruct(shape, dtype)


def lanes_of(rows=1):
    return lax.broadcasted_iota(jnp.int32, (rows, LANES), 1)


def group_total(row):
    lane = lanes_of()
    for step in (1, 2):
        after, before = pltpu.roll(row, LANES - step, 1), pltpu.roll(row, step, 1)
        row = row + jnp.where((lane & step) == 0, after, before)
    return row


def weave(first, second):
    return jnp.where((lanes_of() & 1) == 0, first, second)


def unweave(row, sample):
    if sample == 0:
        return weave(row, pltpu.roll(row, 1, 1))
    return weave(pltpu.roll(row, LANES - 1, 1), row)


def mix_body(feats, cond, null, flags, mixed_out, moments_out):
    samples, tile_rows, tile_cols, channels = feats.shape
    cells = tile_rows * tile_cols
    null32 = null[...].astype(F32)
    means, spreads = [], []
    for sample in range(samples):
        dropped = flags[sample : sample + 1, :].astype(F32).reshape(1, 1, channels)
        mixed = (
            feats[sample].astype(F32) + dropped * null32 + (1.0 - dropped) * cond[sample].astype(F32)
        ).astype(BF16)
        mixed_out[sample] = mixed
        wide = mixed.astype(F32).reshape(cells, channels)
        size = cells * (channels // GROUPS)
        mean = group_total(jnp.sum(wide, axis=0, keepdims=True)) * (1.0 / size)
        away = wide - mean
        means.append(mean)
        spreads.append(group_total(jnp.sum(away * away, axis=0, keepdims=True)))
    row = jnp.concatenate([weave(*means), weave(*spreads)], axis=0)
    moments_out[...] = jnp.broadcast_to(row[None], moments_out.shape)


def merged(rows, count):
    mean = jnp.mean(rows[:, 0:1, :], axis=0)
    away = rows[:, 0:1, :] - mean[None]
    spread = jnp.sum(rows[:, 1:2, :] + count * away * away, axis=0)
    return mean, spread


def merge_body(count, rows, moments_out):
    row = jnp.concatenate(merged(rows[...], count), axis=0)
    moments_out[...] = jnp.broadcast_to(row[None], moments_out.shape)


def sums_body(
    count, cells, rows, padded, mixed, cotangent, grad_act, affine, keep, style_col, demod, weight,
    stats_out, payload_out, act, shifted, total,
):
    samples, tile_rows, tile_cols, channels = cotangent.shape
    size = tile_rows * tile_cols
    mean_all, spread_all = merged(rows[...], count)
    inverse_all = lax.rsqrt(spread_all * (1.0 / cells) + 1e-05)
    gamma, beta = affine[0:1, :], affine[1:2, :]
    sums = [[], [], [], []]
    for sample in range(samples):
        mean, inverse = unweave(mean_all, sample), unweave(inverse_all, sample)
        stats_out[sample : sample + 1, :] = mean
        stats_out[samples + sample : samples + sample + 1, :] = inverse
        around = (padded[sample].astype(F32) - mean[None]) * inverse[None]
        around = around * gamma[None] + beta[None]
        act[...] = around / (1.0 + jnp.exp(-around))
        for side, at in ((0, 0), (1, tile_rows + 1)):
            act[at] = jnp.where(keep[side : side + 1, :] > 0.0, act[at], 0.0)
        for tap in range(3):
            moved = act[:, tap : tap + tile_cols, :].reshape(-1, channels)
            shifted[:, tap * channels : (tap + 1) * channels] = moved.astype(BF16)
        flat_cot = cotangent[sample].reshape(size, channels)
        style_full = jnp.broadcast_to(style_col[:, sample : sample + 1], (channels, channels))
        demod_row = demod[sample : sample + 1, :]
        both = style_full * demod_row
        product = jnp.zeros((channels, channels), F32)
        for row_tap in range(3):
            window = shifted[row_tap * tile_cols : row_tap * tile_cols + size, :]
            grad = lax.dot_general(
                window, flat_cot, (((0,), (0,)), ((), ())), preferred_element_type=F32
            )
            for col_tap in range(3):
                tap = row_tap * 3 + col_tap
                block = grad[col_tap * channels : (col_tap + 1) * channels, :]
                product = product + block * weight[tap]
                here = slice(tap * channels, (tap + 1) * channels)
                part = block * both
                total[here, :] = part if sample == 0 else total[here, :] + part
        sums[0].append(jnp.sum(product * style_full, axis=0, keepdims=True))
        sums[1].append(jnp.sum((product * demod_row).T, axis=0, keepdims=True))
        normalized = (mixed[sample].reshape(size, channels).astype(F32) - mean) * inverse
        pre = normalized * gamma + beta
        sig = 1.0 / (1.0 + jnp.exp(-pre))
        grad_pre = grad_act[sample].reshape(size, channels) * (sig * (1.0 + pre * (1.0 - sig)))
        sums[2].append(jnp.sum(grad_pre * normalized, axis=0, keepdims=True))
        sums[3].append(jnp.sum(grad_pre, axis=0, keepdims=True))
    small = jnp.concatenate(sum(sums, []), axis=0)
    lane = lanes_of(TILE)
    sub = lax.broadcasted_iota(jnp.int32, (TILE, channels), 0)
    quarters = []
    for quarter in range(4):
        turned = pltpu.roll(small, LANES - 32 * quarter, 1) if quarter else small
        piece = jnp.where(lane < 64, turned, pltpu.roll(turned, 64, 1))
        piece = jnp.where((lane & 32) == 0, piece, 0.0)
        quarters.append(split_terms(piece, lane))
    for shard in range(SHARDS):
        main = total[32 * shard : 32 * shard + 32, :]
        start = 8 * channels + 8 * (shard // 2)
        last = total[start : start + 8, :]
        if shard % 2:
            last = pltpu.roll(last, 4, 0)
        extra = quarters[shard % 4][shard // 4 : shard // 4 + 1, :]
        tail = jnp.where(sub < 4, last, jnp.where(sub == 4, extra, 0.0))
        payload_out[shard] = jnp.concatenate([main, tail], axis=0).astype(BF16)


def split_terms(values, lane):
    high = values.astype(BF16).astype(F32)
    return jnp.where(lane < 64, high, values - high)


def resplit(slots):
    row = lax.broadcasted_iota(jnp.int32, slots.shape, slots.ndim - 2)
    lane = lax.broadcasted_iota(jnp.int32, slots.shape, slots.ndim - 1)
    joined = slots + jnp.roll(slots, 64, slots.ndim - 1)
    high = lax.reduce_precision(joined, 8, 7)
    terms = jnp.where(lane < 64, high, joined - high)
    return jnp.where(row == 36, terms, slots).astype(BF16)


def last_body(
    scale, cells, gathered, stats, mixed, cotangent, grad_act, affine, style, style_col, demod,
    power, weight, emb_col, feats_out, weight_out, style_out, affine_out,
):
    samples, tile_rows, tile_cols, channels = cotangent.shape
    size = tile_rows * tile_cols
    lane = lanes_of()
    sub = lax.broadcasted_iota(jnp.int32, (TILE, channels), 0)
    main, tails, small = [], [], []
    for shard in range(SHARDS):
        slot = gathered[shard].astype(F32)
        main.append(slot[0:32, :])
        tails.append(slot[32:40, :])
    for row in range(TILE):
        whole = jnp.zeros((1, channels), F32)
        for quarter in range(4):
            piece = tails[4 * row + quarter][4:5, :]
            piece = piece + pltpu.roll(piece, 64, 1)
            if quarter:
                piece = pltpu.roll(piece, 32 * quarter, 1)
            whole = jnp.where((lane >> 5) == quarter, piece, whole)
        small.append(whole)
    demod_sums, style_sums, gamma_sums, beta_sums = small[0:2], small[2:4], small[4:6], small[6:8]
    gamma, beta = affine[0:1, :], affine[1:2, :]
    affine_out[0:1, :] = scale * (gamma_sums[0] + gamma_sums[1])
    affine_out[1:2, :] = scale * (beta_sums[0] + beta_sums[1])
    shrink = jnp.zeros((channels, channels), F32)
    rows = []
    for sample in range(samples):
        demod_row = demod[sample : sample + 1, :]
        pulled = demod_sums[sample] * (demod_row * demod_row * demod_row)
        style_full = jnp.broadcast_to(style_col[:, sample : sample + 1], (channels, channels))
        shrink = shrink + style_full * style_full * pulled
        spent = jnp.sum((power[...] * pulled).T, axis=0, keepdims=True)
        rows.append(style_sums[sample] - style[sample : sample + 1, :] * spent)
    for tap in range(8):
        for part in range(4):
            here = slice(32 * part, 32 * part + 32)
            weight_out[tap, here, :] = scale * (
                main[4 * tap + part] - shrink[here, :] * weight[tap, here, :]
            )
    for pair in range(16):
        here = slice(8 * pair, 8 * pair + 8)
        block = jnp.where(sub < 4, tails[2 * pair], pltpu.roll(tails[2 * pair + 1], 4, 0))
        weight_out[8, here, :] = scale * (block - shrink[here, :] * weight[8, here, :])
    style_out[...] = scale * (emb_col[:, 0:1] * rows[0] + emb_col[:, 1:2] * rows[1])
    for sample in range(samples):
        mean = stats[sample : sample + 1, :]
        inverse = stats[samples + sample : samples + sample + 1, :]
        product_mean = group_total(gamma * beta_sums[sample]) * (1.0 / cells)
        squared_mean = group_total(gamma * gamma_sums[sample]) * (1.0 / cells)
        normalized = (mixed[sample].reshape(size, channels).astype(F32) - mean) * inverse
        pre = normalized * gamma + beta
        sig = 1.0 / (1.0 + jnp.exp(-pre))
        grad_pre = grad_act[sample].reshape(size, channels) * (sig * (1.0 + pre * (1.0 - sig)))
        change = inverse * (gamma * grad_pre - product_mean - normalized * squared_mean)
        out = cotangent[sample].reshape(size, channels).astype(F32) + change
        feats_out[sample] = out.astype(BF16).reshape(tile_rows, tile_cols, channels)


def apply_taps(padded, taps, tile_rows, tile_cols):
    total = jnp.zeros(padded.shape[:1] + (tile_rows, tile_cols, taps.shape[4]), F32)
    for row_tap in range(3):
        for col_tap in range(3):
            window = padded[:, row_tap : row_tap + tile_rows, col_tap : col_tap + tile_cols]
            total = total + jnp.einsum(
                "bhwi,bio->bhwo", window, taps[:, row_tap, col_tap], preferred_element_type=F32
            )
    return total


def on_device(
    feats, cond, null_field, drop_flags, emb, style_weight, conv_weight, gamma, beta, cotangent
):
    samples, tile_rows, tile_cols, channels = feats.shape
    group_size = channels // GROUPS
    lat_count, lon_count = lax.axis_size(LAT), lax.axis_size(LON)
    devices_all = lat_count * lon_count
    cells_local = tile_rows * tile_cols * group_size
    cells_per_group = cells_local * devices_all
    scale_gradient = 1.0 / math.sqrt(samples * tile_rows * tile_cols * devices_all)
    taps = conv_weight.reshape(9, channels, channels)

    mixed, moments = call(
        mix_body, (array(feats.shape, BF16), array((lon_count, 2, LANES)))
    )(feats, cond, null_field, drop_flags)
    moments = exchange(moments, LON)
    both = extend(jnp.stack([mixed, cotangent]), LON, 3, True)
    moments = call(
        functools.partial(merge_body, cells_local), array((lat_count, 2, LANES))
    )(moments)
    both, moments = lax.optimization_barrier((both, moments))
    moments = exchange(moments, LAT)
    both = extend(both, LAT, 2, False)
    mixed_pad, cot_pad = both[0], both[1]

    style = 1.0 + jnp.dot(emb, style_weight, precision=lax.Precision.HIGHEST)
    power = jnp.sum(conv_weight * conv_weight, axis=(0, 1))
    demod = lax.rsqrt(jnp.dot(style * style, power, precision=lax.Precision.HIGHEST) + 1e-08)
    modded = conv_weight[None] * style[:, None, None, :, None]
    w_eff = (modded * demod[:, None, None, None, :]).astype(BF16)
    back_taps = jnp.swapaxes(w_eff[:, ::-1, ::-1], 3, 4)
    grad_act = apply_taps(cot_pad, back_taps, tile_rows, tile_cols)

    lat_at = lax.axis_index(LAT)
    inside = jnp.stack([lat_at > 0, lat_at < lat_count - 1])
    keep = jnp.broadcast_to(inside.astype(F32)[:, None], (2, LANES))
    affine = jnp.stack([gamma, beta])
    style_col = style.T
    stats, payload = call(
        functools.partial(sums_body, cells_local * lon_count, cells_per_group),
        (array((2 * samples, LANES)), array((SHARDS, SLOT, LANES), BF16)),
        (
            pltpu.VMEM((tile_rows + 2, tile_cols + 2, channels), F32),
            pltpu.VMEM(((tile_rows + 2) * tile_cols, 3 * channels), BF16),
            pltpu.VMEM((9 * channels, channels), F32),
        ),
    )(moments, mixed_pad, mixed, cotangent, grad_act, affine, keep, style_col, demod, taps)

    core_count, near_count = lax.axis_size("c"), lax.axis_size(NEAR)
    payload = payload.reshape(core_count, near_count, SLOT, LANES)
    payload = resplit(jnp.sum(exchange(payload, "c").astype(F32), axis=0))
    payload = resplit(jnp.sum(exchange(payload, NEAR).astype(F32), axis=0))
    payload = resplit(jnp.sum(everyone(payload, LAT).astype(F32), axis=0))
    payload = lax.all_gather(everyone(payload, NEAR), "c")

    mean = stats[:samples][:, None, None, :]
    inverse = stats[samples:][:, None, None, :]
    row_at = jnp.arange(tile_rows + 2)
    inside_rows = ((row_at > 0) | inside[0]) & ((row_at <= tile_rows) | inside[1])
    pre_pad = (mixed_pad.astype(F32) - mean) * inverse * gamma + beta
    act_pad = jnp.where(inside_rows[None, :, None, None], jax.nn.silu(pre_pad), 0.0).astype(BF16)
    conv_out = apply_taps(act_pad, w_eff, tile_rows, tile_cols)
    block_out = (mixed.astype(F32) + conv_out).astype(BF16)

    grad_feats, grad_weight, grad_style, grad_affine = call(
        functools.partial(last_body, scale_gradient, cells_per_group),
        (
            array(feats.shape, BF16),
            array(taps.shape),
            array(style_weight.shape),
            array((2, LANES)),
        ),
    )(
        payload.reshape(SHARDS, SLOT, LANES), stats, mixed, cotangent, grad_act, affine, style,
        style_col, demod, power, taps, emb.T,
    )
    return (
        block_out,
        grad_feats,
        grad_weight.reshape(conv_weight.shape),
        grad_style,
        grad_affine[0],
        grad_affine[1],
    )


def solution(mesh):
    parts = Mesh(mesh.devices.reshape(4, 4, 2, 8, 2), LAT + LON)
    tile = P(None, LAT, LON, None)
    placed = (tile, tile, P(LAT, LON, None), P(), P(), P(), P(), P(), P(), tile)
    return jax.shard_map(
        on_device,
        mesh=parts,
        in_specs=placed,
        out_specs=(tile, tile, P(), P(), P(), P()),
        check_vma=False,
    )
```

time: 124 us -> 117 us (0.944)
  other arithmetic: 9.68 us -> 2.69 us
  matrix products: 9.02 us -> 4.76 us
  Pallas kernels: 0 us -> 4.15 us
    ppermute x4, starting transfers between devices: 9.87 us -> 14.7 us  [shift(): return lax.ppermute(block, axes, pairs)]
    all_to_all x5, starting transfers between devices: 40.5 us -> 36.1 us  [exchange(): return lax.all_to_all(block, axes, 0, 0)]
    pallas_call x0 -> x4, Pallas kernels: none -> 4.15 us  [the longest x1 1.36 us: on_device(): call(functools.partial(last_body, scale_gradient, cells_per_group), (arra...]
    unnamed x17 -> x28, local copies, waits for them, and re-layouts: 2.43 us -> 5.59 us
    dot_general x12 -> x0, matrix products: 2.94 us -> none  [the longest x9 2.04 us: on_device(): jnp.einsum('bhwi,bhwo->bio', window, cotangent, preferred_element_type=F32)]
    reduce_sum x17 -> x3, other arithmetic: 2.31 us -> 0.1 us  [the longest x1 0.05 us: on_device(): payload = resplit(jnp.sum(exchange(payload, 'c').astype(F32), axis=0))]
    dot_general x18, matrix products: 5.68 us -> 3.94 us  [apply_taps(): jnp.einsum('bhwi,bio->bhwo', window, taps[:, row_tap, col_tap], preferred...]
    mul x2 -> x0, other arithmetic: 1.41 us -> none  [the longest x1 0.88 us: on_device(): grad_weight = scale_gradient * (weight_sum - shrink * conv_weight)]
  transfers between devices with their start and end apart: 9 -> 9, of which waited for: 5 -> 6; matrix products, arithmetic and copies ran while one was open for 6% -> 5% of each run, Pallas kernels for 0% -> 0%
where the time goes in v2:
time: 117 us; the launch traced here: 116 us
  starting transfers between devices  50.8 us (43%)
  waiting for transfers between devices  32.9 us (28%)
  blocking collectives  11.9 us (10%)
  local copies, waits for them, and re-layouts  8.03 us (7%)
  matrix products  4.76 us (4%)
  Pallas kernels  4.15 us (4%)
  other arithmetic  2.69 us (2%)
    all_to_all x5, starting transfers between devices, exchange(): return lax.all_to_all(block, axes, 0, 0)  36.1 us
    all_to_all x5, waiting for transfers between devices, exchange(): return lax.all_to_all(block, axes, 0, 0)  29.5 us
    ppermute x4, starting transfers between devices, shift(): return lax.ppermute(block, axes, pairs)  14.7 us
    all_to_all x1, blocking collectives, exchange(): return lax.all_to_all(block, axes, 0, 0)  6.25 us
    all_gather x1, blocking collectives, on_device(): payload = lax.all_gather(everyone(payload, NEAR), 'c')  5.66 us
    unnamed x28, local copies, waits for them, and re-layouts  5.59 us
    dot_general x18, matrix products, apply_taps(): jnp.einsum('bhwi,bio->bhwo', window, taps[:, row_tap, col_tap], preferred...  3.94 us
    ppermute x4, waiting for transfers between devices, shift(): return lax.ppermute(block, axes, pairs)  3.43 us
  transfers between devices with their start and end apart: 9, of which 6 were waited for; matrix products, arithmetic and copies ran while one was open for 5% of the time, Pallas kernels for 0%

profile of v2, /device:TPU:1, one launch (start us, length us, event | category | flops | bytes accessed | tf_op | source)
XLA Modules:
  0.0 116.4 jit_solution(2973587488410261165)
XLA Ops:
  0.7 1.0 copy-done.3
  1.6 0.9 copy-done.4
  2.5 0.8 copy-done.5
  3.4 0.7 copy-done.6
  4.1 1.1 shard_map.145
  5.1 0.8 pad_maximum_fusion.2
  5.9 8.8 %collective-permute-start.1 = (bf16[2,2,8,1,128]{4,3,2,1,0:T(2,128)(2,1)S(1)}, bf16[2,2,8,1,128]{4,3,2,1,0:T(2,128)(2,1)S(1)}, u32[]{:S(2)}, u32[]{:S(2)}) collective-permute-start(bf16[2,2,8,1,128]{4,3,2,1,0:T(2,128)(2,1)S(1)} %get-tuple-element.33), channel_id=1, source_target_pairs={{0,31},{1,0},{2,1},{3,2},{4,3},{5,4},{6,5},{7,6},{8,7},{9,8},{10,9... | collective-permute-start | bytes 24584 | tf_op jit(solution)/shard_map/ppermute | solution.py:30
  14.7 1.9 %collective-permute-start = (bf16[2,2,8,1,128]{4,3,2,1,0:T(2,128)(2,1)S(1)}, bf16[2,2,8,1,128]{4,3,2,1,0:T(2,128)(2,1)S(1)}, u32[]{:S(2)}, u32[]{:S(2)}) collective-permute-start(bf16[2,2,8,1,128]{4,3,2,1,0:T(2,128)(2,1)S(1)} %get-tuple-element.32), channel_id=1, source_target_pairs={{0,1},{1,2},{2,3},{3,4},{4,5},{5,6},{6,7},{7,8},{8,9},{9,10},{10,1... | collective-permute-start | bytes 24584 | tf_op jit(solution)/shard_map/ppermute | solution.py:30
  16.7 5.3 %all-to-all-start = ((f32[32,2,128]{2,1,0:T(2,128)}), f32[32,2,128]{2,1,0:T(2,128)S(1)}, u32[]{:S(2)}, u32[]{:S(2)}) async-start(f32[32,2,128]{2,1,0:T(2,128)} %get-tuple-element.17), calls=%async_computation | async-start | bytes 65536 | tf_op jit(solution)/shard_map/all_to_all | solution.py:41
  22.0 0.2 copy.58
  22.3 0.4 copy-done.9
  22.7 0.6 convolution_add_fusion.16
  23.4 0.2 fusion.2.demod
  23.6 0.3 multiply_convert_fusion
  24.0 0.6 copy-done.10
  24.6 0.2 copy-done.2
  24.8 0.2 pad_maximum_fusion
  25.0 4.9 %all-to-all-done.rows = f32[32,2,128]{2,1,0:T(2,128)S(1)} async-done(((f32[32,2,128]{2,1,0:T(2,128)}), f32[32,2,128]{2,1,0:T(2,128)S(1)}, u32[]{:S(2)}, u32[]{:S(2)}) %all-to-all-start) | async-done | bytes 32800 | tf_op jit(solution)/shard_map/all_to_all | solution.py:41
  29.9 0.7 shard_map.146
  30.6 2.7 %collective-permute-start.2 = (bf16[2,2,1,34,128]{4,3,2,1,0:T(8,128)(2,1)S(1)}, bf16[2,2,1,34,128]{4,3,2,1,0:T(8,128)(2,1)S(1)}, u32[]{:S(2)}, u32[]{:S(2)}) collective-permute-start(bf16[2,2,1,34,128]{4,3,2,1,0:T(8,128)(2,1)S(1)} %get-tuple-element.31), channel_id=1, source_target_pairs={{0,32},{32,64},{64,96},{96,128},{128,160},{160,192},{192,224},{224... | collective-permute-start | bytes 104456 | tf_op jit(solution)/shard_map/ppermute | solution.py:30
  33.3 0.1 add_convert_fusion
  33.4 0.1 copy.71
  33.5 12.2 %all-to-all-start.1 = ((f32[16,2,128]{2,1,0:T(2,128)}), f32[16,2,128]{2,1,0:T(2,128)S(1)}, u32[]{:S(2)}, u32[]{:S(2)}) async-start(f32[16,2,128]{2,1,0:T(2,128)} %shard_map.146), calls=%async_computation.1 | async-start | bytes 32768 | tf_op jit(solution)/shard_map/all_to_all | solution.py:41
  45.8 1.3 %collective-permute-start.3 = (bf16[2,2,1,34,128]{4,3,2,1,0:T(8,128)(2,1)S(1)}, bf16[2,2,1,34,128]{4,3,2,1,0:T(8,128)(2,1)S(1)}, u32[]{:S(2)}, u32[]{:S(2)}) collective-permute-start(bf16[2,2,1,34,128]{4,3,2,1,0:T(8,128)(2,1)S(1)} %get-tuple-element.30), channel_id=1, source_target_pairs={{32,0},{64,32},{96,64},{128,96},{160,128},{192,160},{224,192},{256... | collective-permute-start | bytes 104456 | tf_op jit(solution)/shard_map/ppermute | solution.py:30
  47.1 3.4 %collective-permute-done.3 = bf16[2,2,1,34,128]{4,3,2,1,0:T(8,128)(2,1)S(1)} collective-permute-done((bf16[2,2,1,34,128]{4,3,2,1,0:T(8,128)(2,1)S(1)}, bf16[2,2,1,34,128]{4,3,2,1,0:T(8,128)(2,1)S(1)}, u32[]{:S(2)}, u32[]{:S(2)}) %collective-permute-start.3) | collective-permute-done | bytes 34848 | tf_op jit(solution)/shard_map/ppermute | solution.py:30
  50.6 0.2 fusion.22
  50.8 0.5 copy-done.7
  51.3 0.2 convolution_add_fusion.15
  51.5 0.2 convolution_add_fusion.14
  51.7 0.2 convolution_add_fusion.13
  51.9 0.2 convolution_add_fusion.12
  52.1 0.2 convolution_add_fusion.11
  52.2 0.2 convolution_add_fusion.10
  52.4 0.2 convolution_add_fusion.9
  52.6 0.2 convolution_add_fusion.8.grad_act
  52.8 1.8 %all-to-all-done.1.rows = f32[16,2,128]{2,1,0:T(2,128)S(1)} async-done(((f32[16,2,128]{2,1,0:T(2,128)}), f32[16,2,128]{2,1,0:T(2,128)S(1)}, u32[]{:S(2)}, u32[]{:S(2)}) %all-to-all-start.1) | async-done | bytes 16416 | tf_op jit(solution)/shard_map/all_to_all | solution.py:41
  54.7 1.0 shard_map.147
  55.7 0.2 select_convert_fusion
  55.9 0.2 fusion.13
  56.1 0.2 convolution_add_fusion.7
  56.3 0.2 convolution_add_fusion.6
  56.5 6.2 %all_to_all.30 = bf16[2,16,40,128]{3,2,1,0:T(8,128)(2,1)S(1)} all-to-all(bf16[2,16,40,128]{3,2,1,0:T(8,128)(2,1)S(1)} %bitcast.161), channel_id=1, replica_groups=mesh['zh'=4,'x'=4,'zl'=2,'y'=8,'c'=2] {'c'}, dimensions={0} | all-to-all | bytes 655360 | tf_op jit(solution)/shard_map/all_to_all | solution.py:41
  62.8 0.2 fusion.30
  63.0 0.8 fusion.4
  63.8 3.5 %all-to-all-start.3 = ((bf16[16,40,128]{2,1,0:T(8,128)(2,1)}), bf16[16,40,128]{2,1,0:T(8,128)(2,1)S(1)}, u32[]{:S(2)}, u32[]{:S(2)}) async-start(bf16[16,40,128]{2,1,0:T(8,128)(2,1)} %fusion.4), calls=%async_computation.3 | async-start | bytes 327680 | tf_op jit(solution)/shard_map/all_to_all | solution.py:41
  67.3 0.2 convolution_add_fusion.5
  67.5 0.2 convolution_add_fusion.4
  67.7 7.1 %all-to-all-done.3 = bf16[16,40,128]{2,1,0:T(8,128)(2,1)S(1)} async-done(((bf16[16,40,128]{2,1,0:T(8,128)(2,1)}), bf16[16,40,128]{2,1,0:T(8,128)(2,1)S(1)}, u32[]{:S(2)}, u32[]{:S(2)}) %all-to-all-start.3) | async-done | bytes 163872 | tf_op jit(solution)/shard_map/all_to_all | solution.py:41
  74.9 0.1 fusion.33
  74.9 0.1 fusion.27
  75.0 0.7 broadcast_in_dim.17
  75.7 10.6 %all-to-all-start.4 = ((bf16[16,40,128]{2,1,0:T(8,128)(2,1)}), bf16[16,40,128]{2,1,0:T(8,128)(2,1)S(1)}, u32[]{:S(2)}, u32[]{:S(2)}) async-start(bf16[16,40,128]{2,1,0:T(8,128)(2,1)} %broadcast_in_dim.17), calls=%async_computation.4 | async-start | bytes 327680 | tf_op jit(solution)/shard_map/all_to_all | solution.py:41
  86.3 0.2 convolution_add_fusion.3
  86.5 0.2 convolution_add_fusion.2
  86.7 9.2 %all-to-all-done.4 = bf16[16,40,128]{2,1,0:T(8,128)(2,1)S(1)} async-done(((bf16[16,40,128]{2,1,0:T(8,128)(2,1)}), bf16[16,40,128]{2,1,0:T(8,128)(2,1)S(1)}, u32[]{:S(2)}, u32[]{:S(2)}) %all-to-all-start.4) | async-done | bytes 163872 | tf_op jit(solution)/shard_map/all_to_all | solution.py:41
  96.0 0.1 fusion.29
  96.1 0.7 broadcast_in_dim.18
  96.8 4.5 %all-to-all-start.5 = ((bf16[16,40,128]{2,1,0:T(8,128)(2,1)}), bf16[16,40,128]{2,1,0:T(8,128)(2,1)S(1)}, u32[]{:S(2)}, u32[]{:S(2)}) async-start(bf16[16,40,128]{2,1,0:T(8,128)(2,1)} %broadcast_in_dim.18), calls=%async_computation.5 | async-start | bytes 327680 | tf_op jit(solution)/shard_map/all_to_all | solution.py:41
  101.3 0.2 convolution_add_fusion.1
  101.5 0.9 fusion.1
  102.4 6.5 %all-to-all-done.5 = bf16[16,40,128]{2,1,0:T(8,128)(2,1)S(1)} async-done(((bf16[16,40,128]{2,1,0:T(8,128)(2,1)}), bf16[16,40,128]{2,1,0:T(8,128)(2,1)S(1)}, u32[]{:S(2)}, u32[]{:S(2)}) %all-to-all-start.5) | async-done | bytes 163872 | tf_op jit(solution)/shard_map/all_to_all | solution.py:41
  108.8 5.7 %all-gather.gathered = bf16[32,40,128]{2,1,0:T(8,128)(2,1)S(1)} all-gather(bf16[16,40,128]{2,1,0:T(8,128)(2,1)S(1)} %all-to-all-done.5), channel_id=2, replica_groups=mesh['zh'=4,'x'=4,'zl'=2,'y'=8,'c'=2] {'c'}, dimensions={0}, use_global_device_ids=true | all-gather | bytes 491520 | tf_op jit(solution)/shard_map/all_gather | solution.py:321
  114.5 1.4 %shard_map.148 = (bf16[2,8,32,128]{3,2,1,0:T(8,128)(2,1)}, f32[9,128,128]{2,1,0:T(8,128)}, f32[512,128]{1,0:T(8,128)}, f32[2,128]{1,0:T(2,128)S(1)}) custom-call(bf16[32,40,128]{2,1,0:T(8,128)(2,1)S(1)} %all-gather.gathered, f32[4,128]{1,0:T(4,128)S(1)} %get-tuple-element.20.stats, bf16[2,8,32,128]{3,2,1,0:T(8,128)(2,1)S(1)} %get-tuple-element.16.mixed, ...), custom_call_target="tpu_custom_call" | custom-call | tf_op jit(solution)/shard_map/pallas_call | solution.py:332
  115.8 0.5 slice_bitcast_fusion.38
  (37 shorter events, 0.6 us)
Async XLA Ops:
  0.6 21.7 %copy-start = (f32[512,128]{1,0:T(8,128)S(1)}, f32[512,128]{1,0:T(8,128)}, u32[]{:S(2)}) copy-start(f32[512,128]{1,0:T(8,128)} %param.15) | copy-start | bytes 786436
  0.6 21.3 %copy-start.1 = (f32[3,3,128,128]{3,2,1,0:T(8,128)S(1)}, f32[3,3,128,128]{3,2,1,0:T(8,128)}, u32[]{:S(2)}) copy-start(f32[3,3,128,128]{3,2,1,0:T(8,128)} %param.16) | copy-start | bytes 1769476
  0.7 1.0 copy-start.3
  1.6 0.9 copy-start.4
  2.5 0.8 copy-start.5
  3.4 0.7 copy-start.6
  5.9 18.7 %collective-permute-start.1 = (bf16[2,2,8,1,128]{4,3,2,1,0:T(2,128)(2,1)S(1)}, bf16[2,2,8,1,128]{4,3,2,1,0:T(2,128)(2,1)S(1)}, u32[]{:S(2)}, u32[]{:S(2)}) collective-permute-start(bf16[2,2,8,1,128]{4,3,2,1,0:T(2,128)(2,1)S(1)} %get-tuple-element.33), channel_id=1, source_target_pairs={{0,31},{1,0},{2,1},{3,2},{4,3},{5,4},{6,5},{7,6},{8,7},{9,8},{10,9... | collective-permute-start | bytes 24584 | tf_op jit(solution)/shard_map/ppermute | solution.py:30
  14.7 9.9 %collective-permute-start = (bf16[2,2,8,1,128]{4,3,2,1,0:T(2,128)(2,1)S(1)}, bf16[2,2,8,1,128]{4,3,2,1,0:T(2,128)(2,1)S(1)}, u32[]{:S(2)}, u32[]{:S(2)}) collective-permute-start(bf16[2,2,8,1,128]{4,3,2,1,0:T(2,128)(2,1)S(1)} %get-tuple-element.32), channel_id=1, source_target_pairs={{0,1},{1,2},{2,3},{3,4},{4,5},{5,6},{6,7},{7,8},{8,9},{9,10},{10,1... | collective-permute-start | bytes 24584 | tf_op jit(solution)/shard_map/ppermute | solution.py:30
  16.7 13.2 %all-to-all-start = ((f32[32,2,128]{2,1,0:T(2,128)}), f32[32,2,128]{2,1,0:T(2,128)S(1)}, u32[]{:S(2)}, u32[]{:S(2)}) async-start(f32[32,2,128]{2,1,0:T(2,128)} %get-tuple-element.17), calls=%async_computation | async-start | bytes 65536 | tf_op jit(solution)/shard_map/all_to_all | solution.py:41
  22.0 0.7 copy-start.9
  23.9 0.7 copy-start.10
  23.9 0.7 copy-start.11
  23.9 0.9 copy-start.2
  30.6 16.5 %collective-permute-start.2 = (bf16[2,2,1,34,128]{4,3,2,1,0:T(8,128)(2,1)S(1)}, bf16[2,2,1,34,128]{4,3,2,1,0:T(8,128)(2,1)S(1)}, u32[]{:S(2)}, u32[]{:S(2)}) collective-permute-start(bf16[2,2,1,34,128]{4,3,2,1,0:T(8,128)(2,1)S(1)} %get-tuple-element.31), channel_id=1, source_target_pairs={{0,32},{32,64},{64,96},{96,128},{128,160},{160,192},{192,224},{224... | collective-permute-start | bytes 104456 | tf_op jit(solution)/shard_map/ppermute | solution.py:30
  33.5 21.1 %all-to-all-start.1 = ((f32[16,2,128]{2,1,0:T(2,128)}), f32[16,2,128]{2,1,0:T(2,128)S(1)}, u32[]{:S(2)}, u32[]{:S(2)}) async-start(f32[16,2,128]{2,1,0:T(2,128)} %shard_map.146), calls=%async_computation.1 | async-start | bytes 32768 | tf_op jit(solution)/shard_map/all_to_all | solution.py:41
  45.8 4.8 %collective-permute-start.3 = (bf16[2,2,1,34,128]{4,3,2,1,0:T(8,128)(2,1)S(1)}, bf16[2,2,1,34,128]{4,3,2,1,0:T(8,128)(2,1)S(1)}, u32[]{:S(2)}, u32[]{:S(2)}) collective-permute-start(bf16[2,2,1,34,128]{4,3,2,1,0:T(8,128)(2,1)S(1)} %get-tuple-element.30), channel_id=1, source_target_pairs={{32,0},{64,32},{96,64},{128,96},{160,128},{192,160},{224,192},{256... | collective-permute-start | bytes 104456 | tf_op jit(solution)/shard_map/ppermute | solution.py:30
  50.6 0.8 copy-start.7
  54.7 1.1 copy-start.8
  63.8 11.0 %all-to-all-start.3 = ((bf16[16,40,128]{2,1,0:T(8,128)(2,1)}), bf16[16,40,128]{2,1,0:T(8,128)(2,1)S(1)}, u32[]{:S(2)}, u32[]{:S(2)}) async-start(bf16[16,40,128]{2,1,0:T(8,128)(2,1)} %fusion.4), calls=%async_computation.3 | async-start | bytes 327680 | tf_op jit(solution)/shard_map/all_to_all | solution.py:41
  75.7 20.2 %all-to-all-start.4 = ((bf16[16,40,128]{2,1,0:T(8,128)(2,1)}), bf16[16,40,128]{2,1,0:T(8,128)(2,1)S(1)}, u32[]{:S(2)}, u32[]{:S(2)}) async-start(bf16[16,40,128]{2,1,0:T(8,128)(2,1)} %broadcast_in_dim.17), calls=%async_computation.4 | async-start | bytes 327680 | tf_op jit(solution)/shard_map/all_to_all | solution.py:41
  96.8 12.0 %all-to-all-start.5 = ((bf16[16,40,128]{2,1,0:T(8,128)(2,1)}), bf16[16,40,128]{2,1,0:T(8,128)(2,1)S(1)}, u32[]{:S(2)}, u32[]{:S(2)}) async-start(bf16[16,40,128]{2,1,0:T(8,128)(2,1)} %broadcast_in_dim.18), calls=%async_computation.5 | async-start | bytes 327680 | tf_op jit(solution)/shard_map/all_to_all | solution.py:41

commit v3 on v2

--- a/solution.py
+++ b/solution.py
@@ -45,12 +45,13 @@
     return exchange(jnp.broadcast_to(block[None], (lax.axis_size(axes),) + block.shape), axes)
 
 
-def call(body, outputs, scratch=()):
+def call(body, outputs, scratch=(), room=48, **more):
     return pl.pallas_call(
         body,
         out_shape=outputs,
         scratch_shapes=list(scratch),
-        compiler_params=pltpu.CompilerParams(vmem_limit_bytes=48 * 1024 * 1024),
+        **more,
+        compiler_params=pltpu.CompilerParams(vmem_limit_bytes=room * 1024 * 1024),
     )
 
 
@@ -80,9 +81,21 @@
     return weave(pltpu.roll(row, LANES - 1, 1), row)
 
 
-def mix_body(feats, cond, null, flags, mixed_out, moments_out):
+def mix_body(
+    feats_in, cond_in, null_in, cot_in, flags, mixed_out, moments_out, first_out, last_out,
+    feats, cond, null, cot, arrivals,
+):
+    copies = []
+    for at, (source, target) in enumerate(
+        ((null_in, null), (feats_in, feats), (cond_in, cond), (cot_in, cot))
+    ):
+        copies.append(pltpu.make_async_copy(source, target, arrivals.at[at]))
+        copies[-1].start()
+    for copy in copies[:3]:
+        copy.wait()
     samples, tile_rows, tile_cols, channels = feats.shape
     cells = tile_rows * tile_cols
+    size = cells * (channels // GROUPS)
     null32 = null[...].astype(F32)
     means, spreads = [], []
     for sample in range(samples):
@@ -91,14 +104,21 @@
             feats[sample].astype(F32) + dropped * null32 + (1.0 - dropped) * cond[sample].astype(F32)
         ).astype(BF16)
         mixed_out[sample] = mixed
-        wide = mixed.astype(F32).reshape(cells, channels)
-        size = cells * (channels // GROUPS)
+        wide = mixed.astype(F32)
+        first_out[0, sample] = wide[:, 0, :].astype(BF16)
+        last_out[0, sample] = wide[:, tile_cols - 1, :].astype(BF16)
+        wide = wide.reshape(cells, channels)
         mean = group_total(jnp.sum(wide, axis=0, keepdims=True)) * (1.0 / size)
         away = wide - mean
         means.append(mean)
         spreads.append(group_total(jnp.sum(away * away, axis=0, keepdims=True)))
     row = jnp.concatenate([weave(*means), weave(*spreads)], axis=0)
     moments_out[...] = jnp.broadcast_to(row[None], moments_out.shape)
+    copies[3].wait()
+    for sample in range(samples):
+        wide = cot[sample].astype(F32)
+        first_out[1, sample] = wide[:, 0, :].astype(BF16)
+        last_out[1, sample] = wide[:, tile_cols - 1, :].astype(BF16)
 
 
 def merged(rows, count):
@@ -113,11 +133,52 @@
     moments_out[...] = jnp.broadcast_to(row[None], moments_out.shape)
 
 
+def windows(padded, spread, shifted, rows, cols):
+    spread[...] = padded
+    channels = padded.shape[-1]
+    for tap in range(3):
+        moved = spread[:, tap : tap + cols, :].reshape((rows + 2) * cols, channels)
+        shifted[:, tap * channels : (tap + 1) * channels] = moved.astype(BF16)
+
+
+def back_body(padded, taps, shifted_out, grad_out, spread):
+    samples, rows, cols = padded.shape[0], padded.shape[1] - 2, padded.shape[2] - 2
+    size = rows * cols
+    for sample in range(samples):
+        shifted = shifted_out.at[sample]
+        windows(padded[sample].astype(F32), spread, shifted, rows, cols)
+        total = jnp.zeros((size, taps.shape[3]), F32)
+        for row_tap in range(3):
+            window = shifted[row_tap * cols : row_tap * cols + size, :]
+            total = total + jnp.dot(window, taps[sample, row_tap], preferred_element_type=F32)
+        grad_out[sample] = total
+
+
+def forward_body(padded, taps, stats, affine, keep, block_out, spread, shifted):
+    samples, rows, cols = padded.shape[0], padded.shape[1] - 2, padded.shape[2] - 2
+    size = rows * cols
+    gamma, beta = affine[0:1, :][None], affine[1:2, :][None]
+    row = lax.broadcasted_iota(jnp.int32, spread.shape, 0)
+    inside = ((row > 0) | (keep[0:1, :] > 0.0)[None]) & ((row <= rows) | (keep[1:2, :] > 0.0)[None])
+    for sample in range(samples):
+        mixed = padded[sample].astype(F32)
+        mean = stats[sample : sample + 1, :][None]
+        inverse = stats[samples + sample : samples + sample + 1, :][None]
+        pre = (mixed - mean) * inverse * gamma + beta
+        act = jnp.where(inside, pre / (1.0 + jnp.exp(-pre)), 0.0)
+        windows(act, spread, shifted, rows, cols)
+        total = mixed[1 : 1 + rows, 1 : 1 + cols, :].reshape(size, -1)
+        for row_tap in range(3):
+            window = shifted[row_tap * cols : row_tap * cols + size, :]
+            total = total + jnp.dot(window, taps[sample, row_tap], preferred_element_type=F32)
+        block_out[sample] = total.astype(BF16).reshape(rows, cols, -1)
+
+
 def sums_body(
-    count, cells, rows, padded, mixed, cotangent, grad_act, affine, keep, style_col, demod, weight,
-    stats_out, payload_out, act, shifted, total,
+    count, cells, rows, mixed, shifted, grad_act, affine, style_col, demod, weight,
+    stats_out, payload_out, total,
 ):
-    samples, tile_rows, tile_cols, channels = cotangent.shape
+    samples, tile_rows, tile_cols, channels = mixed.shape
     size = tile_rows * tile_cols
     mean_all, spread_all = merged(rows[...], count)
     inverse_all = lax.rsqrt(spread_all * (1.0 / cells) + 1e-05)
@@ -127,39 +188,31 @@
         mean, inverse = unweave(mean_all, sample), unweave(inverse_all, sample)
         stats_out[sample : sample + 1, :] = mean
         stats_out[samples + sample : samples + sample + 1, :] = inverse
-        around = (padded[sample].astype(F32) - mean[None]) * inverse[None]
-        around = around * gamma[None] + beta[None]
-        act[...] = around / (1.0 + jnp.exp(-around))
-        for side, at in ((0, 0), (1, tile_rows + 1)):
-            act[at] = jnp.where(keep[side : side + 1, :] > 0.0, act[at], 0.0)
-        for tap in range(3):
-            moved = act[:, tap : tap + tile_cols, :].reshape(-1, channels)
-            shifted[:, tap * channels : (tap + 1) * channels] = moved.astype(BF16)
-        flat_cot = cotangent[sample].reshape(size, channels)
+        normalized = (mixed[sample].reshape(size, channels).astype(F32) - mean) * inverse
+        pre = normalized * gamma + beta
+        sig = 1.0 / (1.0 + jnp.exp(-pre))
+        act = (pre * sig).astype(BF16)
+        grad_pre = grad_act[sample] * (sig * (1.0 + pre * (1.0 - sig)))
+        sums[2].append(jnp.sum(grad_pre * normalized, axis=0, keepdims=True))
+        sums[3].append(jnp.sum(grad_pre, axis=0, keepdims=True))
         style_full = jnp.broadcast_to(style_col[:, sample : sample + 1], (channels, channels))
         demod_row = demod[sample : sample + 1, :]
         both = style_full * demod_row
         product = jnp.zeros((channels, channels), F32)
         for row_tap in range(3):
-            window = shifted[row_tap * tile_cols : row_tap * tile_cols + size, :]
+            window = shifted[sample, row_tap * tile_cols : row_tap * tile_cols + size, :]
             grad = lax.dot_general(
-                window, flat_cot, (((0,), (0,)), ((), ())), preferred_element_type=F32
+                act, window, (((0,), (0,)), ((), ())), preferred_element_type=F32
             )
             for col_tap in range(3):
-                tap = row_tap * 3 + col_tap
-                block = grad[col_tap * channels : (col_tap + 1) * channels, :]
+                tap = (2 - row_tap) * 3 + 2 - col_tap
+                block = grad[:, col_tap * channels : (col_tap + 1) * channels]
                 product = product + block * weight[tap]
                 here = slice(tap * channels, (tap + 1) * channels)
                 part = block * both
                 total[here, :] = part if sample == 0 else total[here, :] + part
         sums[0].append(jnp.sum(product * style_full, axis=0, keepdims=True))
         sums[1].append(jnp.sum((product * demod_row).T, axis=0, keepdims=True))
-        normalized = (mixed[sample].reshape(size, channels).astype(F32) - mean) * inverse
-        pre = normalized * gamma + beta
-        sig = 1.0 / (1.0 + jnp.exp(-pre))
-        grad_pre = grad_act[sample].reshape(size, channels) * (sig * (1.0 + pre * (1.0 - sig)))
-        sums[2].append(jnp.sum(grad_pre * normalized, axis=0, keepdims=True))
-        sums[3].append(jnp.sum(grad_pre, axis=0, keepdims=True))
     small = jnp.concatenate(sum(sums, []), axis=0)
     lane = lanes_of(TILE)
     sub = lax.broadcasted_iota(jnp.int32, (TILE, channels), 0)
@@ -248,21 +301,10 @@
         normalized = (mixed[sample].reshape(size, channels).astype(F32) - mean) * inverse
         pre = normalized * gamma + beta
         sig = 1.0 / (1.0 + jnp.exp(-pre))
-        grad_pre = grad_act[sample].reshape(size, channels) * (sig * (1.0 + pre * (1.0 - sig)))
+        grad_pre = grad_act[sample] * (sig * (1.0 + pre * (1.0 - sig)))
         change = inverse * (gamma * grad_pre - product_mean - normalized * squared_mean)
         out = cotangent[sample].reshape(size, channels).astype(F32) + change
         feats_out[sample] = out.astype(BF16).reshape(tile_rows, tile_cols, channels)
-
-
-def apply_taps(padded, taps, tile_rows, tile_cols):
-    total = jnp.zeros(padded.shape[:1] + (tile_rows, tile_cols, taps.shape[4]), F32)
-    for row_tap in range(3):
-        for col_tap in range(3):
-            window = padded[:, row_tap : row_tap + tile_rows, col_tap : col_tap + tile_cols]
-            total = total + jnp.einsum(
-                "bhwi,bio->bhwo", window, taps[:, row_tap, col_tap], preferred_element_type=F32
-            )
-    return total
 
 
 def on_device(
@@ -277,17 +319,34 @@
     scale_gradient = 1.0 / math.sqrt(samples * tile_rows * tile_cols * devices_all)
     taps = conv_weight.reshape(9, channels, channels)
 
-    mixed, moments = call(
-        mix_body, (array(feats.shape, BF16), array((lon_count, 2, LANES)))
-    )(feats, cond, null_field, drop_flags)
-    moments = exchange(moments, LON)
-    both = extend(jnp.stack([mixed, cotangent]), LON, 3, True)
+    anywhere, whole = pl.BlockSpec(memory_space=pl.ANY), pl.BlockSpec(memory_space=pltpu.VMEM)
+    edge = array((2, samples, tile_rows, channels), BF16)
+    mixed, moments, first, last = call(
+        mix_body,
+        (array(feats.shape, BF16), array((lon_count, 2, LANES)), edge, edge),
+        (
+            pltpu.VMEM(feats.shape, BF16),
+            pltpu.VMEM(feats.shape, BF16),
+            pltpu.VMEM(null_field.shape, BF16),
+            pltpu.VMEM(feats.shape, BF16),
+            pltpu.SemaphoreType.DMA((4,)),
+        ),
+        room=60,
+        in_specs=[anywhere] * 4 + [whole],
+    )(feats, cond, null_field, cotangent, drop_flags)
+    rows = exchange(moments, LON)
+    low, high = shift(last, LON, 1, True), shift(first, LON, -1, True)
     moments = call(
-        functools.partial(merge_body, cells_local), array((lat_count, 2, LANES))
-    )(moments)
-    both, moments = lax.optimization_barrier((both, moments))
-    moments = exchange(moments, LAT)
-    both = extend(both, LAT, 2, False)
+        functools.partial(merge_body, cells_local),
+        array((lat_count, 2, LANES)),
+        cost_estimate=pl.CostEstimate(flops=50_000_000_000, bytes_accessed=150_000_000, transcendentals=0),
+    )(rows)
+    both = jnp.concatenate(
+        [low[:, :, :, None], jnp.stack([mixed, cotangent]), high[:, :, :, None]], axis=3
+    )
+    rows = exchange(moments, LAT)
+    low, high = shift(both[:, :, -1:], LAT, 1, False), shift(both[:, :, :1], LAT, -1, False)
+    both = jnp.concatenate([low, both, high], axis=2)
     mixed_pad, cot_pad = both[0], both[1]
 
     style = 1.0 + jnp.dot(emb, style_weight, precision=lax.Precision.HIGHEST)
@@ -295,8 +354,18 @@
     demod = lax.rsqrt(jnp.dot(style * style, power, precision=lax.Precision.HIGHEST) + 1e-08)
     modded = conv_weight[None] * style[:, None, None, :, None]
     w_eff = (modded * demod[:, None, None, None, :]).astype(BF16)
-    back_taps = jnp.swapaxes(w_eff[:, ::-1, ::-1], 3, 4)
-    grad_act = apply_taps(cot_pad, back_taps, tile_rows, tile_cols)
+    wide = (samples, 3, 3 * channels, channels)
+    back_taps = jnp.swapaxes(w_eff[:, ::-1, ::-1], 3, 4).reshape(wide)
+    spread = pltpu.VMEM((tile_rows + 2, tile_cols + 2, channels), F32)
+    stretch = ((tile_rows + 2) * tile_cols, 3 * channels)
+    shifted, grad_act = call(
+        back_body,
+        (
+            array((samples,) + stretch, BF16),
+            array((samples, tile_rows * tile_cols, channels)),
+        ),
+        (spread,),
+    )(cot_pad, back_taps)
 
     lat_at = lax.axis_index(LAT)
     inside = jnp.stack([lat_at > 0, lat_at < lat_count - 1])
@@ -306,28 +375,21 @@
     stats, payload = call(
         functools.partial(sums_body, cells_local * lon_count, cells_per_group),
         (array((2 * samples, LANES)), array((SHARDS, SLOT, LANES), BF16)),
-        (
-            pltpu.VMEM((tile_rows + 2, tile_cols + 2, channels), F32),
-            pltpu.VMEM(((tile_rows + 2) * tile_cols, 3 * channels), BF16),
-            pltpu.VMEM((9 * channels, channels), F32),
-        ),
-    )(moments, mixed_pad, mixed, cotangent, grad_act, affine, keep, style_col, demod, taps)
+        (pltpu.VMEM((9 * channels, channels), F32),),
+    )(rows, mixed, shifted, grad_act, affine, style_col, demod, taps)
 
     core_count, near_count = lax.axis_size("c"), lax.axis_size(NEAR)
-    payload = payload.reshape(core_count, near_count, SLOT, LANES)
-    payload = resplit(jnp.sum(exchange(payload, "c").astype(F32), axis=0))
+    payload = lax.all_gather(payload, "c")
+    payload = payload.reshape(core_count, core_count, near_count, SLOT, LANES)
+    payload = lax.dynamic_index_in_dim(payload, lax.axis_index("c"), 1, False)
+    payload = resplit(jnp.sum(payload.astype(F32), axis=0))
     payload = resplit(jnp.sum(exchange(payload, NEAR).astype(F32), axis=0))
     payload = resplit(jnp.sum(everyone(payload, LAT).astype(F32), axis=0))
     payload = lax.all_gather(everyone(payload, NEAR), "c")
 
-    mean = stats[:samples][:, None, None, :]
-    inverse = stats[samples:][:, None, None, :]
-    row_at = jnp.arange(tile_rows + 2)
-    inside_rows = ((row_at > 0) | inside[0]) & ((row_at <= tile_rows) | inside[1])
-    pre_pad = (mixed_pad.astype(F32) - mean) * inverse * gamma + beta
-    act_pad = jnp.where(inside_rows[None, :, None, None], jax.nn.silu(pre_pad), 0.0).astype(BF16)
-    conv_out = apply_taps(act_pad, w_eff, tile_rows, tile_cols)
-    block_out = (mixed.astype(F32) + conv_out).astype(BF16)
+    block_out = call(
+        forward_body, array(feats.shape, BF16), (spread, pltpu.VMEM(stretch, BF16))
+    )(mixed_pad, w_eff.reshape(wide), stats, affine, keep)
 
     grad_feats, grad_weight, grad_style, grad_affine = call(
         functools.partial(last_body, scale_gradient, cells_per_group),

time: 117 us -> 114 us (0.974)
  blocking collectives: 11.9 us -> 25.5 us
  waiting for transfers between devices: 32.9 us -> 26.9 us
  starting transfers between devices: 50.8 us -> 45.1 us
  local copies, waits for them, and re-layouts: 8.03 us -> 3.92 us
  matrix products: 4.76 us -> 0.82 us
  Pallas kernels: 4.15 us -> 7.63 us
    all_to_all x1, blocking collectives: 6.25 us -> 14.4 us  [exchange(): return lax.all_to_all(block, axes, 0, 0)]
    all_to_all x5 -> x4, waiting for transfers between devices: 29.5 us -> 23.5 us  [exchange(): return lax.all_to_all(block, axes, 0, 0)]
    all_gather x0 -> x1, blocking collectives: none -> 5.54 us  [on_device(): payload = lax.all_gather(payload, 'c')]
    all_to_all x5 -> x4, starting transfers between devices: 36.1 us -> 30.7 us  [exchange(): return lax.all_to_all(block, axes, 0, 0)]
    unnamed x28 -> x18, local copies, waits for them, and re-layouts: 5.59 us -> 1.48 us
    dot_general x18 -> x0, matrix products: 3.94 us -> none  [apply_taps(): jnp.einsum('bhwi,bio->bhwo', window, taps[:, row_tap, col_tap], preferred...]
    pallas_call x1 -> x3, Pallas kernels: 1.07 us -> 4.65 us  [the longest x1 2.93 us: on_device(): call(mix_body, (array(feats.shape, BF16), array((lon_count, 2, LANES)), e...]
  transfers between devices with their start and end apart: 9 -> 8, of which waited for: 6 -> 4; matrix products, arithmetic and copies ran while one was open for 5% -> 3% of each run, Pallas kernels for 0% -> 2%
where the time goes in v3:
time: 114 us; the launch traced here: 113 us
  starting transfers between devices  45.1 us (40%)
  waiting for transfers between devices  26.9 us (24%)
  blocking collectives  25.5 us (22%)
  Pallas kernels  7.63 us (7%)
  local copies, waits for them, and re-layouts  3.92 us (3%)
  other arithmetic  2.29 us (2%)
    all_to_all x4, starting transfers between devices, exchange(): return lax.all_to_all(block, axes, 0, 0)  30.7 us
    all_to_all x4, waiting for transfers between devices, exchange(): return lax.all_to_all(block, axes, 0, 0)  23.5 us
    all_to_all x1, blocking collectives, exchange(): return lax.all_to_all(block, axes, 0, 0)  14.4 us
    ppermute x4, starting transfers between devices, shift(): return lax.ppermute(block, axes, pairs)  14.4 us
    all_gather x1, blocking collectives, on_device(): payload = lax.all_gather(everyone(payload, NEAR), 'c')  5.54 us
    all_gather x1, blocking collectives, on_device(): payload = lax.all_gather(payload, 'c')  5.54 us
    ppermute x4, waiting for transfers between devices, shift(): return lax.ppermute(block, axes, pairs)  3.37 us
    pallas_call x1, Pallas kernels, on_device(): call(mix_body, (array(feats.shape, BF16), array((lon_count, 2, LANES)), e...  2.93 us
  transfers between devices with their start and end apart: 8, of which 4 were waited for; matrix products, arithmetic and copies ran while one was open for 3% of the time, Pallas kernels for 2%

profile of v3, /device:TPU:1, one launch (start us, length us, event | category | flops | bytes accessed | tf_op | source)
XLA Modules:
  0.0 113.2 jit_solution(10384118537493438560)
XLA Ops:
  0.6 0.0 copy-start
  0.6 0.0 copy-start.1
  0.7 2.9 %shard_map.145 = (bf16[2,8,32,128]{3,2,1,0:T(8,128)(2,1)}, f32[32,2,128]{2,1,0:T(2,128)}, bf16[2,2,8,128]{3,2,1,0:T(8,128)(2,1)}, bf16[2,2,8,128]{3,2,1,0:T(8,128)(2,1)}) custom-call(bf16[2,8,32,128]{3,2,1,0:T(8,128)(2,1)} %feats_in.1, bf16[2,8,32,128]{3,2,1,0:T(8,128)(2,1)} %cond_in.1, bf16[8,32,128]{2,1,0:T(8,128)(2,1)} %null_in.1, ...), custom_call_target="tpu_custom_call" | custom-call | tf_op jit(solution)/shard_map/pallas_call | solution.py:324
  3.6 4.6 %collective-permute-start = (bf16[2,2,8,128]{3,2,1,0:T(8,128)(2,1)}, bf16[2,2,8,128]{3,2,1,0:T(8,128)(2,1)S(1)}, u32[]{:S(2)}, u32[]{:S(2)}) collective-permute-start(bf16[2,2,8,128]{3,2,1,0:T(8,128)(2,1)} %get-tuple-element.18), channel_id=1, source_target_pairs={{0,1},{1,2},{2,3},{3,4},{4,5},{5,6},{6,7},{7,8},{8,9},{9,10},{10,1... | collective-permute-start | bytes 24584 | tf_op jit(solution)/shard_map/ppermute | solution.py:30
  8.2 6.1 %collective-permute-start.1 = (bf16[2,2,8,128]{3,2,1,0:T(8,128)(2,1)}, bf16[2,2,8,128]{3,2,1,0:T(8,128)(2,1)S(1)}, u32[]{:S(2)}, u32[]{:S(2)}) collective-permute-start(bf16[2,2,8,128]{3,2,1,0:T(8,128)(2,1)} %get-tuple-element.20), channel_id=1, source_target_pairs={{0,31},{1,0},{2,1},{3,2},{4,3},{5,4},{6,5},{7,6},{8,7},{9,8},{10,9... | collective-permute-start | bytes 24584 | tf_op jit(solution)/shard_map/ppermute | solution.py:30
  14.3 7.4 %all-to-all-start = ((f32[32,2,128]{2,1,0:T(2,128)}), f32[32,2,128]{2,1,0:T(2,128)S(1)}, u32[]{:S(2)}, u32[]{:S(2)}) async-start(f32[32,2,128]{2,1,0:T(2,128)} %get-tuple-element.21), calls=%async_computation | async-start | bytes 65536 | tf_op jit(solution)/shard_map/all_to_all | solution.py:41
  21.7 1.1 multiply_reduce_fusion.power
  22.8 0.0 copy-done.1
  22.8 0.0 copy-start.4
  22.8 0.0 copy-start.5
  22.8 0.0 copy-start.6
  22.9 0.2 copy.51
  23.1 0.0 copy-done
  23.1 0.4 copy-done.4
  23.5 0.6 convolution_add_fusion
  24.1 0.1 copy.50.style
  24.2 0.2 fusion.demod
  24.4 0.0 copy-start.2
  24.4 0.0 copy-start.3
  24.4 0.0 copy-done.5
  24.4 0.0 copy-done.6
  24.5 0.2 multiply_convert_fusion
  24.7 0.0 collective-permute-done
  24.8 0.0 collective-permute-done.1
  24.8 0.6 copy-done.2
  25.3 0.1 copy-done.3
  25.4 2.4 %collective-permute-start.2 = (bf16[2,2,1,34,128]{4,3,2,1,0:T(8,128)(2,1)S(1)}, bf16[2,2,1,34,128]{4,3,2,1,0:T(8,128)(2,1)S(1)}, u32[]{:S(2)}, u32[]{:S(2)}) collective-permute-start(bf16[2,2,1,34,128]{4,3,2,1,0:T(8,128)(2,1)S(1)} %get-tuple-element.34), channel_id=1, source_target_pairs={{0,32},{32,64},{64,96},{96,128},{128,160},{160,192},{192,224},{224... | collective-permute-start | bytes 104456 | tf_op jit(solution)/shard_map/ppermute | solution.py:30
  27.9 1.3 %collective-permute-start.3 = (bf16[2,2,1,34,128]{4,3,2,1,0:T(8,128)(2,1)S(1)}, bf16[2,2,1,34,128]{4,3,2,1,0:T(8,128)(2,1)S(1)}, u32[]{:S(2)}, u32[]{:S(2)}) collective-permute-start(bf16[2,2,1,34,128]{4,3,2,1,0:T(8,128)(2,1)S(1)} %get-tuple-element.35), channel_id=1, source_target_pairs={{32,0},{64,32},{96,64},{128,96},{160,128},{192,160},{224,192},{256... | collective-permute-start | bytes 104456 | tf_op jit(solution)/shard_map/ppermute | solution.py:30
  29.2 0.0 collective-permute-done.2
  29.2 3.4 %collective-permute-done.3 = bf16[2,2,1,34,128]{4,3,2,1,0:T(8,128)(2,1)S(1)} collective-permute-done((bf16[2,2,1,34,128]{4,3,2,1,0:T(8,128)(2,1)S(1)}, bf16[2,2,1,34,128]{4,3,2,1,0:T(8,128)(2,1)S(1)}, u32[]{:S(2)}, u32[]{:S(2)}) %collective-permute-start.3) | collective-permute-done | bytes 34848 | tf_op jit(solution)/shard_map/ppermute | solution.py:30
  32.6 0.2 pad_maximum_fusion
  32.8 0.0 all-to-all-done.rows
  32.8 0.7 shard_map.146
  33.5 15.2 %all-to-all-start.1 = ((f32[16,2,128]{2,1,0:T(2,128)}), f32[16,2,128]{2,1,0:T(2,128)S(1)}, u32[]{:S(2)}, u32[]{:S(2)}) async-start(f32[16,2,128]{2,1,0:T(2,128)} %shard_map.146), calls=%async_computation.1 | async-start | bytes 32768 | tf_op jit(solution)/shard_map/all_to_all | solution.py:41
  48.8 0.5 shard_map.147
  49.2 8.3 %all-to-all-done.1.rows = f32[16,2,128]{2,1,0:T(2,128)S(1)} async-done(((f32[16,2,128]{2,1,0:T(2,128)}), f32[16,2,128]{2,1,0:T(2,128)S(1)}, u32[]{:S(2)}, u32[]{:S(2)}) %all-to-all-start.1) | async-done | bytes 16416 | tf_op jit(solution)/shard_map/all_to_all | solution.py:41
  57.6 0.9 shard_map.148
  58.5 5.5 %all-gather = bf16[64,40,128]{2,1,0:T(8,128)(2,1)S(1)} all-gather(bf16[32,40,128]{2,1,0:T(8,128)(2,1)S(1)} %get-tuple-element.25), channel_id=2, replica_groups=mesh['zh'=4,'x'=4,'zl'=2,'y'=8,'c'=2] {'c'}, dimensions={0}, use_global_device_ids=true | all-gather | bytes 983040 | tf_op jit(solution)/shard_map/all_gather | solution.py:382
  64.1 0.2 fusion.8
  64.2 0.2 fusion.2
  64.4 14.4 %all_to_all.25 = bf16[16,40,128]{2,1,0:T(8,128)(2,1)S(1)} all-to-all(bf16[16,40,128]{2,1,0:T(8,128)(2,1)S(1)} %fusion.2), channel_id=1, replica_groups=mesh['zh'=4,'x'=4,'zl'=2,'y'=8,'c'=2] {'zl','y'}, dimensions={0} | all-to-all | bytes 327680 | tf_op jit(solution)/shard_map/all_to_all | solution.py:41
  78.9 0.1 fusion.10
  79.0 0.1 fusion.5
  79.1 0.7 broadcast_in_dim.13
  79.7 3.5 %all-to-all-start.3 = ((bf16[16,40,128]{2,1,0:T(8,128)(2,1)}), bf16[16,40,128]{2,1,0:T(8,128)(2,1)S(1)}, u32[]{:S(2)}, u32[]{:S(2)}) async-start(bf16[16,40,128]{2,1,0:T(8,128)(2,1)} %broadcast_in_dim.13), calls=%async_computation.3 | async-start | bytes 327680 | tf_op jit(solution)/shard_map/all_to_all | solution.py:41
  83.3 9.5 %all-to-all-done.3 = bf16[16,40,128]{2,1,0:T(8,128)(2,1)S(1)} async-done(((bf16[16,40,128]{2,1,0:T(8,128)(2,1)}), bf16[16,40,128]{2,1,0:T(8,128)(2,1)S(1)}, u32[]{:S(2)}, u32[]{:S(2)}) %all-to-all-start.3) | async-done | bytes 163872 | tf_op jit(solution)/shard_map/all_to_all | solution.py:41
  92.9 0.1 fusion.9
  92.9 0.1 fusion.7
  93.0 0.7 broadcast_in_dim.14
  93.7 4.6 %all-to-all-start.4 = ((bf16[16,40,128]{2,1,0:T(8,128)(2,1)}), bf16[16,40,128]{2,1,0:T(8,128)(2,1)S(1)}, u32[]{:S(2)}, u32[]{:S(2)}) async-start(bf16[16,40,128]{2,1,0:T(8,128)(2,1)} %broadcast_in_dim.14), calls=%async_computation.4 | async-start | bytes 327680 | tf_op jit(solution)/shard_map/all_to_all | solution.py:41
  98.3 0.1 add_convert_fusion
  98.4 0.1 copy.53
  98.5 0.2 multiply_convert_fusion.1.taps
  98.7 0.1 broadcast_in_dim.12.keep
  98.8 1.2 %shard_map.149 = bf16[2,8,32,128]{3,2,1,0:T(8,128)(2,1)} custom-call(bf16[2,10,34,128]{3,2,1,0:T(8,128)(2,1)S(1)} %get-tuple-element.31.padded, bf16[2,3,384,128]{3,2,1,0:T(8,128)(2,1)S(1)} %multiply_convert_fusion.1.taps, f32[4,128]{1,0:T(4,128)S(1)} %get-tuple-element.24.stats, f32[2,128]{1,0:T(2,128)S(1)} %pad_maximum_fusion.5.affine, ...), custom_call_target="tpu_custom_call" | custom-call | tf_op jit(solution)/shard_map/pallas_call | solution.py:390
  100.0 5.7 %all-to-all-done.4 = bf16[16,40,128]{2,1,0:T(8,128)(2,1)S(1)} async-done(((bf16[16,40,128]{2,1,0:T(8,128)(2,1)}), bf16[16,40,128]{2,1,0:T(8,128)(2,1)S(1)}, u32[]{:S(2)}, u32[]{:S(2)}) %all-to-all-start.4) | async-done | bytes 163872 | tf_op jit(solution)/shard_map/all_to_all | solution.py:41
  105.7 5.5 %all-gather.1.gathered = bf16[32,40,128]{2,1,0:T(8,128)(2,1)S(1)} all-gather(bf16[16,40,128]{2,1,0:T(8,128)(2,1)S(1)} %all-to-all-done.4), channel_id=3, replica_groups=mesh['zh'=4,'x'=4,'zl'=2,'y'=8,'c'=2] {'c'}, dimensions={0}, use_global_device_ids=true | all-gather | bytes 491520 | tf_op jit(solution)/shard_map/all_gather | solution.py:388
  111.3 1.4 %shard_map.150 = (bf16[2,8,32,128]{3,2,1,0:T(8,128)(2,1)}, f32[9,128,128]{2,1,0:T(8,128)}, f32[512,128]{1,0:T(8,128)}, f32[2,128]{1,0:T(2,128)S(1)}) custom-call(bf16[32,40,128]{2,1,0:T(8,128)(2,1)S(1)} %all-gather.1.gathered, f32[4,128]{1,0:T(4,128)S(1)} %get-tuple-element.24.stats, bf16[2,8,32,128]{3,2,1,0:T(8,128)(2,1)S(1)} %copy-done.3, ...), custom_call_target="tpu_custom_call" | custom-call | tf_op jit(solution)/shard_map/pallas_call | solution.py:394
  112.6 0.5 slice_bitcast_fusion.2
  (13 shorter events, 0.3 us)
Async XLA Ops:
  0.6 22.5 %copy-start = (f32[512,128]{1,0:T(8,128)S(1)}, f32[512,128]{1,0:T(8,128)}, u32[]{:S(2)}) copy-start(f32[512,128]{1,0:T(8,128)} %param.15) | copy-start | bytes 786436
  0.6 22.2 %copy-start.1 = (f32[3,3,128,128]{3,2,1,0:T(8,128)S(1)}, f32[3,3,128,128]{3,2,1,0:T(8,128)}, u32[]{:S(2)}) copy-start(f32[3,3,128,128]{3,2,1,0:T(8,128)} %param.16) | copy-start | bytes 1769476
  3.6 21.1 %collective-permute-start = (bf16[2,2,8,128]{3,2,1,0:T(8,128)(2,1)}, bf16[2,2,8,128]{3,2,1,0:T(8,128)(2,1)S(1)}, u32[]{:S(2)}, u32[]{:S(2)}) collective-permute-start(bf16[2,2,8,128]{3,2,1,0:T(8,128)(2,1)} %get-tuple-element.18), channel_id=1, source_target_pairs={{0,1},{1,2},{2,3},{3,4},{4,5},{5,6},{6,7},{7,8},{8,9},{9,10},{10,1... | collective-permute-start | bytes 24584 | tf_op jit(solution)/shard_map/ppermute | solution.py:30
  8.2 16.6 %collective-permute-start.1 = (bf16[2,2,8,128]{3,2,1,0:T(8,128)(2,1)}, bf16[2,2,8,128]{3,2,1,0:T(8,128)(2,1)S(1)}, u32[]{:S(2)}, u32[]{:S(2)}) collective-permute-start(bf16[2,2,8,128]{3,2,1,0:T(8,128)(2,1)} %get-tuple-element.20), channel_id=1, source_target_pairs={{0,31},{1,0},{2,1},{3,2},{4,3},{5,4},{6,5},{7,6},{8,7},{9,8},{10,9... | collective-permute-start | bytes 24584 | tf_op jit(solution)/shard_map/ppermute | solution.py:30
  14.3 18.5 %all-to-all-start = ((f32[32,2,128]{2,1,0:T(2,128)}), f32[32,2,128]{2,1,0:T(2,128)S(1)}, u32[]{:S(2)}, u32[]{:S(2)}) async-start(f32[32,2,128]{2,1,0:T(2,128)} %get-tuple-element.21), calls=%async_computation | async-start | bytes 65536 | tf_op jit(solution)/shard_map/all_to_all | solution.py:41
  22.8 0.7 copy-start.4
  22.8 1.6 %copy-start.5 = (f32[128]{0:T(128)S(1)}, f32[128]{0:T(128)}, u32[]{:S(2)}) copy-start(f32[128]{0:T(128)} %param.18) | copy-start | bytes 1540
  22.8 1.6 %copy-start.6 = (f32[128]{0:T(128)S(1)}, f32[128]{0:T(128)}, u32[]{:S(2)}) copy-start(f32[128]{0:T(128)} %param.17) | copy-start | bytes 1540
  24.4 1.0 copy-start.2
  24.4 1.0 copy-start.3
  25.4 3.8 %collective-permute-start.2 = (bf16[2,2,1,34,128]{4,3,2,1,0:T(8,128)(2,1)S(1)}, bf16[2,2,1,34,128]{4,3,2,1,0:T(8,128)(2,1)S(1)}, u32[]{:S(2)}, u32[]{:S(2)}) collective-permute-start(bf16[2,2,1,34,128]{4,3,2,1,0:T(8,128)(2,1)S(1)} %get-tuple-element.34), channel_id=1, source_target_pairs={{0,32},{32,64},{64,96},{96,128},{128,160},{160,192},{192,224},{224... | collective-permute-start | bytes 104456 | tf_op jit(solution)/shard_map/ppermute | solution.py:30
  27.9 4.7 %collective-permute-start.3 = (bf16[2,2,1,34,128]{4,3,2,1,0:T(8,128)(2,1)S(1)}, bf16[2,2,1,34,128]{4,3,2,1,0:T(8,128)(2,1)S(1)}, u32[]{:S(2)}, u32[]{:S(2)}) collective-permute-start(bf16[2,2,1,34,128]{4,3,2,1,0:T(8,128)(2,1)S(1)} %get-tuple-element.35), channel_id=1, source_target_pairs={{32,0},{64,32},{96,64},{128,96},{160,128},{192,160},{224,192},{256... | collective-permute-start | bytes 104456 | tf_op jit(solution)/shard_map/ppermute | solution.py:30
  33.5 24.1 %all-to-all-start.1 = ((f32[16,2,128]{2,1,0:T(2,128)}), f32[16,2,128]{2,1,0:T(2,128)S(1)}, u32[]{:S(2)}, u32[]{:S(2)}) async-start(f32[16,2,128]{2,1,0:T(2,128)} %shard_map.146), calls=%async_computation.1 | async-start | bytes 32768 | tf_op jit(solution)/shard_map/all_to_all | solution.py:41
  79.7 13.1 %all-to-all-start.3 = ((bf16[16,40,128]{2,1,0:T(8,128)(2,1)}), bf16[16,40,128]{2,1,0:T(8,128)(2,1)S(1)}, u32[]{:S(2)}, u32[]{:S(2)}) async-start(bf16[16,40,128]{2,1,0:T(8,128)(2,1)} %broadcast_in_dim.13), calls=%async_computation.3 | async-start | bytes 327680 | tf_op jit(solution)/shard_map/all_to_all | solution.py:41
  93.7 12.0 %all-to-all-start.4 = ((bf16[16,40,128]{2,1,0:T(8,128)(2,1)}), bf16[16,40,128]{2,1,0:T(8,128)(2,1)S(1)}, u32[]{:S(2)}, u32[]{:S(2)}) async-start(bf16[16,40,128]{2,1,0:T(8,128)(2,1)} %broadcast_in_dim.14), calls=%async_computation.4 | async-start | bytes 327680 | tf_op jit(solution)/shard_map/all_to_all | solution.py:41

commit v4 on v3

--- a/solution.py
+++ b/solution.py
@@ -141,17 +141,21 @@
         shifted[:, tap * channels : (tap + 1) * channels] = moved.astype(BF16)
 
 
-def back_body(padded, taps, shifted_out, grad_out, spread):
-    samples, rows, cols = padded.shape[0], padded.shape[1] - 2, padded.shape[2] - 2
-    size = rows * cols
-    for sample in range(samples):
-        shifted = shifted_out.at[sample]
-        windows(padded[sample].astype(F32), spread, shifted, rows, cols)
-        total = jnp.zeros((size, taps.shape[3]), F32)
-        for row_tap in range(3):
-            window = shifted[row_tap * cols : row_tap * cols + size, :]
-            total = total + jnp.dot(window, taps[sample, row_tap], preferred_element_type=F32)
-        grad_out[sample] = total
+def normalize_body(count, cells, rows, mixed, affine, stats_out, act_out, slope_out, norm_out):
+    samples, tile_rows, tile_cols, channels = mixed.shape
+    mean_all, spread_all = merged(rows[...], count)
+    inverse_all = lax.rsqrt(spread_all * (1.0 / cells) + 1e-05)
+    for sample in range(samples):
+        mean, inverse = unweave(mean_all, sample), unweave(inverse_all, sample)
+        stats_out[sample : sample + 1, :] = mean
+        stats_out[samples + sample : samples + sample + 1, :] = inverse
+        flat = mixed[sample].reshape(tile_rows * tile_cols, channels).astype(F32)
+        normalized = (flat - mean) * inverse
+        pre = normalized * affine[0:1, :] + affine[1:2, :]
+        sig = 1.0 / (1.0 + jnp.exp(-pre))
+        norm_out[sample] = normalized
+        act_out[sample] = (pre * sig).astype(BF16)
+        slope_out[sample] = sig * (1.0 + pre * (1.0 - sig))
 
 
 def forward_body(padded, taps, stats, affine, keep, block_out, spread, shifted):
@@ -175,34 +179,26 @@
 
 
 def sums_body(
-    count, cells, rows, mixed, shifted, grad_act, affine, style_col, demod, weight,
-    stats_out, payload_out, total,
+    padded, act, slope, norm, back_taps, style_col, demod, weight,
+    grad_out, payload_out, spread, shifted, total,
 ):
-    samples, tile_rows, tile_cols, channels = mixed.shape
-    size = tile_rows * tile_cols
-    mean_all, spread_all = merged(rows[...], count)
-    inverse_all = lax.rsqrt(spread_all * (1.0 / cells) + 1e-05)
-    gamma, beta = affine[0:1, :], affine[1:2, :]
+    samples, rows, cols = padded.shape[0], padded.shape[1] - 2, padded.shape[2] - 2
+    size, channels = rows * cols, padded.shape[3]
     sums = [[], [], [], []]
     for sample in range(samples):
-        mean, inverse = unweave(mean_all, sample), unweave(inverse_all, sample)
-        stats_out[sample : sample + 1, :] = mean
-        stats_out[samples + sample : samples + sample + 1, :] = inverse
-        normalized = (mixed[sample].reshape(size, channels).astype(F32) - mean) * inverse
-        pre = normalized * gamma + beta
-        sig = 1.0 / (1.0 + jnp.exp(-pre))
-        act = (pre * sig).astype(BF16)
-        grad_pre = grad_act[sample] * (sig * (1.0 + pre * (1.0 - sig)))
-        sums[2].append(jnp.sum(grad_pre * normalized, axis=0, keepdims=True))
-        sums[3].append(jnp.sum(grad_pre, axis=0, keepdims=True))
+        windows(padded[sample].astype(F32), spread, shifted, rows, cols)
         style_full = jnp.broadcast_to(style_col[:, sample : sample + 1], (channels, channels))
         demod_row = demod[sample : sample + 1, :]
         both = style_full * demod_row
         product = jnp.zeros((channels, channels), F32)
+        grad_act = jnp.zeros((size, channels), F32)
         for row_tap in range(3):
-            window = shifted[sample, row_tap * tile_cols : row_tap * tile_cols + size, :]
+            window = shifted[row_tap * cols : row_tap * cols + size, :]
+            grad_act = grad_act + jnp.dot(
+                window, back_taps[sample, row_tap], preferred_element_type=F32
+            )
             grad = lax.dot_general(
-                act, window, (((0,), (0,)), ((), ())), preferred_element_type=F32
+                act[sample], window, (((0,), (0,)), ((), ())), preferred_element_type=F32
             )
             for col_tap in range(3):
                 tap = (2 - row_tap) * 3 + 2 - col_tap
@@ -211,8 +207,12 @@
                 here = slice(tap * channels, (tap + 1) * channels)
                 part = block * both
                 total[here, :] = part if sample == 0 else total[here, :] + part
+        grad_pre = grad_act * slope[sample]
+        grad_out[sample] = grad_pre
         sums[0].append(jnp.sum(product * style_full, axis=0, keepdims=True))
         sums[1].append(jnp.sum((product * demod_row).T, axis=0, keepdims=True))
+        sums[2].append(jnp.sum(grad_pre * norm[sample], axis=0, keepdims=True))
+        sums[3].append(jnp.sum(grad_pre, axis=0, keepdims=True))
     small = jnp.concatenate(sum(sums, []), axis=0)
     lane = lanes_of(TILE)
     sub = lax.broadcasted_iota(jnp.int32, (TILE, channels), 0)
@@ -248,7 +248,7 @@
 
 
 def last_body(
-    scale, cells, gathered, stats, mixed, cotangent, grad_act, affine, style, style_col, demod,
+    scale, cells, gathered, stats, norm, cotangent, grad_pre, affine, style, style_col, demod,
     power, weight, emb_col, feats_out, weight_out, style_out, affine_out,
 ):
     samples, tile_rows, tile_cols, channels = cotangent.shape
@@ -270,7 +270,7 @@
             whole = jnp.where((lane >> 5) == quarter, piece, whole)
         small.append(whole)
     demod_sums, style_sums, gamma_sums, beta_sums = small[0:2], small[2:4], small[4:6], small[6:8]
-    gamma, beta = affine[0:1, :], affine[1:2, :]
+    gamma = affine[0:1, :]
     affine_out[0:1, :] = scale * (gamma_sums[0] + gamma_sums[1])
     affine_out[1:2, :] = scale * (beta_sums[0] + beta_sums[1])
     shrink = jnp.zeros((channels, channels), F32)
@@ -294,15 +294,10 @@
         weight_out[8, here, :] = scale * (block - shrink[here, :] * weight[8, here, :])
     style_out[...] = scale * (emb_col[:, 0:1] * rows[0] + emb_col[:, 1:2] * rows[1])
     for sample in range(samples):
-        mean = stats[sample : sample + 1, :]
         inverse = stats[samples + sample : samples + sample + 1, :]
         product_mean = group_total(gamma * beta_sums[sample]) * (1.0 / cells)
         squared_mean = group_total(gamma * gamma_sums[sample]) * (1.0 / cells)
-        normalized = (mixed[sample].reshape(size, channels).astype(F32) - mean) * inverse
-        pre = normalized * gamma + beta
-        sig = 1.0 / (1.0 + jnp.exp(-pre))
-        grad_pre = grad_act[sample] * (sig * (1.0 + pre * (1.0 - sig)))
-        change = inverse * (gamma * grad_pre - product_mean - normalized * squared_mean)
+        change = inverse * (gamma * grad_pre[sample] - product_mean - norm[sample] * squared_mean)
         out = cotangent[sample].reshape(size, channels).astype(F32) + change
         feats_out[sample] = out.astype(BF16).reshape(tile_rows, tile_cols, channels)
 
@@ -336,16 +331,20 @@
     )(feats, cond, null_field, cotangent, drop_flags)
     rows = exchange(moments, LON)
     low, high = shift(last, LON, 1, True), shift(first, LON, -1, True)
-    moments = call(
-        functools.partial(merge_body, cells_local),
-        array((lat_count, 2, LANES)),
-        cost_estimate=pl.CostEstimate(flops=50_000_000_000, bytes_accessed=150_000_000, transcendentals=0),
-    )(rows)
+    moments = call(functools.partial(merge_body, cells_local), array((lat_count, 2, LANES)))(rows)
+    moments, low, high = lax.optimization_barrier((moments, low, high))
     both = jnp.concatenate(
         [low[:, :, :, None], jnp.stack([mixed, cotangent]), high[:, :, :, None]], axis=3
     )
     rows = exchange(moments, LAT)
     low, high = shift(both[:, :, -1:], LAT, 1, False), shift(both[:, :, :1], LAT, -1, False)
+    affine = jnp.stack([gamma, beta])
+    flat = (samples, tile_rows * tile_cols, channels)
+    stats, act, slope, norm = call(
+        functools.partial(normalize_body, cells_local * lon_count, cells_per_group),
+        (array((2 * samples, LANES)), array(flat, BF16), array(flat), array(flat)),
+    )(rows, mixed, affine)
+    act, low, high = lax.optimization_barrier((act, low, high))
     both = jnp.concatenate([low, both, high], axis=2)
     mixed_pad, cot_pad = both[0], both[1]
 
@@ -358,25 +357,15 @@
     back_taps = jnp.swapaxes(w_eff[:, ::-1, ::-1], 3, 4).reshape(wide)
     spread = pltpu.VMEM((tile_rows + 2, tile_cols + 2, channels), F32)
     stretch = ((tile_rows + 2) * tile_cols, 3 * channels)
-    shifted, grad_act = call(
-        back_body,
-        (
-            array((samples,) + stretch, BF16),
-            array((samples, tile_rows * tile_cols, channels)),
-        ),
-        (spread,),
-    )(cot_pad, back_taps)
-
     lat_at = lax.axis_index(LAT)
     inside = jnp.stack([lat_at > 0, lat_at < lat_count - 1])
     keep = jnp.broadcast_to(inside.astype(F32)[:, None], (2, LANES))
-    affine = jnp.stack([gamma, beta])
     style_col = style.T
-    stats, payload = call(
-        functools.partial(sums_body, cells_local * lon_count, cells_per_group),
-        (array((2 * samples, LANES)), array((SHARDS, SLOT, LANES), BF16)),
-        (pltpu.VMEM((9 * channels, channels), F32),),
-    )(rows, mixed, shifted, grad_act, affine, style_col, demod, taps)
+    grad_pre, payload = call(
+        sums_body,
+        (array(flat), array((SHARDS, SLOT, LANES), BF16)),
+        (spread, pltpu.VMEM(stretch, BF16), pltpu.VMEM((9 * channels, channels), F32)),
+    )(cot_pad, act, slope, norm, back_taps, style_col, demod, taps)
 
     core_count, near_count = lax.axis_size("c"), lax.axis_size(NEAR)
     payload = lax.all_gather(payload, "c")
@@ -400,7 +389,7 @@
             array((2, LANES)),
         ),
     )(
-        payload.reshape(SHARDS, SLOT, LANES), stats, mixed, cotangent, grad_act, affine, style,
+        payload.reshape(SHARDS, SLOT, LANES), stats, norm, cotangent, grad_pre, affine, style,
         style_col, demod, power, taps, emb.T,
     )
     return (

time: 114 us -> 109 us (0.956)
  waiting for transfers between devices: 26.9 us -> 19.3 us
  starting transfers between devices: 45.1 us -> 48.5 us
    all_to_all x4, starting transfers between devices: 30.7 us -> 38.5 us  [exchange(): return lax.all_to_all(block, axes, 0, 0)]
    ppermute x4, starting transfers between devices: 14.4 us -> 10 us  [shift(): return lax.ppermute(block, axes, pairs)]
    all_to_all x4, waiting for transfers between devices: 23.5 us -> 19.3 us  [exchange(): return lax.all_to_all(block, axes, 0, 0)]
    ppermute x4, waiting for transfers between devices: 3.37 us -> 0.01 us  [shift(): return lax.ppermute(block, axes, pairs)]
  transfers between devices with their start and end apart: 8 -> 8, of which waited for: 4 -> 3; matrix products, arithmetic and copies ran while one was open for 3% -> 3% of each run, Pallas kernels for 2% -> 2%
where the time goes in v4:
time: 109 us; the launch traced here: 108 us
  starting transfers between devices  48.5 us (44%)
  blocking collectives  25.5 us (23%)
  waiting for transfers between devices  19.3 us (18%)
  Pallas kernels  7.48 us (7%)
  local copies, waits for them, and re-layouts  3.32 us (3%)
  other arithmetic  2.3 us (2%)
    all_to_all x4, starting transfers between devices, exchange(): return lax.all_to_all(block, axes, 0, 0)  38.5 us
    all_to_all x4, waiting for transfers between devices, exchange(): return lax.all_to_all(block, axes, 0, 0)  19.3 us
    all_to_all x1, blocking collectives, exchange(): return lax.all_to_all(block, axes, 0, 0)  14.1 us
    ppermute x4, starting transfers between devices, shift(): return lax.ppermute(block, axes, pairs)  10 us
    all_gather x1, blocking collectives, on_device(): payload = lax.all_gather(payload, 'c')  5.78 us
    all_gather x1, blocking collectives, on_device(): payload = lax.all_gather(everyone(payload, NEAR), 'c')  5.61 us
    pallas_call x1, Pallas kernels, on_device(): call(mix_body, (array(feats.shape, BF16), array((lon_count, 2, LANES)), e...  2.93 us
  transfers between devices with their start and end apart: 8, of which 3 were waited for; matrix products, arithmetic and copies ran while one was open for 3% of the time, Pallas kernels for 2%

profile of v4, /device:TPU:1, one launch (start us, length us, event | category | flops | bytes accessed | tf_op | source)
XLA Modules:
  0.0 108.2 jit_solution(13597084276473573227)
XLA Ops:
  0.6 0.0 copy-start
  0.6 0.0 copy-start.1
  0.7 2.9 %shard_map.145 = (bf16[2,8,32,128]{3,2,1,0:T(8,128)(2,1)}, f32[32,2,128]{2,1,0:T(2,128)}, bf16[2,2,8,128]{3,2,1,0:T(8,128)(2,1)}, bf16[2,2,8,128]{3,2,1,0:T(8,128)(2,1)}) custom-call(bf16[2,8,32,128]{3,2,1,0:T(8,128)(2,1)} %feats_in.1, bf16[2,8,32,128]{3,2,1,0:T(8,128)(2,1)} %cond_in.1, bf16[8,32,128]{2,1,0:T(8,128)(2,1)} %null_in.1, ...), custom_call_target="tpu_custom_call" | custom-call | tf_op jit(solution)/shard_map/pallas_call | solution.py:319
  3.6 10.6 %all-to-all-start = ((f32[32,2,128]{2,1,0:T(2,128)}), f32[32,2,128]{2,1,0:T(2,128)S(1)}, u32[]{:S(2)}, u32[]{:S(2)}) async-start(f32[32,2,128]{2,1,0:T(2,128)} %get-tuple-element.26), calls=%async_computation | async-start | bytes 65536 | tf_op jit(solution)/shard_map/all_to_all | solution.py:41
  14.2 3.5 %collective-permute-start = (bf16[2,2,8,128]{3,2,1,0:T(8,128)(2,1)}, bf16[2,2,8,128]{3,2,1,0:T(8,128)(2,1)S(1)}, u32[]{:S(2)}, u32[]{:S(2)}) collective-permute-start(bf16[2,2,8,128]{3,2,1,0:T(8,128)(2,1)} %get-tuple-element.27), channel_id=1, source_target_pairs={{0,1},{1,2},{2,3},{3,4},{4,5},{5,6},{6,7},{7,8},{8,9},{9,10},{10,1... | collective-permute-start | bytes 24584 | tf_op jit(solution)/shard_map/ppermute | solution.py:30
  17.7 1.9 %collective-permute-start.1 = (bf16[2,2,8,128]{3,2,1,0:T(8,128)(2,1)}, bf16[2,2,8,128]{3,2,1,0:T(8,128)(2,1)S(1)}, u32[]{:S(2)}, u32[]{:S(2)}) collective-permute-start(bf16[2,2,8,128]{3,2,1,0:T(8,128)(2,1)} %get-tuple-element.28), channel_id=1, source_target_pairs={{0,31},{1,0},{2,1},{3,2},{4,3},{5,4},{6,5},{7,6},{8,7},{9,8},{10,9... | collective-permute-start | bytes 24584 | tf_op jit(solution)/shard_map/ppermute | solution.py:30
  19.7 1.1 %multiply_reduce_fusion.power = f32[128,128]{1,0:T(8,128)S(1)} fusion(f32[3,3,128,128]{3,2,1,0:T(8,128)} %param.16), kind=kLoop, calls=%fused_computation.6 | loop fusion | flops 278528 | bytes 655360 | tf_op jit(solution)/shard_map/reduce_sum | solution.py:352
  20.8 0.0 copy-done.1
  20.8 0.0 copy-start.4
  20.8 0.0 copy-start.5
  20.8 0.0 copy-start.6
  20.8 0.2 copy.51
  21.1 0.0 copy-done
  21.1 0.4 copy-done.4
  21.5 0.6 convolution_add_fusion
  22.1 0.1 copy.50.style
  22.1 0.2 fusion.demod
  22.4 0.0 copy-done.5
  22.4 0.0 copy-done.6
  22.4 0.0 copy-start.2
  22.4 0.0 copy-start.3
  22.5 0.2 multiply_convert_fusion
  22.7 0.0 all-to-all-done.rows
  22.7 0.7 shard_map.146
  23.4 0.0 collective-permute-done
  23.4 0.0 collective-permute-done.1
  23.4 11.7 %all-to-all-start.1 = ((f32[16,2,128]{2,1,0:T(2,128)}), f32[16,2,128]{2,1,0:T(2,128)S(1)}, u32[]{:S(2)}, u32[]{:S(2)}) async-start(f32[16,2,128]{2,1,0:T(2,128)} %shard_map.146), calls=%async_computation.1 | async-start | bytes 32768 | tf_op jit(solution)/shard_map/all_to_all | solution.py:41
  35.2 0.0 copy-done.2
  35.2 0.0 copy-done.3
  35.2 3.3 %collective-permute-start.2 = (bf16[2,2,1,34,128]{4,3,2,1,0:T(8,128)(2,1)S(1)}, bf16[2,2,1,34,128]{4,3,2,1,0:T(8,128)(2,1)S(1)}, u32[]{:S(2)}, u32[]{:S(2)}) collective-permute-start(bf16[2,2,1,34,128]{4,3,2,1,0:T(8,128)(2,1)S(1)} %get-tuple-element.51), channel_id=1, source_target_pairs={{0,32},{32,64},{64,96},{96,128},{128,160},{160,192},{192,224},{224... | collective-permute-start | bytes 104456 | tf_op jit(solution)/shard_map/ppermute | solution.py:30
  38.5 1.3 %collective-permute-start.3 = (bf16[2,2,1,34,128]{4,3,2,1,0:T(8,128)(2,1)S(1)}, bf16[2,2,1,34,128]{4,3,2,1,0:T(8,128)(2,1)S(1)}, u32[]{:S(2)}, u32[]{:S(2)}) collective-permute-start(bf16[2,2,1,34,128]{4,3,2,1,0:T(8,128)(2,1)S(1)} %get-tuple-element.50), channel_id=1, source_target_pairs={{32,0},{64,32},{96,64},{128,96},{160,128},{192,160},{224,192},{256... | collective-permute-start | bytes 104456 | tf_op jit(solution)/shard_map/ppermute | solution.py:30
  39.9 4.1 %all-to-all-done.1.rows = f32[16,2,128]{2,1,0:T(2,128)S(1)} async-done(((f32[16,2,128]{2,1,0:T(2,128)}), f32[16,2,128]{2,1,0:T(2,128)S(1)}, u32[]{:S(2)}, u32[]{:S(2)}) %all-to-all-start.1) | async-done | bytes 16416 | tf_op jit(solution)/shard_map/all_to_all | solution.py:41
  44.0 0.3 shard_map.147
  44.2 0.0 collective-permute-done.2
  44.2 0.0 collective-permute-done.3
  44.2 0.2 pad_maximum_fusion
  44.5 1.0 shard_map.149
  45.5 5.8 %all-gather = bf16[64,40,128]{2,1,0:T(8,128)(2,1)S(1)} all-gather(bf16[32,40,128]{2,1,0:T(8,128)(2,1)S(1)} %get-tuple-element.40), channel_id=2, replica_groups=mesh['zh'=4,'x'=4,'zl'=2,'y'=8,'c'=2] {'c'}, dimensions={0}, use_global_device_ids=true | all-gather | bytes 983040 | tf_op jit(solution)/shard_map/all_gather | solution.py:371
  51.3 0.2 fusion.8
  51.5 0.2 fusion.2
  51.7 14.1 %all_to_all.25 = bf16[16,40,128]{2,1,0:T(8,128)(2,1)S(1)} all-to-all(bf16[16,40,128]{2,1,0:T(8,128)(2,1)S(1)} %fusion.2), channel_id=1, replica_groups=mesh['zh'=4,'x'=4,'zl'=2,'y'=8,'c'=2] {'zl','y'}, dimensions={0} | all-to-all | bytes 327680 | tf_op jit(solution)/shard_map/all_to_all | solution.py:41
  65.8 0.1 fusion.10
  65.9 0.1 fusion.5
  66.0 0.7 broadcast_in_dim.13
  66.6 11.5 %all-to-all-start.3 = ((bf16[16,40,128]{2,1,0:T(8,128)(2,1)}), bf16[16,40,128]{2,1,0:T(8,128)(2,1)S(1)}, u32[]{:S(2)}, u32[]{:S(2)}) async-start(bf16[16,40,128]{2,1,0:T(8,128)(2,1)} %broadcast_in_dim.13), calls=%async_computation.3 | async-start | bytes 327680 | tf_op jit(solution)/shard_map/all_to_all | solution.py:41
  78.1 9.4 %all-to-all-done.3 = bf16[16,40,128]{2,1,0:T(8,128)(2,1)S(1)} async-done(((bf16[16,40,128]{2,1,0:T(8,128)(2,1)}), bf16[16,40,128]{2,1,0:T(8,128)(2,1)S(1)}, u32[]{:S(2)}, u32[]{:S(2)}) %all-to-all-start.3) | async-done | bytes 163872 | tf_op jit(solution)/shard_map/all_to_all | solution.py:41
  87.6 0.1 fusion.9
  87.6 0.1 fusion.7
  87.7 0.7 broadcast_in_dim.14
  88.4 4.8 %all-to-all-start.4 = ((bf16[16,40,128]{2,1,0:T(8,128)(2,1)}), bf16[16,40,128]{2,1,0:T(8,128)(2,1)S(1)}, u32[]{:S(2)}, u32[]{:S(2)}) async-start(bf16[16,40,128]{2,1,0:T(8,128)(2,1)} %broadcast_in_dim.14), calls=%async_computation.4 | async-start | bytes 327680 | tf_op jit(solution)/shard_map/all_to_all | solution.py:41
  93.2 0.1 add_convert_fusion
  93.3 0.1 copy.53
  93.4 0.2 multiply_convert_fusion.1.taps
  93.6 0.1 broadcast_in_dim.12.keep
  93.7 1.2 %shard_map.148 = bf16[2,8,32,128]{3,2,1,0:T(8,128)(2,1)} custom-call(bf16[2,10,34,128]{3,2,1,0:T(8,128)(2,1)S(1)} %get-tuple-element.47.padded, bf16[2,3,384,128]{3,2,1,0:T(8,128)(2,1)S(1)} %multiply_convert_fusion.1.taps, f32[4,128]{1,0:T(4,128)S(1)} %get-tuple-element.36.stats, f32[2,128]{1,0:T(2,128)S(1)} %pad_maximum_fusion.5.affine, ...), custom_call_target="tpu_custom_call" | custom-call | tf_op jit(solution)/shard_map/pallas_call | solution.py:379
  95.0 5.8 %all-to-all-done.4 = bf16[16,40,128]{2,1,0:T(8,128)(2,1)S(1)} async-done(((bf16[16,40,128]{2,1,0:T(8,128)(2,1)}), bf16[16,40,128]{2,1,0:T(8,128)(2,1)S(1)}, u32[]{:S(2)}, u32[]{:S(2)}) %all-to-all-start.4) | async-done | bytes 163872 | tf_op jit(solution)/shard_map/all_to_all | solution.py:41
  100.7 5.6 %all-gather.1.gathered = bf16[32,40,128]{2,1,0:T(8,128)(2,1)S(1)} all-gather(bf16[16,40,128]{2,1,0:T(8,128)(2,1)S(1)} %all-to-all-done.4), channel_id=3, replica_groups=mesh['zh'=4,'x'=4,'zl'=2,'y'=8,'c'=2] {'c'}, dimensions={0}, use_global_device_ids=true | all-gather | bytes 491520 | tf_op jit(solution)/shard_map/all_gather | solution.py:377
  106.4 1.3 %shard_map.150 = (bf16[2,8,32,128]{3,2,1,0:T(8,128)(2,1)}, f32[9,128,128]{2,1,0:T(8,128)}, f32[512,128]{1,0:T(8,128)}, f32[2,128]{1,0:T(2,128)S(1)}) custom-call(bf16[32,40,128]{2,1,0:T(8,128)(2,1)S(1)} %all-gather.1.gathered, f32[4,128]{1,0:T(4,128)S(1)} %get-tuple-element.36.stats, f32[2,256,128]{2,1,0:T(8,128)S(1)} %get-tuple-element.39.norm, ...), custom_call_target="tpu_custom_call" | custom-call | tf_op jit(solution)/shard_map/pallas_call | solution.py:383
  107.7 0.5 slice_bitcast_fusion.2
  (13 shorter events, 0.3 us)
Async XLA Ops:
  0.6 20.4 %copy-start = (f32[512,128]{1,0:T(8,128)S(1)}, f32[512,128]{1,0:T(8,128)}, u32[]{:S(2)}) copy-start(f32[512,128]{1,0:T(8,128)} %param.15) | copy-start | bytes 786436
  0.6 20.1 %copy-start.1 = (f32[3,3,128,128]{3,2,1,0:T(8,128)S(1)}, f32[3,3,128,128]{3,2,1,0:T(8,128)}, u32[]{:S(2)}) copy-start(f32[3,3,128,128]{3,2,1,0:T(8,128)} %param.16) | copy-start | bytes 1769476
  3.6 19.1 %all-to-all-start = ((f32[32,2,128]{2,1,0:T(2,128)}), f32[32,2,128]{2,1,0:T(2,128)S(1)}, u32[]{:S(2)}, u32[]{:S(2)}) async-start(f32[32,2,128]{2,1,0:T(2,128)} %get-tuple-element.26), calls=%async_computation | async-start | bytes 65536 | tf_op jit(solution)/shard_map/all_to_all | solution.py:41
  14.2 9.2 %collective-permute-start = (bf16[2,2,8,128]{3,2,1,0:T(8,128)(2,1)}, bf16[2,2,8,128]{3,2,1,0:T(8,128)(2,1)S(1)}, u32[]{:S(2)}, u32[]{:S(2)}) collective-permute-start(bf16[2,2,8,128]{3,2,1,0:T(8,128)(2,1)} %get-tuple-element.27), channel_id=1, source_target_pairs={{0,1},{1,2},{2,3},{3,4},{4,5},{5,6},{6,7},{7,8},{8,9},{9,10},{10,1... | collective-permute-start | bytes 24584 | tf_op jit(solution)/shard_map/ppermute | solution.py:30
  17.7 5.7 %collective-permute-start.1 = (bf16[2,2,8,128]{3,2,1,0:T(8,128)(2,1)}, bf16[2,2,8,128]{3,2,1,0:T(8,128)(2,1)S(1)}, u32[]{:S(2)}, u32[]{:S(2)}) collective-permute-start(bf16[2,2,8,128]{3,2,1,0:T(8,128)(2,1)} %get-tuple-element.28), channel_id=1, source_target_pairs={{0,31},{1,0},{2,1},{3,2},{4,3},{5,4},{6,5},{7,6},{8,7},{9,8},{10,9... | collective-permute-start | bytes 24584 | tf_op jit(solution)/shard_map/ppermute | solution.py:30
  20.8 0.7 copy-start.4
  20.8 1.6 %copy-start.5 = (f32[128]{0:T(128)S(1)}, f32[128]{0:T(128)}, u32[]{:S(2)}) copy-start(f32[128]{0:T(128)} %param.18) | copy-start | bytes 1540
  20.8 1.6 %copy-start.6 = (f32[128]{0:T(128)S(1)}, f32[128]{0:T(128)}, u32[]{:S(2)}) copy-start(f32[128]{0:T(128)} %param.17) | copy-start | bytes 1540
  22.4 12.7 %copy-start.2 = (bf16[2,8,32,128]{3,2,1,0:T(8,128)(2,1)S(1)}, bf16[2,8,32,128]{3,2,1,0:T(8,128)(2,1)}, u32[]{:S(2)}) copy-start(bf16[2,8,32,128]{3,2,1,0:T(8,128)(2,1)} %cotangent.1) | copy-start | bytes 393220
  22.4 12.7 %copy-start.3 = (bf16[2,8,32,128]{3,2,1,0:T(8,128)(2,1)S(1)}, bf16[2,8,32,128]{3,2,1,0:T(8,128)(2,1)}, u32[]{:S(2)}) copy-start(bf16[2,8,32,128]{3,2,1,0:T(8,128)(2,1)} %get-tuple-element.30.mixed) | copy-start | bytes 393220
  23.4 20.5 %all-to-all-start.1 = ((f32[16,2,128]{2,1,0:T(2,128)}), f32[16,2,128]{2,1,0:T(2,128)S(1)}, u32[]{:S(2)}, u32[]{:S(2)}) async-start(f32[16,2,128]{2,1,0:T(2,128)} %shard_map.146), calls=%async_computation.1 | async-start | bytes 32768 | tf_op jit(solution)/shard_map/all_to_all | solution.py:41
  35.2 9.0 %collective-permute-start.2 = (bf16[2,2,1,34,128]{4,3,2,1,0:T(8,128)(2,1)S(1)}, bf16[2,2,1,34,128]{4,3,2,1,0:T(8,128)(2,1)S(1)}, u32[]{:S(2)}, u32[]{:S(2)}) collective-permute-start(bf16[2,2,1,34,128]{4,3,2,1,0:T(8,128)(2,1)S(1)} %get-tuple-element.51), channel_id=1, source_target_pairs={{0,32},{32,64},{64,96},{96,128},{128,160},{160,192},{192,224},{224... | collective-permute-start | bytes 104456 | tf_op jit(solution)/shard_map/ppermute | solution.py:30
  38.5 5.7 %collective-permute-start.3 = (bf16[2,2,1,34,128]{4,3,2,1,0:T(8,128)(2,1)S(1)}, bf16[2,2,1,34,128]{4,3,2,1,0:T(8,128)(2,1)S(1)}, u32[]{:S(2)}, u32[]{:S(2)}) collective-permute-start(bf16[2,2,1,34,128]{4,3,2,1,0:T(8,128)(2,1)S(1)} %get-tuple-element.50), channel_id=1, source_target_pairs={{32,0},{64,32},{96,64},{128,96},{160,128},{192,160},{224,192},{256... | collective-permute-start | bytes 104456 | tf_op jit(solution)/shard_map/ppermute | solution.py:30
  66.6 20.9 %all-to-all-start.3 = ((bf16[16,40,128]{2,1,0:T(8,128)(2,1)}), bf16[16,40,128]{2,1,0:T(8,128)(2,1)S(1)}, u32[]{:S(2)}, u32[]{:S(2)}) async-start(bf16[16,40,128]{2,1,0:T(8,128)(2,1)} %broadcast_in_dim.13), calls=%async_computation.3 | async-start | bytes 327680 | tf_op jit(solution)/shard_map/all_to_all | solution.py:41
  88.4 12.3 %all-to-all-start.4 = ((bf16[16,40,128]{2,1,0:T(8,128)(2,1)}), bf16[16,40,128]{2,1,0:T(8,128)(2,1)S(1)}, u32[]{:S(2)}, u32[]{:S(2)}) async-start(bf16[16,40,128]{2,1,0:T(8,128)(2,1)} %broadcast_in_dim.14), calls=%async_computation.4 | async-start | bytes 327680 | tf_op jit(solution)/shard_map/all_to_all | solution.py:41

commit v5 on v4

--- a/solution.py
+++ b/solution.py
@@ -81,8 +81,36 @@
     return weave(pltpu.roll(row, LANES - 1, 1), row)
 
 
+def place(axes):
+    index = 0
+    for axis in axes:
+        index = index * lax.axis_size(axis) + lax.axis_index(axis)
+    return index
+
+
+def three_terms(value):
+    terms = []
+    for _ in range(3):
+        terms.append(value.astype(BF16).astype(F32))
+        value = value - terms[-1]
+    return terms
+
+
+def merged(slots, count):
+    rows = slots[:, 0:8, :].astype(F32)
+    means = rows[:, 0:1, :] + rows[:, 1:2, :] + rows[:, 2:3, :]
+    spreads = rows[:, 3:4, :] + rows[:, 4:5, :] + rows[:, 5:6, :]
+    mean = jnp.mean(means, axis=0)
+    away = means - mean[None]
+    return mean, jnp.sum(spreads + count * away * away, axis=0)
+
+
+def header(mean, spread):
+    return three_terms(mean) + three_terms(spread) + [jnp.zeros((2, LANES), F32)]
+
+
 def mix_body(
-    feats_in, cond_in, null_in, cot_in, flags, mixed_out, moments_out, first_out, last_out,
+    feats_in, cond_in, null_in, cot_in, flags, mixed_out, slots_out,
     feats, cond, null, cot, arrivals,
 ):
     copies = []
@@ -104,58 +132,57 @@
             feats[sample].astype(F32) + dropped * null32 + (1.0 - dropped) * cond[sample].astype(F32)
         ).astype(BF16)
         mixed_out[sample] = mixed
-        wide = mixed.astype(F32)
-        first_out[0, sample] = wide[:, 0, :].astype(BF16)
-        last_out[0, sample] = wide[:, tile_cols - 1, :].astype(BF16)
-        wide = wide.reshape(cells, channels)
+        wide = mixed.astype(F32).reshape(cells, channels)
         mean = group_total(jnp.sum(wide, axis=0, keepdims=True)) * (1.0 / size)
         away = wide - mean
         means.append(mean)
         spreads.append(group_total(jnp.sum(away * away, axis=0, keepdims=True)))
-    row = jnp.concatenate([weave(*means), weave(*spreads)], axis=0)
-    moments_out[...] = jnp.broadcast_to(row[None], moments_out.shape)
+    rows = header(weave(*means), weave(*spreads))
     copies[3].wait()
+    firsts, lasts = [], []
     for sample in range(samples):
         wide = cot[sample].astype(F32)
-        first_out[1, sample] = wide[:, 0, :].astype(BF16)
-        last_out[1, sample] = wide[:, tile_cols - 1, :].astype(BF16)
-
-
-def merged(rows, count):
-    mean = jnp.mean(rows[:, 0:1, :], axis=0)
-    away = rows[:, 0:1, :] - mean[None]
-    spread = jnp.sum(rows[:, 1:2, :] + count * away * away, axis=0)
-    return mean, spread
-
-
-def merge_body(count, rows, moments_out):
-    row = jnp.concatenate(merged(rows[...], count), axis=0)
-    moments_out[...] = jnp.broadcast_to(row[None], moments_out.shape)
-
-
-def windows(padded, spread, shifted, rows, cols):
-    spread[...] = padded
-    channels = padded.shape[-1]
+        firsts.append(wide[:, 0, :])
+        lasts.append(wide[:, tile_cols - 1, :])
+    slots_out[...] = jnp.broadcast_to(
+        jnp.concatenate(rows + firsts, axis=0).astype(BF16)[None], slots_out.shape
+    )
+    after = lax.rem(place(LON) + 1, slots_out.shape[0])
+    slots_out[after] = jnp.concatenate(rows + lasts, axis=0).astype(BF16)
+
+
+def merge_body(count, slots, cot, wide_out, slots_out, edge):
+    samples, tile_rows, tile_cols, channels = cot.shape
+    lon_count, lat_count = slots.shape[0], slots_out.shape[0]
+    mean, spread = merged(slots, count)
+    me = place(LON)
+    before = slots[lax.rem(me + lon_count - 1, lon_count)].astype(F32)
+    after = slots[lax.rem(me + 1, lon_count)].astype(F32)
+    for sample in range(samples):
+        here = slice(8 + sample * tile_rows, 8 + (sample + 1) * tile_rows)
+        wide_out[sample, :, 0, :] = before[here, :]
+        wide_out[sample, :, 1 : 1 + tile_cols, :] = cot[sample].astype(F32)
+        wide_out[sample, :, 1 + tile_cols, :] = after[here, :]
+    edge[...] = jnp.zeros(edge.shape, F32)
+    edge[0:8, :] = jnp.concatenate(header(mean, spread), axis=0)
+    span = tile_cols + 2
+    for sample in range(samples):
+        edge[8 + sample * span : 8 + (sample + 1) * span, :] = wide_out[sample, 0]
+    slots_out[...] = jnp.broadcast_to(edge[...].astype(BF16)[None], slots_out.shape)
+    for sample in range(samples):
+        edge[8 + sample * span : 8 + (sample + 1) * span, :] = wide_out[sample, tile_rows - 1]
+    row = place(LAT)
+
+    @pl.when(row < lat_count - 1)
+    def _():
+        slots_out[row + 1] = edge[...].astype(BF16)
+
+
+def windows(spread, shifted, rows, cols):
+    channels = spread.shape[-1]
     for tap in range(3):
         moved = spread[:, tap : tap + cols, :].reshape((rows + 2) * cols, channels)
         shifted[:, tap * channels : (tap + 1) * channels] = moved.astype(BF16)
-
-
-def normalize_body(count, cells, rows, mixed, affine, stats_out, act_out, slope_out, norm_out):
-    samples, tile_rows, tile_cols, channels = mixed.shape
-    mean_all, spread_all = merged(rows[...], count)
-    inverse_all = lax.rsqrt(spread_all * (1.0 / cells) + 1e-05)
-    for sample in range(samples):
-        mean, inverse = unweave(mean_all, sample), unweave(inverse_all, sample)
-        stats_out[sample : sample + 1, :] = mean
-        stats_out[samples + sample : samples + sample + 1, :] = inverse
-        flat = mixed[sample].reshape(tile_rows * tile_cols, channels).astype(F32)
-        normalized = (flat - mean) * inverse
-        pre = normalized * affine[0:1, :] + affine[1:2, :]
-        sig = 1.0 / (1.0 + jnp.exp(-pre))
-        norm_out[sample] = normalized
-        act_out[sample] = (pre * sig).astype(BF16)
-        slope_out[sample] = sig * (1.0 + pre * (1.0 - sig))
 
 
 def forward_body(padded, taps, stats, affine, keep, block_out, spread, shifted):
@@ -170,7 +197,8 @@
         inverse = stats[samples + sample : samples + sample + 1, :][None]
         pre = (mixed - mean) * inverse * gamma + beta
         act = jnp.where(inside, pre / (1.0 + jnp.exp(-pre)), 0.0)
-        windows(act, spread, shifted, rows, cols)
+        spread[...] = act
+        windows(spread, shifted, rows, cols)
         total = mixed[1 : 1 + rows, 1 : 1 + cols, :].reshape(size, -1)
         for row_tap in range(3):
             window = shifted[row_tap * cols : row_tap * cols + size, :]
@@ -179,14 +207,35 @@
 
 
 def sums_body(
-    padded, act, slope, norm, back_taps, style_col, demod, weight,
-    grad_out, payload_out, spread, shifted, total,
+    count, cells, slots, mixed, wide, affine, back_taps, style_col, demod, weight,
+    stats_out, norm_out, grad_out, payload_out, edge, spread, shifted, total,
 ):
-    samples, rows, cols = padded.shape[0], padded.shape[1] - 2, padded.shape[2] - 2
-    size, channels = rows * cols, padded.shape[3]
+    samples, rows, cols, channels = mixed.shape
+    size, span = rows * cols, cols + 2
+    mean_all, spread_all = merged(slots, count)
+    inverse_all = lax.rsqrt(spread_all * (1.0 / cells) + 1e-05)
+    lat_count, row = slots.shape[0], place(LAT)
+    below = slots[lax.max(row - 1, 0)].astype(F32)
+    above = slots[lax.min(row + 1, lat_count - 1)].astype(F32)
+    edge[0] = jnp.where(row > 0, below, 0.0)
+    edge[1] = jnp.where(row < lat_count - 1, above, 0.0)
     sums = [[], [], [], []]
     for sample in range(samples):
-        windows(padded[sample].astype(F32), spread, shifted, rows, cols)
+        mean, inverse = unweave(mean_all, sample), unweave(inverse_all, sample)
+        stats_out[sample : sample + 1, :] = mean
+        stats_out[samples + sample : samples + sample + 1, :] = inverse
+        flat = mixed[sample].reshape(size, channels).astype(F32)
+        norm = (flat - mean) * inverse
+        pre = norm * affine[0:1, :] + affine[1:2, :]
+        sig = 1.0 / (1.0 + jnp.exp(-pre))
+        norm_out[sample] = norm
+        act = (pre * sig).astype(BF16)
+        slope = sig * (1.0 + pre * (1.0 - sig))
+        here = slice(8 + sample * span, 8 + (sample + 1) * span)
+        spread[0] = edge[0, here, :]
+        spread[1 : 1 + rows] = wide[sample]
+        spread[1 + rows] = edge[1, here, :]
+        windows(spread, shifted, rows, cols)
         style_full = jnp.broadcast_to(style_col[:, sample : sample + 1], (channels, channels))
         demod_row = demod[sample : sample + 1, :]
         both = style_full * demod_row
@@ -198,7 +247,7 @@
                 window, back_taps[sample, row_tap], preferred_element_type=F32
             )
             grad = lax.dot_general(
-                act[sample], window, (((0,), (0,)), ((), ())), preferred_element_type=F32
+                act, window, (((0,), (0,)), ((), ())), preferred_element_type=F32
             )
             for col_tap in range(3):
                 tap = (2 - row_tap) * 3 + 2 - col_tap
@@ -207,11 +256,11 @@
                 here = slice(tap * channels, (tap + 1) * channels)
                 part = block * both
                 total[here, :] = part if sample == 0 else total[here, :] + part
-        grad_pre = grad_act * slope[sample]
+        grad_pre = grad_act * slope
         grad_out[sample] = grad_pre
         sums[0].append(jnp.sum(product * style_full, axis=0, keepdims=True))
         sums[1].append(jnp.sum((product * demod_row).T, axis=0, keepdims=True))
-        sums[2].append(jnp.sum(grad_pre * norm[sample], axis=0, keepdims=True))
+        sums[2].append(jnp.sum(grad_pre * norm, axis=0, keepdims=True))
         sums[3].append(jnp.sum(grad_pre, axis=0, keepdims=True))
     small = jnp.concatenate(sum(sums, []), axis=0)
     lane = lanes_of(TILE)
@@ -249,7 +298,7 @@
 
 def last_body(
     scale, cells, gathered, stats, norm, cotangent, grad_pre, affine, style, style_col, demod,
-    power, weight, emb_col, feats_out, weight_out, style_out, affine_out,
+    power, weight, emb_col, feats_out, weight_out, style_out, gamma_out, beta_out,
 ):
     samples, tile_rows, tile_cols, channels = cotangent.shape
     size = tile_rows * tile_cols
@@ -271,8 +320,8 @@
         small.append(whole)
     demod_sums, style_sums, gamma_sums, beta_sums = small[0:2], small[2:4], small[4:6], small[6:8]
     gamma = affine[0:1, :]
-    affine_out[0:1, :] = scale * (gamma_sums[0] + gamma_sums[1])
-    affine_out[1:2, :] = scale * (beta_sums[0] + beta_sums[1])
+    gamma_out[...] = scale * (gamma_sums[0] + gamma_sums[1])
+    beta_out[...] = scale * (beta_sums[0] + beta_sums[1])
     shrink = jnp.zeros((channels, channels), F32)
     rows = []
     for sample in range(samples):
@@ -315,10 +364,12 @@
     taps = conv_weight.reshape(9, channels, channels)
 
     anywhere, whole = pl.BlockSpec(memory_space=pl.ANY), pl.BlockSpec(memory_space=pltpu.VMEM)
-    edge = array((2, samples, tile_rows, channels), BF16)
-    mixed, moments, first, last = call(
+    head = 8
+    lon_slot = head + samples * tile_rows
+    lat_slot = -(-(head + samples * (tile_cols + 2)) // 16) * 16
+    mixed, slots = call(
         mix_body,
-        (array(feats.shape, BF16), array((lon_count, 2, LANES)), edge, edge),
+        (array(feats.shape, BF16), array((lon_count, lon_slot, LANES), BF16)),
         (
             pltpu.VMEM(feats.shape, BF16),
             pltpu.VMEM(feats.shape, BF16),
@@ -329,64 +380,76 @@
         room=60,
         in_specs=[anywhere] * 4 + [whole],
     )(feats, cond, null_field, cotangent, drop_flags)
-    rows = exchange(moments, LON)
-    low, high = shift(last, LON, 1, True), shift(first, LON, -1, True)
-    moments = call(functools.partial(merge_body, cells_local), array((lat_count, 2, LANES)))(rows)
-    moments, low, high = lax.optimization_barrier((moments, low, high))
-    both = jnp.concatenate(
-        [low[:, :, :, None], jnp.stack([mixed, cotangent]), high[:, :, :, None]], axis=3
-    )
-    rows = exchange(moments, LAT)
-    low, high = shift(both[:, :, -1:], LAT, 1, False), shift(both[:, :, :1], LAT, -1, False)
+    slots = exchange(slots, LON)
+    wide_cot, slots = call(
+        functools.partial(merge_body, cells_local),
+        (
+            array((samples, tile_rows, tile_cols + 2, channels)),
+            array((lat_count, lat_slot, LANES), BF16),
+        ),
+        (pltpu.VMEM((lat_slot, LANES), F32),),
+    )(slots, cotangent)
+    slots = exchange(slots, LAT)
     affine = jnp.stack([gamma, beta])
-    flat = (samples, tile_rows * tile_cols, channels)
-    stats, act, slope, norm = call(
-        functools.partial(normalize_body, cells_local * lon_count, cells_per_group),
-        (array((2 * samples, LANES)), array(flat, BF16), array(flat), array(flat)),
-    )(rows, mixed, affine)
-    act, low, high = lax.optimization_barrier((act, low, high))
-    both = jnp.concatenate([low, both, high], axis=2)
-    mixed_pad, cot_pad = both[0], both[1]
 
     style = 1.0 + jnp.dot(emb, style_weight, precision=lax.Precision.HIGHEST)
     power = jnp.sum(conv_weight * conv_weight, axis=(0, 1))
     demod = lax.rsqrt(jnp.dot(style * style, power, precision=lax.Precision.HIGHEST) + 1e-08)
     modded = conv_weight[None] * style[:, None, None, :, None]
     w_eff = (modded * demod[:, None, None, None, :]).astype(BF16)
-    wide = (samples, 3, 3 * channels, channels)
-    back_taps = jnp.swapaxes(w_eff[:, ::-1, ::-1], 3, 4).reshape(wide)
+    taps_shape = (samples, 3, 3 * channels, channels)
+    back_taps = jnp.swapaxes(w_eff[:, ::-1, ::-1], 3, 4).reshape(taps_shape)
     spread = pltpu.VMEM((tile_rows + 2, tile_cols + 2, channels), F32)
-    stretch = ((tile_rows + 2) * tile_cols, 3 * channels)
-    lat_at = lax.axis_index(LAT)
-    inside = jnp.stack([lat_at > 0, lat_at < lat_count - 1])
-    keep = jnp.broadcast_to(inside.astype(F32)[:, None], (2, LANES))
+    shifted = pltpu.VMEM(((tile_rows + 2) * tile_cols, 3 * channels), BF16)
+    flat = (samples, tile_rows * tile_cols, channels)
     style_col = style.T
-    grad_pre, payload = call(
-        sums_body,
-        (array(flat), array((SHARDS, SLOT, LANES), BF16)),
-        (spread, pltpu.VMEM(stretch, BF16), pltpu.VMEM((9 * channels, channels), F32)),
-    )(cot_pad, act, slope, norm, back_taps, style_col, demod, taps)
+    stats, norm, grad_pre, payload = call(
+        functools.partial(sums_body, cells_local * lon_count, cells_per_group),
+        (
+            array((2 * samples, LANES)),
+            array(flat),
+            array(flat),
+            array((SHARDS, SLOT, LANES), BF16),
+        ),
+        (
+            pltpu.VMEM((2, lat_slot, LANES), F32),
+            spread,
+            shifted,
+            pltpu.VMEM((9 * channels, channels), F32),
+        ),
+    )(slots, mixed, wide_cot, affine, back_taps, style_col, demod, taps)
 
     core_count, near_count = lax.axis_size("c"), lax.axis_size(NEAR)
     payload = lax.all_gather(payload, "c")
     payload = payload.reshape(core_count, core_count, near_count, SLOT, LANES)
     payload = lax.dynamic_index_in_dim(payload, lax.axis_index("c"), 1, False)
     payload = resplit(jnp.sum(payload.astype(F32), axis=0))
+    payload, mixed = lax.optimization_barrier((payload, mixed))
+    low, high = shift(mixed[:, :, -1:], LON, 1, True), shift(mixed[:, :, :1], LON, -1, True)
     payload = resplit(jnp.sum(exchange(payload, NEAR).astype(F32), axis=0))
+    payload, low, high = lax.optimization_barrier((payload, low, high))
+    padded = jnp.concatenate([low, mixed, high], axis=2)
+    low, high = shift(padded[:, -1:], LAT, 1, False), shift(padded[:, :1], LAT, -1, False)
     payload = resplit(jnp.sum(everyone(payload, LAT).astype(F32), axis=0))
+    payload, low, high = lax.optimization_barrier((payload, low, high))
+    padded = jnp.concatenate([low, padded, high], axis=1)
     payload = lax.all_gather(everyone(payload, NEAR), "c")
 
-    block_out = call(
-        forward_body, array(feats.shape, BF16), (spread, pltpu.VMEM(stretch, BF16))
-    )(mixed_pad, w_eff.reshape(wide), stats, affine, keep)
-
-    grad_feats, grad_weight, grad_style, grad_affine = call(
+    lat_at = lax.axis_index(LAT)
+    inside = jnp.stack([lat_at > 0, lat_at < lat_count - 1])
+    keep = jnp.broadcast_to(inside.astype(F32)[:, None], (2, LANES))
+    block_out = call(forward_body, array(feats.shape, BF16), (spread, shifted))(
+        padded, w_eff.reshape(taps_shape), stats, affine, keep
+    )
+
+    grad_feats, grad_weight, grad_style, grad_gamma, grad_beta = call(
         functools.partial(last_body, scale_gradient, cells_per_group),
         (
             array(feats.shape, BF16),
             array(taps.shape),
             array(style_weight.shape),
-            array((2, LANES)),
+            array((1, LANES)),
+            array((1, LANES)),
         ),
     )(
         payload.reshape(SHARDS, SLOT, LANES), stats, norm, cotangent, grad_pre, affine, style,
@@ -397,8 +460,8 @@
         grad_feats,
         grad_weight.reshape(conv_weight.shape),
         grad_style,
-        grad_affine[0],
-        grad_affine[1],
+        grad_gamma[0],
+        grad_beta[0],
     )
 
 

time: 109 us -> 108 us (level)
  the two profiles are of different devices: /device:TPU:1 before, /device:TPU:135 now
where the time goes in v5:
time: 108 us; the launch traced here: 107 us
  starting transfers between devices  50 us (46%)
  waiting for transfers between devices  33.9 us (31%)
  blocking collectives  7.75 us (7%)
  Pallas kernels  7.57 us (7%)
  local copies, waits for them, and re-layouts  3.45 us (3%)
  other arithmetic  2.6 us (2%)
    all_to_all x5, starting transfers between devices, exchange(): return lax.all_to_all(block, axes, 0, 0)  37.3 us
    all_to_all x5, waiting for transfers between devices, exchange(): return lax.all_to_all(block, axes, 0, 0)  26.2 us
    ppermute x4, starting transfers between devices, shift(): return lax.ppermute(block, axes, pairs)  12.7 us
    ppermute x4, waiting for transfers between devices, shift(): return lax.ppermute(block, axes, pairs)  7.74 us
    all_gather x1, blocking collectives, on_device(): payload = lax.all_gather(everyone(payload, NEAR), 'c')  5.07 us
    pallas_call x1, Pallas kernels, on_device(): call(mix_body, (array(feats.shape, BF16), array((lon_count, lon_slot, LAN...  2.97 us
    all_gather x1, blocking collectives, on_device(): payload = lax.all_gather(payload, 'c')  2.68 us
  transfers between devices with their start and end apart: 9, of which 6 were waited for; matrix products, arithmetic and copies ran while one was open for 4% of the time, Pallas kernels for 1%

profile of v5, /device:TPU:135, one launch (start us, length us, event | category | flops | bytes accessed | tf_op | source)
XLA Modules:
  0.0 107.1 jit_solution(367717966266425200)
XLA Ops:
  0.6 0.0 copy-start
  0.6 0.0 copy-start.1
  0.7 0.0 copy-start.4
  0.7 3.0 %shard_map.145 = (bf16[2,8,32,128]{3,2,1,0:T(8,128)(2,1)}, bf16[32,24,128]{2,1,0:T(8,128)(2,1)}) custom-call(bf16[2,8,32,128]{3,2,1,0:T(8,128)(2,1)} %feats_in.1, bf16[2,8,32,128]{3,2,1,0:T(8,128)(2,1)} %cond_in.1, bf16[8,32,128]{2,1,0:T(8,128)(2,1)} %null_in.1, bf16[2,8,32,128]{3,2,1,0:T(8,128)(2,1)} %cotangent.1, s32[2,128]{1,0:T(2,128)} %flags.1), custom_call_target="tpu_custom_call" | custom-call | tf_op jit(solution)/shard_map/pallas_call | solution.py:370
  3.6 0.0 copy-start.3
  3.7 9.9 %all-to-all-start = ((bf16[32,24,128]{2,1,0:T(8,128)(2,1)}), bf16[32,24,128]{2,1,0:T(8,128)(2,1)S(1)}, u32[]{:S(2)}, u32[]{:S(2)}) async-start(bf16[32,24,128]{2,1,0:T(8,128)(2,1)} %get-tuple-element.27), calls=%async_computation | async-start | bytes 393216 | tf_op jit(solution)/shard_map/all_to_all | solution.py:41
  13.5 0.0 copy-done.1
  13.6 0.0 copy-done
  13.6 0.0 copy-done.4
  13.6 0.6 convolution_add_fusion
  14.2 9.5 %all-to-all-done.slots = bf16[32,24,128]{2,1,0:T(8,128)(2,1)S(1)} async-done(((bf16[32,24,128]{2,1,0:T(8,128)(2,1)}), bf16[32,24,128]{2,1,0:T(8,128)(2,1)S(1)}, u32[]{:S(2)}, u32[]{:S(2)}) %all-to-all-start) | async-done | bytes 196640 | tf_op jit(solution)/shard_map/all_to_all | solution.py:41
  23.7 0.0 copy-done.3
  23.7 0.8 shard_map.146
  24.6 10.0 %all-to-all-start.1 = ((bf16[16,80,128]{2,1,0:T(8,128)(2,1)}), bf16[16,80,128]{2,1,0:T(8,128)(2,1)S(1)}, u32[]{:S(2)}, u32[]{:S(2)}) async-start(bf16[16,80,128]{2,1,0:T(8,128)(2,1)} %get-tuple-element.28), calls=%async_computation.1 | async-start | bytes 655360 | tf_op jit(solution)/shard_map/all_to_all | solution.py:41
  34.6 0.2 fusion.demod
  34.8 0.1 copy.43.style
  34.9 0.3 copy.40
  35.2 1.1 multiply_convert_fusion.1
  36.2 0.0 copy-start.5
  36.2 0.0 copy-start.6
  36.2 0.0 copy-start.2
  36.2 1.1 %rev.3 = bf16[2,3,3,128,128]{3,4,2,1,0:T(8,128)(2,1)S(1)} reverse(bf16[2,3,3,128,128]{3,4,2,1,0:T(8,128)(2,1)} %multiply_convert_fusion.1), dimensions={1,2} | reverse | bytes 1179648 | tf_op jit(solution)/shard_map/rev | solution.py:401
  37.4 0.0 copy-done.5
  37.4 0.0 copy-done.6
  37.4 8.9 %all-to-all-done.1.slots = bf16[16,80,128]{2,1,0:T(8,128)(2,1)S(1)} async-done(((bf16[16,80,128]{2,1,0:T(8,128)(2,1)}), bf16[16,80,128]{2,1,0:T(8,128)(2,1)S(1)}, u32[]{:S(2)}, u32[]{:S(2)}) %all-to-all-start.1) | async-done | bytes 327712 | tf_op jit(solution)/shard_map/all_to_all | solution.py:41
  46.3 0.0 copy-done.2
  46.3 1.2 %shard_map.147 = (f32[4,128]{1,0:T(4,128)S(1)}, f32[2,256,128]{2,1,0:T(8,128)S(1)}, f32[2,256,128]{2,1,0:T(8,128)S(1)}, bf16[32,40,128]{2,1,0:T(8,128)(2,1)S(1)}) custom-call(bf16[16,80,128]{2,1,0:T(8,128)(2,1)S(1)} %all-to-all-done.1.slots, bf16[2,8,32,128]{3,2,1,0:T(8,128)(2,1)S(1)} %copy-done.2, f32[2,8,34,128]{3,2,1,0:T(8,128)S(1)} %get-tuple-element.30.wide, ...), custom_call_target="tpu_custom_call" | custom-call | tf_op jit(solution)/shard_map/pallas_call | solution.py:406
  47.5 2.7 %all-gather = bf16[64,40,128]{2,1,0:T(8,128)(2,1)S(1)} all-gather(bf16[32,40,128]{2,1,0:T(8,128)(2,1)S(1)} %get-tuple-element.31), channel_id=2, replica_groups=mesh['zh'=4,'x'=4,'zl'=2,'y'=8,'c'=2] {'c'}, dimensions={0}, use_global_device_ids=true | all-gather | bytes 983040 | tf_op jit(solution)/shard_map/all_gather | solution.py:423
  50.2 0.2 fusion.8
  50.4 0.8 fusion.2
  51.2 3.5 %all-to-all-start.2 = ((bf16[16,40,128]{2,1,0:T(8,128)(2,1)}), bf16[16,40,128]{2,1,0:T(8,128)(2,1)S(1)}, u32[]{:S(2)}, u32[]{:S(2)}) async-start(bf16[16,40,128]{2,1,0:T(8,128)(2,1)} %fusion.2), calls=%async_computation.2 | async-start | bytes 327680 | tf_op jit(solution)/shard_map/all_to_all | solution.py:41
  54.8 3.7 %collective-permute-start = (bf16[2,8,1,128]{3,2,1,0:T(2,128)(2,1)S(1)}, bf16[2,8,1,128]{3,2,1,0:T(2,128)(2,1)S(1)}, u32[]{:S(2)}, u32[]{:S(2)}) collective-permute-start(bf16[2,8,1,128]{3,2,1,0:T(2,128)(2,1)S(1)} %get-tuple-element.53), channel_id=1, source_target_pairs={{0,1},{1,2},{2,3},{3,4},{4,5},{5,6},{6,7},{7,8},{8,9},{9,10},{10,1... | collective-permute-start | bytes 12296 | tf_op jit(solution)/shard_map/ppermute | solution.py:30
  58.5 1.9 %collective-permute-start.1 = (bf16[2,8,1,128]{3,2,1,0:T(2,128)(2,1)S(1)}, bf16[2,8,1,128]{3,2,1,0:T(2,128)(2,1)S(1)}, u32[]{:S(2)}, u32[]{:S(2)}) collective-permute-start(bf16[2,8,1,128]{3,2,1,0:T(2,128)(2,1)S(1)} %get-tuple-element.52), channel_id=1, source_target_pairs={{0,31},{1,0},{2,1},{3,2},{4,3},{5,4},{6,5},{7,6},{8,7},{9,8},{10,9... | collective-permute-start | bytes 12296 | tf_op jit(solution)/shard_map/ppermute | solution.py:30
  60.4 1.9 %all-to-all-done.2 = bf16[16,40,128]{2,1,0:T(8,128)(2,1)S(1)} async-done(((bf16[16,40,128]{2,1,0:T(8,128)(2,1)}), bf16[16,40,128]{2,1,0:T(8,128)(2,1)S(1)}, u32[]{:S(2)}, u32[]{:S(2)}) %all-to-all-start.2) | async-done | bytes 163872 | tf_op jit(solution)/shard_map/all_to_all | solution.py:41
  62.3 0.1 fusion.11
  62.4 0.1 fusion.5
  62.5 0.0 collective-permute-done
  62.5 1.1 %collective-permute-done.1 = bf16[2,8,1,128]{3,2,1,0:T(2,128)(2,1)S(1)} collective-permute-done((bf16[2,8,1,128]{3,2,1,0:T(2,128)(2,1)S(1)}, bf16[2,8,1,128]{3,2,1,0:T(2,128)(2,1)S(1)}, u32[]{:S(2)}, u32[]{:S(2)}) %collective-permute-start.1) | collective-permute-done | bytes 4128 | tf_op jit(solution)/shard_map/ppermute | solution.py:30
  63.6 0.7 broadcast_in_dim.6
  64.3 6.3 %all-to-all-start.3 = ((bf16[16,40,128]{2,1,0:T(8,128)(2,1)}), bf16[16,40,128]{2,1,0:T(8,128)(2,1)S(1)}, u32[]{:S(2)}, u32[]{:S(2)}) async-start(bf16[16,40,128]{2,1,0:T(8,128)(2,1)} %broadcast_in_dim.6), calls=%async_computation.3 | async-start | bytes 327680 | tf_op jit(solution)/shard_map/all_to_all | solution.py:41
  70.6 0.1 copy.45
  70.8 0.1 add_convert_fusion
  70.9 5.2 %collective-permute-start.2 = (bf16[2,1,34,128]{3,2,1,0:T(8,128)(2,1)S(1)}, bf16[2,1,34,128]{3,2,1,0:T(8,128)(2,1)S(1)}, u32[]{:S(2)}, u32[]{:S(2)}) collective-permute-start(bf16[2,1,34,128]{3,2,1,0:T(8,128)(2,1)S(1)} %get-tuple-element.51), channel_id=1, source_target_pairs={{0,32},{32,64},{64,96},{96,128},{128,160},{160,192},{192,224},{224... | collective-permute-start | bytes 52232 | tf_op jit(solution)/shard_map/ppermute | solution.py:30
  76.1 1.9 %collective-permute-start.3 = (bf16[2,1,34,128]{3,2,1,0:T(8,128)(2,1)S(1)}, bf16[2,1,34,128]{3,2,1,0:T(8,128)(2,1)S(1)}, u32[]{:S(2)}, u32[]{:S(2)}) collective-permute-start(bf16[2,1,34,128]{3,2,1,0:T(8,128)(2,1)S(1)} %get-tuple-element.50), channel_id=1, source_target_pairs={{32,0},{64,32},{96,64},{128,96},{160,128},{192,160},{224,192},{256... | collective-permute-start | bytes 52232 | tf_op jit(solution)/shard_map/ppermute | solution.py:30
  78.0 0.0 all-to-all-done.3
  78.1 0.1 fusion.10
  78.1 0.1 fusion.7
  78.2 0.0 collective-permute-done.2
  78.2 6.6 %collective-permute-done.3 = bf16[2,1,34,128]{3,2,1,0:T(8,128)(2,1)S(1)} collective-permute-done((bf16[2,1,34,128]{3,2,1,0:T(8,128)(2,1)S(1)}, bf16[2,1,34,128]{3,2,1,0:T(8,128)(2,1)S(1)}, u32[]{:S(2)}, u32[]{:S(2)}) %collective-permute-start.3) | collective-permute-done | bytes 17440 | tf_op jit(solution)/shard_map/ppermute | solution.py:30
  84.8 0.7 broadcast_in_dim.8
  85.5 7.6 %all-to-all-start.4 = ((bf16[16,40,128]{2,1,0:T(8,128)(2,1)}), bf16[16,40,128]{2,1,0:T(8,128)(2,1)S(1)}, u32[]{:S(2)}, u32[]{:S(2)}) async-start(bf16[16,40,128]{2,1,0:T(8,128)(2,1)} %broadcast_in_dim.8), calls=%async_computation.4 | async-start | bytes 327680 | tf_op jit(solution)/shard_map/all_to_all | solution.py:41
  93.1 0.2 multiply_convert_fusion.taps
  93.3 0.1 pad_maximum_fusion.padded
  93.4 0.1 broadcast_in_dim.7.keep
  93.5 1.2 %shard_map.148 = bf16[2,8,32,128]{3,2,1,0:T(8,128)(2,1)} custom-call(bf16[2,10,34,128]{3,2,1,0:T(8,128)(2,1)S(1)} %pad_maximum_fusion.padded, bf16[2,3,384,128]{3,2,1,0:T(8,128)(2,1)S(1)} %multiply_convert_fusion.taps, f32[4,128]{1,0:T(4,128)S(1)} %get-tuple-element.39.stats, f32[2,128]{1,0:T(2,128)S(1)} %pad_maximum_fusion.4.affine, ...), custom_call_target="tpu_custom_call" | custom-call | tf_op jit(solution)/shard_map/pallas_call | solution.py:441
  94.7 6.0 %all-to-all-done.4 = bf16[16,40,128]{2,1,0:T(8,128)(2,1)S(1)} async-done(((bf16[16,40,128]{2,1,0:T(8,128)(2,1)}), bf16[16,40,128]{2,1,0:T(8,128)(2,1)S(1)}, u32[]{:S(2)}, u32[]{:S(2)}) %all-to-all-start.4) | async-done | bytes 163872 | tf_op jit(solution)/shard_map/all_to_all | solution.py:41
  100.7 5.1 %all-gather.1.gathered = bf16[32,40,128]{2,1,0:T(8,128)(2,1)S(1)} all-gather(bf16[16,40,128]{2,1,0:T(8,128)(2,1)S(1)} %all-to-all-done.4), channel_id=3, replica_groups=mesh['zh'=4,'x'=4,'zl'=2,'y'=8,'c'=2] {'c'}, dimensions={0}, use_global_device_ids=true | all-gather | bytes 491520 | tf_op jit(solution)/shard_map/all_gather | solution.py:436
  105.7 1.3 %shard_map.149 = (bf16[2,8,32,128]{3,2,1,0:T(8,128)(2,1)}, f32[9,128,128]{2,1,0:T(8,128)}, f32[512,128]{1,0:T(8,128)}, f32[1,128]{1,0:T(1,128)}, f32[1,128]{1,0:T(1,128)}) custom-call(bf16[32,40,128]{2,1,0:T(8,128)(2,1)S(1)} %all-gather.1.gathered, f32[4,128]{1,0:T(4,128)S(1)} %get-tuple-element.39.stats, f32[2,256,128]{2,1,0:T(8,128)S(1)} %get-tuple-element.41.norm, ...), custom_call_target="tpu_custom_call" | custom-call | tf_op jit(solution)/shard_map/pallas_call | solution.py:445
  (11 shorter events, 0.2 us)
Async XLA Ops:
  0.6 13.0 %copy-start = (f32[512,128]{1,0:T(8,128)S(1)}, f32[512,128]{1,0:T(8,128)}, u32[]{:S(2)}) copy-start(f32[512,128]{1,0:T(8,128)} %param.15) | copy-start | bytes 786436
  0.6 12.9 %copy-start.1 = (f32[3,3,128,128]{3,2,1,0:T(8,128)S(1)}, f32[3,3,128,128]{3,2,1,0:T(8,128)}, u32[]{:S(2)}) copy-start(f32[3,3,128,128]{3,2,1,0:T(8,128)} %param.16) | copy-start | bytes 1769476
  0.7 13.0 %copy-start.4 = (f32[2,512]{1,0:T(2,128)S(1)}, f32[2,512]{1,0:T(2,128)}, u32[]{:S(2)}) copy-start(f32[2,512]{1,0:T(2,128)} %param.14) | copy-start | bytes 12292
  3.6 20.1 %copy-start.3 = (bf16[2,8,32,128]{3,2,1,0:T(8,128)(2,1)S(1)}, bf16[2,8,32,128]{3,2,1,0:T(8,128)(2,1)}, u32[]{:S(2)}) copy-start(bf16[2,8,32,128]{3,2,1,0:T(8,128)(2,1)} %cotangent.1) | copy-start | bytes 393220
  3.7 20.1 %all-to-all-start = ((bf16[32,24,128]{2,1,0:T(8,128)(2,1)}), bf16[32,24,128]{2,1,0:T(8,128)(2,1)S(1)}, u32[]{:S(2)}, u32[]{:S(2)}) async-start(bf16[32,24,128]{2,1,0:T(8,128)(2,1)} %get-tuple-element.27), calls=%async_computation | async-start | bytes 393216 | tf_op jit(solution)/shard_map/all_to_all | solution.py:41
  24.6 21.7 %all-to-all-start.1 = ((bf16[16,80,128]{2,1,0:T(8,128)(2,1)}), bf16[16,80,128]{2,1,0:T(8,128)(2,1)S(1)}, u32[]{:S(2)}, u32[]{:S(2)}) async-start(bf16[16,80,128]{2,1,0:T(8,128)(2,1)} %get-tuple-element.28), calls=%async_computation.1 | async-start | bytes 655360 | tf_op jit(solution)/shard_map/all_to_all | solution.py:41
  36.2 1.2 %copy-start.5 = (f32[128]{0:T(128)S(1)}, f32[128]{0:T(128)}, u32[]{:S(2)}) copy-start(f32[128]{0:T(128)} %param.18) | copy-start | bytes 1540
  36.2 1.2 %copy-start.6 = (f32[128]{0:T(128)S(1)}, f32[128]{0:T(128)}, u32[]{:S(2)}) copy-start(f32[128]{0:T(128)} %param.17) | copy-start | bytes 1540
  36.2 10.1 %copy-start.2 = (bf16[2,8,32,128]{3,2,1,0:T(8,128)(2,1)S(1)}, bf16[2,8,32,128]{3,2,1,0:T(8,128)(2,1)}, u32[]{:S(2)}) copy-start(bf16[2,8,32,128]{3,2,1,0:T(8,128)(2,1)} %get-tuple-element.33.mixed) | copy-start | bytes 393220
  51.2 11.0 %all-to-all-start.2 = ((bf16[16,40,128]{2,1,0:T(8,128)(2,1)}), bf16[16,40,128]{2,1,0:T(8,128)(2,1)S(1)}, u32[]{:S(2)}, u32[]{:S(2)}) async-start(bf16[16,40,128]{2,1,0:T(8,128)(2,1)} %fusion.2), calls=%async_computation.2 | async-start | bytes 327680 | tf_op jit(solution)/shard_map/all_to_all | solution.py:41
  54.8 7.7 %collective-permute-start = (bf16[2,8,1,128]{3,2,1,0:T(2,128)(2,1)S(1)}, bf16[2,8,1,128]{3,2,1,0:T(2,128)(2,1)S(1)}, u32[]{:S(2)}, u32[]{:S(2)}) collective-permute-start(bf16[2,8,1,128]{3,2,1,0:T(2,128)(2,1)S(1)} %get-tuple-element.53), channel_id=1, source_target_pairs={{0,1},{1,2},{2,3},{3,4},{4,5},{5,6},{6,7},{7,8},{8,9},{9,10},{10,1... | collective-permute-start | bytes 12296 | tf_op jit(solution)/shard_map/ppermute | solution.py:30
  58.5 5.1 %collective-permute-start.1 = (bf16[2,8,1,128]{3,2,1,0:T(2,128)(2,1)S(1)}, bf16[2,8,1,128]{3,2,1,0:T(2,128)(2,1)S(1)}, u32[]{:S(2)}, u32[]{:S(2)}) collective-permute-start(bf16[2,8,1,128]{3,2,1,0:T(2,128)(2,1)S(1)} %get-tuple-element.52), channel_id=1, source_target_pairs={{0,31},{1,0},{2,1},{3,2},{4,3},{5,4},{6,5},{7,6},{8,7},{9,8},{10,9... | collective-permute-start | bytes 12296 | tf_op jit(solution)/shard_map/ppermute | solution.py:30
  64.3 13.7 %all-to-all-start.3 = ((bf16[16,40,128]{2,1,0:T(8,128)(2,1)}), bf16[16,40,128]{2,1,0:T(8,128)(2,1)S(1)}, u32[]{:S(2)}, u32[]{:S(2)}) async-start(bf16[16,40,128]{2,1,0:T(8,128)(2,1)} %broadcast_in_dim.6), calls=%async_computation.3 | async-start | bytes 327680 | tf_op jit(solution)/shard_map/all_to_all | solution.py:41
  70.9 7.3 %collective-permute-start.2 = (bf16[2,1,34,128]{3,2,1,0:T(8,128)(2,1)S(1)}, bf16[2,1,34,128]{3,2,1,0:T(8,128)(2,1)S(1)}, u32[]{:S(2)}, u32[]{:S(2)}) collective-permute-start(bf16[2,1,34,128]{3,2,1,0:T(8,128)(2,1)S(1)} %get-tuple-element.51), channel_id=1, source_target_pairs={{0,32},{32,64},{64,96},{96,128},{128,160},{160,192},{192,224},{224... | collective-permute-start | bytes 52232 | tf_op jit(solution)/shard_map/ppermute | solution.py:30
  76.1 8.7 %collective-permute-start.3 = (bf16[2,1,34,128]{3,2,1,0:T(8,128)(2,1)S(1)}, bf16[2,1,34,128]{3,2,1,0:T(8,128)(2,1)S(1)}, u32[]{:S(2)}, u32[]{:S(2)}) collective-permute-start(bf16[2,1,34,128]{3,2,1,0:T(8,128)(2,1)S(1)} %get-tuple-element.50), channel_id=1, source_target_pairs={{32,0},{64,32},{96,64},{128,96},{160,128},{192,160},{224,192},{256... | collective-permute-start | bytes 52232 | tf_op jit(solution)/shard_map/ppermute | solution.py:30
  85.5 15.2 %all-to-all-start.4 = ((bf16[16,40,128]{2,1,0:T(8,128)(2,1)}), bf16[16,40,128]{2,1,0:T(8,128)(2,1)S(1)}, u32[]{:S(2)}, u32[]{:S(2)}) async-start(bf16[16,40,128]{2,1,0:T(8,128)(2,1)} %broadcast_in_dim.8), calls=%async_computation.4 | async-start | bytes 327680 | tf_op jit(solution)/shard_map/all_to_all | solution.py:41

commit v6 on v5

--- a/solution.py
+++ b/solution.py
@@ -178,6 +178,35 @@
         slots_out[row + 1] = edge[...].astype(BF16)
 
 
+def weights_body(
+    emb, style_weight, weight, style_out, column_out, demod_out, power_out, emb_out, back_out, taps_out,
+):
+    samples, channels = emb.shape[0], weight.shape[2]
+    exact = lax.Precision.HIGHEST
+    style = 1.0 + jnp.dot(
+        emb[...], style_weight[...], precision=exact, preferred_element_type=F32
+    )
+    power = jnp.zeros((channels, channels), F32)
+    for tap in range(9):
+        power = power + weight[tap] * weight[tap]
+    squares = jnp.dot(style * style, power, precision=exact, preferred_element_type=F32)
+    demod = lax.rsqrt(squares + 1e-08)
+    style_out[...] = style
+    demod_out[...] = demod
+    power_out[...] = power
+    for sample in range(samples):
+        here = slice(sample, sample + 1)
+        column = jnp.broadcast_to(style[here, :], (channels, channels)).T
+        column_out[sample] = column
+        emb_out[sample] = jnp.broadcast_to(emb[here, :], (channels, emb.shape[1])).T
+        for tap in range(9):
+            row, col = tap // 3, tap % 3
+            block = weight[tap] * column * demod[here, :]
+            taps_out[sample, row, col * channels : (col + 1) * channels, :] = block.astype(BF16)
+            row, col = 2 - row, 2 - col
+            back_out[sample, row, col * channels : (col + 1) * channels, :] = block.T.astype(BF16)
+
+
 def windows(spread, shifted, rows, cols):
     channels = spread.shape[-1]
     for tap in range(3):
@@ -185,17 +214,16 @@
         shifted[:, tap * channels : (tap + 1) * channels] = moved.astype(BF16)
 
 
-def forward_body(padded, taps, stats, affine, keep, block_out, spread, shifted):
+def forward_body(padded, taps, stats, gamma, beta, block_out, spread, shifted):
     samples, rows, cols = padded.shape[0], padded.shape[1] - 2, padded.shape[2] - 2
     size = rows * cols
-    gamma, beta = affine[0:1, :][None], affine[1:2, :][None]
-    row = lax.broadcasted_iota(jnp.int32, spread.shape, 0)
-    inside = ((row > 0) | (keep[0:1, :] > 0.0)[None]) & ((row <= rows) | (keep[1:2, :] > 0.0)[None])
+    row = lax.broadcasted_iota(jnp.int32, spread.shape, 0) + place(LAT) * rows
+    inside = (row > 0) & (row <= rows * lax.axis_size(LAT))
     for sample in range(samples):
         mixed = padded[sample].astype(F32)
         mean = stats[sample : sample + 1, :][None]
         inverse = stats[samples + sample : samples + sample + 1, :][None]
-        pre = (mixed - mean) * inverse * gamma + beta
+        pre = (mixed - mean) * inverse * gamma[...][None] + beta[...][None]
         act = jnp.where(inside, pre / (1.0 + jnp.exp(-pre)), 0.0)
         spread[...] = act
         windows(spread, shifted, rows, cols)
@@ -207,7 +235,7 @@
 
 
 def sums_body(
-    count, cells, slots, mixed, wide, affine, back_taps, style_col, demod, weight,
+    count, cells, slots, mixed, wide, gamma, beta, back_taps, column, demod, weight,
     stats_out, norm_out, grad_out, payload_out, edge, spread, shifted, total,
 ):
     samples, rows, cols, channels = mixed.shape
@@ -226,7 +254,7 @@
         stats_out[samples + sample : samples + sample + 1, :] = inverse
         flat = mixed[sample].reshape(size, channels).astype(F32)
         norm = (flat - mean) * inverse
-        pre = norm * affine[0:1, :] + affine[1:2, :]
+        pre = norm * gamma[...] + beta[...]
         sig = 1.0 / (1.0 + jnp.exp(-pre))
         norm_out[sample] = norm
         act = (pre * sig).astype(BF16)
@@ -236,7 +264,7 @@
         spread[1 : 1 + rows] = wide[sample]
         spread[1 + rows] = edge[1, here, :]
         windows(spread, shifted, rows, cols)
-        style_full = jnp.broadcast_to(style_col[:, sample : sample + 1], (channels, channels))
+        style_full = column[sample]
         demod_row = demod[sample : sample + 1, :]
         both = style_full * demod_row
         product = jnp.zeros((channels, channels), F32)
@@ -297,8 +325,8 @@
 
 
 def last_body(
-    scale, cells, gathered, stats, norm, cotangent, grad_pre, affine, style, style_col, demod,
-    power, weight, emb_col, feats_out, weight_out, style_out, gamma_out, beta_out,
+    scale, cells, gathered, stats, norm, cotangent, grad_pre, gamma, style, column, demod,
+    power, weight, emb_full, feats_out, weight_out, style_out, gamma_out, beta_out,
 ):
     samples, tile_rows, tile_cols, channels = cotangent.shape
     size = tile_rows * tile_cols
@@ -319,7 +347,7 @@
             whole = jnp.where((lane >> 5) == quarter, piece, whole)
         small.append(whole)
     demod_sums, style_sums, gamma_sums, beta_sums = small[0:2], small[2:4], small[4:6], small[6:8]
-    gamma = affine[0:1, :]
+    gain = gamma[...]
     gamma_out[...] = scale * (gamma_sums[0] + gamma_sums[1])
     beta_out[...] = scale * (beta_sums[0] + beta_sums[1])
     shrink = jnp.zeros((channels, channels), F32)
@@ -327,7 +355,7 @@
     for sample in range(samples):
         demod_row = demod[sample : sample + 1, :]
         pulled = demod_sums[sample] * (demod_row * demod_row * demod_row)
-        style_full = jnp.broadcast_to(style_col[:, sample : sample + 1], (channels, channels))
+        style_full = column[sample]
         shrink = shrink + style_full * style_full * pulled
         spent = jnp.sum((power[...] * pulled).T, axis=0, keepdims=True)
         rows.append(style_sums[sample] - style[sample : sample + 1, :] * spent)
@@ -341,12 +369,12 @@
         here = slice(8 * pair, 8 * pair + 8)
         block = jnp.where(sub < 4, tails[2 * pair], pltpu.roll(tails[2 * pair + 1], 4, 0))
         weight_out[8, here, :] = scale * (block - shrink[here, :] * weight[8, here, :])
-    style_out[...] = scale * (emb_col[:, 0:1] * rows[0] + emb_col[:, 1:2] * rows[1])
+    style_out[...] = scale * (emb_full[0] * rows[0] + emb_full[1] * rows[1])
     for sample in range(samples):
         inverse = stats[samples + sample : samples + sample + 1, :]
-        product_mean = group_total(gamma * beta_sums[sample]) * (1.0 / cells)
-        squared_mean = group_total(gamma * gamma_sums[sample]) * (1.0 / cells)
-        change = inverse * (gamma * grad_pre[sample] - product_mean - norm[sample] * squared_mean)
+        product_mean = group_total(gain * beta_sums[sample]) * (1.0 / cells)
+        squared_mean = group_total(gain * gamma_sums[sample]) * (1.0 / cells)
+        change = inverse * (gain * grad_pre[sample] - product_mean - norm[sample] * squared_mean)
         out = cotangent[sample].reshape(size, channels).astype(F32) + change
         feats_out[sample] = out.astype(BF16).reshape(tile_rows, tile_cols, channels)
 
@@ -381,6 +409,7 @@
         in_specs=[anywhere] * 4 + [whole],
     )(feats, cond, null_field, cotangent, drop_flags)
     slots = exchange(slots, LON)
+    low, high = shift(mixed[:, :, -1:], LON, 1, True), shift(mixed[:, :, :1], LON, -1, True)
     wide_cot, slots = call(
         functools.partial(merge_body, cells_local),
         (
@@ -389,20 +418,28 @@
         ),
         (pltpu.VMEM((lat_slot, LANES), F32),),
     )(slots, cotangent)
+    slots, low, high = lax.optimization_barrier((slots, low, high))
     slots = exchange(slots, LAT)
-    affine = jnp.stack([gamma, beta])
-
-    style = 1.0 + jnp.dot(emb, style_weight, precision=lax.Precision.HIGHEST)
-    power = jnp.sum(conv_weight * conv_weight, axis=(0, 1))
-    demod = lax.rsqrt(jnp.dot(style * style, power, precision=lax.Precision.HIGHEST) + 1e-08)
-    modded = conv_weight[None] * style[:, None, None, :, None]
-    w_eff = (modded * demod[:, None, None, None, :]).astype(BF16)
+    padded = jnp.concatenate([low, mixed, high], axis=2)
+    low, high = shift(padded[:, -1:], LAT, 1, False), shift(padded[:, :1], LAT, -1, False)
+    gamma, beta = gamma[None], beta[None]
+
     taps_shape = (samples, 3, 3 * channels, channels)
-    back_taps = jnp.swapaxes(w_eff[:, ::-1, ::-1], 3, 4).reshape(taps_shape)
+    style, column, demod, power, emb_full, back_taps, fore_taps = call(
+        weights_body,
+        (
+            array((samples, channels)),
+            array((samples, channels, channels)),
+            array((samples, channels)),
+            array((channels, channels)),
+            array((samples,) + style_weight.shape),
+            array(taps_shape, BF16),
+            array(taps_shape, BF16),
+        ),
+    )(emb, style_weight, taps)
     spread = pltpu.VMEM((tile_rows + 2, tile_cols + 2, channels), F32)
     shifted = pltpu.VMEM(((tile_rows + 2) * tile_cols, 3 * channels), BF16)
     flat = (samples, tile_rows * tile_cols, channels)
-    style_col = style.T
     stats, norm, grad_pre, payload = call(
         functools.partial(sums_body, cells_local * lon_count, cells_per_group),
         (
@@ -417,29 +454,21 @@
             shifted,
             pltpu.VMEM((9 * channels, channels), F32),
         ),
-    )(slots, mixed, wide_cot, affine, back_taps, style_col, demod, taps)
-
+    )(slots, mixed, wide_cot, gamma, beta, back_taps, column, demod, taps)
+
+    payload, low, high = lax.optimization_barrier((payload, low, high))
+    padded = jnp.concatenate([low, padded, high], axis=1)
     core_count, near_count = lax.axis_size("c"), lax.axis_size(NEAR)
     payload = lax.all_gather(payload, "c")
     payload = payload.reshape(core_count, core_count, near_count, SLOT, LANES)
     payload = lax.dynamic_index_in_dim(payload, lax.axis_index("c"), 1, False)
     payload = resplit(jnp.sum(payload.astype(F32), axis=0))
-    payload, mixed = lax.optimization_barrier((payload, mixed))
-    low, high = shift(mixed[:, :, -1:], LON, 1, True), shift(mixed[:, :, :1], LON, -1, True)
     payload = resplit(jnp.sum(exchange(payload, NEAR).astype(F32), axis=0))
-    payload, low, high = lax.optimization_barrier((payload, low, high))
-    padded = jnp.concatenate([low, mixed, high], axis=2)
-    low, high = shift(padded[:, -1:], LAT, 1, False), shift(padded[:, :1], LAT, -1, False)
     payload = resplit(jnp.sum(everyone(payload, LAT).astype(F32), axis=0))
-    payload, low, high = lax.optimization_barrier((payload, low, high))
-    padded = jnp.concatenate([low, padded, high], axis=1)
     payload = lax.all_gather(everyone(payload, NEAR), "c")
 
-    lat_at = lax.axis_index(LAT)
-    inside = jnp.stack([lat_at > 0, lat_at < lat_count - 1])
-    keep = jnp.broadcast_to(inside.astype(F32)[:, None], (2, LANES))
     block_out = call(forward_body, array(feats.shape, BF16), (spread, shifted))(
-        padded, w_eff.reshape(taps_shape), stats, affine, keep
+        padded, fore_taps, stats, gamma, beta
     )
 
     grad_feats, grad_weight, grad_style, grad_gamma, grad_beta = call(
@@ -452,8 +481,8 @@
             array((1, LANES)),
         ),
     )(
-        payload.reshape(SHARDS, SLOT, LANES), stats, norm, cotangent, grad_pre, affine, style,
-        style_col, demod, power, taps, emb.T,
+        payload.reshape(SHARDS, SLOT, LANES), stats, norm, cotangent, grad_pre, gamma, style,
+        column, demod, power, taps, emb_full,
     )
     return (
         block_out,

time: 108 us -> 104 us (0.963)
  the two profiles are of different devices: /device:TPU:135 before, /device:TPU:1 now
where the time goes in v6:
time: 104 us; the launch traced here: 103 us
  starting transfers between devices  37.3 us (36%)
  blocking collectives  37.2 us (36%)
  waiting for transfers between devices  15.5 us (15%)
  Pallas kernels  8.22 us (8%)
  local copies, waits for them, and re-layouts  3.36 us (3%)
    all_to_all x3, starting transfers between devices, exchange(): return lax.all_to_all(block, axes, 0, 0)  27.2 us
    all_to_all x2, blocking collectives, exchange(): return lax.all_to_all(block, axes, 0, 0)  26.7 us
    all_to_all x3, waiting for transfers between devices, exchange(): return lax.all_to_all(block, axes, 0, 0)  15.5 us
    ppermute x4, starting transfers between devices, shift(): return lax.ppermute(block, axes, pairs)  10.1 us
    all_gather x1, blocking collectives, on_device(): payload = lax.all_gather(everyone(payload, NEAR), 'c')  5.61 us
    all_gather x1, blocking collectives, on_device(): payload = lax.all_gather(payload, 'c')  4.92 us
    pallas_call x1, Pallas kernels, on_device(): call(mix_body, (array(feats.shape, BF16), array((lon_count, lon_slot, LAN...  2.89 us
    unnamed x22, local copies, waits for them, and re-layouts  2.33 us
  transfers between devices with their start and end apart: 7, of which 3 were waited for; matrix products, arithmetic and copies ran while one was open for 0% of the time, Pallas kernels for 4%

profile of v6, /device:TPU:1, one launch (start us, length us, event | category | flops | bytes accessed | tf_op | source)
XLA Modules:
  0.0 103.0 jit_solution(8297817046611421118)
XLA Ops:
  0.6 2.9 %shard_map.145 = (bf16[2,8,32,128]{3,2,1,0:T(8,128)(2,1)}, bf16[32,24,128]{2,1,0:T(8,128)(2,1)}) custom-call(bf16[2,8,32,128]{3,2,1,0:T(8,128)(2,1)} %feats_in.1, bf16[2,8,32,128]{3,2,1,0:T(8,128)(2,1)} %cond_in.1, bf16[8,32,128]{2,1,0:T(8,128)(2,1)} %null_in.1, bf16[2,8,32,128]{3,2,1,0:T(8,128)(2,1)} %cotangent.1, s32[2,128]{1,0:T(2,128)} %flags.1), custom_call_target="tpu_custom_call" | custom-call | tf_op jit(solution)/shard_map/pallas_call | solution.py:398
  3.5 0.0 copy-start.1
  3.5 0.0 copy-start.2
  3.6 10.7 %all-to-all-start = ((bf16[32,24,128]{2,1,0:T(8,128)(2,1)}), bf16[32,24,128]{2,1,0:T(8,128)(2,1)S(1)}, u32[]{:S(2)}, u32[]{:S(2)}) async-start(bf16[32,24,128]{2,1,0:T(8,128)(2,1)} %get-tuple-element.32), calls=%async_computation | async-start | bytes 393216 | tf_op jit(solution)/shard_map/all_to_all | solution.py:41
  14.3 0.0 copy-done.1
  14.3 3.5 %collective-permute-start = (bf16[2,8,1,128]{3,2,1,0:T(2,128)(2,1)S(1)}, bf16[2,8,1,128]{3,2,1,0:T(2,128)(2,1)S(1)}, u32[]{:S(2)}, u32[]{:S(2)}) collective-permute-start(bf16[2,8,1,128]{3,2,1,0:T(2,128)(2,1)S(1)} %get-tuple-element.63), channel_id=1, source_target_pairs={{0,1},{1,2},{2,3},{3,4},{4,5},{5,6},{6,7},{7,8},{8,9},{9,10},{10,1... | collective-permute-start | bytes 12296 | tf_op jit(solution)/shard_map/ppermute | solution.py:30
  17.9 0.0 copy-start
  17.9 2.1 %collective-permute-start.1 = (bf16[2,8,1,128]{3,2,1,0:T(2,128)(2,1)S(1)}, bf16[2,8,1,128]{3,2,1,0:T(2,128)(2,1)S(1)}, u32[]{:S(2)}, u32[]{:S(2)}) collective-permute-start(bf16[2,8,1,128]{3,2,1,0:T(2,128)(2,1)S(1)} %get-tuple-element.62), channel_id=1, source_target_pairs={{0,31},{1,0},{2,1},{3,2},{4,3},{5,4},{6,5},{7,6},{8,7},{9,8},{10,9... | collective-permute-start | bytes 12296 | tf_op jit(solution)/shard_map/ppermute | solution.py:30
  19.9 4.5 %all-to-all-done.slots = bf16[32,24,128]{2,1,0:T(8,128)(2,1)S(1)} async-done(((bf16[32,24,128]{2,1,0:T(8,128)(2,1)}), bf16[32,24,128]{2,1,0:T(8,128)(2,1)S(1)}, u32[]{:S(2)}, u32[]{:S(2)}) %all-to-all-start) | async-done | bytes 196640 | tf_op jit(solution)/shard_map/all_to_all | solution.py:41
  24.5 0.0 copy-done.2
  24.5 0.8 shard_map.146
  25.3 0.0 collective-permute-done
  25.3 0.0 collective-permute-done.1
  25.3 11.7 %all-to-all-start.1 = ((bf16[16,80,128]{2,1,0:T(8,128)(2,1)}), bf16[16,80,128]{2,1,0:T(8,128)(2,1)S(1)}, u32[]{:S(2)}, u32[]{:S(2)}) async-start(bf16[16,80,128]{2,1,0:T(8,128)(2,1)} %get-tuple-element.35), calls=%async_computation.1 | async-start | bytes 655360 | tf_op jit(solution)/shard_map/all_to_all | solution.py:41
  37.1 3.3 %collective-permute-start.2 = (bf16[2,1,34,128]{3,2,1,0:T(8,128)(2,1)S(1)}, bf16[2,1,34,128]{3,2,1,0:T(8,128)(2,1)S(1)}, u32[]{:S(2)}, u32[]{:S(2)}) collective-permute-start(bf16[2,1,34,128]{3,2,1,0:T(8,128)(2,1)S(1)} %get-tuple-element.61), channel_id=1, source_target_pairs={{0,32},{32,64},{64,96},{96,128},{128,160},{160,192},{192,224},{224... | collective-permute-start | bytes 52232 | tf_op jit(solution)/shard_map/ppermute | solution.py:30
  40.4 1.3 %collective-permute-start.3 = (bf16[2,1,34,128]{3,2,1,0:T(8,128)(2,1)S(1)}, bf16[2,1,34,128]{3,2,1,0:T(8,128)(2,1)S(1)}, u32[]{:S(2)}, u32[]{:S(2)}) collective-permute-start(bf16[2,1,34,128]{3,2,1,0:T(8,128)(2,1)S(1)} %get-tuple-element.60), channel_id=1, source_target_pairs={{32,0},{64,32},{96,64},{128,96},{160,128},{192,160},{224,192},{256... | collective-permute-start | bytes 52232 | tf_op jit(solution)/shard_map/ppermute | solution.py:30
  41.7 0.0 copy-start.9
  41.7 0.0 copy-done
  41.7 0.7 copy-done.9
  42.4 0.0 copy-start.7
  42.4 0.9 copy-done.7
  43.3 0.8 shard_map.147
  44.1 4.8 %all-to-all-done.1.slots = bf16[16,80,128]{2,1,0:T(8,128)(2,1)S(1)} async-done(((bf16[16,80,128]{2,1,0:T(8,128)(2,1)}), bf16[16,80,128]{2,1,0:T(8,128)(2,1)S(1)}, u32[]{:S(2)}, u32[]{:S(2)}) %all-to-all-start.1) | async-done | bytes 327712 | tf_op jit(solution)/shard_map/all_to_all | solution.py:41
  48.8 0.0 copy-start.8
  48.8 0.0 copy-start.10
  48.8 0.7 copy-done.8
  49.5 0.0 copy-done.10
  49.5 1.2 %shard_map.148 = (f32[4,128]{1,0:T(4,128)S(1)}, f32[2,256,128]{2,1,0:T(8,128)S(1)}, f32[2,256,128]{2,1,0:T(8,128)S(1)}, bf16[32,40,128]{2,1,0:T(8,128)(2,1)S(1)}) custom-call(bf16[16,80,128]{2,1,0:T(8,128)(2,1)S(1)} %all-to-all-done.1.slots, bf16[2,8,32,128]{3,2,1,0:T(8,128)(2,1)S(1)} %copy-done.1, f32[2,8,34,128]{3,2,1,0:T(8,128)S(1)} %get-tuple-element.36.wide, ...), custom_call_target="tpu_custom_call" | custom-call | tf_op jit(solution)/shard_map/pallas_call | solution.py:443
  50.7 0.0 copy-start.3
  50.7 0.0 copy-start.5
  50.7 0.0 collective-permute-done.2
  50.7 0.0 collective-permute-done.3
  50.7 4.9 %all-gather = bf16[64,40,128]{2,1,0:T(8,128)(2,1)S(1)} all-gather(bf16[32,40,128]{2,1,0:T(8,128)(2,1)S(1)} %get-tuple-element.47), channel_id=2, replica_groups=mesh['zh'=4,'x'=4,'zl'=2,'y'=8,'c'=2] {'c'}, dimensions={0}, use_global_device_ids=true | all-gather | bytes 983040 | tf_op jit(solution)/shard_map/all_gather | solution.py:462
  55.7 0.0 copy-done.3
  55.7 0.0 copy-done.5
  55.7 0.2 fusion.6
  55.9 0.2 fusion.1
  56.1 11.3 %all_to_all.25 = bf16[16,40,128]{2,1,0:T(8,128)(2,1)S(1)} all-to-all(bf16[16,40,128]{2,1,0:T(8,128)(2,1)S(1)} %fusion.1), channel_id=1, replica_groups=mesh['zh'=4,'x'=4,'zl'=2,'y'=8,'c'=2] {'zl','y'}, dimensions={0} | all-to-all | bytes 327680 | tf_op jit(solution)/shard_map/all_to_all | solution.py:41
  67.4 0.1 fusion.9
  67.4 0.1 fusion.3
  67.6 15.4 %all_to_all.26 = bf16[16,40,128]{2,1,0:T(8,128)(2,1)S(1)} all-to-all(bf16[16,40,128]{2,1,0:T(8,128)(2,1)S(1)} %broadcast_in_dim.20), channel_id=1, replica_groups=mesh['zh'=4,'x'=4,'zl'=2,'y'=8,'c'=2] {'zh','x'}, dimensions={0} | all-to-all | bytes 327680 | tf_op jit(solution)/shard_map/all_to_all | solution.py:41
  83.0 0.1 fusion.8
  83.1 0.1 fusion.5
  83.2 0.7 broadcast_in_dim.21
  83.9 4.8 %all-to-all-start.4 = ((bf16[16,40,128]{2,1,0:T(8,128)(2,1)}), bf16[16,40,128]{2,1,0:T(8,128)(2,1)S(1)}, u32[]{:S(2)}, u32[]{:S(2)}) async-start(bf16[16,40,128]{2,1,0:T(8,128)(2,1)} %broadcast_in_dim.21), calls=%async_computation.4 | async-start | bytes 327680 | tf_op jit(solution)/shard_map/all_to_all | solution.py:41
  88.6 0.1 pad_maximum_fusion.padded
  88.7 0.0 copy-start.6
  88.7 1.3 %shard_map.149 = bf16[2,8,32,128]{3,2,1,0:T(8,128)(2,1)} custom-call(bf16[2,10,34,128]{3,2,1,0:T(8,128)(2,1)S(1)} %pad_maximum_fusion.padded, bf16[2,3,384,128]{3,2,1,0:T(8,128)(2,1)S(1)} %get-tuple-element.45.taps, f32[4,128]{1,0:T(4,128)S(1)} %get-tuple-element.46.stats, f32[1,128]{1,0:T(1,128)S(1)} %bitcast.11, f32[1,128]{1,0:T(1,128)S(1)} %bitcast.14), custom_call_target="tpu_custom_call" | custom-call | tf_op jit(solution)/shard_map/pallas_call | solution.py:470
  90.0 0.0 copy-start.4
  90.0 6.2 %all-to-all-done.4 = bf16[16,40,128]{2,1,0:T(8,128)(2,1)S(1)} async-done(((bf16[16,40,128]{2,1,0:T(8,128)(2,1)}), bf16[16,40,128]{2,1,0:T(8,128)(2,1)S(1)}, u32[]{:S(2)}, u32[]{:S(2)}) %all-to-all-start.4) | async-done | bytes 163872 | tf_op jit(solution)/shard_map/all_to_all | solution.py:41
  96.2 5.6 %all-gather.1.gathered = bf16[32,40,128]{2,1,0:T(8,128)(2,1)S(1)} all-gather(bf16[16,40,128]{2,1,0:T(8,128)(2,1)S(1)} %all-to-all-done.4), channel_id=3, replica_groups=mesh['zh'=4,'x'=4,'zl'=2,'y'=8,'c'=2] {'c'}, dimensions={0}, use_global_device_ids=true | all-gather | bytes 491520 | tf_op jit(solution)/shard_map/all_gather | solution.py:468
  101.8 0.0 copy-done.6
  101.8 0.0 copy-done.4
  101.8 1.2 %shard_map.150 = (bf16[2,8,32,128]{3,2,1,0:T(8,128)(2,1)}, f32[9,128,128]{2,1,0:T(8,128)}, f32[512,128]{1,0:T(8,128)}, f32[1,128]{1,0:T(1,128)}, f32[1,128]{1,0:T(1,128)}) custom-call(bf16[32,40,128]{2,1,0:T(8,128)(2,1)S(1)} %all-gather.1.gathered, f32[4,128]{1,0:T(4,128)S(1)} %get-tuple-element.46.stats, f32[2,256,128]{2,1,0:T(8,128)S(1)} %copy-done.4, ...), custom_call_target="tpu_custom_call" | custom-call | tf_op jit(solution)/shard_map/pallas_call | solution.py:474
  (8 shorter events, 0.2 us)
Async XLA Ops:
  3.5 10.7 %copy-start.1 = (bf16[2,8,32,128]{3,2,1,0:T(8,128)(2,1)S(1)}, bf16[2,8,32,128]{3,2,1,0:T(8,128)(2,1)}, u32[]{:S(2)}) copy-start(bf16[2,8,32,128]{3,2,1,0:T(8,128)(2,1)} %get-tuple-element.34.mixed) | copy-start | bytes 393220
  3.5 20.9 %copy-start.2 = (bf16[2,8,32,128]{3,2,1,0:T(8,128)(2,1)S(1)}, bf16[2,8,32,128]{3,2,1,0:T(8,128)(2,1)}, u32[]{:S(2)}) copy-start(bf16[2,8,32,128]{3,2,1,0:T(8,128)(2,1)} %cotangent.1) | copy-start | bytes 393220
  3.6 20.9 %all-to-all-start = ((bf16[32,24,128]{2,1,0:T(8,128)(2,1)}), bf16[32,24,128]{2,1,0:T(8,128)(2,1)S(1)}, u32[]{:S(2)}, u32[]{:S(2)}) async-start(bf16[32,24,128]{2,1,0:T(8,128)(2,1)} %get-tuple-element.32), calls=%async_computation | async-start | bytes 393216 | tf_op jit(solution)/shard_map/all_to_all | solution.py:41
  14.3 11.0 %collective-permute-start = (bf16[2,8,1,128]{3,2,1,0:T(2,128)(2,1)S(1)}, bf16[2,8,1,128]{3,2,1,0:T(2,128)(2,1)S(1)}, u32[]{:S(2)}, u32[]{:S(2)}) collective-permute-start(bf16[2,8,1,128]{3,2,1,0:T(2,128)(2,1)S(1)} %get-tuple-element.63), channel_id=1, source_target_pairs={{0,1},{1,2},{2,3},{3,4},{4,5},{5,6},{6,7},{7,8},{8,9},{9,10},{10,1... | collective-permute-start | bytes 12296 | tf_op jit(solution)/shard_map/ppermute | solution.py:30
  17.9 23.8 %copy-start = (f32[3,3,128,128]{3,2,1,0:T(8,128)S(1)}, f32[3,3,128,128]{3,2,1,0:T(8,128)}, u32[]{:S(2)}) copy-start(f32[3,3,128,128]{3,2,1,0:T(8,128)} %param.16) | copy-start | bytes 1769476
  17.9 7.5 %collective-permute-start.1 = (bf16[2,8,1,128]{3,2,1,0:T(2,128)(2,1)S(1)}, bf16[2,8,1,128]{3,2,1,0:T(2,128)(2,1)S(1)}, u32[]{:S(2)}, u32[]{:S(2)}) collective-permute-start(bf16[2,8,1,128]{3,2,1,0:T(2,128)(2,1)S(1)} %get-tuple-element.62), channel_id=1, source_target_pairs={{0,31},{1,0},{2,1},{3,2},{4,3},{5,4},{6,5},{7,6},{8,7},{9,8},{10,9... | collective-permute-start | bytes 12296 | tf_op jit(solution)/shard_map/ppermute | solution.py:30
  25.3 23.5 %all-to-all-start.1 = ((bf16[16,80,128]{2,1,0:T(8,128)(2,1)}), bf16[16,80,128]{2,1,0:T(8,128)(2,1)S(1)}, u32[]{:S(2)}, u32[]{:S(2)}) async-start(bf16[16,80,128]{2,1,0:T(8,128)(2,1)} %get-tuple-element.35), calls=%async_computation.1 | async-start | bytes 655360 | tf_op jit(solution)/shard_map/all_to_all | solution.py:41
  37.1 13.7 %collective-permute-start.2 = (bf16[2,1,34,128]{3,2,1,0:T(8,128)(2,1)S(1)}, bf16[2,1,34,128]{3,2,1,0:T(8,128)(2,1)S(1)}, u32[]{:S(2)}, u32[]{:S(2)}) collective-permute-start(bf16[2,1,34,128]{3,2,1,0:T(8,128)(2,1)S(1)} %get-tuple-element.61), channel_id=1, source_target_pairs={{0,32},{32,64},{64,96},{96,128},{128,160},{160,192},{192,224},{224... | collective-permute-start | bytes 52232 | tf_op jit(solution)/shard_map/ppermute | solution.py:30
  40.4 10.4 %collective-permute-start.3 = (bf16[2,1,34,128]{3,2,1,0:T(8,128)(2,1)S(1)}, bf16[2,1,34,128]{3,2,1,0:T(8,128)(2,1)S(1)}, u32[]{:S(2)}, u32[]{:S(2)}) collective-permute-start(bf16[2,1,34,128]{3,2,1,0:T(8,128)(2,1)S(1)} %get-tuple-element.60), channel_id=1, source_target_pairs={{32,0},{64,32},{96,64},{128,96},{160,128},{192,160},{224,192},{256... | collective-permute-start | bytes 52232 | tf_op jit(solution)/shard_map/ppermute | solution.py:30
  41.7 0.7 copy-start.9
  42.4 0.9 copy-start.7
  48.8 0.7 copy-start.8
  48.8 0.7 copy-start.10
  50.7 5.0 %copy-start.3 = (f32[2,256,128]{2,1,0:T(8,128)}, f32[2,256,128]{2,1,0:T(8,128)S(1)}, u32[]{:S(2)}) copy-start(f32[2,256,128]{2,1,0:T(8,128)S(1)} %get-tuple-element.48.norm) | copy-start | bytes 786436
  50.7 5.0 %copy-start.5 = (f32[2,256,128]{2,1,0:T(8,128)}, f32[2,256,128]{2,1,0:T(8,128)S(1)}, u32[]{:S(2)}) copy-start(f32[2,256,128]{2,1,0:T(8,128)S(1)} %get-tuple-element.49.grad_pre) | copy-start | bytes 786436
  83.9 12.3 %all-to-all-start.4 = ((bf16[16,40,128]{2,1,0:T(8,128)(2,1)}), bf16[16,40,128]{2,1,0:T(8,128)(2,1)S(1)}, u32[]{:S(2)}, u32[]{:S(2)}) async-start(bf16[16,40,128]{2,1,0:T(8,128)(2,1)} %broadcast_in_dim.21), calls=%async_computation.4 | async-start | bytes 327680 | tf_op jit(solution)/shard_map/all_to_all | solution.py:41
  88.7 13.1 %copy-start.6 = (f32[2,256,128]{2,1,0:T(8,128)S(1)}, f32[2,256,128]{2,1,0:T(8,128)}, u32[]{:S(2)}) copy-start(f32[2,256,128]{2,1,0:T(8,128)} %copy-done.5) | copy-start | bytes 786436
  90.0 11.8 %copy-start.4 = (f32[2,256,128]{2,1,0:T(8,128)S(1)}, f32[2,256,128]{2,1,0:T(8,128)}, u32[]{:S(2)}) copy-start(f32[2,256,128]{2,1,0:T(8,128)} %copy-done.3) | copy-start | bytes 786436

commit v7 on v6

--- a/solution.py
+++ b/solution.py
@@ -109,62 +109,69 @@
     return three_terms(mean) + three_terms(spread) + [jnp.zeros((2, LANES), F32)]
 
 
+def fetcher(arrivals):
+    used = iter(range(arrivals.shape[0]))
+
+    def fetch(source, target):
+        copy = pltpu.make_async_copy(source, target, arrivals.at[next(used)])
+        copy.start()
+        return copy
+
+    return fetch
+
+
 def mix_body(
-    feats_in, cond_in, null_in, cot_in, flags, mixed_out, slots_out,
-    feats, cond, null, cot, arrivals,
+    feats_in, cond_in, null_in, cot_in, flags_in, mixed_out, moments_out, first_out, last_out,
+    feats, cond, null, cot, flags, arrivals,
 ):
-    copies = []
-    for at, (source, target) in enumerate(
-        ((null_in, null), (feats_in, feats), (cond_in, cond), (cot_in, cot))
-    ):
-        copies.append(pltpu.make_async_copy(source, target, arrivals.at[at]))
-        copies[-1].start()
-    for copy in copies[:3]:
-        copy.wait()
+    fetch = fetcher(arrivals)
+    flags_copy, null_copy = fetch(flags_in, flags), fetch(null_in, null)
+    field_copies = [
+        (fetch(feats_in.at[sample], feats.at[sample]), fetch(cond_in.at[sample], cond.at[sample]))
+        for sample in range(feats.shape[0])
+    ]
+    cot_copy = fetch(cot_in, cot)
+    flags_copy.wait()
+    null_copy.wait()
     samples, tile_rows, tile_cols, channels = feats.shape
     cells = tile_rows * tile_cols
     size = cells * (channels // GROUPS)
     null32 = null[...].astype(F32)
     means, spreads = [], []
     for sample in range(samples):
+        for copy in field_copies[sample]:
+            copy.wait()
         dropped = flags[sample : sample + 1, :].astype(F32).reshape(1, 1, channels)
         mixed = (
             feats[sample].astype(F32) + dropped * null32 + (1.0 - dropped) * cond[sample].astype(F32)
         ).astype(BF16)
         mixed_out[sample] = mixed
-        wide = mixed.astype(F32).reshape(cells, channels)
+        wide = mixed.astype(F32)
+        first_out[0, sample] = wide[:, 0, :].astype(BF16)
+        last_out[0, sample] = wide[:, tile_cols - 1, :].astype(BF16)
+        wide = wide.reshape(cells, channels)
         mean = group_total(jnp.sum(wide, axis=0, keepdims=True)) * (1.0 / size)
         away = wide - mean
         means.append(mean)
         spreads.append(group_total(jnp.sum(away * away, axis=0, keepdims=True)))
-    rows = header(weave(*means), weave(*spreads))
-    copies[3].wait()
-    firsts, lasts = [], []
+    moments = jnp.concatenate([weave(*means), weave(*spreads)], axis=0)
+    moments_out[...] = jnp.broadcast_to(moments[None], moments_out.shape)
+    cot_copy.wait()
     for sample in range(samples):
         wide = cot[sample].astype(F32)
-        firsts.append(wide[:, 0, :])
-        lasts.append(wide[:, tile_cols - 1, :])
-    slots_out[...] = jnp.broadcast_to(
-        jnp.concatenate(rows + firsts, axis=0).astype(BF16)[None], slots_out.shape
-    )
-    after = lax.rem(place(LON) + 1, slots_out.shape[0])
-    slots_out[after] = jnp.concatenate(rows + lasts, axis=0).astype(BF16)
-
-
-def merge_body(count, slots, cot, wide_out, slots_out, edge):
+        first_out[1, sample] = wide[:, 0, :].astype(BF16)
+        last_out[1, sample] = wide[:, tile_cols - 1, :].astype(BF16)
+
+
+def build_body(moments, low, high, cot, wide_out, slots_out, edge):
     samples, tile_rows, tile_cols, channels = cot.shape
-    lon_count, lat_count = slots.shape[0], slots_out.shape[0]
-    mean, spread = merged(slots, count)
-    me = place(LON)
-    before = slots[lax.rem(me + lon_count - 1, lon_count)].astype(F32)
-    after = slots[lax.rem(me + 1, lon_count)].astype(F32)
-    for sample in range(samples):
-        here = slice(8 + sample * tile_rows, 8 + (sample + 1) * tile_rows)
-        wide_out[sample, :, 0, :] = before[here, :]
+    lat_count = slots_out.shape[0]
+    for sample in range(samples):
+        wide_out[sample, :, 0, :] = low[1, sample].astype(F32)
         wide_out[sample, :, 1 : 1 + tile_cols, :] = cot[sample].astype(F32)
-        wide_out[sample, :, 1 + tile_cols, :] = after[here, :]
+        wide_out[sample, :, 1 + tile_cols, :] = high[1, sample].astype(F32)
     edge[...] = jnp.zeros(edge.shape, F32)
-    edge[0:8, :] = jnp.concatenate(header(mean, spread), axis=0)
+    edge[0:8, :] = jnp.concatenate(header(moments[0:1, :], moments[1:2, :]), axis=0)
     span = tile_cols + 2
     for sample in range(samples):
         edge[8 + sample * span : 8 + (sample + 1) * span, :] = wide_out[sample, 0]
@@ -179,16 +186,19 @@
 
 
 def weights_body(
-    emb, style_weight, weight, style_out, column_out, demod_out, power_out, emb_out, back_out, taps_out,
+    emb, style_weight, gamma, beta, weight,
+    gamma_out, beta_out, style_out, column_out, demod_out, power_out, emb_out, back_out, taps_out,
 ):
+    gamma_out[...] = gamma[...]
+    beta_out[...] = beta[...]
+    power = jnp.zeros(weight.shape[1:], F32)
+    for tap in range(9):
+        power = power + weight[tap] * weight[tap]
     samples, channels = emb.shape[0], weight.shape[2]
     exact = lax.Precision.HIGHEST
     style = 1.0 + jnp.dot(
         emb[...], style_weight[...], precision=exact, preferred_element_type=F32
     )
-    power = jnp.zeros((channels, channels), F32)
-    for tap in range(9):
-        power = power + weight[tap] * weight[tap]
     squares = jnp.dot(style * style, power, precision=exact, preferred_element_type=F32)
     demod = lax.rsqrt(squares + 1e-08)
     style_out[...] = style
@@ -391,43 +401,48 @@
     scale_gradient = 1.0 / math.sqrt(samples * tile_rows * tile_cols * devices_all)
     taps = conv_weight.reshape(9, channels, channels)
 
-    anywhere, whole = pl.BlockSpec(memory_space=pl.ANY), pl.BlockSpec(memory_space=pltpu.VMEM)
-    head = 8
-    lon_slot = head + samples * tile_rows
-    lat_slot = -(-(head + samples * (tile_cols + 2)) // 16) * 16
-    mixed, slots = call(
+    lat_slot = -(-(8 + samples * (tile_cols + 2)) // 16) * 16
+    edges = array((2, samples, tile_rows, channels), BF16)
+    mixed, moments, first, last = call(
         mix_body,
-        (array(feats.shape, BF16), array((lon_count, lon_slot, LANES), BF16)),
+        (array(feats.shape, BF16), array((lon_count, 2, LANES)), edges, edges),
         (
             pltpu.VMEM(feats.shape, BF16),
             pltpu.VMEM(feats.shape, BF16),
             pltpu.VMEM(null_field.shape, BF16),
             pltpu.VMEM(feats.shape, BF16),
-            pltpu.SemaphoreType.DMA((4,)),
+            pltpu.VMEM(drop_flags.shape, jnp.int32),
+            pltpu.SemaphoreType.DMA((2 * samples + 3,)),
         ),
         room=60,
-        in_specs=[anywhere] * 4 + [whole],
+        in_specs=[pl.BlockSpec(memory_space=pl.ANY)] * 5,
     )(feats, cond, null_field, cotangent, drop_flags)
-    slots = exchange(slots, LON)
-    low, high = shift(mixed[:, :, -1:], LON, 1, True), shift(mixed[:, :, :1], LON, -1, True)
+    rows = exchange(moments, LON)
+    low, high = shift(last, LON, 1, True), shift(first, LON, -1, True)
+    mean = jnp.mean(rows[:, :1], axis=0)
+    away = rows[:, :1] - mean
+    moments = jnp.concatenate(
+        [mean, jnp.sum(rows[:, 1:] + cells_local * (away * away), axis=0)], axis=0
+    )
+    moments, low, high = lax.optimization_barrier((moments, low, high))
     wide_cot, slots = call(
-        functools.partial(merge_body, cells_local),
+        build_body,
         (
             array((samples, tile_rows, tile_cols + 2, channels)),
             array((lat_count, lat_slot, LANES), BF16),
         ),
         (pltpu.VMEM((lat_slot, LANES), F32),),
-    )(slots, cotangent)
-    slots, low, high = lax.optimization_barrier((slots, low, high))
+    )(moments, low, high, cotangent)
     slots = exchange(slots, LAT)
-    padded = jnp.concatenate([low, mixed, high], axis=2)
+    padded = jnp.concatenate([low[0][:, :, None], mixed, high[0][:, :, None]], axis=2)
     low, high = shift(padded[:, -1:], LAT, 1, False), shift(padded[:, :1], LAT, -1, False)
-    gamma, beta = gamma[None], beta[None]
 
     taps_shape = (samples, 3, 3 * channels, channels)
-    style, column, demod, power, emb_full, back_taps, fore_taps = call(
+    gamma, beta, style, column, demod, power, emb_full, back_taps, fore_taps = call(
         weights_body,
         (
+            array((1, channels)),
+            array((1, channels)),
             array((samples, channels)),
             array((samples, channels, channels)),
             array((samples, channels)),
@@ -436,7 +451,7 @@
             array(taps_shape, BF16),
             array(taps_shape, BF16),
         ),
-    )(emb, style_weight, taps)
+    )(emb, style_weight, gamma[None], beta[None], taps)
     spread = pltpu.VMEM((tile_rows + 2, tile_cols + 2, channels), F32)
     shifted = pltpu.VMEM(((tile_rows + 2) * tile_cols, 3 * channels), BF16)
     flat = (samples, tile_rows * tile_cols, channels)

time: 104 us -> 104 us (level)
  blocking collectives: 37.2 us -> 41.3 us
  waiting for transfers between devices: 15.5 us -> 13 us
    all_to_all x2, blocking collectives: 26.7 us -> 30.5 us  [exchange(): return lax.all_to_all(block, axes, 0, 0)]
    all_to_all x3, waiting for transfers between devices: 15.5 us -> 12.2 us  [exchange(): return lax.all_to_all(block, axes, 0, 0)]
  transfers between devices with their start and end apart: 7 -> 7, of which waited for: 3 -> 4; matrix products, arithmetic and copies ran while one was open for 0% -> 0% of each run, Pallas kernels for 4% -> 3%
where the time goes in v7:
time: 104 us
  blocking collectives  41.3 us (40%)
  starting transfers between devices  37.4 us (36%)
  waiting for transfers between devices  13 us (12%)
  Pallas kernels  7.74 us (7%)
  local copies, waits for them, and re-layouts  2.7 us (3%)
    all_to_all x2, blocking collectives, exchange(): return lax.all_to_all(block, axes, 0, 0)  30.5 us
    all_to_all x3, starting transfers between devices, exchange(): return lax.all_to_all(block, axes, 0, 0)  27.3 us
    all_to_all x3, waiting for transfers between devices, exchange(): return lax.all_to_all(block, axes, 0, 0)  12.2 us
    ppermute x4, starting transfers between devices, shift(): return lax.ppermute(block, axes, pairs)  10.1 us
    all_gather x1, blocking collectives, on_device(): payload = lax.all_gather(everyone(payload, NEAR), 'c')  5.61 us
    all_gather x1, blocking collectives, on_device(): payload = lax.all_gather(payload, 'c')  5.22 us
    pallas_call x1, Pallas kernels, on_device(): call(mix_body, (array(feats.shape, BF16), array((lon_count, 2, LANES)), e...  2.47 us
  transfers between devices with their start and end apart: 7, of which 4 were waited for; matrix products, arithmetic and copies ran while one was open for 0% of the time, Pallas kernels for 3%

profile of v7, /device:TPU:1, one launch (start us, length us, event | category | flops | bytes accessed | tf_op | source)
XLA Modules:
  0.0 103.8 jit_solution(13230795342795755788)
XLA Ops:
  0.6 2.5 %shard_map.145 = (bf16[2,8,32,128]{3,2,1,0:T(8,128)(2,1)}, f32[32,2,128]{2,1,0:T(2,128)}, bf16[2,2,8,128]{3,2,1,0:T(8,128)(2,1)}, bf16[2,2,8,128]{3,2,1,0:T(8,128)(2,1)}) custom-call(bf16[2,8,32,128]{3,2,1,0:T(8,128)(2,1)} %feats_in.1, bf16[2,8,32,128]{3,2,1,0:T(8,128)(2,1)} %cond_in.1, bf16[8,32,128]{2,1,0:T(8,128)(2,1)} %null_in.1, ...), custom_call_target="tpu_custom_call" | custom-call | tf_op jit(solution)/shard_map/pallas_call | solution.py:406
  3.1 0.0 copy-start.1
  3.1 10.7 %all-to-all-start = ((f32[32,2,128]{2,1,0:T(2,128)}), f32[32,2,128]{2,1,0:T(2,128)S(1)}, u32[]{:S(2)}, u32[]{:S(2)}) async-start(f32[32,2,128]{2,1,0:T(2,128)} %get-tuple-element.36), calls=%async_computation | async-start | bytes 65536 | tf_op jit(solution)/shard_map/all_to_all | solution.py:41
  13.8 0.0 copy-start
  13.8 3.7 %collective-permute-start = (bf16[2,2,8,128]{3,2,1,0:T(8,128)(2,1)}, bf16[2,2,8,128]{3,2,1,0:T(8,128)(2,1)S(1)}, u32[]{:S(2)}, u32[]{:S(2)}) collective-permute-start(bf16[2,2,8,128]{3,2,1,0:T(8,128)(2,1)} %get-tuple-element.37), channel_id=1, source_target_pairs={{0,1},{1,2},{2,3},{3,4},{4,5},{5,6},{6,7},{7,8},{8,9},{9,10},{10,1... | collective-permute-start | bytes 24584 | tf_op jit(solution)/shard_map/ppermute | solution.py:30
  17.5 1.9 %collective-permute-start.1 = (bf16[2,2,8,128]{3,2,1,0:T(8,128)(2,1)}, bf16[2,2,8,128]{3,2,1,0:T(8,128)(2,1)S(1)}, u32[]{:S(2)}, u32[]{:S(2)}) collective-permute-start(bf16[2,2,8,128]{3,2,1,0:T(8,128)(2,1)} %get-tuple-element.38), channel_id=1, source_target_pairs={{0,31},{1,0},{2,1},{3,2},{4,3},{5,4},{6,5},{7,6},{8,7},{9,8},{10,9... | collective-permute-start | bytes 24584 | tf_op jit(solution)/shard_map/ppermute | solution.py:30
  19.5 2.3 %all-to-all-done = f32[32,2,128]{2,1,0:T(2,128)S(1)} async-done(((f32[32,2,128]{2,1,0:T(2,128)}), f32[32,2,128]{2,1,0:T(2,128)S(1)}, u32[]{:S(2)}, u32[]{:S(2)}) %all-to-all-start) | async-done | bytes 32800 | tf_op jit(solution)/shard_map/all_to_all | solution.py:41
  21.8 0.1 fusion.6
  21.9 0.0 collective-permute-done.low
  21.9 0.8 collective-permute-done.1.high
  22.7 0.0 copy-done.1
  22.7 0.8 shard_map.146
  23.5 0.0 copy-start.2
  23.5 11.8 %all-to-all-start.1 = ((bf16[16,80,128]{2,1,0:T(8,128)(2,1)}), bf16[16,80,128]{2,1,0:T(8,128)(2,1)S(1)}, u32[]{:S(2)}, u32[]{:S(2)}) async-start(bf16[16,80,128]{2,1,0:T(8,128)(2,1)} %get-tuple-element.42), calls=%async_computation.1 | async-start | bytes 655360 | tf_op jit(solution)/shard_map/all_to_all | solution.py:41
  35.4 0.0 copy-done.2
  35.4 3.3 %collective-permute-start.2 = (bf16[2,1,34,128]{3,2,1,0:T(8,128)(2,1)S(1)}, bf16[2,1,34,128]{3,2,1,0:T(8,128)(2,1)S(1)}, u32[]{:S(2)}, u32[]{:S(2)}) collective-permute-start(bf16[2,1,34,128]{3,2,1,0:T(8,128)(2,1)S(1)} %get-tuple-element.69), channel_id=1, source_target_pairs={{0,32},{32,64},{64,96},{96,128},{128,160},{160,192},{192,224},{224... | collective-permute-start | bytes 52232 | tf_op jit(solution)/shard_map/ppermute | solution.py:30
  38.7 1.3 %collective-permute-start.3 = (bf16[2,1,34,128]{3,2,1,0:T(8,128)(2,1)S(1)}, bf16[2,1,34,128]{3,2,1,0:T(8,128)(2,1)S(1)}, u32[]{:S(2)}, u32[]{:S(2)}) collective-permute-start(bf16[2,1,34,128]{3,2,1,0:T(8,128)(2,1)S(1)} %get-tuple-element.68), channel_id=1, source_target_pairs={{32,0},{64,32},{96,64},{128,96},{160,128},{192,160},{224,192},{256... | collective-permute-start | bytes 52232 | tf_op jit(solution)/shard_map/ppermute | solution.py:30
  40.0 0.0 copy-start.8
  40.0 0.0 copy-start.9
  40.0 0.0 copy-start.10
  40.1 0.0 copy-done
  40.1 0.6 copy-done.8
  40.7 0.0 copy-done.9
  40.7 0.0 copy-done.10
  40.7 0.0 copy-start.7
  40.7 0.9 copy-done.7
  41.7 0.8 shard_map.147
  42.4 3.7 %all-to-all-done.1.slots = bf16[16,80,128]{2,1,0:T(8,128)(2,1)S(1)} async-done(((bf16[16,80,128]{2,1,0:T(8,128)(2,1)}), bf16[16,80,128]{2,1,0:T(8,128)(2,1)S(1)}, u32[]{:S(2)}, u32[]{:S(2)}) %all-to-all-start.1) | async-done | bytes 327712 | tf_op jit(solution)/shard_map/all_to_all | solution.py:41
  46.1 1.2 %shard_map.148 = (f32[4,128]{1,0:T(4,128)S(1)}, f32[2,256,128]{2,1,0:T(8,128)S(1)}, f32[2,256,128]{2,1,0:T(8,128)S(1)}, bf16[32,40,128]{2,1,0:T(8,128)(2,1)S(1)}) custom-call(bf16[16,80,128]{2,1,0:T(8,128)(2,1)S(1)} %all-to-all-done.1.slots, bf16[2,8,32,128]{3,2,1,0:T(8,128)(2,1)S(1)} %copy-done.2, f32[2,8,34,128]{3,2,1,0:T(8,128)S(1)} %get-tuple-element.44.wide, ...), custom_call_target="tpu_custom_call" | custom-call | tf_op jit(solution)/shard_map/pallas_call | solution.py:458
  47.3 0.0 copy-start.3
  47.4 0.0 copy-start.5
  47.4 0.0 collective-permute-done.2
  47.4 0.0 collective-permute-done.3
  47.4 5.2 %all-gather = bf16[64,40,128]{2,1,0:T(8,128)(2,1)S(1)} all-gather(bf16[32,40,128]{2,1,0:T(8,128)(2,1)S(1)} %get-tuple-element.55), channel_id=2, replica_groups=mesh['zh'=4,'x'=4,'zl'=2,'y'=8,'c'=2] {'c'}, dimensions={0}, use_global_device_ids=true | all-gather | bytes 983040 | tf_op jit(solution)/shard_map/all_gather | solution.py:477
  52.6 0.0 copy-done.3
  52.6 0.0 copy-done.5
  52.7 0.2 fusion.8
  52.8 0.2 fusion.1
  53.0 14.3 %all_to_all.25 = bf16[16,40,128]{2,1,0:T(8,128)(2,1)S(1)} all-to-all(bf16[16,40,128]{2,1,0:T(8,128)(2,1)S(1)} %fusion.1), channel_id=1, replica_groups=mesh['zh'=4,'x'=4,'zl'=2,'y'=8,'c'=2] {'zl','y'}, dimensions={0} | all-to-all | bytes 327680 | tf_op jit(solution)/shard_map/all_to_all | solution.py:41
  67.3 0.1 fusion.10
  67.4 0.1 fusion.3
  67.5 16.2 %all_to_all.26 = bf16[16,40,128]{2,1,0:T(8,128)(2,1)S(1)} all-to-all(bf16[16,40,128]{2,1,0:T(8,128)(2,1)S(1)} %broadcast_in_dim.10), channel_id=1, replica_groups=mesh['zh'=4,'x'=4,'zl'=2,'y'=8,'c'=2] {'zh','x'}, dimensions={0} | all-to-all | bytes 327680 | tf_op jit(solution)/shard_map/all_to_all | solution.py:41
  83.7 0.1 fusion.9
  83.8 0.1 fusion.5
  83.9 0.7 broadcast_in_dim.22
  84.6 4.8 %all-to-all-start.4 = ((bf16[16,40,128]{2,1,0:T(8,128)(2,1)}), bf16[16,40,128]{2,1,0:T(8,128)(2,1)S(1)}, u32[]{:S(2)}, u32[]{:S(2)}) async-start(bf16[16,40,128]{2,1,0:T(8,128)(2,1)} %broadcast_in_dim.22), calls=%async_computation.4 | async-start | bytes 327680 | tf_op jit(solution)/shard_map/all_to_all | solution.py:41
  89.4 0.1 pad_maximum_fusion.padded
  89.4 0.0 copy-start.6
  89.5 1.3 %shard_map.149 = bf16[2,8,32,128]{3,2,1,0:T(8,128)(2,1)} custom-call(bf16[2,10,34,128]{3,2,1,0:T(8,128)(2,1)S(1)} %pad_maximum_fusion.padded, bf16[2,3,384,128]{3,2,1,0:T(8,128)(2,1)S(1)} %get-tuple-element.53.taps, f32[4,128]{1,0:T(4,128)S(1)} %get-tuple-element.54.stats, f32[1,128]{1,0:T(1,128)S(1)} %get-tuple-element.45.gamma, ...), custom_call_target="tpu_custom_call" | custom-call | tf_op jit(solution)/shard_map/pallas_call | solution.py:485
  90.7 0.0 copy-start.4
  90.7 6.2 %all-to-all-done.4 = bf16[16,40,128]{2,1,0:T(8,128)(2,1)S(1)} async-done(((bf16[16,40,128]{2,1,0:T(8,128)(2,1)}), bf16[16,40,128]{2,1,0:T(8,128)(2,1)S(1)}, u32[]{:S(2)}, u32[]{:S(2)}) %all-to-all-start.4) | async-done | bytes 163872 | tf_op jit(solution)/shard_map/all_to_all | solution.py:41
  96.9 5.6 %all-gather.1.gathered = bf16[32,40,128]{2,1,0:T(8,128)(2,1)S(1)} all-gather(bf16[16,40,128]{2,1,0:T(8,128)(2,1)S(1)} %all-to-all-done.4), channel_id=3, replica_groups=mesh['zh'=4,'x'=4,'zl'=2,'y'=8,'c'=2] {'c'}, dimensions={0}, use_global_device_ids=true | all-gather | bytes 491520 | tf_op jit(solution)/shard_map/all_gather | solution.py:483
  102.5 0.0 copy-done.6
  102.5 0.0 copy-done.4
  102.5 1.2 %shard_map.150 = (bf16[2,8,32,128]{3,2,1,0:T(8,128)(2,1)}, f32[9,128,128]{2,1,0:T(8,128)}, f32[512,128]{1,0:T(8,128)}, f32[1,128]{1,0:T(1,128)}, f32[1,128]{1,0:T(1,128)}) custom-call(bf16[32,40,128]{2,1,0:T(8,128)(2,1)S(1)} %all-gather.1.gathered, f32[4,128]{1,0:T(4,128)S(1)} %get-tuple-element.54.stats, f32[2,256,128]{2,1,0:T(8,128)S(1)} %copy-done.4, ...), custom_call_target="tpu_custom_call" | custom-call | tf_op jit(solution)/shard_map/pallas_call | solution.py:489
  (14 shorter events, 0.2 us)
Async XLA Ops:
  3.1 19.6 %copy-start.1 = (bf16[2,8,32,128]{3,2,1,0:T(8,128)(2,1)S(1)}, bf16[2,8,32,128]{3,2,1,0:T(8,128)(2,1)}, u32[]{:S(2)}) copy-start(bf16[2,8,32,128]{3,2,1,0:T(8,128)(2,1)} %cotangent.1) | copy-start | bytes 393220
  3.1 18.6 %all-to-all-start = ((f32[32,2,128]{2,1,0:T(2,128)}), f32[32,2,128]{2,1,0:T(2,128)S(1)}, u32[]{:S(2)}, u32[]{:S(2)}) async-start(f32[32,2,128]{2,1,0:T(2,128)} %get-tuple-element.36), calls=%async_computation | async-start | bytes 65536 | tf_op jit(solution)/shard_map/all_to_all | solution.py:41
  13.8 26.2 %copy-start = (f32[3,3,128,128]{3,2,1,0:T(8,128)S(1)}, f32[3,3,128,128]{3,2,1,0:T(8,128)}, u32[]{:S(2)}) copy-start(f32[3,3,128,128]{3,2,1,0:T(8,128)} %param.16) | copy-start | bytes 1769476
  13.8 8.0 %collective-permute-start = (bf16[2,2,8,128]{3,2,1,0:T(8,128)(2,1)}, bf16[2,2,8,128]{3,2,1,0:T(8,128)(2,1)S(1)}, u32[]{:S(2)}, u32[]{:S(2)}) collective-permute-start(bf16[2,2,8,128]{3,2,1,0:T(8,128)(2,1)} %get-tuple-element.37), channel_id=1, source_target_pairs={{0,1},{1,2},{2,3},{3,4},{4,5},{5,6},{6,7},{7,8},{8,9},{9,10},{10,1... | collective-permute-start | bytes 24584 | tf_op jit(solution)/shard_map/ppermute | solution.py:30
  17.5 5.2 %collective-permute-start.1 = (bf16[2,2,8,128]{3,2,1,0:T(8,128)(2,1)}, bf16[2,2,8,128]{3,2,1,0:T(8,128)(2,1)S(1)}, u32[]{:S(2)}, u32[]{:S(2)}) collective-permute-start(bf16[2,2,8,128]{3,2,1,0:T(8,128)(2,1)} %get-tuple-element.38), channel_id=1, source_target_pairs={{0,31},{1,0},{2,1},{3,2},{4,3},{5,4},{6,5},{7,6},{8,7},{9,8},{10,9... | collective-permute-start | bytes 24584 | tf_op jit(solution)/shard_map/ppermute | solution.py:30
  23.5 11.9 %copy-start.2 = (bf16[2,8,32,128]{3,2,1,0:T(8,128)(2,1)S(1)}, bf16[2,8,32,128]{3,2,1,0:T(8,128)(2,1)}, u32[]{:S(2)}) copy-start(bf16[2,8,32,128]{3,2,1,0:T(8,128)(2,1)} %get-tuple-element.43.mixed) | copy-start | bytes 393220
  23.5 22.6 %all-to-all-start.1 = ((bf16[16,80,128]{2,1,0:T(8,128)(2,1)}), bf16[16,80,128]{2,1,0:T(8,128)(2,1)S(1)}, u32[]{:S(2)}, u32[]{:S(2)}) async-start(bf16[16,80,128]{2,1,0:T(8,128)(2,1)} %get-tuple-element.42), calls=%async_computation.1 | async-start | bytes 655360 | tf_op jit(solution)/shard_map/all_to_all | solution.py:41
  35.4 11.9 %collective-permute-start.2 = (bf16[2,1,34,128]{3,2,1,0:T(8,128)(2,1)S(1)}, bf16[2,1,34,128]{3,2,1,0:T(8,128)(2,1)S(1)}, u32[]{:S(2)}, u32[]{:S(2)}) collective-permute-start(bf16[2,1,34,128]{3,2,1,0:T(8,128)(2,1)S(1)} %get-tuple-element.69), channel_id=1, source_target_pairs={{0,32},{32,64},{64,96},{96,128},{128,160},{160,192},{192,224},{224... | collective-permute-start | bytes 52232 | tf_op jit(solution)/shard_map/ppermute | solution.py:30
  38.7 8.7 %collective-permute-start.3 = (bf16[2,1,34,128]{3,2,1,0:T(8,128)(2,1)S(1)}, bf16[2,1,34,128]{3,2,1,0:T(8,128)(2,1)S(1)}, u32[]{:S(2)}, u32[]{:S(2)}) collective-permute-start(bf16[2,1,34,128]{3,2,1,0:T(8,128)(2,1)S(1)} %get-tuple-element.68), channel_id=1, source_target_pairs={{32,0},{64,32},{96,64},{128,96},{160,128},{192,160},{224,192},{256... | collective-permute-start | bytes 52232 | tf_op jit(solution)/shard_map/ppermute | solution.py:30
  40.0 0.7 copy-start.8
  40.0 0.7 copy-start.9
  40.0 0.7 copy-start.10
  40.7 1.0 copy-start.7
  47.3 5.3 %copy-start.3 = (f32[2,256,128]{2,1,0:T(8,128)}, f32[2,256,128]{2,1,0:T(8,128)S(1)}, u32[]{:S(2)}) copy-start(f32[2,256,128]{2,1,0:T(8,128)S(1)} %get-tuple-element.56.norm) | copy-start | bytes 786436
  47.4 5.3 %copy-start.5 = (f32[2,256,128]{2,1,0:T(8,128)}, f32[2,256,128]{2,1,0:T(8,128)S(1)}, u32[]{:S(2)}) copy-start(f32[2,256,128]{2,1,0:T(8,128)S(1)} %get-tuple-element.57.grad_pre) | copy-start | bytes 786436
  84.6 12.3 %all-to-all-start.4 = ((bf16[16,40,128]{2,1,0:T(8,128)(2,1)}), bf16[16,40,128]{2,1,0:T(8,128)(2,1)S(1)}, u32[]{:S(2)}, u32[]{:S(2)}) async-start(bf16[16,40,128]{2,1,0:T(8,128)(2,1)} %broadcast_in_dim.22), calls=%async_computation.4 | async-start | bytes 327680 | tf_op jit(solution)/shard_map/all_to_all | solution.py:41
  89.4 13.1 %copy-start.6 = (f32[2,256,128]{2,1,0:T(8,128)S(1)}, f32[2,256,128]{2,1,0:T(8,128)}, u32[]{:S(2)}) copy-start(f32[2,256,128]{2,1,0:T(8,128)} %copy-done.5) | copy-start | bytes 786436
  90.7 11.8 %copy-start.4 = (f32[2,256,128]{2,1,0:T(8,128)S(1)}, f32[2,256,128]{2,1,0:T(8,128)}, u32[]{:S(2)}) copy-start(f32[2,256,128]{2,1,0:T(8,128)} %copy-done.3) | copy-start | bytes 786436

commit v8 on v7

--- a/solution.py
+++ b/solution.py
@@ -471,8 +471,6 @@
         ),
     )(slots, mixed, wide_cot, gamma, beta, back_taps, column, demod, taps)
 
-    payload, low, high = lax.optimization_barrier((payload, low, high))
-    padded = jnp.concatenate([low, padded, high], axis=1)
     core_count, near_count = lax.axis_size("c"), lax.axis_size(NEAR)
     payload = lax.all_gather(payload, "c")
     payload = payload.reshape(core_count, core_count, near_count, SLOT, LANES)
@@ -480,6 +478,8 @@
     payload = resplit(jnp.sum(payload.astype(F32), axis=0))
     payload = resplit(jnp.sum(exchange(payload, NEAR).astype(F32), axis=0))
     payload = resplit(jnp.sum(everyone(payload, LAT).astype(F32), axis=0))
+    payload, low, high = lax.optimization_barrier((payload, low, high))
+    padded = jnp.concatenate([low, padded, high], axis=1)
     payload = lax.all_gather(everyone(payload, NEAR), "c")
 
     block_out = call(forward_body, array(feats.shape, BF16), (spread, shifted))(

time: 104 us -> 104 us (level)
  the two profiles are of different devices: /device:TPU:1 before, /device:TPU:143 now
where the time goes in v8:
time: 104 us; the launch traced here: 103 us
  starting transfers between devices  43.3 us (42%)
  waiting for transfers between devices  23.7 us (23%)
  blocking collectives  23.5 us (23%)
  Pallas kernels  7.77 us (7%)
  local copies, waits for them, and re-layouts  3.33 us (3%)
    all_to_all x4, starting transfers between devices, exchange(): return lax.all_to_all(block, axes, 0, 0)  30.9 us
    all_to_all x4, waiting for transfers between devices, exchange(): return lax.all_to_all(block, axes, 0, 0)  15.8 us
    all_to_all x1, blocking collectives, exchange(): return lax.all_to_all(block, axes, 0, 0)  15.1 us
    ppermute x4, starting transfers between devices, shift(): return lax.ppermute(block, axes, pairs)  12.4 us
    ppermute x4, waiting for transfers between devices, shift(): return lax.ppermute(block, axes, pairs)  7.94 us
    all_gather x1, blocking collectives, on_device(): payload = lax.all_gather(everyone(payload, NEAR), 'c')  5.94 us
    pallas_call x1, Pallas kernels, on_device(): call(mix_body, (array(feats.shape, BF16), array((lon_count, 2, LANES)), e...  2.5 us
    all_gather x1, blocking collectives, on_device(): payload = lax.all_gather(payload, 'c')  2.44 us
  transfers between devices with their start and end apart: 8, of which 5 were waited for; matrix products, arithmetic and copies ran while one was open for 0% of the time, Pallas kernels for 2%

profile of v8, /device:TPU:143, one launch (start us, length us, event | category | flops | bytes accessed | tf_op | source)
XLA Modules:
  0.0 103.2 jit_solution(17530646119342254170)
XLA Ops:
  0.6 0.0 copy-start.1
  0.6 2.5 %shard_map.145 = (bf16[2,8,32,128]{3,2,1,0:T(8,128)(2,1)}, f32[32,2,128]{2,1,0:T(2,128)}, bf16[2,2,8,128]{3,2,1,0:T(8,128)(2,1)}, bf16[2,2,8,128]{3,2,1,0:T(8,128)(2,1)}) custom-call(bf16[2,8,32,128]{3,2,1,0:T(8,128)(2,1)} %feats_in.1, bf16[2,8,32,128]{3,2,1,0:T(8,128)(2,1)} %cond_in.1, bf16[8,32,128]{2,1,0:T(8,128)(2,1)} %null_in.1, ...), custom_call_target="tpu_custom_call" | custom-call | tf_op jit(solution)/shard_map/pallas_call | solution.py:406
  3.2 0.0 copy-start
  3.2 10.0 %all-to-all-start = ((f32[32,2,128]{2,1,0:T(2,128)}), f32[32,2,128]{2,1,0:T(2,128)S(1)}, u32[]{:S(2)}, u32[]{:S(2)}) async-start(f32[32,2,128]{2,1,0:T(2,128)} %get-tuple-element.36), calls=%async_computation | async-start | bytes 65536 | tf_op jit(solution)/shard_map/all_to_all | solution.py:41
  13.1 3.3 %collective-permute-start = (bf16[2,2,8,128]{3,2,1,0:T(8,128)(2,1)}, bf16[2,2,8,128]{3,2,1,0:T(8,128)(2,1)S(1)}, u32[]{:S(2)}, u32[]{:S(2)}) collective-permute-start(bf16[2,2,8,128]{3,2,1,0:T(8,128)(2,1)} %get-tuple-element.37), channel_id=1, source_target_pairs={{0,1},{1,2},{2,3},{3,4},{4,5},{5,6},{6,7},{7,8},{8,9},{9,10},{10,1... | collective-permute-start | bytes 24584 | tf_op jit(solution)/shard_map/ppermute | solution.py:30
  16.5 1.9 %collective-permute-start.1 = (bf16[2,2,8,128]{3,2,1,0:T(8,128)(2,1)}, bf16[2,2,8,128]{3,2,1,0:T(8,128)(2,1)S(1)}, u32[]{:S(2)}, u32[]{:S(2)}) collective-permute-start(bf16[2,2,8,128]{3,2,1,0:T(8,128)(2,1)} %get-tuple-element.38), channel_id=1, source_target_pairs={{0,31},{1,0},{2,1},{3,2},{4,3},{5,4},{6,5},{7,6},{8,7},{9,8},{10,9... | collective-permute-start | bytes 24584 | tf_op jit(solution)/shard_map/ppermute | solution.py:30
  18.4 1.8 %all-to-all-done = f32[32,2,128]{2,1,0:T(2,128)S(1)} async-done(((f32[32,2,128]{2,1,0:T(2,128)}), f32[32,2,128]{2,1,0:T(2,128)S(1)}, u32[]{:S(2)}, u32[]{:S(2)}) %all-to-all-start) | async-done | bytes 32800 | tf_op jit(solution)/shard_map/all_to_all | solution.py:41
  20.3 0.1 fusion.6
  20.3 0.0 collective-permute-done.low
  20.3 1.3 %collective-permute-done.1.high = bf16[2,2,8,128]{3,2,1,0:T(8,128)(2,1)S(1)} collective-permute-done((bf16[2,2,8,128]{3,2,1,0:T(8,128)(2,1)}, bf16[2,2,8,128]{3,2,1,0:T(8,128)(2,1)S(1)}, u32[]{:S(2)}, u32[]{:S(2)}) %collective-permute-start.1) | collective-permute-done | bytes 8224 | tf_op jit(solution)/shard_map/ppermute | solution.py:30
  21.7 0.0 copy-done.1
  21.7 0.8 shard_map.146
  22.5 10.0 %all-to-all-start.1 = ((bf16[16,80,128]{2,1,0:T(8,128)(2,1)}), bf16[16,80,128]{2,1,0:T(8,128)(2,1)S(1)}, u32[]{:S(2)}, u32[]{:S(2)}) async-start(bf16[16,80,128]{2,1,0:T(8,128)(2,1)} %get-tuple-element.42), calls=%async_computation.1 | async-start | bytes 655360 | tf_op jit(solution)/shard_map/all_to_all | solution.py:41
  32.4 0.0 copy-start.8
  32.5 0.0 copy-start.9
  32.5 0.0 copy-start.10
  32.5 0.0 copy-done
  32.5 0.6 copy-done.8
  33.1 0.0 copy-done.9
  33.1 0.0 copy-done.10
  33.1 0.0 copy-start.7
  33.1 0.9 copy-done.7
  34.1 0.0 copy-start.2
  34.1 0.8 shard_map.147
  34.9 7.9 %all-to-all-done.1.slots = bf16[16,80,128]{2,1,0:T(8,128)(2,1)S(1)} async-done(((bf16[16,80,128]{2,1,0:T(8,128)(2,1)}), bf16[16,80,128]{2,1,0:T(8,128)(2,1)S(1)}, u32[]{:S(2)}, u32[]{:S(2)}) %all-to-all-start.1) | async-done | bytes 327712 | tf_op jit(solution)/shard_map/all_to_all | solution.py:41
  42.8 0.0 copy-done.2
  42.8 1.2 %shard_map.148 = (f32[4,128]{1,0:T(4,128)S(1)}, f32[2,256,128]{2,1,0:T(8,128)S(1)}, f32[2,256,128]{2,1,0:T(8,128)S(1)}, bf16[32,40,128]{2,1,0:T(8,128)(2,1)S(1)}) custom-call(bf16[16,80,128]{2,1,0:T(8,128)(2,1)S(1)} %all-to-all-done.1.slots, bf16[2,8,32,128]{3,2,1,0:T(8,128)(2,1)S(1)} %copy-done.2, f32[2,8,34,128]{3,2,1,0:T(8,128)S(1)} %get-tuple-element.44.wide, ...), custom_call_target="tpu_custom_call" | custom-call | tf_op jit(solution)/shard_map/pallas_call | solution.py:458
  44.0 0.0 copy-start.3
  44.0 0.0 copy-start.5
  44.0 2.4 %all-gather = bf16[64,40,128]{2,1,0:T(8,128)(2,1)S(1)} all-gather(bf16[32,40,128]{2,1,0:T(8,128)(2,1)S(1)} %get-tuple-element.50), channel_id=2, replica_groups=mesh['zh'=4,'x'=4,'zl'=2,'y'=8,'c'=2] {'c'}, dimensions={0}, use_global_device_ids=true | all-gather | bytes 983040 | tf_op jit(solution)/shard_map/all_gather | solution.py:475
  46.5 0.0 copy-done.3
  46.5 0.0 copy-done.5
  46.5 0.2 fusion.8
  46.7 0.2 fusion.1
  46.8 15.1 %all_to_all.25 = bf16[16,40,128]{2,1,0:T(8,128)(2,1)S(1)} all-to-all(bf16[16,40,128]{2,1,0:T(8,128)(2,1)S(1)} %fusion.1), channel_id=1, replica_groups=mesh['zh'=4,'x'=4,'zl'=2,'y'=8,'c'=2] {'zl','y'}, dimensions={0} | all-to-all | bytes 327680 | tf_op jit(solution)/shard_map/all_to_all | solution.py:41
  62.0 0.1 fusion.10
  62.1 0.1 fusion.3
  62.2 0.7 broadcast_in_dim.10
  62.8 6.6 %all-to-all-start.3 = ((bf16[16,40,128]{2,1,0:T(8,128)(2,1)}), bf16[16,40,128]{2,1,0:T(8,128)(2,1)S(1)}, u32[]{:S(2)}, u32[]{:S(2)}) async-start(bf16[16,40,128]{2,1,0:T(8,128)(2,1)} %broadcast_in_dim.10), calls=%async_computation.3 | async-start | bytes 327680 | tf_op jit(solution)/shard_map/all_to_all | solution.py:41
  69.5 5.2 %collective-permute-start.2 = (bf16[2,1,34,128]{3,2,1,0:T(8,128)(2,1)S(1)}, bf16[2,1,34,128]{3,2,1,0:T(8,128)(2,1)S(1)}, u32[]{:S(2)}, u32[]{:S(2)}) collective-permute-start(bf16[2,1,34,128]{3,2,1,0:T(8,128)(2,1)S(1)} %get-tuple-element.69), channel_id=1, source_target_pairs={{0,32},{32,64},{64,96},{96,128},{128,160},{160,192},{192,224},{224... | collective-permute-start | bytes 52232 | tf_op jit(solution)/shard_map/ppermute | solution.py:30
  74.7 1.9 %collective-permute-start.3 = (bf16[2,1,34,128]{3,2,1,0:T(8,128)(2,1)S(1)}, bf16[2,1,34,128]{3,2,1,0:T(8,128)(2,1)S(1)}, u32[]{:S(2)}, u32[]{:S(2)}) collective-permute-start(bf16[2,1,34,128]{3,2,1,0:T(8,128)(2,1)S(1)} %get-tuple-element.68), channel_id=1, source_target_pairs={{32,0},{64,32},{96,64},{128,96},{160,128},{192,160},{224,192},{256... | collective-permute-start | bytes 52232 | tf_op jit(solution)/shard_map/ppermute | solution.py:30
  76.6 0.0 all-to-all-done.3
  76.7 0.1 fusion.9
  76.7 0.1 fusion.5
  76.8 0.0 collective-permute-done.2
  76.8 6.6 %collective-permute-done.3 = bf16[2,1,34,128]{3,2,1,0:T(8,128)(2,1)S(1)} collective-permute-done((bf16[2,1,34,128]{3,2,1,0:T(8,128)(2,1)S(1)}, bf16[2,1,34,128]{3,2,1,0:T(8,128)(2,1)S(1)}, u32[]{:S(2)}, u32[]{:S(2)}) %collective-permute-start.3) | collective-permute-done | bytes 17440 | tf_op jit(solution)/shard_map/ppermute | solution.py:30
  83.4 0.7 broadcast_in_dim.22
  84.1 4.4 %all-to-all-start.4 = ((bf16[16,40,128]{2,1,0:T(8,128)(2,1)}), bf16[16,40,128]{2,1,0:T(8,128)(2,1)S(1)}, u32[]{:S(2)}, u32[]{:S(2)}) async-start(bf16[16,40,128]{2,1,0:T(8,128)(2,1)} %broadcast_in_dim.22), calls=%async_computation.4 | async-start | bytes 327680 | tf_op jit(solution)/shard_map/all_to_all | solution.py:41
  88.5 0.1 pad_maximum_fusion.padded
  88.6 0.0 copy-start.6
  88.6 1.3 %shard_map.149 = bf16[2,8,32,128]{3,2,1,0:T(8,128)(2,1)} custom-call(bf16[2,10,34,128]{3,2,1,0:T(8,128)(2,1)S(1)} %pad_maximum_fusion.padded, bf16[2,3,384,128]{3,2,1,0:T(8,128)(2,1)S(1)} %get-tuple-element.53.taps, f32[4,128]{1,0:T(4,128)S(1)} %get-tuple-element.54.stats, f32[1,128]{1,0:T(1,128)S(1)} %get-tuple-element.45.gamma, ...), custom_call_target="tpu_custom_call" | custom-call | tf_op jit(solution)/shard_map/pallas_call | solution.py:485
  89.9 0.0 copy-start.4
  89.9 6.1 %all-to-all-done.4 = bf16[16,40,128]{2,1,0:T(8,128)(2,1)S(1)} async-done(((bf16[16,40,128]{2,1,0:T(8,128)(2,1)}), bf16[16,40,128]{2,1,0:T(8,128)(2,1)S(1)}, u32[]{:S(2)}, u32[]{:S(2)}) %all-to-all-start.4) | async-done | bytes 163872 | tf_op jit(solution)/shard_map/all_to_all | solution.py:41
  96.0 5.9 %all-gather.1.gathered = bf16[32,40,128]{2,1,0:T(8,128)(2,1)S(1)} all-gather(bf16[16,40,128]{2,1,0:T(8,128)(2,1)S(1)} %all-to-all-done.4), channel_id=3, replica_groups=mesh['zh'=4,'x'=4,'zl'=2,'y'=8,'c'=2] {'c'}, dimensions={0}, use_global_device_ids=true | all-gather | bytes 491520 | tf_op jit(solution)/shard_map/all_gather | solution.py:483
  101.9 0.0 copy-done.6
  101.9 0.0 copy-done.4
  101.9 1.2 %shard_map.150 = (bf16[2,8,32,128]{3,2,1,0:T(8,128)(2,1)}, f32[9,128,128]{2,1,0:T(8,128)}, f32[512,128]{1,0:T(8,128)}, f32[1,128]{1,0:T(1,128)}, f32[1,128]{1,0:T(1,128)}) custom-call(bf16[32,40,128]{2,1,0:T(8,128)(2,1)S(1)} %all-gather.1.gathered, f32[4,128]{1,0:T(4,128)S(1)} %get-tuple-element.54.stats, f32[2,256,128]{2,1,0:T(8,128)S(1)} %copy-done.4, ...), custom_call_target="tpu_custom_call" | custom-call | tf_op jit(solution)/shard_map/pallas_call | solution.py:489
  (13 shorter events, 0.2 us)
Async XLA Ops:
  0.6 21.0 %copy-start.1 = (bf16[2,8,32,128]{3,2,1,0:T(8,128)(2,1)S(1)}, bf16[2,8,32,128]{3,2,1,0:T(8,128)(2,1)}, u32[]{:S(2)}) copy-start(bf16[2,8,32,128]{3,2,1,0:T(8,128)(2,1)} %cotangent.1) | copy-start | bytes 393220
  3.2 29.3 %copy-start = (f32[3,3,128,128]{3,2,1,0:T(8,128)S(1)}, f32[3,3,128,128]{3,2,1,0:T(8,128)}, u32[]{:S(2)}) copy-start(f32[3,3,128,128]{3,2,1,0:T(8,128)} %param.16) | copy-start | bytes 1769476
  3.2 17.0 %all-to-all-start = ((f32[32,2,128]{2,1,0:T(2,128)}), f32[32,2,128]{2,1,0:T(2,128)S(1)}, u32[]{:S(2)}, u32[]{:S(2)}) async-start(f32[32,2,128]{2,1,0:T(2,128)} %get-tuple-element.36), calls=%async_computation | async-start | bytes 65536 | tf_op jit(solution)/shard_map/all_to_all | solution.py:41
  13.1 7.2 %collective-permute-start = (bf16[2,2,8,128]{3,2,1,0:T(8,128)(2,1)}, bf16[2,2,8,128]{3,2,1,0:T(8,128)(2,1)S(1)}, u32[]{:S(2)}, u32[]{:S(2)}) collective-permute-start(bf16[2,2,8,128]{3,2,1,0:T(8,128)(2,1)} %get-tuple-element.37), channel_id=1, source_target_pairs={{0,1},{1,2},{2,3},{3,4},{4,5},{5,6},{6,7},{7,8},{8,9},{9,10},{10,1... | collective-permute-start | bytes 24584 | tf_op jit(solution)/shard_map/ppermute | solution.py:30
  16.5 5.2 %collective-permute-start.1 = (bf16[2,2,8,128]{3,2,1,0:T(8,128)(2,1)}, bf16[2,2,8,128]{3,2,1,0:T(8,128)(2,1)S(1)}, u32[]{:S(2)}, u32[]{:S(2)}) collective-permute-start(bf16[2,2,8,128]{3,2,1,0:T(8,128)(2,1)} %get-tuple-element.38), channel_id=1, source_target_pairs={{0,31},{1,0},{2,1},{3,2},{4,3},{5,4},{6,5},{7,6},{8,7},{9,8},{10,9... | collective-permute-start | bytes 24584 | tf_op jit(solution)/shard_map/ppermute | solution.py:30
  22.5 20.3 %all-to-all-start.1 = ((bf16[16,80,128]{2,1,0:T(8,128)(2,1)}), bf16[16,80,128]{2,1,0:T(8,128)(2,1)S(1)}, u32[]{:S(2)}, u32[]{:S(2)}) async-start(bf16[16,80,128]{2,1,0:T(8,128)(2,1)} %get-tuple-element.42), calls=%async_computation.1 | async-start | bytes 655360 | tf_op jit(solution)/shard_map/all_to_all | solution.py:41
  32.4 0.7 copy-start.8
  32.5 0.7 copy-start.9
  32.5 0.7 copy-start.10
  33.1 1.0 copy-start.7
  34.1 8.7 %copy-start.2 = (bf16[2,8,32,128]{3,2,1,0:T(8,128)(2,1)S(1)}, bf16[2,8,32,128]{3,2,1,0:T(8,128)(2,1)}, u32[]{:S(2)}) copy-start(bf16[2,8,32,128]{3,2,1,0:T(8,128)(2,1)} %get-tuple-element.43.mixed) | copy-start | bytes 393220
  44.0 2.5 %copy-start.3 = (f32[2,256,128]{2,1,0:T(8,128)}, f32[2,256,128]{2,1,0:T(8,128)S(1)}, u32[]{:S(2)}) copy-start(f32[2,256,128]{2,1,0:T(8,128)S(1)} %get-tuple-element.56.norm) | copy-start | bytes 786436
  44.0 2.5 %copy-start.5 = (f32[2,256,128]{2,1,0:T(8,128)}, f32[2,256,128]{2,1,0:T(8,128)S(1)}, u32[]{:S(2)}) copy-start(f32[2,256,128]{2,1,0:T(8,128)S(1)} %get-tuple-element.57.grad_pre) | copy-start | bytes 786436
  62.8 13.8 %all-to-all-start.3 = ((bf16[16,40,128]{2,1,0:T(8,128)(2,1)}), bf16[16,40,128]{2,1,0:T(8,128)(2,1)S(1)}, u32[]{:S(2)}, u32[]{:S(2)}) async-start(bf16[16,40,128]{2,1,0:T(8,128)(2,1)} %broadcast_in_dim.10), calls=%async_computation.3 | async-start | bytes 327680 | tf_op jit(solution)/shard_map/all_to_all | solution.py:41
  69.5 7.3 %collective-permute-start.2 = (bf16[2,1,34,128]{3,2,1,0:T(8,128)(2,1)S(1)}, bf16[2,1,34,128]{3,2,1,0:T(8,128)(2,1)S(1)}, u32[]{:S(2)}, u32[]{:S(2)}) collective-permute-start(bf16[2,1,34,128]{3,2,1,0:T(8,128)(2,1)S(1)} %get-tuple-element.69), channel_id=1, source_target_pairs={{0,32},{32,64},{64,96},{96,128},{128,160},{160,192},{192,224},{224... | collective-permute-start | bytes 52232 | tf_op jit(solution)/shard_map/ppermute | solution.py:30
  74.7 8.7 %collective-permute-start.3 = (bf16[2,1,34,128]{3,2,1,0:T(8,128)(2,1)S(1)}, bf16[2,1,34,128]{3,2,1,0:T(8,128)(2,1)S(1)}, u32[]{:S(2)}, u32[]{:S(2)}) collective-permute-start(bf16[2,1,34,128]{3,2,1,0:T(8,128)(2,1)S(1)} %get-tuple-element.68), channel_id=1, source_target_pairs={{32,0},{64,32},{96,64},{128,96},{160,128},{192,160},{224,192},{256... | collective-permute-start | bytes 52232 | tf_op jit(solution)/shard_map/ppermute | solution.py:30
  84.1 11.9 %all-to-all-start.4 = ((bf16[16,40,128]{2,1,0:T(8,128)(2,1)}), bf16[16,40,128]{2,1,0:T(8,128)(2,1)S(1)}, u32[]{:S(2)}, u32[]{:S(2)}) async-start(bf16[16,40,128]{2,1,0:T(8,128)(2,1)} %broadcast_in_dim.22), calls=%async_computation.4 | async-start | bytes 327680 | tf_op jit(solution)/shard_map/all_to_all | solution.py:41
  88.6 13.3 %copy-start.6 = (f32[2,256,128]{2,1,0:T(8,128)S(1)}, f32[2,256,128]{2,1,0:T(8,128)}, u32[]{:S(2)}) copy-start(f32[2,256,128]{2,1,0:T(8,128)} %copy-done.5) | copy-start | bytes 786436
  89.9 12.0 %copy-start.4 = (f32[2,256,128]{2,1,0:T(8,128)S(1)}, f32[2,256,128]{2,1,0:T(8,128)}, u32[]{:S(2)}) copy-start(f32[2,256,128]{2,1,0:T(8,128)} %copy-done.3) | copy-start | bytes 786436

commit v9 on v8

--- a/solution.py
+++ b/solution.py
@@ -30,22 +30,11 @@
     return lax.ppermute(block, axes, pairs)
 
 
-def extend(block, axes, dim, periodic):
-    last = block.shape[dim] - 1
-    low = shift(lax.slice_in_dim(block, last, last + 1, axis=dim), axes, 1, periodic)
-    high = shift(lax.slice_in_dim(block, 0, 1, axis=dim), axes, -1, periodic)
-    return jnp.concatenate([low, block, high], axis=dim)
-
-
 def exchange(block, axes):
     return lax.all_to_all(block, axes, 0, 0)
 
 
-def everyone(block, axes):
-    return exchange(jnp.broadcast_to(block[None], (lax.axis_size(axes),) + block.shape), axes)
-
-
-def call(body, outputs, scratch=(), room=48, **more):
+def call(body, outputs, scratch=(), room=24, **more):
     return pl.pallas_call(
         body,
         out_shape=outputs,
@@ -121,7 +110,7 @@
 
 
 def mix_body(
-    feats_in, cond_in, null_in, cot_in, flags_in, mixed_out, moments_out, first_out, last_out,
+    feats_in, cond_in, null_in, cot_in, flags_in, mixed_out, slots_out, edges_out,
     feats, cond, null, cot, flags, arrivals,
 ):
     fetch = fetcher(arrivals)
@@ -137,7 +126,7 @@
     cells = tile_rows * tile_cols
     size = cells * (channels // GROUPS)
     null32 = null[...].astype(F32)
-    means, spreads = [], []
+    means, spreads, firsts, lasts = [], [], [], []
     for sample in range(samples):
         for copy in field_copies[sample]:
             copy.wait()
@@ -147,31 +136,43 @@
         ).astype(BF16)
         mixed_out[sample] = mixed
         wide = mixed.astype(F32)
-        first_out[0, sample] = wide[:, 0, :].astype(BF16)
-        last_out[0, sample] = wide[:, tile_cols - 1, :].astype(BF16)
+        firsts.append(wide[:, 0, :])
+        lasts.append(wide[:, tile_cols - 1, :])
         wide = wide.reshape(cells, channels)
         mean = group_total(jnp.sum(wide, axis=0, keepdims=True)) * (1.0 / size)
         away = wide - mean
         means.append(mean)
         spreads.append(group_total(jnp.sum(away * away, axis=0, keepdims=True)))
-    moments = jnp.concatenate([weave(*means), weave(*spreads)], axis=0)
-    moments_out[...] = jnp.broadcast_to(moments[None], moments_out.shape)
+    spare = jnp.zeros((SLOT - 2 * samples * tile_rows, channels), F32)
+    edges_out[...] = jnp.concatenate(firsts + lasts + [spare], axis=0).astype(BF16)
+    rows = header(weave(*means), weave(*spreads))
     cot_copy.wait()
+    firsts, lasts = [], []
     for sample in range(samples):
         wide = cot[sample].astype(F32)
-        first_out[1, sample] = wide[:, 0, :].astype(BF16)
-        last_out[1, sample] = wide[:, tile_cols - 1, :].astype(BF16)
-
-
-def build_body(moments, low, high, cot, wide_out, slots_out, edge):
+        firsts.append(wide[:, 0, :])
+        lasts.append(wide[:, tile_cols - 1, :])
+    slots_out[...] = jnp.broadcast_to(
+        jnp.concatenate(rows + firsts, axis=0).astype(BF16)[None], slots_out.shape
+    )
+    after = lax.rem(place(LON) + 1, slots_out.shape[0])
+    slots_out[after] = jnp.concatenate(rows + lasts, axis=0).astype(BF16)
+
+
+def merge_body(count, slots, cot, wide_out, slots_out, edge):
     samples, tile_rows, tile_cols, channels = cot.shape
-    lat_count = slots_out.shape[0]
-    for sample in range(samples):
-        wide_out[sample, :, 0, :] = low[1, sample].astype(F32)
+    lon_count, lat_count = slots.shape[0], slots_out.shape[0]
+    mean, spread = merged(slots, count)
+    me = place(LON)
+    before = slots[lax.rem(me + lon_count - 1, lon_count)].astype(F32)
+    after = slots[lax.rem(me + 1, lon_count)].astype(F32)
+    for sample in range(samples):
+        here = slice(8 + sample * tile_rows, 8 + (sample + 1) * tile_rows)
+        wide_out[sample, :, 0, :] = before[here, :]
         wide_out[sample, :, 1 : 1 + tile_cols, :] = cot[sample].astype(F32)
-        wide_out[sample, :, 1 + tile_cols, :] = high[1, sample].astype(F32)
+        wide_out[sample, :, 1 + tile_cols, :] = after[here, :]
     edge[...] = jnp.zeros(edge.shape, F32)
-    edge[0:8, :] = jnp.concatenate(header(moments[0:1, :], moments[1:2, :]), axis=0)
+    edge[0:8, :] = jnp.concatenate(header(mean, spread), axis=0)
     span = tile_cols + 2
     for sample in range(samples):
         edge[8 + sample * span : 8 + (sample + 1) * span, :] = wide_out[sample, 0]
@@ -224,20 +225,21 @@
         shifted[:, tap * channels : (tap + 1) * channels] = moved.astype(BF16)
 
 
-def forward_body(padded, taps, stats, gamma, beta, block_out, spread, shifted):
-    samples, rows, cols = padded.shape[0], padded.shape[1] - 2, padded.shape[2] - 2
+def forward_body(wide, low, high, taps, stats, gamma, beta, block_out, spread, shifted):
+    samples, rows, cols = wide.shape[0], wide.shape[1], wide.shape[2] - 2
     size = rows * cols
     row = lax.broadcasted_iota(jnp.int32, spread.shape, 0) + place(LAT) * rows
     inside = (row > 0) & (row <= rows * lax.axis_size(LAT))
     for sample in range(samples):
-        mixed = padded[sample].astype(F32)
+        spread[0] = low[sample].astype(F32)
+        spread[1 : 1 + rows] = wide[sample]
+        spread[1 + rows] = high[sample].astype(F32)
         mean = stats[sample : sample + 1, :][None]
         inverse = stats[samples + sample : samples + sample + 1, :][None]
-        pre = (mixed - mean) * inverse * gamma[...][None] + beta[...][None]
-        act = jnp.where(inside, pre / (1.0 + jnp.exp(-pre)), 0.0)
-        spread[...] = act
+        pre = (spread[...] - mean) * inverse * gamma[...][None] + beta[...][None]
+        spread[...] = jnp.where(inside, pre / (1.0 + jnp.exp(-pre)), 0.0)
         windows(spread, shifted, rows, cols)
-        total = mixed[1 : 1 + rows, 1 : 1 + cols, :].reshape(size, -1)
+        total = wide[sample, :, 1 : 1 + cols, :].reshape(size, -1)
         for row_tap in range(3):
             window = shifted[row_tap * cols : row_tap * cols + size, :]
             total = total + jnp.dot(window, taps[sample, row_tap], preferred_element_type=F32)
@@ -245,7 +247,7 @@
 
 
 def sums_body(
-    count, cells, slots, mixed, wide, gamma, beta, back_taps, column, demod, weight,
+    count, cells, slots, mixed, edges, wide, gamma, beta, back_taps, column, demod, weight,
     stats_out, norm_out, grad_out, payload_out, edge, spread, shifted, total,
 ):
     samples, rows, cols, channels = mixed.shape
@@ -300,6 +302,7 @@
         sums[1].append(jnp.sum((product * demod_row).T, axis=0, keepdims=True))
         sums[2].append(jnp.sum(grad_pre * norm, axis=0, keepdims=True))
         sums[3].append(jnp.sum(grad_pre, axis=0, keepdims=True))
+    payload_out[SHARDS] = edges[...]
     small = jnp.concatenate(sum(sums, []), axis=0)
     lane = lanes_of(TILE)
     sub = lax.broadcasted_iota(jnp.int32, (TILE, channels), 0)
@@ -326,12 +329,51 @@
 
 
 def resplit(slots):
-    row = lax.broadcasted_iota(jnp.int32, slots.shape, slots.ndim - 2)
-    lane = lax.broadcasted_iota(jnp.int32, slots.shape, slots.ndim - 1)
-    joined = slots + jnp.roll(slots, 64, slots.ndim - 1)
-    high = lax.reduce_precision(joined, 8, 7)
-    terms = jnp.where(lane < 64, high, joined - high)
-    return jnp.where(row == 36, terms, slots).astype(BF16)
+    main, tail = slots[:, 0:32, :], slots[:, 32:SLOT, :]
+    flat = tail.reshape(-1, LANES)
+    lane = lax.broadcasted_iota(jnp.int32, flat.shape, 1)
+    row = lax.broadcasted_iota(jnp.int32, flat.shape, 0) & 7
+    terms = split_terms(flat + pltpu.roll(flat, 64, 1), lane)
+    tail = jnp.where(row == 4, terms, flat).reshape(tail.shape)
+    return jnp.concatenate([main, tail], axis=1)
+
+
+def core_body(gathered, slots_out, other_out):
+    core, near_count = place(("c",)), slots_out.shape[0]
+    mine = pl.ds(core * near_count, near_count)
+    total = gathered[0, mine].astype(F32) + gathered[1, mine].astype(F32)
+    other = gathered[1 - core, SHARDS]
+    other_out[...] = other
+    other = other.astype(F32)
+    half = slots_out.shape[1] - SLOT
+    passed = jnp.where(core == 0, other[half : 2 * half, :], other[0:half, :])
+    passed = jnp.broadcast_to(passed[None], (near_count,) + passed.shape)
+    slots_out[...] = jnp.concatenate([resplit(total), passed], axis=1).astype(BF16)
+
+
+def near_body(slots, other, mixed, slots_out, wide_out, top_out, bottom_out):
+    samples, rows, cols, _ = mixed.shape
+    count, half = slots.shape[0], samples * rows
+    core, near = place(("c",)), place(NEAR)
+    total = jnp.sum(slots[:, 0:SLOT, :].astype(F32), axis=0)
+    slots_out[...] = jnp.broadcast_to(resplit(total[None]).astype(BF16), slots_out.shape)
+    apart = lax.rem(jnp.where(core == 0, near + count - 1, near + 1), count)
+    passed = slots[apart].astype(F32)[SLOT : SLOT + half, :]
+    mate = other[...].astype(F32)
+    low = jnp.where(core == 0, passed, mate[half : 2 * half, :])
+    high = jnp.where(core == 0, mate[0:half, :], passed)
+    for sample in range(samples):
+        here = slice(sample * rows, (sample + 1) * rows)
+        wide_out[sample, :, 0, :] = low[here, :]
+        wide_out[sample, :, 1 : 1 + cols, :] = mixed[sample].astype(F32)
+        wide_out[sample, :, 1 + cols, :] = high[here, :]
+        top_out[sample] = wide_out[sample, 0].astype(BF16)
+        bottom_out[sample] = wide_out[sample, rows - 1].astype(BF16)
+
+
+def lat_body(slots, slots_out):
+    total = jnp.sum(slots[...].astype(F32), axis=0)
+    slots_out[...] = jnp.broadcast_to(resplit(total[None]).astype(BF16), slots_out.shape)
 
 
 def last_body(
@@ -402,10 +444,14 @@
     taps = conv_weight.reshape(9, channels, channels)
 
     lat_slot = -(-(8 + samples * (tile_cols + 2)) // 16) * 16
-    edges = array((2, samples, tile_rows, channels), BF16)
-    mixed, moments, first, last = call(
+    lon_slot = 8 + samples * tile_rows
+    mixed, slots, edges = call(
         mix_body,
-        (array(feats.shape, BF16), array((lon_count, 2, LANES)), edges, edges),
+        (
+            array(feats.shape, BF16),
+            array((lon_count, lon_slot, LANES), BF16),
+            array((SLOT, LANES), BF16),
+        ),
         (
             pltpu.VMEM(feats.shape, BF16),
             pltpu.VMEM(feats.shape, BF16),
@@ -417,25 +463,16 @@
         room=60,
         in_specs=[pl.BlockSpec(memory_space=pl.ANY)] * 5,
     )(feats, cond, null_field, cotangent, drop_flags)
-    rows = exchange(moments, LON)
-    low, high = shift(last, LON, 1, True), shift(first, LON, -1, True)
-    mean = jnp.mean(rows[:, :1], axis=0)
-    away = rows[:, :1] - mean
-    moments = jnp.concatenate(
-        [mean, jnp.sum(rows[:, 1:] + cells_local * (away * away), axis=0)], axis=0
-    )
-    moments, low, high = lax.optimization_barrier((moments, low, high))
+    slots = exchange(slots, LON)
     wide_cot, slots = call(
-        build_body,
+        functools.partial(merge_body, cells_local),
         (
             array((samples, tile_rows, tile_cols + 2, channels)),
             array((lat_count, lat_slot, LANES), BF16),
         ),
         (pltpu.VMEM((lat_slot, LANES), F32),),
-    )(moments, low, high, cotangent)
+    )(slots, cotangent)
     slots = exchange(slots, LAT)
-    padded = jnp.concatenate([low[0][:, :, None], mixed, high[0][:, :, None]], axis=2)
-    low, high = shift(padded[:, -1:], LAT, 1, False), shift(padded[:, :1], LAT, -1, False)
 
     taps_shape = (samples, 3, 3 * channels, channels)
     gamma, beta, style, column, demod, power, emb_full, back_taps, fore_taps = call(
@@ -461,7 +498,7 @@
             array((2 * samples, LANES)),
             array(flat),
             array(flat),
-            array((SHARDS, SLOT, LANES), BF16),
+            array((SHARDS + 1, SLOT, LANES), BF16),
         ),
         (
             pltpu.VMEM((2, lat_slot, LANES), F32),
@@ -469,21 +506,30 @@
             shifted,
             pltpu.VMEM((9 * channels, channels), F32),
         ),
-    )(slots, mixed, wide_cot, gamma, beta, back_taps, column, demod, taps)
-
-    core_count, near_count = lax.axis_size("c"), lax.axis_size(NEAR)
-    payload = lax.all_gather(payload, "c")
-    payload = payload.reshape(core_count, core_count, near_count, SLOT, LANES)
-    payload = lax.dynamic_index_in_dim(payload, lax.axis_index("c"), 1, False)
-    payload = resplit(jnp.sum(payload.astype(F32), axis=0))
-    payload = resplit(jnp.sum(exchange(payload, NEAR).astype(F32), axis=0))
-    payload = resplit(jnp.sum(everyone(payload, LAT).astype(F32), axis=0))
-    payload, low, high = lax.optimization_barrier((payload, low, high))
-    padded = jnp.concatenate([low, padded, high], axis=1)
-    payload = lax.all_gather(everyone(payload, NEAR), "c")
-
+    )(slots, mixed, edges, wide_cot, gamma, beta, back_taps, column, demod, taps)
+
+    near_count = lax.axis_size(NEAR)
+    half = samples * tile_rows
+    slots, other = call(
+        core_body,
+        (array((near_count, SLOT + half, LANES), BF16), array((SLOT, LANES), BF16)),
+    )(lax.all_gather(payload, "c"))
+    border = array((samples, tile_cols + 2, channels), BF16)
+    slots, wide_mixed, top, bottom = call(
+        near_body,
+        (
+            array((lat_count, SLOT, LANES), BF16),
+            array((samples, tile_rows, tile_cols + 2, channels)),
+            border,
+            border,
+        ),
+    )(exchange(slots, NEAR), other, mixed)
+    low, high = shift(bottom, LAT, 1, False), shift(top, LAT, -1, False)
+    slots = call(lat_body, array((near_count, SLOT, LANES), BF16))(exchange(slots, LAT))
+    slots, low, high = lax.optimization_barrier((slots, low, high))
+    payload = lax.all_gather(exchange(slots, NEAR), "c")
     block_out = call(forward_body, array(feats.shape, BF16), (spread, shifted))(
-        padded, fore_taps, stats, gamma, beta
+        wide_mixed, low, high, fore_taps, stats, gamma, beta
     )
 
     grad_feats, grad_weight, grad_style, grad_gamma, grad_beta = call(

time: 104 us -> 103 us (level)
  blocking collectives: 23.5 us -> 44.9 us
  starting transfers between devices: 43.3 us -> 28.2 us
  waiting for transfers between devices: 23.7 us -> 17.2 us
  Pallas kernels: 7.77 us -> 9.45 us
    all_to_all x1 -> x2, blocking collectives: 15.1 us -> 31.9 us  [exchange(): return lax.all_to_all(block, axes, 0, 0)]
    all_to_all x4 -> x3, starting transfers between devices: 30.9 us -> 21 us  [exchange(): return lax.all_to_all(block, axes, 0, 0)]
    ppermute x4 -> x2, starting transfers between devices: 12.4 us -> 7.11 us  [shift(): return lax.ppermute(block, axes, pairs)]
    all_to_all x4 -> x3, waiting for transfers between devices: 15.8 us -> 11.1 us  [exchange(): return lax.all_to_all(block, axes, 0, 0)]
    all_gather x2, blocking collectives: 8.38 us -> 13 us  [the longest x1 7 us: on_device(): lax.all_gather(payload, 'c')]
    ppermute x4 -> x2, waiting for transfers between devices: 7.94 us -> 6.03 us  [shift(): return lax.ppermute(block, axes, pairs)]
    pallas_call x2 -> x5, Pallas kernels: 3.3 us -> 5.02 us  [the longest x1 2.52 us: on_device(): call(mix_body, (array(feats.shape, BF16), array((lon_count, lon_slot, LAN...]
    broadcast_in_dim x2 -> x0, local copies, waits for them, and re-layouts: 1.35 us -> none  [everyone(): jnp.broadcast_to(block[None], (lax.axis_size(axes),) + block.shape)]
  transfers between devices with their start and end apart: 8 -> 5, of which waited for: 5 -> 3; matrix products, arithmetic and copies ran while one was open for 0% -> 0% of each run, Pallas kernels for 2% -> 3%
where the time goes in v9:
time: 103 us
  blocking collectives  44.9 us (44%)
  starting transfers between devices  28.2 us (27%)
  waiting for transfers between devices  17.2 us (17%)
  Pallas kernels  9.45 us (9%)
  local copies, waits for them, and re-layouts  2.34 us (2%)
    all_to_all x2, blocking collectives, exchange(): return lax.all_to_all(block, axes, 0, 0)  31.9 us
    all_to_all x3, starting transfers between devices, exchange(): return lax.all_to_all(block, axes, 0, 0)  21 us
    all_to_all x3, waiting for transfers between devices, exchange(): return lax.all_to_all(block, axes, 0, 0)  11.1 us
    ppermute x2, starting transfers between devices, shift(): return lax.ppermute(block, axes, pairs)  7.11 us
    all_gather x1, blocking collectives, on_device(): lax.all_gather(payload, 'c')  7 us
    ppermute x2, waiting for transfers between devices, shift(): return lax.ppermute(block, axes, pairs)  6.03 us
    all_gather x1, blocking collectives, on_device(): payload = lax.all_gather(exchange(slots, NEAR), 'c')  6 us
    pallas_call x1, Pallas kernels, on_device(): call(mix_body, (array(feats.shape, BF16), array((lon_count, lon_slot, LAN...  2.52 us
  transfers between devices with their start and end apart: 5, of which 3 were waited for; matrix products, arithmetic and copies ran while one was open for 0% of the time, Pallas kernels for 3%

profile of v9, /device:TPU:143, one launch (start us, length us, event | category | flops | bytes accessed | tf_op | source)
XLA Modules:
  0.0 102.8 jit_solution(7286927805590236321)
XLA Ops:
  0.6 2.5 %shard_map.145 = (bf16[2,8,32,128]{3,2,1,0:T(8,128)(2,1)}, bf16[32,24,128]{2,1,0:T(8,128)(2,1)}, bf16[40,128]{1,0:T(8,128)(2,1)}) custom-call(bf16[2,8,32,128]{3,2,1,0:T(8,128)(2,1)} %feats_in.1, bf16[2,8,32,128]{3,2,1,0:T(8,128)(2,1)} %cond_in.1, bf16[8,32,128]{2,1,0:T(8,128)(2,1)} %null_in.1, bf16[2,8,32,128]{3,2,1,0:T(8,128)(2,1)} %cotangent.1, ...), custom_call_target="tpu_custom_call" | custom-call | tf_op jit(solution)/shard_map/pallas_call | solution.py:448
  3.2 0.0 copy-start.1
  3.2 19.4 %all_to_all.25.slots = bf16[32,24,128]{2,1,0:T(8,128)(2,1)S(1)} all-to-all(bf16[32,24,128]{2,1,0:T(8,128)(2,1)} %get-tuple-element.38), channel_id=1, replica_groups=mesh['zh'=4,'x'=4,'zl'=2,'y'=8,'c'=2] {'zl','y','c'}, dimensions={0} | all-to-all | bytes 393216 | tf_op jit(solution)/shard_map/all_to_all | solution.py:34
  22.6 0.0 copy-done.1
  22.6 0.0 copy-start
  22.6 0.8 shard_map.146
  23.5 10.0 %all-to-all-start.1 = ((bf16[16,80,128]{2,1,0:T(8,128)(2,1)}), bf16[16,80,128]{2,1,0:T(8,128)(2,1)S(1)}, u32[]{:S(2)}, u32[]{:S(2)}) async-start(bf16[16,80,128]{2,1,0:T(8,128)(2,1)} %get-tuple-element.39), calls=%async_computation.1 | async-start | bytes 655360 | tf_op jit(solution)/shard_map/all_to_all | solution.py:34
  33.5 0.0 copy-start.9
  33.5 0.0 copy-start.10
  33.5 0.0 copy-start.11
  33.5 0.0 copy-done
  33.5 0.6 copy-done.9
  34.1 0.0 copy-done.10
  34.1 0.0 copy-done.11
  34.1 0.0 copy-start.7
  34.1 0.9 copy-done.7
  35.1 0.0 copy-start.2
  35.1 0.8 shard_map.147
  35.9 0.0 copy-start.8
  35.9 4.9 %all-to-all-done.1.slots = bf16[16,80,128]{2,1,0:T(8,128)(2,1)S(1)} async-done(((bf16[16,80,128]{2,1,0:T(8,128)(2,1)}), bf16[16,80,128]{2,1,0:T(8,128)(2,1)S(1)}, u32[]{:S(2)}, u32[]{:S(2)}) %all-to-all-start.1) | async-done | bytes 327712 | tf_op jit(solution)/shard_map/all_to_all | solution.py:34
  40.8 0.0 copy-done.2
  40.8 0.0 copy-done.8
  40.8 1.2 %shard_map.148 = (f32[4,128]{1,0:T(4,128)S(1)}, f32[2,256,128]{2,1,0:T(8,128)S(1)}, f32[2,256,128]{2,1,0:T(8,128)S(1)}, bf16[33,40,128]{2,1,0:T(8,128)(2,1)S(1)}) custom-call(bf16[16,80,128]{2,1,0:T(8,128)(2,1)S(1)} %all-to-all-done.1.slots, bf16[2,8,32,128]{3,2,1,0:T(8,128)(2,1)S(1)} %copy-done.2, bf16[40,128]{1,0:T(8,128)(2,1)S(1)} %copy-done.8, ...), custom_call_target="tpu_custom_call" | custom-call | tf_op jit(solution)/shard_map/pallas_call | solution.py:495
  42.0 0.0 copy-start.5
  42.0 0.7 copy-done.5
  42.7 0.0 copy-start.3
  42.7 7.0 %all-gather = bf16[66,40,128]{2,1,0:T(8,128)(2,1)S(1)} all-gather(bf16[33,40,128]{2,1,0:T(8,128)(2,1)S(1)} %get-tuple-element.48), channel_id=2, replica_groups=mesh['zh'=4,'x'=4,'zl'=2,'y'=8,'c'=2] {'c'}, dimensions={0}, use_global_device_ids=true | all-gather | bytes 1013760 | tf_op jit(solution)/shard_map/all_gather | solution.py:516
  49.7 0.0 copy-done.3
  49.7 0.1 shard_map.149
  49.8 12.4 %all_to_all.26.slots = bf16[16,56,128]{2,1,0:T(8,128)(2,1)S(1)} all-to-all(bf16[16,56,128]{2,1,0:T(8,128)(2,1)S(1)} %get-tuple-element.49), channel_id=1, replica_groups=mesh['zh'=4,'x'=4,'zl'=2,'y'=8,'c'=2] {'zl','y'}, dimensions={0} | all-to-all | bytes 458752 | tf_op jit(solution)/shard_map/all_to_all | solution.py:34
  62.3 0.8 shard_map.150
  63.1 6.2 %all-to-all-start.3 = ((bf16[16,40,128]{2,1,0:T(8,128)(2,1)}), bf16[16,40,128]{2,1,0:T(8,128)(2,1)S(1)}, u32[]{:S(2)}, u32[]{:S(2)}) async-start(bf16[16,40,128]{2,1,0:T(8,128)(2,1)} %get-tuple-element.52), calls=%async_computation.3 | async-start | bytes 327680 | tf_op jit(solution)/shard_map/all_to_all | solution.py:34
  69.3 5.2 %collective-permute-start = (bf16[2,34,128]{2,1,0:T(8,128)(2,1)S(1)}, bf16[2,34,128]{2,1,0:T(8,128)(2,1)S(1)}, u32[]{:S(2)}, u32[]{:S(2)}) collective-permute-start(bf16[2,34,128]{2,1,0:T(8,128)(2,1)S(1)} %get-tuple-element.53), channel_id=1, source_target_pairs={{0,32},{32,64},{64,96},{96,128},{128,160},{160,192},{192,224},{224... | collective-permute-start | bytes 52232 | tf_op jit(solution)/shard_map/ppermute | solution.py:30
  74.5 1.9 %collective-permute-start.1 = (bf16[2,34,128]{2,1,0:T(8,128)(2,1)S(1)}, bf16[2,34,128]{2,1,0:T(8,128)(2,1)S(1)}, u32[]{:S(2)}, u32[]{:S(2)}) collective-permute-start(bf16[2,34,128]{2,1,0:T(8,128)(2,1)S(1)} %get-tuple-element.54), channel_id=1, source_target_pairs={{32,0},{64,32},{96,64},{128,96},{160,128},{192,160},{224,192},{256... | collective-permute-start | bytes 52232 | tf_op jit(solution)/shard_map/ppermute | solution.py:30
  76.4 0.0 all-to-all-done.3.slots
  76.4 0.8 shard_map.151
  77.2 0.0 collective-permute-done.low
  77.2 6.0 %collective-permute-done.1.high = bf16[2,34,128]{2,1,0:T(8,128)(2,1)S(1)} collective-permute-done((bf16[2,34,128]{2,1,0:T(8,128)(2,1)S(1)}, bf16[2,34,128]{2,1,0:T(8,128)(2,1)S(1)}, u32[]{:S(2)}, u32[]{:S(2)}) %collective-permute-start.1) | collective-permute-done | bytes 17440 | tf_op jit(solution)/shard_map/ppermute | solution.py:30
  83.3 4.8 %all-to-all-start.4 = ((bf16[16,40,128]{2,1,0:T(8,128)(2,1)}), bf16[16,40,128]{2,1,0:T(8,128)(2,1)S(1)}, u32[]{:S(2)}, u32[]{:S(2)}) async-start(bf16[16,40,128]{2,1,0:T(8,128)(2,1)} %shard_map.151), calls=%async_computation.4 | async-start | bytes 327680 | tf_op jit(solution)/shard_map/all_to_all | solution.py:34
  88.1 0.0 copy-start.6
  88.1 1.2 %shard_map.152 = bf16[2,8,32,128]{3,2,1,0:T(8,128)(2,1)} custom-call(f32[2,8,34,128]{3,2,1,0:T(8,128)S(1)} %get-tuple-element.51.wide, bf16[2,34,128]{2,1,0:T(8,128)(2,1)S(1)} %collective-permute-done.low, bf16[2,34,128]{2,1,0:T(8,128)(2,1)S(1)} %collective-permute-done.1.high, bf16[2,3,384,128]{3,2,1,0:T(8,128)(2,1)S(1)} %get-tuple-element.57.taps, ...), custom_call_target="tpu_custom_call" | custom-call | tf_op jit(solution)/shard_map/pallas_call | solution.py:531
  89.3 0.0 copy-start.4
  89.3 6.2 %all-to-all-done.4 = bf16[16,40,128]{2,1,0:T(8,128)(2,1)S(1)} async-done(((bf16[16,40,128]{2,1,0:T(8,128)(2,1)}), bf16[16,40,128]{2,1,0:T(8,128)(2,1)S(1)}, u32[]{:S(2)}, u32[]{:S(2)}) %all-to-all-start.4) | async-done | bytes 163872 | tf_op jit(solution)/shard_map/all_to_all | solution.py:34
  95.5 6.0 %all-gather.1.gathered = bf16[32,40,128]{2,1,0:T(8,128)(2,1)S(1)} all-gather(bf16[16,40,128]{2,1,0:T(8,128)(2,1)S(1)} %all-to-all-done.4), channel_id=3, replica_groups=mesh['zh'=4,'x'=4,'zl'=2,'y'=8,'c'=2] {'c'}, dimensions={0}, use_global_device_ids=true | all-gather | bytes 491520 | tf_op jit(solution)/shard_map/all_gather | solution.py:530
  101.5 0.0 copy-done.6
  101.5 0.0 copy-done.4
  101.5 1.2 %shard_map.153 = (bf16[2,8,32,128]{3,2,1,0:T(8,128)(2,1)}, f32[9,128,128]{2,1,0:T(8,128)}, f32[512,128]{1,0:T(8,128)}, f32[1,128]{1,0:T(1,128)}, f32[1,128]{1,0:T(1,128)}) custom-call(bf16[32,40,128]{2,1,0:T(8,128)(2,1)S(1)} %all-gather.1.gathered, f32[4,128]{1,0:T(4,128)S(1)} %get-tuple-element.58.stats, f32[2,256,128]{2,1,0:T(8,128)S(1)} %copy-done.4, ...), custom_call_target="tpu_custom_call" | custom-call | tf_op jit(solution)/shard_map/pallas_call | solution.py:535
Async XLA Ops:
  3.2 19.5 %copy-start.1 = (bf16[2,8,32,128]{3,2,1,0:T(8,128)(2,1)S(1)}, bf16[2,8,32,128]{3,2,1,0:T(8,128)(2,1)}, u32[]{:S(2)}) copy-start(bf16[2,8,32,128]{3,2,1,0:T(8,128)(2,1)} %cotangent.1) | copy-start | bytes 393220
  22.6 10.9 %copy-start = (f32[3,3,128,128]{3,2,1,0:T(8,128)S(1)}, f32[3,3,128,128]{3,2,1,0:T(8,128)}, u32[]{:S(2)}) copy-start(f32[3,3,128,128]{3,2,1,0:T(8,128)} %param.16) | copy-start | bytes 1769476
  23.5 17.4 %all-to-all-start.1 = ((bf16[16,80,128]{2,1,0:T(8,128)(2,1)}), bf16[16,80,128]{2,1,0:T(8,128)(2,1)S(1)}, u32[]{:S(2)}, u32[]{:S(2)}) async-start(bf16[16,80,128]{2,1,0:T(8,128)(2,1)} %get-tuple-element.39), calls=%async_computation.1 | async-start | bytes 655360 | tf_op jit(solution)/shard_map/all_to_all | solution.py:34
  33.5 0.7 copy-start.9
  33.5 0.7 copy-start.10
  33.5 0.7 copy-start.11
  34.1 1.0 copy-start.7
  35.1 5.7 %copy-start.2 = (bf16[2,8,32,128]{3,2,1,0:T(8,128)(2,1)S(1)}, bf16[2,8,32,128]{3,2,1,0:T(8,128)(2,1)}, u32[]{:S(2)}) copy-start(bf16[2,8,32,128]{3,2,1,0:T(8,128)(2,1)} %get-tuple-element.40.mixed) | copy-start | bytes 393220
  35.9 5.0 %copy-start.8 = (bf16[40,128]{1,0:T(8,128)(2,1)S(1)}, bf16[40,128]{1,0:T(8,128)(2,1)}, u32[]{:S(2)}) copy-start(bf16[40,128]{1,0:T(8,128)(2,1)} %get-tuple-element.41.edges) | copy-start | bytes 30724
  42.0 0.7 copy-start.5
  42.7 7.0 %copy-start.3 = (f32[2,256,128]{2,1,0:T(8,128)}, f32[2,256,128]{2,1,0:T(8,128)S(1)}, u32[]{:S(2)}) copy-start(f32[2,256,128]{2,1,0:T(8,128)S(1)} %get-tuple-element.60.norm) | copy-start | bytes 786436
  63.1 13.4 %all-to-all-start.3 = ((bf16[16,40,128]{2,1,0:T(8,128)(2,1)}), bf16[16,40,128]{2,1,0:T(8,128)(2,1)S(1)}, u32[]{:S(2)}, u32[]{:S(2)}) async-start(bf16[16,40,128]{2,1,0:T(8,128)(2,1)} %get-tuple-element.52), calls=%async_computation.3 | async-start | bytes 327680 | tf_op jit(solution)/shard_map/all_to_all | solution.py:34
  69.3 7.9 %collective-permute-start = (bf16[2,34,128]{2,1,0:T(8,128)(2,1)S(1)}, bf16[2,34,128]{2,1,0:T(8,128)(2,1)S(1)}, u32[]{:S(2)}, u32[]{:S(2)}) collective-permute-start(bf16[2,34,128]{2,1,0:T(8,128)(2,1)S(1)} %get-tuple-element.53), channel_id=1, source_target_pairs={{0,32},{32,64},{64,96},{96,128},{128,160},{160,192},{192,224},{224... | collective-permute-start | bytes 52232 | tf_op jit(solution)/shard_map/ppermute | solution.py:30
  74.5 8.7 %collective-permute-start.1 = (bf16[2,34,128]{2,1,0:T(8,128)(2,1)S(1)}, bf16[2,34,128]{2,1,0:T(8,128)(2,1)S(1)}, u32[]{:S(2)}, u32[]{:S(2)}) collective-permute-start(bf16[2,34,128]{2,1,0:T(8,128)(2,1)S(1)} %get-tuple-element.54), channel_id=1, source_target_pairs={{32,0},{64,32},{96,64},{128,96},{160,128},{192,160},{224,192},{256... | collective-permute-start | bytes 52232 | tf_op jit(solution)/shard_map/ppermute | solution.py:30
  83.3 12.3 %all-to-all-start.4 = ((bf16[16,40,128]{2,1,0:T(8,128)(2,1)}), bf16[16,40,128]{2,1,0:T(8,128)(2,1)S(1)}, u32[]{:S(2)}, u32[]{:S(2)}) async-start(bf16[16,40,128]{2,1,0:T(8,128)(2,1)} %shard_map.151), calls=%async_computation.4 | async-start | bytes 327680 | tf_op jit(solution)/shard_map/all_to_all | solution.py:34
  88.1 13.4 %copy-start.6 = (f32[2,256,128]{2,1,0:T(8,128)S(1)}, f32[2,256,128]{2,1,0:T(8,128)}, u32[]{:S(2)}) copy-start(f32[2,256,128]{2,1,0:T(8,128)} %copy-done.5) | copy-start | bytes 786436
  89.3 12.2 %copy-start.4 = (f32[2,256,128]{2,1,0:T(8,128)S(1)}, f32[2,256,128]{2,1,0:T(8,128)}, u32[]{:S(2)}) copy-start(f32[2,256,128]{2,1,0:T(8,128)} %copy-done.3) | copy-start | bytes 786436

commit v10 on v9

--- a/solution.py
+++ b/solution.py
@@ -110,7 +110,7 @@
 
 
 def mix_body(
-    feats_in, cond_in, null_in, cot_in, flags_in, mixed_out, slots_out, edges_out,
+    feats_in, cond_in, null_in, cot_in, flags_in, mixed_out, slots_out, top_out, bottom_out,
     feats, cond, null, cot, flags, arrivals,
 ):
     fetch = fetcher(arrivals)
@@ -126,7 +126,7 @@
     cells = tile_rows * tile_cols
     size = cells * (channels // GROUPS)
     null32 = null[...].astype(F32)
-    means, spreads, firsts, lasts = [], [], [], []
+    means, spreads = [], []
     for sample in range(samples):
         for copy in field_copies[sample]:
             copy.wait()
@@ -135,20 +135,19 @@
             feats[sample].astype(F32) + dropped * null32 + (1.0 - dropped) * cond[sample].astype(F32)
         ).astype(BF16)
         mixed_out[sample] = mixed
-        wide = mixed.astype(F32)
-        firsts.append(wide[:, 0, :])
-        lasts.append(wide[:, tile_cols - 1, :])
-        wide = wide.reshape(cells, channels)
+        top_out[0, sample] = mixed[0]
+        bottom_out[0, sample] = mixed[tile_rows - 1]
+        wide = mixed.astype(F32).reshape(cells, channels)
         mean = group_total(jnp.sum(wide, axis=0, keepdims=True)) * (1.0 / size)
         away = wide - mean
         means.append(mean)
         spreads.append(group_total(jnp.sum(away * away, axis=0, keepdims=True)))
-    spare = jnp.zeros((SLOT - 2 * samples * tile_rows, channels), F32)
-    edges_out[...] = jnp.concatenate(firsts + lasts + [spare], axis=0).astype(BF16)
     rows = header(weave(*means), weave(*spreads))
     cot_copy.wait()
     firsts, lasts = [], []
     for sample in range(samples):
+        top_out[1, sample] = cot[sample, 0]
+        bottom_out[1, sample] = cot[sample, tile_rows - 1]
         wide = cot[sample].astype(F32)
         firsts.append(wide[:, 0, :])
         lasts.append(wide[:, tile_cols - 1, :])
@@ -159,7 +158,7 @@
     slots_out[after] = jnp.concatenate(rows + lasts, axis=0).astype(BF16)
 
 
-def merge_body(count, slots, cot, wide_out, slots_out, edge):
+def merge_body(count, slots, cot, wide_out, slots_out):
     samples, tile_rows, tile_cols, channels = cot.shape
     lon_count, lat_count = slots.shape[0], slots_out.shape[0]
     mean, spread = merged(slots, count)
@@ -171,19 +170,41 @@
         wide_out[sample, :, 0, :] = before[here, :]
         wide_out[sample, :, 1 : 1 + tile_cols, :] = cot[sample].astype(F32)
         wide_out[sample, :, 1 + tile_cols, :] = after[here, :]
-    edge[...] = jnp.zeros(edge.shape, F32)
-    edge[0:8, :] = jnp.concatenate(header(mean, spread), axis=0)
-    span = tile_cols + 2
-    for sample in range(samples):
-        edge[8 + sample * span : 8 + (sample + 1) * span, :] = wide_out[sample, 0]
-    slots_out[...] = jnp.broadcast_to(edge[...].astype(BF16)[None], slots_out.shape)
-    for sample in range(samples):
-        edge[8 + sample * span : 8 + (sample + 1) * span, :] = wide_out[sample, tile_rows - 1]
+    rows = header(mean, spread)
+
+    def slot(row):
+        corners = [
+            wide_out[sample, row, side : side + 1, :]
+            for sample in range(samples)
+            for side in (0, 1 + tile_cols)
+        ]
+        spare = jnp.zeros((slots_out.shape[1] - 8 - len(corners), channels), F32)
+        return jnp.concatenate(rows + corners + [spare], axis=0).astype(BF16)
+
+    slots_out[...] = jnp.broadcast_to(slot(0)[None], slots_out.shape)
     row = place(LAT)
 
     @pl.when(row < lat_count - 1)
     def _():
-        slots_out[row + 1] = edge[...].astype(BF16)
+        slots_out[row + 1] = slot(tile_rows - 1)
+
+
+def columns_body(mixed, low, high, edges_out, send_out):
+    samples, _, tile_cols, channels = mixed.shape
+    spare = [jnp.zeros((send_out.shape[0] - edges_out.shape[0] // 2, channels), F32)]
+
+    def column(at):
+        parts = []
+        for sample in range(samples):
+            parts.append(low[0, sample].astype(F32)[at : at + 1, :])
+            parts.append(mixed[sample].astype(F32)[:, at, :])
+            parts.append(high[0, sample].astype(F32)[at : at + 1, :])
+        return parts
+
+    first, last = column(0), column(tile_cols - 1)
+    edges_out[...] = jnp.concatenate(first + last, axis=0).astype(BF16)
+    first, last = jnp.concatenate(first + spare, axis=0), jnp.concatenate(last + spare, axis=0)
+    send_out[...] = jnp.where(place(("c",)) == 0, first, last).astype(BF16)
 
 
 def weights_body(
@@ -225,21 +246,31 @@
         shifted[:, tap * channels : (tap + 1) * channels] = moved.astype(BF16)
 
 
-def forward_body(wide, low, high, taps, stats, gamma, beta, block_out, spread, shifted):
-    samples, rows, cols = wide.shape[0], wide.shape[1], wide.shape[2] - 2
+def forward_body(
+    mixed, low, high, other, passed, taps, stats, gamma, beta, block_out, spread, shifted
+):
+    samples, rows, cols, _ = mixed.shape
     size = rows * cols
     row = lax.broadcasted_iota(jnp.int32, spread.shape, 0) + place(LAT) * rows
     inside = (row > 0) & (row <= rows * lax.axis_size(LAT))
-    for sample in range(samples):
-        spread[0] = low[sample].astype(F32)
-        spread[1 : 1 + rows] = wide[sample]
-        spread[1 + rows] = high[sample].astype(F32)
+    core = place(("c",))
+    mate, away = other[...].astype(F32), passed[...].astype(F32)
+    half = samples * (rows + 2)
+    left = jnp.where(core == 0, away[:half, :], mate[half : 2 * half, :])
+    right = jnp.where(core == 0, mate[:half, :], away[:half, :])
+    for sample in range(samples):
+        here = slice(sample * (rows + 2), (sample + 1) * (rows + 2))
+        spread[:, 0, :] = left[here, :]
+        spread[:, 1 + cols, :] = right[here, :]
+        spread[0, 1 : 1 + cols, :] = low[0, sample].astype(F32)
+        spread[1 : 1 + rows, 1 : 1 + cols, :] = mixed[sample].astype(F32)
+        spread[1 + rows, 1 : 1 + cols, :] = high[0, sample].astype(F32)
         mean = stats[sample : sample + 1, :][None]
         inverse = stats[samples + sample : samples + sample + 1, :][None]
         pre = (spread[...] - mean) * inverse * gamma[...][None] + beta[...][None]
         spread[...] = jnp.where(inside, pre / (1.0 + jnp.exp(-pre)), 0.0)
         windows(spread, shifted, rows, cols)
-        total = wide[sample, :, 1 : 1 + cols, :].reshape(size, -1)
+        total = mixed[sample].astype(F32).reshape(size, -1)
         for row_tap in range(3):
             window = shifted[row_tap * cols : row_tap * cols + size, :]
             total = total + jnp.dot(window, taps[sample, row_tap], preferred_element_type=F32)
@@ -247,11 +278,13 @@
 
 
 def sums_body(
-    count, cells, slots, mixed, edges, wide, gamma, beta, back_taps, column, demod, weight,
-    stats_out, norm_out, grad_out, payload_out, edge, spread, shifted, total,
+    count, cells, slots, mixed, edges, wide, low, high, gamma, beta, back_taps, column, demod,
+    weight, stats_out, grad_far, payload_out, edge, spread, shifted, total, grad_out, arrivals,
 ):
     samples, rows, cols, channels = mixed.shape
-    size, span = rows * cols, cols + 2
+    size = rows * cols
+    fetch = fetcher(arrivals)
+    copies = []
     mean_all, spread_all = merged(slots, count)
     inverse_all = lax.rsqrt(spread_all * (1.0 / cells) + 1e-05)
     lat_count, row = slots.shape[0], place(LAT)
@@ -268,13 +301,14 @@
         norm = (flat - mean) * inverse
         pre = norm * gamma[...] + beta[...]
         sig = 1.0 / (1.0 + jnp.exp(-pre))
-        norm_out[sample] = norm
         act = (pre * sig).astype(BF16)
         slope = sig * (1.0 + pre * (1.0 - sig))
-        here = slice(8 + sample * span, 8 + (sample + 1) * span)
-        spread[0] = edge[0, here, :]
         spread[1 : 1 + rows] = wide[sample]
-        spread[1 + rows] = edge[1, here, :]
+        for at, halo, corner in ((0, low, edge[0]), (1 + rows, high, edge[1])):
+            spread[at, 1 : 1 + cols, :] = halo[1, sample].astype(F32)
+            start = 8 + 2 * sample
+            spread[at, 0:1, :] = corner[start : start + 1, :]
+            spread[at, 1 + cols : 2 + cols, :] = corner[start + 1 : start + 2, :]
         windows(spread, shifted, rows, cols)
         style_full = column[sample]
         demod_row = demod[sample : sample + 1, :]
@@ -298,6 +332,7 @@
                 total[here, :] = part if sample == 0 else total[here, :] + part
         grad_pre = grad_act * slope
         grad_out[sample] = grad_pre
+        copies.append(fetch(grad_out.at[sample], grad_far.at[sample]))
         sums[0].append(jnp.sum(product * style_full, axis=0, keepdims=True))
         sums[1].append(jnp.sum((product * demod_row).T, axis=0, keepdims=True))
         sums[2].append(jnp.sum(grad_pre * norm, axis=0, keepdims=True))
@@ -321,6 +356,8 @@
         extra = quarters[shard % 4][shard // 4 : shard // 4 + 1, :]
         tail = jnp.where(sub < 4, last, jnp.where(sub == 4, extra, 0.0))
         payload_out[shard] = jnp.concatenate([main, tail], axis=0).astype(BF16)
+    for copy in copies:
+        copy.wait()
 
 
 def split_terms(values, lane):
@@ -342,42 +379,17 @@
     core, near_count = place(("c",)), slots_out.shape[0]
     mine = pl.ds(core * near_count, near_count)
     total = gathered[0, mine].astype(F32) + gathered[1, mine].astype(F32)
-    other = gathered[1 - core, SHARDS]
-    other_out[...] = other
-    other = other.astype(F32)
-    half = slots_out.shape[1] - SLOT
-    passed = jnp.where(core == 0, other[half : 2 * half, :], other[0:half, :])
-    passed = jnp.broadcast_to(passed[None], (near_count,) + passed.shape)
-    slots_out[...] = jnp.concatenate([resplit(total), passed], axis=1).astype(BF16)
-
-
-def near_body(slots, other, mixed, slots_out, wide_out, top_out, bottom_out):
-    samples, rows, cols, _ = mixed.shape
-    count, half = slots.shape[0], samples * rows
-    core, near = place(("c",)), place(NEAR)
-    total = jnp.sum(slots[:, 0:SLOT, :].astype(F32), axis=0)
-    slots_out[...] = jnp.broadcast_to(resplit(total[None]).astype(BF16), slots_out.shape)
-    apart = lax.rem(jnp.where(core == 0, near + count - 1, near + 1), count)
-    passed = slots[apart].astype(F32)[SLOT : SLOT + half, :]
-    mate = other[...].astype(F32)
-    low = jnp.where(core == 0, passed, mate[half : 2 * half, :])
-    high = jnp.where(core == 0, mate[0:half, :], passed)
-    for sample in range(samples):
-        here = slice(sample * rows, (sample + 1) * rows)
-        wide_out[sample, :, 0, :] = low[here, :]
-        wide_out[sample, :, 1 : 1 + cols, :] = mixed[sample].astype(F32)
-        wide_out[sample, :, 1 + cols, :] = high[here, :]
-        top_out[sample] = wide_out[sample, 0].astype(BF16)
-        bottom_out[sample] = wide_out[sample, rows - 1].astype(BF16)
-
-
-def lat_body(slots, slots_out):
+    other_out[...] = gathered[1 - core, SHARDS]
+    slots_out[...] = resplit(total).astype(BF16)
+
+
+def sum_body(slots, slots_out):
     total = jnp.sum(slots[...].astype(F32), axis=0)
     slots_out[...] = jnp.broadcast_to(resplit(total[None]).astype(BF16), slots_out.shape)
 
 
 def last_body(
-    scale, cells, gathered, stats, norm, cotangent, grad_pre, gamma, style, column, demod,
+    scale, cells, gathered, stats, mixed, cotangent, grad_pre, gamma, style, column, demod,
     power, weight, emb_full, feats_out, weight_out, style_out, gamma_out, beta_out,
 ):
     samples, tile_rows, tile_cols, channels = cotangent.shape
@@ -426,7 +438,9 @@
         inverse = stats[samples + sample : samples + sample + 1, :]
         product_mean = group_total(gain * beta_sums[sample]) * (1.0 / cells)
         squared_mean = group_total(gain * gamma_sums[sample]) * (1.0 / cells)
-        change = inverse * (gain * grad_pre[sample] - product_mean - norm[sample] * squared_mean)
+        flat = mixed[sample].astype(F32).reshape(size, channels)
+        norm = (flat - stats[sample : sample + 1, :]) * inverse
+        change = inverse * (gain * grad_pre[sample] - product_mean - norm * squared_mean)
         out = cotangent[sample].reshape(size, channels).astype(F32) + change
         feats_out[sample] = out.astype(BF16).reshape(tile_rows, tile_cols, channels)
 
@@ -443,15 +457,11 @@
     scale_gradient = 1.0 / math.sqrt(samples * tile_rows * tile_cols * devices_all)
     taps = conv_weight.reshape(9, channels, channels)
 
-    lat_slot = -(-(8 + samples * (tile_cols + 2)) // 16) * 16
-    lon_slot = 8 + samples * tile_rows
-    mixed, slots, edges = call(
+    lon_slot, lat_slot = 8 + samples * tile_rows, 16
+    rim = array((2, samples, tile_cols, channels), BF16)
+    mixed, slots, top, bottom = call(
         mix_body,
-        (
-            array(feats.shape, BF16),
-            array((lon_count, lon_slot, LANES), BF16),
-            array((SLOT, LANES), BF16),
-        ),
+        (array(feats.shape, BF16), array((lon_count, lon_slot, LANES), BF16), rim, rim),
         (
             pltpu.VMEM(feats.shape, BF16),
             pltpu.VMEM(feats.shape, BF16),
@@ -464,15 +474,22 @@
         in_specs=[pl.BlockSpec(memory_space=pl.ANY)] * 5,
     )(feats, cond, null_field, cotangent, drop_flags)
     slots = exchange(slots, LON)
+    low, high = shift(bottom, LAT, 1, False), shift(top, LAT, -1, False)
     wide_cot, slots = call(
         functools.partial(merge_body, cells_local),
         (
             array((samples, tile_rows, tile_cols + 2, channels)),
             array((lat_count, lat_slot, LANES), BF16),
         ),
-        (pltpu.VMEM((lat_slot, LANES), F32),),
     )(slots, cotangent)
+    slots, low, high = lax.optimization_barrier((slots, low, high))
     slots = exchange(slots, LAT)
+    half = samples * (tile_rows + 2)
+    edges, passed = call(
+        columns_body, (array((SLOT, LANES), BF16), array((-(-half // 8) * 8, LANES), BF16))
+    )(mixed, low, high)
+    pairs = [(i, (i + 1) % lon_count) for i in range(1, lon_count, 2)]
+    passed = lax.ppermute(passed, LON, pairs + [(target, source) for source, target in pairs])
 
     taps_shape = (samples, 3, 3 * channels, channels)
     gamma, beta, style, column, demod, power, emb_full, back_taps, fore_taps = call(
@@ -492,11 +509,11 @@
     spread = pltpu.VMEM((tile_rows + 2, tile_cols + 2, channels), F32)
     shifted = pltpu.VMEM(((tile_rows + 2) * tile_cols, 3 * channels), BF16)
     flat = (samples, tile_rows * tile_cols, channels)
-    stats, norm, grad_pre, payload = call(
+    near = pl.BlockSpec(memory_space=pltpu.VMEM)
+    stats, grad_pre, payload = call(
         functools.partial(sums_body, cells_local * lon_count, cells_per_group),
         (
             array((2 * samples, LANES)),
-            array(flat),
             array(flat),
             array((SHARDS + 1, SLOT, LANES), BF16),
         ),
@@ -505,31 +522,26 @@
             spread,
             shifted,
             pltpu.VMEM((9 * channels, channels), F32),
+            pltpu.VMEM(flat, F32),
+            pltpu.SemaphoreType.DMA((samples,)),
         ),
-    )(slots, mixed, edges, wide_cot, gamma, beta, back_taps, column, demod, taps)
+        out_specs=(near, pl.BlockSpec(memory_space=pltpu.HBM), near),
+    )(
+        slots, mixed, edges, wide_cot, low, high, gamma, beta, back_taps, column, demod, taps
+    )
 
     near_count = lax.axis_size(NEAR)
-    half = samples * tile_rows
-    slots, other = call(
-        core_body,
-        (array((near_count, SLOT + half, LANES), BF16), array((SLOT, LANES), BF16)),
-    )(lax.all_gather(payload, "c"))
-    border = array((samples, tile_cols + 2, channels), BF16)
-    slots, wide_mixed, top, bottom = call(
-        near_body,
-        (
-            array((lat_count, SLOT, LANES), BF16),
-            array((samples, tile_rows, tile_cols + 2, channels)),
-            border,
-            border,
-        ),
-    )(exchange(slots, NEAR), other, mixed)
-    low, high = shift(bottom, LAT, 1, False), shift(top, LAT, -1, False)
-    slots = call(lat_body, array((near_count, SLOT, LANES), BF16))(exchange(slots, LAT))
-    slots, low, high = lax.optimization_barrier((slots, low, high))
+    shard = array((near_count, SLOT, LANES), BF16)
+    slots, other = call(core_body, (shard, array((SLOT, LANES), BF16)))(
+        lax.all_gather(payload, "c")
+    )
+    slots, passed = lax.optimization_barrier((slots, passed))
+    summed = array((lat_count, SLOT, LANES), BF16)
+    slots = call(sum_body, summed)(exchange(slots, NEAR))
+    slots = call(sum_body, shard)(exchange(slots, LAT))
     payload = lax.all_gather(exchange(slots, NEAR), "c")
     block_out = call(forward_body, array(feats.shape, BF16), (spread, shifted))(
-        wide_mixed, low, high, fore_taps, stats, gamma, beta
+        mixed, low, high, other, passed, fore_taps, stats, gamma, beta
     )
 
     grad_feats, grad_weight, grad_style, grad_gamma, grad_beta = call(
@@ -542,7 +554,7 @@
             array((1, LANES)),
         ),
     )(
-        payload.reshape(SHARDS, SLOT, LANES), stats, norm, cotangent, grad_pre, gamma, style,
+        payload.reshape(SHARDS, SLOT, LANES), stats, mixed, cotangent, grad_pre, gamma, style,
         column, demod, power, taps, emb_full,
     )
     return (

time: 103 us -> 101 us (0.981)
  the two profiles are of different devices: /device:TPU:143 before, /device:TPU:1 now
where the time goes in v10:
time: 101 us
  blocking collectives  38.5 us (38%)
  starting transfers between devices  37.4 us (37%)
  waiting for transfers between devices  13.7 us (14%)
  Pallas kernels  9.51 us (9%)
    all_to_all x3, starting transfers between devices, exchange(): return lax.all_to_all(block, axes, 0, 0)  27.4 us
    all_to_all x2, blocking collectives, exchange(): return lax.all_to_all(block, axes, 0, 0)  27.4 us
    all_to_all x3, waiting for transfers between devices, exchange(): return lax.all_to_all(block, axes, 0, 0)  13.7 us
    all_gather x1, blocking collectives, on_device(): payload = lax.all_gather(exchange(slots, NEAR), 'c')  5.61 us
    all_gather x1, blocking collectives, on_device(): lax.all_gather(payload, 'c')  5.46 us
    ppermute x1, starting transfers between devices, on_device(): lax.ppermute(passed, LON, pairs + [(target, source) for source, target in...  5.43 us
    ppermute x2, starting transfers between devices, shift(): return lax.ppermute(block, axes, pairs)  4.54 us
    pallas_call x1, Pallas kernels, on_device(): call(mix_body, (array(feats.shape, BF16), array((lon_count, lon_slot, LAN...  2.59 us
  transfers between devices with their start and end apart: 6, of which 3 were waited for; matrix products, arithmetic and copies ran while one was open for 0% of the time, Pallas kernels for 5%

profile of v10, /device:TPU:1, one launch (start us, length us, event | category | flops | bytes accessed | tf_op | source)
XLA Modules:
  0.0 100.8 jit_solution(9361759422327641651)
XLA Ops:
  0.6 0.0 copy-start
  0.6 2.6 %shard_map.145 = (bf16[2,8,32,128]{3,2,1,0:T(8,128)(2,1)}, bf16[32,24,128]{2,1,0:T(8,128)(2,1)}, bf16[2,2,32,128]{3,2,1,0:T(8,128)(2,1)}, bf16[2,2,32,128]{3,2,1,0:T(8,128)(2,1)}) custom-call(bf16[2,8,32,128]{3,2,1,0:T(8,128)(2,1)} %feats_in.1, bf16[2,8,32,128]{3,2,1,0:T(8,128)(2,1)} %cond_in.1, bf16[8,32,128]{2,1,0:T(8,128)(2,1)} %null_in.1, ...), custom_call_target="tpu_custom_call" | custom-call | tf_op jit(solution)/shard_map/pallas_call | solution.py:462
  3.2 0.0 copy-start.8
  3.3 0.0 copy-start.7
  3.3 0.0 copy-start.2
  3.3 10.7 %all-to-all-start = ((bf16[32,24,128]{2,1,0:T(8,128)(2,1)}), bf16[32,24,128]{2,1,0:T(8,128)(2,1)S(1)}, u32[]{:S(2)}, u32[]{:S(2)}) async-start(bf16[32,24,128]{2,1,0:T(8,128)(2,1)} %get-tuple-element.39), calls=%async_computation | async-start | bytes 393216 | tf_op jit(solution)/shard_map/all_to_all | solution.py:34
  14.0 0.0 copy-start.3
  14.0 0.0 copy-done.8
  14.0 3.2 %collective-permute-start = (bf16[2,2,32,128]{3,2,1,0:T(8,128)(2,1)S(1)}, bf16[2,2,32,128]{3,2,1,0:T(8,128)(2,1)S(1)}, u32[]{:S(2)}, u32[]{:S(2)}) collective-permute-start(bf16[2,2,32,128]{3,2,1,0:T(8,128)(2,1)S(1)} %copy-done.8), channel_id=1, source_target_pairs={{0,32},{32,64},{64,96},{96,128},{128,160},{160,192},{192,224},{224... | collective-permute-start | bytes 98312 | tf_op jit(solution)/shard_map/ppermute | solution.py:30
  17.3 0.0 copy-done.7
  17.3 1.3 %collective-permute-start.1 = (bf16[2,2,32,128]{3,2,1,0:T(8,128)(2,1)S(1)}, bf16[2,2,32,128]{3,2,1,0:T(8,128)(2,1)S(1)}, u32[]{:S(2)}, u32[]{:S(2)}) collective-permute-start(bf16[2,2,32,128]{3,2,1,0:T(8,128)(2,1)S(1)} %copy-done.7), channel_id=1, source_target_pairs={{32,0},{64,32},{96,64},{128,96},{160,128},{192,160},{224,192},{256... | collective-permute-start | bytes 98312 | tf_op jit(solution)/shard_map/ppermute | solution.py:30
  18.6 5.6 %all-to-all-done.slots = bf16[32,24,128]{2,1,0:T(8,128)(2,1)S(1)} async-done(((bf16[32,24,128]{2,1,0:T(8,128)(2,1)}), bf16[32,24,128]{2,1,0:T(8,128)(2,1)S(1)}, u32[]{:S(2)}, u32[]{:S(2)}) %all-to-all-start) | async-done | bytes 196640 | tf_op jit(solution)/shard_map/all_to_all | solution.py:34
  24.2 0.0 copy-done.2
  24.2 0.7 shard_map.146
  24.9 0.0 collective-permute-done.low
  24.9 0.0 collective-permute-done.1.high
  24.9 12.2 %all-to-all-start.1 = ((bf16[16,16,128]{2,1,0:T(8,128)(2,1)}), bf16[16,16,128]{2,1,0:T(8,128)(2,1)S(1)}, u32[]{:S(2)}, u32[]{:S(2)}) async-start(bf16[16,16,128]{2,1,0:T(8,128)(2,1)} %get-tuple-element.45), calls=%async_computation.1 | async-start | bytes 131072 | tf_op jit(solution)/shard_map/all_to_all | solution.py:34
  37.2 0.0 copy-start.4
  37.2 0.0 copy-start.5
  37.2 0.0 copy-start.6
  37.2 0.0 copy-done
  37.2 0.0 copy-done.3
  37.2 0.6 copy-done.4
  37.9 0.0 copy-done.5
  37.9 0.0 copy-done.6
  37.9 0.0 copy-start.1
  37.9 0.8 shard_map.148
  38.6 0.1 copy-done.1
  38.8 5.4 %collective-permute-start.2 = (bf16[24,128]{1,0:T(8,128)(2,1)S(1)}, bf16[24,128]{1,0:T(8,128)(2,1)S(1)}, u32[]{:S(2)}, u32[]{:S(2)}) collective-permute-start(bf16[24,128]{1,0:T(8,128)(2,1)S(1)} %get-tuple-element.56), channel_id=1, source_target_pairs={{1,2},{3,4},{5,6},{7,8},{9,10},{11,12},{13,14},{15,16},{17,18},{19... | collective-permute-start | bytes 18440 | tf_op jit(solution)/shard_map/ppermute | solution.py:492
  44.2 1.9 %all-to-all-done.1.slots = bf16[16,16,128]{2,1,0:T(8,128)(2,1)S(1)} async-done(((bf16[16,16,128]{2,1,0:T(8,128)(2,1)}), bf16[16,16,128]{2,1,0:T(8,128)(2,1)S(1)}, u32[]{:S(2)}, u32[]{:S(2)}) %all-to-all-start.1) | async-done | bytes 65568 | tf_op jit(solution)/shard_map/all_to_all | solution.py:34
  46.1 1.9 %shard_map.149 = (f32[4,128]{1,0:T(4,128)S(1)}, f32[2,256,128]{2,1,0:T(8,128)S(1)}, bf16[33,40,128]{2,1,0:T(8,128)(2,1)S(1)}) custom-call(bf16[16,16,128]{2,1,0:T(8,128)(2,1)S(1)} %all-to-all-done.1.slots, bf16[2,8,32,128]{3,2,1,0:T(8,128)(2,1)S(1)} %copy-done.1, bf16[40,128]{1,0:T(8,128)(2,1)S(1)} %get-tuple-element.46.edges, ...), custom_call_target="tpu_custom_call" | custom-call | tf_op jit(solution)/shard_map/pallas_call | solution.py:513
  48.0 5.5 %all-gather = bf16[66,40,128]{2,1,0:T(8,128)(2,1)S(1)} all-gather(bf16[33,40,128]{2,1,0:T(8,128)(2,1)S(1)} %get-tuple-element.53), channel_id=2, replica_groups=mesh['zh'=4,'x'=4,'zl'=2,'y'=8,'c'=2] {'c'}, dimensions={0}, use_global_device_ids=true | all-gather | bytes 1013760 | tf_op jit(solution)/shard_map/all_gather | solution.py:536
  53.5 0.1 shard_map.150
  53.6 0.0 collective-permute-done.2.passed
  53.6 14.5 %all_to_all.25.slots = bf16[16,40,128]{2,1,0:T(8,128)(2,1)S(1)} all-to-all(bf16[16,40,128]{2,1,0:T(8,128)(2,1)S(1)} %get-tuple-element.60), channel_id=1, replica_groups=mesh['zh'=4,'x'=4,'zl'=2,'y'=8,'c'=2] {'zl','y'}, dimensions={0} | all-to-all | bytes 327680 | tf_op jit(solution)/shard_map/all_to_all | solution.py:34
  68.1 0.1 shard_map.152
  68.2 12.9 %all_to_all.26.slots = bf16[16,40,128]{2,1,0:T(8,128)(2,1)S(1)} all-to-all(bf16[16,40,128]{2,1,0:T(8,128)(2,1)S(1)} %shard_map.152), channel_id=1, replica_groups=mesh['zh'=4,'x'=4,'zl'=2,'y'=8,'c'=2] {'zh','x'}, dimensions={0} | all-to-all | bytes 327680 | tf_op jit(solution)/shard_map/all_to_all | solution.py:34
  81.1 0.8 shard_map.153
  81.9 4.5 %all-to-all-start.4 = ((bf16[16,40,128]{2,1,0:T(8,128)(2,1)}), bf16[16,40,128]{2,1,0:T(8,128)(2,1)S(1)}, u32[]{:S(2)}, u32[]{:S(2)}) async-start(bf16[16,40,128]{2,1,0:T(8,128)(2,1)} %shard_map.153), calls=%async_computation.4 | async-start | bytes 327680 | tf_op jit(solution)/shard_map/all_to_all | solution.py:34
  86.4 1.3 %shard_map.151 = bf16[2,8,32,128]{3,2,1,0:T(8,128)(2,1)} custom-call(bf16[2,8,32,128]{3,2,1,0:T(8,128)(2,1)S(1)} %copy-done.1, bf16[2,2,32,128]{3,2,1,0:T(8,128)(2,1)S(1)} %collective-permute-done.low, bf16[2,2,32,128]{3,2,1,0:T(8,128)(2,1)S(1)} %collective-permute-done.1.high, bf16[40,128]{1,0:T(8,128)(2,1)S(1)} %get-tuple-element.54.other, ...), custom_call_target="tpu_custom_call" | custom-call | tf_op jit(solution)/shard_map/pallas_call | solution.py:543
  87.7 6.2 %all-to-all-done.4 = bf16[16,40,128]{2,1,0:T(8,128)(2,1)S(1)} async-done(((bf16[16,40,128]{2,1,0:T(8,128)(2,1)}), bf16[16,40,128]{2,1,0:T(8,128)(2,1)S(1)}, u32[]{:S(2)}, u32[]{:S(2)}) %all-to-all-start.4) | async-done | bytes 163872 | tf_op jit(solution)/shard_map/all_to_all | solution.py:34
  93.9 5.6 %all-gather.1.gathered = bf16[32,40,128]{2,1,0:T(8,128)(2,1)S(1)} all-gather(bf16[16,40,128]{2,1,0:T(8,128)(2,1)S(1)} %all-to-all-done.4), channel_id=3, replica_groups=mesh['zh'=4,'x'=4,'zl'=2,'y'=8,'c'=2] {'c'}, dimensions={0}, use_global_device_ids=true | all-gather | bytes 491520 | tf_op jit(solution)/shard_map/all_gather | solution.py:542
  99.5 1.2 %shard_map.154 = (bf16[2,8,32,128]{3,2,1,0:T(8,128)(2,1)}, f32[9,128,128]{2,1,0:T(8,128)}, f32[512,128]{1,0:T(8,128)}, f32[1,128]{1,0:T(1,128)}, f32[1,128]{1,0:T(1,128)}) custom-call(bf16[32,40,128]{2,1,0:T(8,128)(2,1)S(1)} %all-gather.1.gathered, f32[4,128]{1,0:T(4,128)S(1)} %get-tuple-element.59.stats, bf16[2,8,32,128]{3,2,1,0:T(8,128)(2,1)S(1)} %copy-done.1, ...), custom_call_target="tpu_custom_call" | custom-call | tf_op jit(solution)/shard_map/pallas_call | solution.py:547
  (1 shorter events, 0.0 us)
Async XLA Ops:
  0.6 36.6 %copy-start = (f32[3,3,128,128]{3,2,1,0:T(8,128)S(1)}, f32[3,3,128,128]{3,2,1,0:T(8,128)}, u32[]{:S(2)}) copy-start(f32[3,3,128,128]{3,2,1,0:T(8,128)} %param.16) | copy-start | bytes 1769476
  3.2 10.8 %copy-start.8 = (bf16[2,2,32,128]{3,2,1,0:T(8,128)(2,1)S(1)}, bf16[2,2,32,128]{3,2,1,0:T(8,128)(2,1)}, u32[]{:S(2)}) copy-start(bf16[2,2,32,128]{3,2,1,0:T(8,128)(2,1)} %get-tuple-element.41) | copy-start | bytes 98308
  3.3 14.0 %copy-start.7 = (bf16[2,2,32,128]{3,2,1,0:T(8,128)(2,1)S(1)}, bf16[2,2,32,128]{3,2,1,0:T(8,128)(2,1)}, u32[]{:S(2)}) copy-start(bf16[2,2,32,128]{3,2,1,0:T(8,128)(2,1)} %get-tuple-element.42) | copy-start | bytes 98308
  3.3 20.9 %copy-start.2 = (bf16[2,8,32,128]{3,2,1,0:T(8,128)(2,1)S(1)}, bf16[2,8,32,128]{3,2,1,0:T(8,128)(2,1)}, u32[]{:S(2)}) copy-start(bf16[2,8,32,128]{3,2,1,0:T(8,128)(2,1)} %cotangent.1) | copy-start | bytes 393220
  3.3 20.9 %all-to-all-start = ((bf16[32,24,128]{2,1,0:T(8,128)(2,1)}), bf16[32,24,128]{2,1,0:T(8,128)(2,1)S(1)}, u32[]{:S(2)}, u32[]{:S(2)}) async-start(bf16[32,24,128]{2,1,0:T(8,128)(2,1)} %get-tuple-element.39), calls=%async_computation | async-start | bytes 393216 | tf_op jit(solution)/shard_map/all_to_all | solution.py:34
  14.0 23.2 %copy-start.3 = (f32[512,128]{1,0:T(8,128)S(1)}, f32[512,128]{1,0:T(8,128)}, u32[]{:S(2)}) copy-start(f32[512,128]{1,0:T(8,128)} %style_weight.1) | copy-start | bytes 786436
  14.0 10.9 %collective-permute-start = (bf16[2,2,32,128]{3,2,1,0:T(8,128)(2,1)S(1)}, bf16[2,2,32,128]{3,2,1,0:T(8,128)(2,1)S(1)}, u32[]{:S(2)}, u32[]{:S(2)}) collective-permute-start(bf16[2,2,32,128]{3,2,1,0:T(8,128)(2,1)S(1)} %copy-done.8), channel_id=1, source_target_pairs={{0,32},{32,64},{64,96},{96,128},{128,160},{160,192},{192,224},{224... | collective-permute-start | bytes 98312 | tf_op jit(solution)/shard_map/ppermute | solution.py:30
  17.3 7.7 %collective-permute-start.1 = (bf16[2,2,32,128]{3,2,1,0:T(8,128)(2,1)S(1)}, bf16[2,2,32,128]{3,2,1,0:T(8,128)(2,1)S(1)}, u32[]{:S(2)}, u32[]{:S(2)}) collective-permute-start(bf16[2,2,32,128]{3,2,1,0:T(8,128)(2,1)S(1)} %copy-done.7), channel_id=1, source_target_pairs={{32,0},{64,32},{96,64},{128,96},{160,128},{192,160},{224,192},{256... | collective-permute-start | bytes 98312 | tf_op jit(solution)/shard_map/ppermute | solution.py:30
  24.9 21.2 %all-to-all-start.1 = ((bf16[16,16,128]{2,1,0:T(8,128)(2,1)}), bf16[16,16,128]{2,1,0:T(8,128)(2,1)S(1)}, u32[]{:S(2)}, u32[]{:S(2)}) async-start(bf16[16,16,128]{2,1,0:T(8,128)(2,1)} %get-tuple-element.45), calls=%async_computation.1 | async-start | bytes 131072 | tf_op jit(solution)/shard_map/all_to_all | solution.py:34
  37.2 0.7 copy-start.4
  37.2 0.7 copy-start.5
  37.2 0.7 copy-start.6
  37.9 0.9 copy-start.1
  38.8 14.8 %collective-permute-start.2 = (bf16[24,128]{1,0:T(8,128)(2,1)S(1)}, bf16[24,128]{1,0:T(8,128)(2,1)S(1)}, u32[]{:S(2)}, u32[]{:S(2)}) collective-permute-start(bf16[24,128]{1,0:T(8,128)(2,1)S(1)} %get-tuple-element.56), channel_id=1, source_target_pairs={{1,2},{3,4},{5,6},{7,8},{9,10},{11,12},{13,14},{15,16},{17,18},{19... | collective-permute-start | bytes 18440 | tf_op jit(solution)/shard_map/ppermute | solution.py:492
  81.9 12.1 %all-to-all-start.4 = ((bf16[16,40,128]{2,1,0:T(8,128)(2,1)}), bf16[16,40,128]{2,1,0:T(8,128)(2,1)S(1)}, u32[]{:S(2)}, u32[]{:S(2)}) async-start(bf16[16,40,128]{2,1,0:T(8,128)(2,1)} %shard_map.153), calls=%async_computation.4 | async-start | bytes 327680 | tf_op jit(solution)/shard_map/all_to_all | solution.py:34

commit v11 on v9

--- a/solution.py
+++ b/solution.py
@@ -110,7 +110,7 @@
 
 
 def mix_body(
-    feats_in, cond_in, null_in, cot_in, flags_in, mixed_out, slots_out, edges_out,
+    feats_in, cond_in, null_in, cot_in, flags_in, mixed_out, slots_out, edges_out, send_out,
     feats, cond, null, cot, flags, arrivals,
 ):
     fetch = fetcher(arrivals)
@@ -145,6 +145,10 @@
         spreads.append(group_total(jnp.sum(away * away, axis=0, keepdims=True)))
     spare = jnp.zeros((SLOT - 2 * samples * tile_rows, channels), F32)
     edges_out[...] = jnp.concatenate(firsts + lasts + [spare], axis=0).astype(BF16)
+    chosen = [
+        jnp.where(place(("c",)) == 0, first, last) for first, last in zip(firsts, lasts, strict=True)
+    ]
+    send_out[...] = jnp.concatenate(chosen, axis=0).astype(BF16)
     rows = header(weave(*means), weave(*spreads))
     cot_copy.wait()
     firsts, lasts = [], []
@@ -248,7 +252,7 @@
 
 def sums_body(
     count, cells, slots, mixed, edges, wide, gamma, beta, back_taps, column, demod, weight,
-    stats_out, norm_out, grad_out, payload_out, edge, spread, shifted, total,
+    stats_out, grad_far, payload_out, edge, spread, shifted, total, grad_out, arrivals,
 ):
     samples, rows, cols, channels = mixed.shape
     size, span = rows * cols, cols + 2
@@ -259,7 +263,9 @@
     above = slots[lax.min(row + 1, lat_count - 1)].astype(F32)
     edge[0] = jnp.where(row > 0, below, 0.0)
     edge[1] = jnp.where(row < lat_count - 1, above, 0.0)
+    fetch = fetcher(arrivals)
     sums = [[], [], [], []]
+    acts, copies = [], []
     for sample in range(samples):
         mean, inverse = unweave(mean_all, sample), unweave(inverse_all, sample)
         stats_out[sample : sample + 1, :] = mean
@@ -268,26 +274,32 @@
         norm = (flat - mean) * inverse
         pre = norm * gamma[...] + beta[...]
         sig = 1.0 / (1.0 + jnp.exp(-pre))
-        norm_out[sample] = norm
-        act = (pre * sig).astype(BF16)
-        slope = sig * (1.0 + pre * (1.0 - sig))
+        acts.append((pre * sig).astype(BF16))
         here = slice(8 + sample * span, 8 + (sample + 1) * span)
         spread[0] = edge[0, here, :]
         spread[1 : 1 + rows] = wide[sample]
         spread[1 + rows] = edge[1, here, :]
-        windows(spread, shifted, rows, cols)
+        windows(spread, shifted.at[sample], rows, cols)
+        grad_act = jnp.zeros((size, channels), F32)
+        for row_tap in range(3):
+            window = shifted[sample, row_tap * cols : row_tap * cols + size, :]
+            grad_act = grad_act + jnp.dot(
+                window, back_taps[sample, row_tap], preferred_element_type=F32
+            )
+        grad_pre = grad_act * (sig * (1.0 + pre * (1.0 - sig)))
+        grad_out[sample] = grad_pre
+        copies.append(fetch(grad_out.at[sample], grad_far.at[sample]))
+        sums[2].append(jnp.sum(grad_pre * norm, axis=0, keepdims=True))
+        sums[3].append(jnp.sum(grad_pre, axis=0, keepdims=True))
+    for sample in range(samples):
         style_full = column[sample]
         demod_row = demod[sample : sample + 1, :]
         both = style_full * demod_row
         product = jnp.zeros((channels, channels), F32)
-        grad_act = jnp.zeros((size, channels), F32)
         for row_tap in range(3):
-            window = shifted[row_tap * cols : row_tap * cols + size, :]
-            grad_act = grad_act + jnp.dot(
-                window, back_taps[sample, row_tap], preferred_element_type=F32
-            )
+            window = shifted[sample, row_tap * cols : row_tap * cols + size, :]
             grad = lax.dot_general(
-                act, window, (((0,), (0,)), ((), ())), preferred_element_type=F32
+                acts[sample], window, (((0,), (0,)), ((), ())), preferred_element_type=F32
             )
             for col_tap in range(3):
                 tap = (2 - row_tap) * 3 + 2 - col_tap
@@ -296,12 +308,8 @@
                 here = slice(tap * channels, (tap + 1) * channels)
                 part = block * both
                 total[here, :] = part if sample == 0 else total[here, :] + part
-        grad_pre = grad_act * slope
-        grad_out[sample] = grad_pre
         sums[0].append(jnp.sum(product * style_full, axis=0, keepdims=True))
         sums[1].append(jnp.sum((product * demod_row).T, axis=0, keepdims=True))
-        sums[2].append(jnp.sum(grad_pre * norm, axis=0, keepdims=True))
-        sums[3].append(jnp.sum(grad_pre, axis=0, keepdims=True))
     payload_out[SHARDS] = edges[...]
     small = jnp.concatenate(sum(sums, []), axis=0)
     lane = lanes_of(TILE)
@@ -321,6 +329,8 @@
         extra = quarters[shard % 4][shard // 4 : shard // 4 + 1, :]
         tail = jnp.where(sub < 4, last, jnp.where(sub == 4, extra, 0.0))
         payload_out[shard] = jnp.concatenate([main, tail], axis=0).astype(BF16)
+    for copy in copies:
+        copy.wait()
 
 
 def split_terms(values, lane):
@@ -342,26 +352,19 @@
     core, near_count = place(("c",)), slots_out.shape[0]
     mine = pl.ds(core * near_count, near_count)
     total = gathered[0, mine].astype(F32) + gathered[1, mine].astype(F32)
-    other = gathered[1 - core, SHARDS]
-    other_out[...] = other
-    other = other.astype(F32)
-    half = slots_out.shape[1] - SLOT
-    passed = jnp.where(core == 0, other[half : 2 * half, :], other[0:half, :])
-    passed = jnp.broadcast_to(passed[None], (near_count,) + passed.shape)
-    slots_out[...] = jnp.concatenate([resplit(total), passed], axis=1).astype(BF16)
-
-
-def near_body(slots, other, mixed, slots_out, wide_out, top_out, bottom_out):
+    other_out[...] = gathered[1 - core, SHARDS]
+    slots_out[...] = resplit(total).astype(BF16)
+
+
+def near_body(slots, other, passed, mixed, slots_out, wide_out, top_out, bottom_out):
     samples, rows, cols, _ = mixed.shape
-    count, half = slots.shape[0], samples * rows
-    core, near = place(("c",)), place(NEAR)
-    total = jnp.sum(slots[:, 0:SLOT, :].astype(F32), axis=0)
+    half, core = samples * rows, place(("c",))
+    total = jnp.sum(slots[...].astype(F32), axis=0)
     slots_out[...] = jnp.broadcast_to(resplit(total[None]).astype(BF16), slots_out.shape)
-    apart = lax.rem(jnp.where(core == 0, near + count - 1, near + 1), count)
-    passed = slots[apart].astype(F32)[SLOT : SLOT + half, :]
+    away = passed[...].astype(F32)
     mate = other[...].astype(F32)
-    low = jnp.where(core == 0, passed, mate[half : 2 * half, :])
-    high = jnp.where(core == 0, mate[0:half, :], passed)
+    low = jnp.where(core == 0, away, mate[half : 2 * half, :])
+    high = jnp.where(core == 0, mate[0:half, :], away)
     for sample in range(samples):
         here = slice(sample * rows, (sample + 1) * rows)
         wide_out[sample, :, 0, :] = low[here, :]
@@ -377,7 +380,7 @@
 
 
 def last_body(
-    scale, cells, gathered, stats, norm, cotangent, grad_pre, gamma, style, column, demod,
+    scale, cells, gathered, stats, mixed, cotangent, grad_pre, gamma, style, column, demod,
     power, weight, emb_full, feats_out, weight_out, style_out, gamma_out, beta_out,
 ):
     samples, tile_rows, tile_cols, channels = cotangent.shape
@@ -426,7 +429,9 @@
         inverse = stats[samples + sample : samples + sample + 1, :]
         product_mean = group_total(gain * beta_sums[sample]) * (1.0 / cells)
         squared_mean = group_total(gain * gamma_sums[sample]) * (1.0 / cells)
-        change = inverse * (gain * grad_pre[sample] - product_mean - norm[sample] * squared_mean)
+        flat = mixed[sample].astype(F32).reshape(size, channels)
+        norm = (flat - stats[sample : sample + 1, :]) * inverse
+        change = inverse * (gain * grad_pre[sample] - product_mean - norm * squared_mean)
         out = cotangent[sample].reshape(size, channels).astype(F32) + change
         feats_out[sample] = out.astype(BF16).reshape(tile_rows, tile_cols, channels)
 
@@ -444,13 +449,15 @@
     taps = conv_weight.reshape(9, channels, channels)
 
     lat_slot = -(-(8 + samples * (tile_cols + 2)) // 16) * 16
-    lon_slot = 8 + samples * tile_rows
-    mixed, slots, edges = call(
+    half = samples * tile_rows
+    lon_slot = 8 + half
+    mixed, slots, edges, passed = call(
         mix_body,
         (
             array(feats.shape, BF16),
             array((lon_count, lon_slot, LANES), BF16),
             array((SLOT, LANES), BF16),
+            array((half, LANES), BF16),
         ),
         (
             pltpu.VMEM(feats.shape, BF16),
@@ -472,7 +479,10 @@
         ),
         (pltpu.VMEM((lat_slot, LANES), F32),),
     )(slots, cotangent)
+    slots, passed = lax.optimization_barrier((slots, passed))
     slots = exchange(slots, LAT)
+    pairs = [(i, (i + 1) % lon_count) for i in range(1, lon_count, 2)]
+    passed = lax.ppermute(passed, LON, pairs + [(target, source) for source, target in pairs])
 
     taps_shape = (samples, 3, 3 * channels, channels)
     gamma, beta, style, column, demod, power, emb_full, back_taps, fore_taps = call(
@@ -492,28 +502,32 @@
     spread = pltpu.VMEM((tile_rows + 2, tile_cols + 2, channels), F32)
     shifted = pltpu.VMEM(((tile_rows + 2) * tile_cols, 3 * channels), BF16)
     flat = (samples, tile_rows * tile_cols, channels)
-    stats, norm, grad_pre, payload = call(
+    near = pl.BlockSpec(memory_space=pltpu.VMEM)
+    stats, grad_pre, payload = call(
         functools.partial(sums_body, cells_local * lon_count, cells_per_group),
         (
             array((2 * samples, LANES)),
             array(flat),
-            array(flat),
             array((SHARDS + 1, SLOT, LANES), BF16),
         ),
         (
             pltpu.VMEM((2, lat_slot, LANES), F32),
             spread,
-            shifted,
+            pltpu.VMEM((samples, (tile_rows + 2) * tile_cols, 3 * channels), BF16),
             pltpu.VMEM((9 * channels, channels), F32),
-        ),
+            pltpu.VMEM(flat, F32),
+            pltpu.SemaphoreType.DMA((samples,)),
+        ),
+        out_specs=(near, pl.BlockSpec(memory_space=pltpu.HBM), near),
+        room=52,
     )(slots, mixed, edges, wide_cot, gamma, beta, back_taps, column, demod, taps)
 
     near_count = lax.axis_size(NEAR)
-    half = samples * tile_rows
     slots, other = call(
         core_body,
-        (array((near_count, SLOT + half, LANES), BF16), array((SLOT, LANES), BF16)),
+        (array((near_count, SLOT, LANES), BF16), array((SLOT, LANES), BF16)),
     )(lax.all_gather(payload, "c"))
+    slots, passed = lax.optimization_barrier((slots, passed))
     border = array((samples, tile_cols + 2, channels), BF16)
     slots, wide_mixed, top, bottom = call(
         near_body,
@@ -523,7 +537,7 @@
             border,
             border,
         ),
-    )(exchange(slots, NEAR), other, mixed)
+    )(exchange(slots, NEAR), other, passed, mixed)
     low, high = shift(bottom, LAT, 1, False), shift(top, LAT, -1, False)
     slots = call(lat_body, array((near_count, SLOT, LANES), BF16))(exchange(slots, LAT))
     slots, low, high = lax.optimization_barrier((slots, low, high))
@@ -542,7 +556,7 @@
             array((1, LANES)),
         ),
     )(
-        payload.reshape(SHARDS, SLOT, LANES), stats, norm, cotangent, grad_pre, gamma, style,
+        payload.reshape(SHARDS, SLOT, LANES), stats, mixed, cotangent, grad_pre, gamma, style,
         column, demod, power, taps, emb_full,
     )
     return (

time: 103 us -> 103 us (level)
  waiting for transfers between devices: 17.2 us -> 13.6 us
  starting transfers between devices: 28.2 us -> 31.6 us
  Pallas kernels: 9.45 us -> 11.2 us
    ppermute x0 -> x1, starting transfers between devices: none -> 3.72 us  [on_device(): lax.ppermute(passed, LON, pairs + [(target, source) for source, target in...]
    all_to_all x3, waiting for transfers between devices: 11.1 us -> 7.55 us  [exchange(): return lax.all_to_all(block, axes, 0, 0)]
    pallas_call x1, Pallas kernels: 1.19 us -> 2.94 us  [on_device(): call(functools.partial(sums_body, cells_local * lon_count, cells_per_grou...]
    unnamed x24 -> x22, local copies, waits for them, and re-layouts: 2.34 us -> 1.49 us
  transfers between devices with their start and end apart: 5 -> 6, of which waited for: 3 -> 3; matrix products, arithmetic and copies ran while one was open for 0% -> 0% of each run, Pallas kernels for 3% -> 6%
where the time goes in v11:
time: 103 us
  blocking collectives  43.9 us (43%)
  starting transfers between devices  31.6 us (31%)
  waiting for transfers between devices  13.6 us (13%)
  Pallas kernels  11.2 us (11%)
  local copies, waits for them, and re-layouts  1.49 us (1%)
    all_to_all x2, blocking collectives, exchange(): return lax.all_to_all(block, axes, 0, 0)  31 us
    all_to_all x3, starting transfers between devices, exchange(): return lax.all_to_all(block, axes, 0, 0)  20.7 us
    all_to_all x3, waiting for transfers between devices, exchange(): return lax.all_to_all(block, axes, 0, 0)  7.55 us
    ppermute x2, starting transfers between devices, shift(): return lax.ppermute(block, axes, pairs)  7.11 us
    all_gather x1, blocking collectives, on_device(): lax.all_gather(payload, 'c')  6.99 us
    ppermute x2, waiting for transfers between devices, shift(): return lax.ppermute(block, axes, pairs)  6.04 us
    all_gather x1, blocking collectives, on_device(): payload = lax.all_gather(exchange(slots, NEAR), 'c')  5.94 us
    ppermute x1, starting transfers between devices, on_device(): lax.ppermute(passed, LON, pairs + [(target, source) for source, target in...  3.72 us
  transfers between devices with their start and end apart: 6, of which 3 were waited for; matrix products, arithmetic and copies ran while one was open for 0% of the time, Pallas kernels for 6%

profile of v11, /device:TPU:143, one launch (start us, length us, event | category | flops | bytes accessed | tf_op | source)
XLA Modules:
  0.0 102.5 jit_solution(1925626564744196283)
XLA Ops:
  0.6 2.5 %shard_map.145 = (bf16[2,8,32,128]{3,2,1,0:T(8,128)(2,1)}, bf16[32,24,128]{2,1,0:T(8,128)(2,1)}, bf16[40,128]{1,0:T(8,128)(2,1)}, bf16[16,128]{1,0:T(8,128)(2,1)}) custom-call(bf16[2,8,32,128]{3,2,1,0:T(8,128)(2,1)} %feats_in.1, bf16[2,8,32,128]{3,2,1,0:T(8,128)(2,1)} %cond_in.1, bf16[8,32,128]{2,1,0:T(8,128)(2,1)} %null_in.1, ...), custom_call_target="tpu_custom_call" | custom-call | tf_op jit(solution)/shard_map/pallas_call | solution.py:454
  3.2 0.0 copy-start.3
  3.2 19.4 %all_to_all.25.slots = bf16[32,24,128]{2,1,0:T(8,128)(2,1)S(1)} all-to-all(bf16[32,24,128]{2,1,0:T(8,128)(2,1)} %get-tuple-element.42), channel_id=1, replica_groups=mesh['zh'=4,'x'=4,'zl'=2,'y'=8,'c'=2] {'zl','y','c'}, dimensions={0} | all-to-all | bytes 393216 | tf_op jit(solution)/shard_map/all_to_all | solution.py:34
  22.6 0.0 copy-done.3
  22.6 0.0 copy-start
  22.6 0.9 shard_map.146
  23.5 0.0 copy-start.5
  23.5 10.1 %all-to-all-start.1 = ((bf16[16,80,128]{2,1,0:T(8,128)(2,1)}), bf16[16,80,128]{2,1,0:T(8,128)(2,1)S(1)}, u32[]{:S(2)}, u32[]{:S(2)}) async-start(bf16[16,80,128]{2,1,0:T(8,128)(2,1)} %get-tuple-element.45), calls=%async_computation.1 | async-start | bytes 655360 | tf_op jit(solution)/shard_map/all_to_all | solution.py:34
  33.6 0.0 copy-start.7
  33.6 0.0 copy-start.8
  33.6 0.0 copy-start.9
  33.6 0.0 copy-done
  33.6 0.0 copy-done.5
  33.6 0.6 copy-done.7
  34.3 0.0 copy-done.8
  34.3 0.0 copy-done.9
  34.3 0.0 copy-start.10
  34.3 0.0 copy-start.2
  34.3 0.8 shard_map.147
  35.1 0.0 copy-start.4
  35.1 0.8 copy-done.4
  35.9 0.0 copy-done.10
  35.9 0.0 copy-start.6
  35.9 3.7 %collective-permute-start = (bf16[16,128]{1,0:T(8,128)(2,1)S(1)}, bf16[16,128]{1,0:T(8,128)(2,1)S(1)}, u32[]{:S(2)}, u32[]{:S(2)}) collective-permute-start(bf16[16,128]{1,0:T(8,128)(2,1)S(1)} %copy-done.10), channel_id=1, source_target_pairs={{1,2},{3,4},{5,6},{7,8},{9,10},{11,12},{13,14},{15,16},{17,18},{19... | collective-permute-start | bytes 12296 | tf_op jit(solution)/shard_map/ppermute | solution.py:485
  39.6 1.3 %all-to-all-done.1.slots = bf16[16,80,128]{2,1,0:T(8,128)(2,1)S(1)} async-done(((bf16[16,80,128]{2,1,0:T(8,128)(2,1)}), bf16[16,80,128]{2,1,0:T(8,128)(2,1)S(1)}, u32[]{:S(2)}, u32[]{:S(2)}) %all-to-all-start.1) | async-done | bytes 327712 | tf_op jit(solution)/shard_map/all_to_all | solution.py:34
  41.0 0.0 copy-done.2
  41.0 0.0 copy-done.6
  41.0 2.9 %shard_map.148 = (f32[4,128]{1,0:T(4,128)S(1)}, f32[2,256,128]{2,1,0:T(8,128)S(1)}, bf16[33,40,128]{2,1,0:T(8,128)(2,1)S(1)}) custom-call(bf16[16,80,128]{2,1,0:T(8,128)(2,1)S(1)} %all-to-all-done.1.slots, bf16[2,8,32,128]{3,2,1,0:T(8,128)(2,1)S(1)} %copy-done.2, bf16[40,128]{1,0:T(8,128)(2,1)S(1)} %copy-done.6, ...), custom_call_target="tpu_custom_call" | custom-call | tf_op jit(solution)/shard_map/pallas_call | solution.py:506
  43.9 7.0 %all-gather = bf16[66,40,128]{2,1,0:T(8,128)(2,1)S(1)} all-gather(bf16[33,40,128]{2,1,0:T(8,128)(2,1)S(1)} %get-tuple-element.54), channel_id=2, replica_groups=mesh['zh'=4,'x'=4,'zl'=2,'y'=8,'c'=2] {'c'}, dimensions={0}, use_global_device_ids=true | all-gather | bytes 1013760 | tf_op jit(solution)/shard_map/all_gather | solution.py:529
  50.9 0.1 shard_map.149
  51.0 0.0 collective-permute-done.passed
  51.0 11.5 %all_to_all.26.slots = bf16[16,40,128]{2,1,0:T(8,128)(2,1)S(1)} all-to-all(bf16[16,40,128]{2,1,0:T(8,128)(2,1)S(1)} %get-tuple-element.57), channel_id=1, replica_groups=mesh['zh'=4,'x'=4,'zl'=2,'y'=8,'c'=2] {'zl','y'}, dimensions={0} | all-to-all | bytes 327680 | tf_op jit(solution)/shard_map/all_to_all | solution.py:34
  62.6 0.8 shard_map.150
  63.3 6.2 %all-to-all-start.3 = ((bf16[16,40,128]{2,1,0:T(8,128)(2,1)}), bf16[16,40,128]{2,1,0:T(8,128)(2,1)S(1)}, u32[]{:S(2)}, u32[]{:S(2)}) async-start(bf16[16,40,128]{2,1,0:T(8,128)(2,1)} %get-tuple-element.61), calls=%async_computation.3 | async-start | bytes 327680 | tf_op jit(solution)/shard_map/all_to_all | solution.py:34
  69.6 5.2 %collective-permute-start.1 = (bf16[2,34,128]{2,1,0:T(8,128)(2,1)S(1)}, bf16[2,34,128]{2,1,0:T(8,128)(2,1)S(1)}, u32[]{:S(2)}, u32[]{:S(2)}) collective-permute-start(bf16[2,34,128]{2,1,0:T(8,128)(2,1)S(1)} %get-tuple-element.62), channel_id=1, source_target_pairs={{0,32},{32,64},{64,96},{96,128},{128,160},{160,192},{192,224},{224... | collective-permute-start | bytes 52232 | tf_op jit(solution)/shard_map/ppermute | solution.py:30
  74.8 1.9 %collective-permute-start.2 = (bf16[2,34,128]{2,1,0:T(8,128)(2,1)S(1)}, bf16[2,34,128]{2,1,0:T(8,128)(2,1)S(1)}, u32[]{:S(2)}, u32[]{:S(2)}) collective-permute-start(bf16[2,34,128]{2,1,0:T(8,128)(2,1)S(1)} %get-tuple-element.63), channel_id=1, source_target_pairs={{32,0},{64,32},{96,64},{128,96},{160,128},{192,160},{224,192},{256... | collective-permute-start | bytes 52232 | tf_op jit(solution)/shard_map/ppermute | solution.py:30
  76.7 0.0 all-to-all-done.3.slots
  76.7 0.8 shard_map.151
  77.5 0.0 collective-permute-done.1.low
  77.5 6.0 %collective-permute-done.2.high = bf16[2,34,128]{2,1,0:T(8,128)(2,1)S(1)} collective-permute-done((bf16[2,34,128]{2,1,0:T(8,128)(2,1)S(1)}, bf16[2,34,128]{2,1,0:T(8,128)(2,1)S(1)}, u32[]{:S(2)}, u32[]{:S(2)}) %collective-permute-start.2) | collective-permute-done | bytes 17440 | tf_op jit(solution)/shard_map/ppermute | solution.py:30
  83.5 4.4 %all-to-all-start.4 = ((bf16[16,40,128]{2,1,0:T(8,128)(2,1)}), bf16[16,40,128]{2,1,0:T(8,128)(2,1)S(1)}, u32[]{:S(2)}, u32[]{:S(2)}) async-start(bf16[16,40,128]{2,1,0:T(8,128)(2,1)} %shard_map.151), calls=%async_computation.4 | async-start | bytes 327680 | tf_op jit(solution)/shard_map/all_to_all | solution.py:34
  87.9 0.0 copy-start.1
  87.9 1.2 %shard_map.152 = bf16[2,8,32,128]{3,2,1,0:T(8,128)(2,1)} custom-call(f32[2,8,34,128]{3,2,1,0:T(8,128)S(1)} %get-tuple-element.60.wide, bf16[2,34,128]{2,1,0:T(8,128)(2,1)S(1)} %collective-permute-done.1.low, bf16[2,34,128]{2,1,0:T(8,128)(2,1)S(1)} %collective-permute-done.2.high, bf16[2,3,384,128]{3,2,1,0:T(8,128)(2,1)S(1)} %get-tuple-element.66.taps, ...), custom_call_target="tpu_custom_call" | custom-call | tf_op jit(solution)/shard_map/pallas_call | solution.py:545
  89.2 6.2 %all-to-all-done.4 = bf16[16,40,128]{2,1,0:T(8,128)(2,1)S(1)} async-done(((bf16[16,40,128]{2,1,0:T(8,128)(2,1)}), bf16[16,40,128]{2,1,0:T(8,128)(2,1)S(1)}, u32[]{:S(2)}, u32[]{:S(2)}) %all-to-all-start.4) | async-done | bytes 163872 | tf_op jit(solution)/shard_map/all_to_all | solution.py:34
  95.4 5.9 %all-gather.1.gathered = bf16[32,40,128]{2,1,0:T(8,128)(2,1)S(1)} all-gather(bf16[16,40,128]{2,1,0:T(8,128)(2,1)S(1)} %all-to-all-done.4), channel_id=3, replica_groups=mesh['zh'=4,'x'=4,'zl'=2,'y'=8,'c'=2] {'c'}, dimensions={0}, use_global_device_ids=true | all-gather | bytes 491520 | tf_op jit(solution)/shard_map/all_gather | solution.py:544
  101.3 0.0 copy-done.1
  101.3 1.2 %shard_map.153 = (bf16[2,8,32,128]{3,2,1,0:T(8,128)(2,1)}, f32[9,128,128]{2,1,0:T(8,128)}, f32[512,128]{1,0:T(8,128)}, f32[1,128]{1,0:T(1,128)}, f32[1,128]{1,0:T(1,128)}) custom-call(bf16[32,40,128]{2,1,0:T(8,128)(2,1)S(1)} %all-gather.1.gathered, f32[4,128]{1,0:T(4,128)S(1)} %get-tuple-element.67.stats, bf16[2,8,32,128]{3,2,1,0:T(8,128)(2,1)S(1)} %copy-done.2, ...), custom_call_target="tpu_custom_call" | custom-call | tf_op jit(solution)/shard_map/pallas_call | solution.py:549
Async XLA Ops:
  3.2 19.5 %copy-start.3 = (bf16[2,8,32,128]{3,2,1,0:T(8,128)(2,1)S(1)}, bf16[2,8,32,128]{3,2,1,0:T(8,128)(2,1)}, u32[]{:S(2)}) copy-start(bf16[2,8,32,128]{3,2,1,0:T(8,128)(2,1)} %cotangent.1) | copy-start | bytes 393220
  22.6 11.0 %copy-start = (f32[3,3,128,128]{3,2,1,0:T(8,128)S(1)}, f32[3,3,128,128]{3,2,1,0:T(8,128)}, u32[]{:S(2)}) copy-start(f32[3,3,128,128]{3,2,1,0:T(8,128)} %param.16) | copy-start | bytes 1769476
  23.5 10.2 %copy-start.5 = (f32[512,128]{1,0:T(8,128)S(1)}, f32[512,128]{1,0:T(8,128)}, u32[]{:S(2)}) copy-start(f32[512,128]{1,0:T(8,128)} %style_weight.1) | copy-start | bytes 786436
  23.5 17.5 %all-to-all-start.1 = ((bf16[16,80,128]{2,1,0:T(8,128)(2,1)}), bf16[16,80,128]{2,1,0:T(8,128)(2,1)S(1)}, u32[]{:S(2)}, u32[]{:S(2)}) async-start(bf16[16,80,128]{2,1,0:T(8,128)(2,1)} %get-tuple-element.45), calls=%async_computation.1 | async-start | bytes 655360 | tf_op jit(solution)/shard_map/all_to_all | solution.py:34
  33.6 0.7 copy-start.7
  33.6 0.7 copy-start.8
  33.6 0.7 copy-start.9
  34.3 1.6 %copy-start.10 = (bf16[16,128]{1,0:T(8,128)(2,1)S(1)}, bf16[16,128]{1,0:T(8,128)(2,1)}, u32[]{:S(2)}) copy-start(bf16[16,128]{1,0:T(8,128)(2,1)} %get-tuple-element.56) | copy-start | bytes 12292
  34.3 6.7 %copy-start.2 = (bf16[2,8,32,128]{3,2,1,0:T(8,128)(2,1)S(1)}, bf16[2,8,32,128]{3,2,1,0:T(8,128)(2,1)}, u32[]{:S(2)}) copy-start(bf16[2,8,32,128]{3,2,1,0:T(8,128)(2,1)} %get-tuple-element.46.mixed) | copy-start | bytes 393220
  35.1 0.8 copy-start.4
  35.9 5.1 %copy-start.6 = (bf16[40,128]{1,0:T(8,128)(2,1)S(1)}, bf16[40,128]{1,0:T(8,128)(2,1)}, u32[]{:S(2)}) copy-start(bf16[40,128]{1,0:T(8,128)(2,1)} %get-tuple-element.47.edges) | copy-start | bytes 30724
  35.9 15.1 %collective-permute-start = (bf16[16,128]{1,0:T(8,128)(2,1)S(1)}, bf16[16,128]{1,0:T(8,128)(2,1)S(1)}, u32[]{:S(2)}, u32[]{:S(2)}) collective-permute-start(bf16[16,128]{1,0:T(8,128)(2,1)S(1)} %copy-done.10), channel_id=1, source_target_pairs={{1,2},{3,4},{5,6},{7,8},{9,10},{11,12},{13,14},{15,16},{17,18},{19... | collective-permute-start | bytes 12296 | tf_op jit(solution)/shard_map/ppermute | solution.py:485
  63.3 13.3 %all-to-all-start.3 = ((bf16[16,40,128]{2,1,0:T(8,128)(2,1)}), bf16[16,40,128]{2,1,0:T(8,128)(2,1)S(1)}, u32[]{:S(2)}, u32[]{:S(2)}) async-start(bf16[16,40,128]{2,1,0:T(8,128)(2,1)} %get-tuple-element.61), calls=%async_computation.3 | async-start | bytes 327680 | tf_op jit(solution)/shard_map/all_to_all | solution.py:34
  69.6 7.9 %collective-permute-start.1 = (bf16[2,34,128]{2,1,0:T(8,128)(2,1)S(1)}, bf16[2,34,128]{2,1,0:T(8,128)(2,1)S(1)}, u32[]{:S(2)}, u32[]{:S(2)}) collective-permute-start(bf16[2,34,128]{2,1,0:T(8,128)(2,1)S(1)} %get-tuple-element.62), channel_id=1, source_target_pairs={{0,32},{32,64},{64,96},{96,128},{128,160},{160,192},{192,224},{224... | collective-permute-start | bytes 52232 | tf_op jit(solution)/shard_map/ppermute | solution.py:30
  74.8 8.7 %collective-permute-start.2 = (bf16[2,34,128]{2,1,0:T(8,128)(2,1)S(1)}, bf16[2,34,128]{2,1,0:T(8,128)(2,1)S(1)}, u32[]{:S(2)}, u32[]{:S(2)}) collective-permute-start(bf16[2,34,128]{2,1,0:T(8,128)(2,1)S(1)} %get-tuple-element.63), channel_id=1, source_target_pairs={{32,0},{64,32},{96,64},{128,96},{160,128},{192,160},{224,192},{256... | collective-permute-start | bytes 52232 | tf_op jit(solution)/shard_map/ppermute | solution.py:30
  83.5 11.9 %all-to-all-start.4 = ((bf16[16,40,128]{2,1,0:T(8,128)(2,1)}), bf16[16,40,128]{2,1,0:T(8,128)(2,1)S(1)}, u32[]{:S(2)}, u32[]{:S(2)}) async-start(bf16[16,40,128]{2,1,0:T(8,128)(2,1)} %shard_map.151), calls=%async_computation.4 | async-start | bytes 327680 | tf_op jit(solution)/shard_map/all_to_all | solution.py:34
  87.9 13.4 %copy-start.1 = (f32[3,3,128,128]{3,2,1,0:T(8,128)S(1)}, f32[3,3,128,128]{3,2,1,0:T(8,128)}, u32[]{:S(2)}) copy-start(f32[3,3,128,128]{3,2,1,0:T(8,128)} %param.16) | copy-start | bytes 1769476

commit v12 on v10

--- a/solution.py
+++ b/solution.py
@@ -20,14 +20,16 @@
 LANES = 128
 
 
-def shift(block, axes, step, periodic):
+def swap(block, axes, first, periodic):
     count = lax.axis_size(axes)
-    pairs = [(i, i + step) for i in range(count)]
-    if periodic:
-        pairs = [(source, target % count) for source, target in pairs]
-    else:
-        pairs = [(source, target) for source, target in pairs if 0 <= target < count]
-    return lax.ppermute(block, axes, pairs)
+    pairs = [(i, (i + 1) % count) for i in range(first, count, 2) if periodic or i + 1 < count]
+    return lax.ppermute(block, axes, pairs + [(target, source) for source, target in pairs])
+
+
+def halos(inner, outer, field, sample):
+    near, far = inner[field, sample].astype(F32), outer[field, sample].astype(F32)
+    even = lax.rem(place(LAT), 2) == 0
+    return jnp.where(even, far, near), jnp.where(even, near, far)
 
 
 def exchange(block, axes):
@@ -110,7 +112,7 @@
 
 
 def mix_body(
-    feats_in, cond_in, null_in, cot_in, flags_in, mixed_out, slots_out, top_out, bottom_out,
+    feats_in, cond_in, null_in, cot_in, flags_in, mixed_out, slots_out, inner_out, outer_out,
     feats, cond, null, cot, flags, arrivals,
 ):
     fetch = fetcher(arrivals)
@@ -125,6 +127,13 @@
     samples, tile_rows, tile_cols, channels = feats.shape
     cells = tile_rows * tile_cols
     size = cells * (channels // GROUPS)
+    even = lax.rem(place(LAT), 2) == 0
+
+    def put_rims(field, sample, top, bottom):
+        top, bottom = top.astype(F32), bottom.astype(F32)
+        inner_out[field, sample] = jnp.where(even, bottom, top).astype(BF16)
+        outer_out[field, sample] = jnp.where(even, top, bottom).astype(BF16)
+
     null32 = null[...].astype(F32)
     means, spreads = [], []
     for sample in range(samples):
@@ -135,8 +144,7 @@
             feats[sample].astype(F32) + dropped * null32 + (1.0 - dropped) * cond[sample].astype(F32)
         ).astype(BF16)
         mixed_out[sample] = mixed
-        top_out[0, sample] = mixed[0]
-        bottom_out[0, sample] = mixed[tile_rows - 1]
+        put_rims(0, sample, mixed[0], mixed[tile_rows - 1])
         wide = mixed.astype(F32).reshape(cells, channels)
         mean = group_total(jnp.sum(wide, axis=0, keepdims=True)) * (1.0 / size)
         away = wide - mean
@@ -146,8 +154,7 @@
     cot_copy.wait()
     firsts, lasts = [], []
     for sample in range(samples):
-        top_out[1, sample] = cot[sample, 0]
-        bottom_out[1, sample] = cot[sample, tile_rows - 1]
+        put_rims(1, sample, cot[sample, 0], cot[sample, tile_rows - 1])
         wide = cot[sample].astype(F32)
         firsts.append(wide[:, 0, :])
         lasts.append(wide[:, tile_cols - 1, :])
@@ -189,16 +196,17 @@
         slots_out[row + 1] = slot(tile_rows - 1)
 
 
-def columns_body(mixed, low, high, edges_out, send_out):
+def columns_body(mixed, inner, outer, edges_out, send_out):
     samples, _, tile_cols, channels = mixed.shape
     spare = [jnp.zeros((send_out.shape[0] - edges_out.shape[0] // 2, channels), F32)]
 
     def column(at):
         parts = []
         for sample in range(samples):
-            parts.append(low[0, sample].astype(F32)[at : at + 1, :])
+            low, high = halos(inner, outer, 0, sample)
+            parts.append(low[at : at + 1, :])
             parts.append(mixed[sample].astype(F32)[:, at, :])
-            parts.append(high[0, sample].astype(F32)[at : at + 1, :])
+            parts.append(high[at : at + 1, :])
         return parts
 
     first, last = column(0), column(tile_cols - 1)
@@ -247,7 +255,7 @@
 
 
 def forward_body(
-    mixed, low, high, other, passed, taps, stats, gamma, beta, block_out, spread, shifted
+    mixed, inner, outer, other, passed, taps, stats, gamma, beta, block_out, spread, shifted
 ):
     samples, rows, cols, _ = mixed.shape
     size = rows * cols
@@ -262,9 +270,10 @@
         here = slice(sample * (rows + 2), (sample + 1) * (rows + 2))
         spread[:, 0, :] = left[here, :]
         spread[:, 1 + cols, :] = right[here, :]
-        spread[0, 1 : 1 + cols, :] = low[0, sample].astype(F32)
+        low, high = halos(inner, outer, 0, sample)
+        spread[0, 1 : 1 + cols, :] = low
         spread[1 : 1 + rows, 1 : 1 + cols, :] = mixed[sample].astype(F32)
-        spread[1 + rows, 1 : 1 + cols, :] = high[0, sample].astype(F32)
+        spread[1 + rows, 1 : 1 + cols, :] = high
         mean = stats[sample : sample + 1, :][None]
         inverse = stats[samples + sample : samples + sample + 1, :][None]
         pre = (spread[...] - mean) * inverse * gamma[...][None] + beta[...][None]
@@ -278,13 +287,11 @@
 
 
 def sums_body(
-    count, cells, slots, mixed, edges, wide, low, high, gamma, beta, back_taps, column, demod,
-    weight, stats_out, grad_far, payload_out, edge, spread, shifted, total, grad_out, arrivals,
+    count, cells, slots, mixed, edges, wide, inner, outer, gamma, beta, back_taps, column, demod,
+    weight, stats_out, grad_out, payload_out, edge, spread, shifted, total,
 ):
     samples, rows, cols, channels = mixed.shape
     size = rows * cols
-    fetch = fetcher(arrivals)
-    copies = []
     mean_all, spread_all = merged(slots, count)
     inverse_all = lax.rsqrt(spread_all * (1.0 / cells) + 1e-05)
     lat_count, row = slots.shape[0], place(LAT)
@@ -304,8 +311,9 @@
         act = (pre * sig).astype(BF16)
         slope = sig * (1.0 + pre * (1.0 - sig))
         spread[1 : 1 + rows] = wide[sample]
+        low, high = halos(inner, outer, 1, sample)
         for at, halo, corner in ((0, low, edge[0]), (1 + rows, high, edge[1])):
-            spread[at, 1 : 1 + cols, :] = halo[1, sample].astype(F32)
+            spread[at, 1 : 1 + cols, :] = halo
             start = 8 + 2 * sample
             spread[at, 0:1, :] = corner[start : start + 1, :]
             spread[at, 1 + cols : 2 + cols, :] = corner[start + 1 : start + 2, :]
@@ -332,7 +340,6 @@
                 total[here, :] = part if sample == 0 else total[here, :] + part
         grad_pre = grad_act * slope
         grad_out[sample] = grad_pre
-        copies.append(fetch(grad_out.at[sample], grad_far.at[sample]))
         sums[0].append(jnp.sum(product * style_full, axis=0, keepdims=True))
         sums[1].append(jnp.sum((product * demod_row).T, axis=0, keepdims=True))
         sums[2].append(jnp.sum(grad_pre * norm, axis=0, keepdims=True))
@@ -356,8 +363,6 @@
         extra = quarters[shard % 4][shard // 4 : shard // 4 + 1, :]
         tail = jnp.where(sub < 4, last, jnp.where(sub == 4, extra, 0.0))
         payload_out[shard] = jnp.concatenate([main, tail], axis=0).astype(BF16)
-    for copy in copies:
-        copy.wait()
 
 
 def split_terms(values, lane):
@@ -459,7 +464,7 @@
 
     lon_slot, lat_slot = 8 + samples * tile_rows, 16
     rim = array((2, samples, tile_cols, channels), BF16)
-    mixed, slots, top, bottom = call(
+    mixed, slots, inner, outer = call(
         mix_body,
         (array(feats.shape, BF16), array((lon_count, lon_slot, LANES), BF16), rim, rim),
         (
@@ -474,7 +479,7 @@
         in_specs=[pl.BlockSpec(memory_space=pl.ANY)] * 5,
     )(feats, cond, null_field, cotangent, drop_flags)
     slots = exchange(slots, LON)
-    low, high = shift(bottom, LAT, 1, False), shift(top, LAT, -1, False)
+    inner, outer = swap(inner, LAT, 0, False), swap(outer, LAT, 1, False)
     wide_cot, slots = call(
         functools.partial(merge_body, cells_local),
         (
@@ -482,14 +487,13 @@
             array((lat_count, lat_slot, LANES), BF16),
         ),
     )(slots, cotangent)
-    slots, low, high = lax.optimization_barrier((slots, low, high))
+    slots, inner, outer = lax.optimization_barrier((slots, inner, outer))
     slots = exchange(slots, LAT)
     half = samples * (tile_rows + 2)
     edges, passed = call(
         columns_body, (array((SLOT, LANES), BF16), array((-(-half // 8) * 8, LANES), BF16))
-    )(mixed, low, high)
-    pairs = [(i, (i + 1) % lon_count) for i in range(1, lon_count, 2)]
-    passed = lax.ppermute(passed, LON, pairs + [(target, source) for source, target in pairs])
+    )(mixed, inner, outer)
+    passed = swap(passed, LON, 1, True)
 
     taps_shape = (samples, 3, 3 * channels, channels)
     gamma, beta, style, column, demod, power, emb_full, back_taps, fore_taps = call(
@@ -509,7 +513,6 @@
     spread = pltpu.VMEM((tile_rows + 2, tile_cols + 2, channels), F32)
     shifted = pltpu.VMEM(((tile_rows + 2) * tile_cols, 3 * channels), BF16)
     flat = (samples, tile_rows * tile_cols, channels)
-    near = pl.BlockSpec(memory_space=pltpu.VMEM)
     stats, grad_pre, payload = call(
         functools.partial(sums_body, cells_local * lon_count, cells_per_group),
         (
@@ -522,12 +525,10 @@
             spread,
             shifted,
             pltpu.VMEM((9 * channels, channels), F32),
-            pltpu.VMEM(flat, F32),
-            pltpu.SemaphoreType.DMA((samples,)),
         ),
-        out_specs=(near, pl.BlockSpec(memory_space=pltpu.HBM), near),
+        room=52,
     )(
-        slots, mixed, edges, wide_cot, low, high, gamma, beta, back_taps, column, demod, taps
+        slots, mixed, edges, wide_cot, inner, outer, gamma, beta, back_taps, column, demod, taps
     )
 
     near_count = lax.axis_size(NEAR)
@@ -541,7 +542,7 @@
     slots = call(sum_body, shard)(exchange(slots, LAT))
     payload = lax.all_gather(exchange(slots, NEAR), "c")
     block_out = call(forward_body, array(feats.shape, BF16), (spread, shifted))(
-        mixed, low, high, other, passed, fore_taps, stats, gamma, beta
+        mixed, inner, outer, other, passed, fore_taps, stats, gamma, beta
     )
 
     grad_feats, grad_weight, grad_style, grad_gamma, grad_beta = call(

time: 101 us -> 100 us (0.990)
  starting transfers between devices: 37.4 us -> 35.3 us
  waiting for transfers between devices: 13.7 us -> 15.4 us
    all_to_all x3, waiting for transfers between devices: 13.7 us -> 15.4 us  [exchange(): return lax.all_to_all(block, axes, 0, 0)]
    ppermute x3, starting transfers between devices: 9.97 us -> 8.42 us  [swap(): lax.ppermute(block, axes, pairs + [(target, source) for source, target in...]
where the time goes in v12:
time: 100 us; the launch traced here: 99.7 us
  blocking collectives  37.5 us (38%)
  starting transfers between devices  35.3 us (35%)
  waiting for transfers between devices  15.4 us (15%)
  Pallas kernels  9.89 us (10%)
    all_to_all x3, starting transfers between devices, exchange(): return lax.all_to_all(block, axes, 0, 0)  26.9 us
    all_to_all x2, blocking collectives, exchange(): return lax.all_to_all(block, axes, 0, 0)  26.8 us
    all_to_all x3, waiting for transfers between devices, exchange(): return lax.all_to_all(block, axes, 0, 0)  15.4 us
    ppermute x3, starting transfers between devices, swap(): lax.ppermute(block, axes, pairs + [(target, source) for source, target in...  8.42 us
    all_gather x1, blocking collectives, on_device(): payload = lax.all_gather(exchange(slots, NEAR), 'c')  5.61 us
    all_gather x1, blocking collectives, on_device(): lax.all_gather(payload, 'c')  5.11 us
    pallas_call x1, Pallas kernels, on_device(): call(mix_body, (array(feats.shape, BF16), array((lon_count, lon_slot, LAN...  2.59 us
    pallas_call x1, Pallas kernels, on_device(): call(functools.partial(sums_body, cells_local * lon_count, cells_per_grou...  2.26 us
  transfers between devices with their start and end apart: 6, of which 3 were waited for; matrix products, arithmetic and copies ran while one was open for 0% of the time, Pallas kernels for 5%

profile of v12, /device:TPU:1, one launch (start us, length us, event | category | flops | bytes accessed | tf_op | source)
XLA Modules:
  0.0 99.7 jit_solution(6131105572758669608)
XLA Ops:
  0.6 0.0 copy-start
  0.6 2.6 %shard_map.145 = (bf16[2,8,32,128]{3,2,1,0:T(8,128)(2,1)}, bf16[32,24,128]{2,1,0:T(8,128)(2,1)}, bf16[2,2,32,128]{3,2,1,0:T(8,128)(2,1)}, bf16[2,2,32,128]{3,2,1,0:T(8,128)(2,1)}) custom-call(bf16[2,8,32,128]{3,2,1,0:T(8,128)(2,1)} %feats_in.1, bf16[2,8,32,128]{3,2,1,0:T(8,128)(2,1)} %cond_in.1, bf16[8,32,128]{2,1,0:T(8,128)(2,1)} %null_in.1, ...), custom_call_target="tpu_custom_call" | custom-call | tf_op jit(solution)/shard_map/pallas_call | solution.py:467
  3.2 0.0 copy-start.9
  3.3 0.0 copy-start.8
  3.3 0.0 copy-start.3
  3.3 10.7 %all-to-all-start = ((bf16[32,24,128]{2,1,0:T(8,128)(2,1)}), bf16[32,24,128]{2,1,0:T(8,128)(2,1)S(1)}, u32[]{:S(2)}, u32[]{:S(2)}) async-start(bf16[32,24,128]{2,1,0:T(8,128)(2,1)} %get-tuple-element.39), calls=%async_computation | async-start | bytes 393216 | tf_op jit(solution)/shard_map/all_to_all | solution.py:36
  14.0 0.0 copy-start.4
  14.0 0.0 copy-done.9
  14.0 3.3 %collective-permute-start = (bf16[2,2,32,128]{3,2,1,0:T(8,128)(2,1)S(1)}, bf16[2,2,32,128]{3,2,1,0:T(8,128)(2,1)S(1)}, u32[]{:S(2)}, u32[]{:S(2)}) collective-permute-start(bf16[2,2,32,128]{3,2,1,0:T(8,128)(2,1)S(1)} %copy-done.9), channel_id=1, source_target_pairs={{0,32},{64,96},{128,160},{192,224},{256,288},{320,352},{384,416},{... | collective-permute-start | bytes 98312 | tf_op jit(solution)/shard_map/ppermute | solution.py:26
  17.3 0.0 copy-done.8
  17.3 0.7 collective-permute-start.1
  18.0 6.3 %all-to-all-done.slots = bf16[32,24,128]{2,1,0:T(8,128)(2,1)S(1)} async-done(((bf16[32,24,128]{2,1,0:T(8,128)(2,1)}), bf16[32,24,128]{2,1,0:T(8,128)(2,1)S(1)}, u32[]{:S(2)}, u32[]{:S(2)}) %all-to-all-start) | async-done | bytes 196640 | tf_op jit(solution)/shard_map/all_to_all | solution.py:36
  24.2 0.0 copy-done.3
  24.2 0.7 shard_map.146
  25.0 0.0 collective-permute-done.inner
  25.0 0.0 collective-permute-done.1.outer
  25.0 11.6 %all-to-all-start.1 = ((bf16[16,16,128]{2,1,0:T(8,128)(2,1)}), bf16[16,16,128]{2,1,0:T(8,128)(2,1)S(1)}, u32[]{:S(2)}, u32[]{:S(2)}) async-start(bf16[16,16,128]{2,1,0:T(8,128)(2,1)} %get-tuple-element.45), calls=%async_computation.1 | async-start | bytes 131072 | tf_op jit(solution)/shard_map/all_to_all | solution.py:36
  36.6 0.0 copy-start.5
  36.7 0.0 copy-start.6
  36.7 0.0 copy-start.7
  36.7 0.0 copy-done
  36.7 0.0 copy-done.4
  36.7 0.6 copy-done.5
  37.3 0.0 copy-done.6
  37.3 0.0 copy-done.7
  37.3 0.0 copy-start.2
  37.3 0.8 shard_map.148
  38.1 0.1 copy-done.2
  38.3 4.5 %collective-permute-start.2 = (bf16[24,128]{1,0:T(8,128)(2,1)S(1)}, bf16[24,128]{1,0:T(8,128)(2,1)S(1)}, u32[]{:S(2)}, u32[]{:S(2)}) collective-permute-start(bf16[24,128]{1,0:T(8,128)(2,1)S(1)} %get-tuple-element.56), channel_id=1, source_target_pairs={{1,2},{3,4},{5,6},{7,8},{9,10},{11,12},{13,14},{15,16},{17,18},{19... | collective-permute-start | bytes 18440 | tf_op jit(solution)/shard_map/ppermute | solution.py:26
  42.8 2.9 %all-to-all-done.1.slots = bf16[16,16,128]{2,1,0:T(8,128)(2,1)S(1)} async-done(((bf16[16,16,128]{2,1,0:T(8,128)(2,1)}), bf16[16,16,128]{2,1,0:T(8,128)(2,1)S(1)}, u32[]{:S(2)}, u32[]{:S(2)}) %all-to-all-start.1) | async-done | bytes 65568 | tf_op jit(solution)/shard_map/all_to_all | solution.py:36
  45.7 2.3 %shard_map.149 = (f32[4,128]{1,0:T(4,128)S(1)}, f32[2,256,128]{2,1,0:T(8,128)S(1)}, bf16[33,40,128]{2,1,0:T(8,128)(2,1)S(1)}) custom-call(bf16[16,16,128]{2,1,0:T(8,128)(2,1)S(1)} %all-to-all-done.1.slots, bf16[2,8,32,128]{3,2,1,0:T(8,128)(2,1)S(1)} %copy-done.2, bf16[40,128]{1,0:T(8,128)(2,1)S(1)} %get-tuple-element.46.edges, ...), custom_call_target="tpu_custom_call" | custom-call | tf_op jit(solution)/shard_map/pallas_call | solution.py:516
  47.9 5.1 %all-gather = bf16[66,40,128]{2,1,0:T(8,128)(2,1)S(1)} all-gather(bf16[33,40,128]{2,1,0:T(8,128)(2,1)S(1)} %get-tuple-element.53), channel_id=2, replica_groups=mesh['zh'=4,'x'=4,'zl'=2,'y'=8,'c'=2] {'c'}, dimensions={0}, use_global_device_ids=true | all-gather | bytes 1013760 | tf_op jit(solution)/shard_map/all_gather | solution.py:537
  53.0 0.1 shard_map.150
  53.2 0.0 collective-permute-done.2.passed
  53.2 13.8 %all_to_all.25.slots = bf16[16,40,128]{2,1,0:T(8,128)(2,1)S(1)} all-to-all(bf16[16,40,128]{2,1,0:T(8,128)(2,1)S(1)} %get-tuple-element.60), channel_id=1, replica_groups=mesh['zh'=4,'x'=4,'zl'=2,'y'=8,'c'=2] {'zl','y'}, dimensions={0} | all-to-all | bytes 327680 | tf_op jit(solution)/shard_map/all_to_all | solution.py:36
  67.0 0.1 shard_map.152
  67.1 12.9 %all_to_all.26.slots = bf16[16,40,128]{2,1,0:T(8,128)(2,1)S(1)} all-to-all(bf16[16,40,128]{2,1,0:T(8,128)(2,1)S(1)} %shard_map.152), channel_id=1, replica_groups=mesh['zh'=4,'x'=4,'zl'=2,'y'=8,'c'=2] {'zh','x'}, dimensions={0} | all-to-all | bytes 327680 | tf_op jit(solution)/shard_map/all_to_all | solution.py:36
  80.0 0.8 shard_map.153
  80.8 4.5 %all-to-all-start.4 = ((bf16[16,40,128]{2,1,0:T(8,128)(2,1)}), bf16[16,40,128]{2,1,0:T(8,128)(2,1)S(1)}, u32[]{:S(2)}, u32[]{:S(2)}) async-start(bf16[16,40,128]{2,1,0:T(8,128)(2,1)} %shard_map.153), calls=%async_computation.4 | async-start | bytes 327680 | tf_op jit(solution)/shard_map/all_to_all | solution.py:36
  85.3 0.0 copy-start.1
  85.3 1.3 %shard_map.151 = bf16[2,8,32,128]{3,2,1,0:T(8,128)(2,1)} custom-call(bf16[2,8,32,128]{3,2,1,0:T(8,128)(2,1)S(1)} %copy-done.2, bf16[2,2,32,128]{3,2,1,0:T(8,128)(2,1)S(1)} %collective-permute-done.inner, bf16[2,2,32,128]{3,2,1,0:T(8,128)(2,1)S(1)} %collective-permute-done.1.outer, bf16[40,128]{1,0:T(8,128)(2,1)S(1)} %get-tuple-element.54.other, ...), custom_call_target="tpu_custom_call" | custom-call | tf_op jit(solution)/shard_map/pallas_call | solution.py:544
  86.6 6.2 %all-to-all-done.4 = bf16[16,40,128]{2,1,0:T(8,128)(2,1)S(1)} async-done(((bf16[16,40,128]{2,1,0:T(8,128)(2,1)}), bf16[16,40,128]{2,1,0:T(8,128)(2,1)S(1)}, u32[]{:S(2)}, u32[]{:S(2)}) %all-to-all-start.4) | async-done | bytes 163872 | tf_op jit(solution)/shard_map/all_to_all | solution.py:36
  92.9 5.6 %all-gather.1.gathered = bf16[32,40,128]{2,1,0:T(8,128)(2,1)S(1)} all-gather(bf16[16,40,128]{2,1,0:T(8,128)(2,1)S(1)} %all-to-all-done.4), channel_id=3, replica_groups=mesh['zh'=4,'x'=4,'zl'=2,'y'=8,'c'=2] {'c'}, dimensions={0}, use_global_device_ids=true | all-gather | bytes 491520 | tf_op jit(solution)/shard_map/all_gather | solution.py:543
  98.5 0.0 copy-done.1
  98.5 1.2 %shard_map.154 = (bf16[2,8,32,128]{3,2,1,0:T(8,128)(2,1)}, f32[9,128,128]{2,1,0:T(8,128)}, f32[512,128]{1,0:T(8,128)}, f32[1,128]{1,0:T(1,128)}, f32[1,128]{1,0:T(1,128)}) custom-call(bf16[32,40,128]{2,1,0:T(8,128)(2,1)S(1)} %all-gather.1.gathered, f32[4,128]{1,0:T(4,128)S(1)} %get-tuple-element.59.stats, bf16[2,8,32,128]{3,2,1,0:T(8,128)(2,1)S(1)} %copy-done.2, ...), custom_call_target="tpu_custom_call" | custom-call | tf_op jit(solution)/shard_map/pallas_call | solution.py:548
  (1 shorter events, 0.0 us)
Async XLA Ops:
  0.6 36.0 %copy-start = (f32[3,3,128,128]{3,2,1,0:T(8,128)S(1)}, f32[3,3,128,128]{3,2,1,0:T(8,128)}, u32[]{:S(2)}) copy-start(f32[3,3,128,128]{3,2,1,0:T(8,128)} %param.16) | copy-start | bytes 1769476
  3.2 10.8 %copy-start.9 = (bf16[2,2,32,128]{3,2,1,0:T(8,128)(2,1)S(1)}, bf16[2,2,32,128]{3,2,1,0:T(8,128)(2,1)}, u32[]{:S(2)}) copy-start(bf16[2,2,32,128]{3,2,1,0:T(8,128)(2,1)} %get-tuple-element.41) | copy-start | bytes 98308
  3.3 14.0 %copy-start.8 = (bf16[2,2,32,128]{3,2,1,0:T(8,128)(2,1)S(1)}, bf16[2,2,32,128]{3,2,1,0:T(8,128)(2,1)}, u32[]{:S(2)}) copy-start(bf16[2,2,32,128]{3,2,1,0:T(8,128)(2,1)} %get-tuple-element.42) | copy-start | bytes 98308
  3.3 21.0 %copy-start.3 = (bf16[2,8,32,128]{3,2,1,0:T(8,128)(2,1)S(1)}, bf16[2,8,32,128]{3,2,1,0:T(8,128)(2,1)}, u32[]{:S(2)}) copy-start(bf16[2,8,32,128]{3,2,1,0:T(8,128)(2,1)} %cotangent.1) | copy-start | bytes 393220
  3.3 21.0 %all-to-all-start = ((bf16[32,24,128]{2,1,0:T(8,128)(2,1)}), bf16[32,24,128]{2,1,0:T(8,128)(2,1)S(1)}, u32[]{:S(2)}, u32[]{:S(2)}) async-start(bf16[32,24,128]{2,1,0:T(8,128)(2,1)} %get-tuple-element.39), calls=%async_computation | async-start | bytes 393216 | tf_op jit(solution)/shard_map/all_to_all | solution.py:36
  14.0 22.7 %copy-start.4 = (f32[512,128]{1,0:T(8,128)S(1)}, f32[512,128]{1,0:T(8,128)}, u32[]{:S(2)}) copy-start(f32[512,128]{1,0:T(8,128)} %style_weight.1) | copy-start | bytes 786436
  14.0 11.0 %collective-permute-start = (bf16[2,2,32,128]{3,2,1,0:T(8,128)(2,1)S(1)}, bf16[2,2,32,128]{3,2,1,0:T(8,128)(2,1)S(1)}, u32[]{:S(2)}, u32[]{:S(2)}) collective-permute-start(bf16[2,2,32,128]{3,2,1,0:T(8,128)(2,1)S(1)} %copy-done.9), channel_id=1, source_target_pairs={{0,32},{64,96},{128,160},{192,224},{256,288},{320,352},{384,416},{... | collective-permute-start | bytes 98312 | tf_op jit(solution)/shard_map/ppermute | solution.py:26
  17.3 7.7 %collective-permute-start.1 = (bf16[2,2,32,128]{3,2,1,0:T(8,128)(2,1)S(1)}, bf16[2,2,32,128]{3,2,1,0:T(8,128)(2,1)S(1)}, u32[]{:S(2)}, u32[]{:S(2)}) collective-permute-start(bf16[2,2,32,128]{3,2,1,0:T(8,128)(2,1)S(1)} %copy-done.8), channel_id=1, source_target_pairs={{32,64},{96,128},{160,192},{224,256},{288,320},{352,384},{416,448}... | collective-permute-start | bytes 98312 | tf_op jit(solution)/shard_map/ppermute | solution.py:26
  25.0 20.7 %all-to-all-start.1 = ((bf16[16,16,128]{2,1,0:T(8,128)(2,1)}), bf16[16,16,128]{2,1,0:T(8,128)(2,1)S(1)}, u32[]{:S(2)}, u32[]{:S(2)}) async-start(bf16[16,16,128]{2,1,0:T(8,128)(2,1)} %get-tuple-element.45), calls=%async_computation.1 | async-start | bytes 131072 | tf_op jit(solution)/shard_map/all_to_all | solution.py:36
  36.6 0.7 copy-start.5
  36.7 0.7 copy-start.6
  36.7 0.7 copy-start.7
  37.3 0.9 copy-start.2
  38.3 14.9 %collective-permute-start.2 = (bf16[24,128]{1,0:T(8,128)(2,1)S(1)}, bf16[24,128]{1,0:T(8,128)(2,1)S(1)}, u32[]{:S(2)}, u32[]{:S(2)}) collective-permute-start(bf16[24,128]{1,0:T(8,128)(2,1)S(1)} %get-tuple-element.56), channel_id=1, source_target_pairs={{1,2},{3,4},{5,6},{7,8},{9,10},{11,12},{13,14},{15,16},{17,18},{19... | collective-permute-start | bytes 18440 | tf_op jit(solution)/shard_map/ppermute | solution.py:26
  80.8 12.1 %all-to-all-start.4 = ((bf16[16,40,128]{2,1,0:T(8,128)(2,1)}), bf16[16,40,128]{2,1,0:T(8,128)(2,1)S(1)}, u32[]{:S(2)}, u32[]{:S(2)}) async-start(bf16[16,40,128]{2,1,0:T(8,128)(2,1)} %shard_map.153), calls=%async_computation.4 | async-start | bytes 327680 | tf_op jit(solution)/shard_map/all_to_all | solution.py:36
  85.3 13.2 %copy-start.1 = (f32[3,3,128,128]{3,2,1,0:T(8,128)S(1)}, f32[3,3,128,128]{3,2,1,0:T(8,128)}, u32[]{:S(2)}) copy-start(f32[3,3,128,128]{3,2,1,0:T(8,128)} %param.16) | copy-start | bytes 1769476

commit v13 on v12

--- a/solution.py
+++ b/solution.py
@@ -487,7 +487,7 @@
             array((lat_count, lat_slot, LANES), BF16),
         ),
     )(slots, cotangent)
-    slots, inner, outer = lax.optimization_barrier((slots, inner, outer))
+    slots, inner = lax.optimization_barrier((slots, inner))
     slots = exchange(slots, LAT)
     half = samples * (tile_rows + 2)
     edges, passed = call(
@@ -526,7 +526,6 @@
             shifted,
             pltpu.VMEM((9 * channels, channels), F32),
         ),
-        room=52,
     )(
         slots, mixed, edges, wide_cot, inner, outer, gamma, beta, back_taps, column, demod, taps
     )

time: 100 us -> 105 us (1.050)
  blocking collectives: 37.5 us -> 42.8 us
  Pallas kernels: 9.89 us -> 8.81 us
    all_to_all x2, blocking collectives: 26.8 us -> 32 us  [exchange(): return lax.all_to_all(block, axes, 0, 0)]
    pallas_call x1, Pallas kernels: 2.26 us -> 1.19 us  [on_device(): call(functools.partial(sums_body, cells_local * lon_count, cells_per_grou...]
  transfers between devices with their start and end apart: 6 -> 6, of which waited for: 3 -> 3; matrix products, arithmetic and copies ran while one was open for 0% -> 0% of each run, Pallas kernels for 5% -> 4%
where the time goes in v13:
time: 105 us; the launch traced here: 104 us
  blocking collectives  42.8 us (41%)
  starting transfers between devices  35.3 us (34%)
  waiting for transfers between devices  15.4 us (15%)
  Pallas kernels  8.81 us (8%)
    all_to_all x2, blocking collectives, exchange(): return lax.all_to_all(block, axes, 0, 0)  32 us
    all_to_all x3, starting transfers between devices, exchange(): return lax.all_to_all(block, axes, 0, 0)  27 us
    all_to_all x3, waiting for transfers between devices, exchange(): return lax.all_to_all(block, axes, 0, 0)  15.4 us
    ppermute x3, starting transfers between devices, swap(): lax.ppermute(block, axes, pairs + [(target, source) for source, target in...  8.27 us
    all_gather x1, blocking collectives, on_device(): payload = lax.all_gather(exchange(slots, NEAR), 'c')  5.61 us
    all_gather x1, blocking collectives, on_device(): lax.all_gather(payload, 'c')  5.19 us
    pallas_call x1, Pallas kernels, on_device(): call(mix_body, (array(feats.shape, BF16), array((lon_count, lon_slot, LAN...  2.59 us
  transfers between devices with their start and end apart: 6, of which 3 were waited for; matrix products, arithmetic and copies ran while one was open for 0% of the time, Pallas kernels for 4%

profile of v13, /device:TPU:1, one launch (start us, length us, event | category | flops | bytes accessed | tf_op | source)
XLA Modules:
  0.0 104.0 jit_solution(8653422347845244917)
XLA Ops:
  0.6 0.0 copy-start
  0.6 2.6 %shard_map.145 = (bf16[2,8,32,128]{3,2,1,0:T(8,128)(2,1)}, bf16[32,24,128]{2,1,0:T(8,128)(2,1)}, bf16[2,2,32,128]{3,2,1,0:T(8,128)(2,1)}, bf16[2,2,32,128]{3,2,1,0:T(8,128)(2,1)}) custom-call(bf16[2,8,32,128]{3,2,1,0:T(8,128)(2,1)} %feats_in.1, bf16[2,8,32,128]{3,2,1,0:T(8,128)(2,1)} %cond_in.1, bf16[8,32,128]{2,1,0:T(8,128)(2,1)} %null_in.1, ...), custom_call_target="tpu_custom_call" | custom-call | tf_op jit(solution)/shard_map/pallas_call | solution.py:467
  3.2 0.0 copy-start.8
  3.3 0.0 copy-start.2
  3.3 10.7 %all-to-all-start = ((bf16[32,24,128]{2,1,0:T(8,128)(2,1)}), bf16[32,24,128]{2,1,0:T(8,128)(2,1)S(1)}, u32[]{:S(2)}, u32[]{:S(2)}) async-start(bf16[32,24,128]{2,1,0:T(8,128)(2,1)} %get-tuple-element.38), calls=%async_computation | async-start | bytes 393216 | tf_op jit(solution)/shard_map/all_to_all | solution.py:36
  14.0 0.0 copy-start.3
  14.0 0.0 copy-done.8
  14.0 3.3 %collective-permute-start = (bf16[2,2,32,128]{3,2,1,0:T(8,128)(2,1)S(1)}, bf16[2,2,32,128]{3,2,1,0:T(8,128)(2,1)S(1)}, u32[]{:S(2)}, u32[]{:S(2)}) collective-permute-start(bf16[2,2,32,128]{3,2,1,0:T(8,128)(2,1)S(1)} %copy-done.8), channel_id=1, source_target_pairs={{0,32},{64,96},{128,160},{192,224},{256,288},{320,352},{384,416},{... | collective-permute-start | bytes 98312 | tf_op jit(solution)/shard_map/ppermute | solution.py:26
  17.3 6.9 %all-to-all-done.slots = bf16[32,24,128]{2,1,0:T(8,128)(2,1)S(1)} async-done(((bf16[32,24,128]{2,1,0:T(8,128)(2,1)}), bf16[32,24,128]{2,1,0:T(8,128)(2,1)S(1)}, u32[]{:S(2)}, u32[]{:S(2)}) %all-to-all-start) | async-done | bytes 196640 | tf_op jit(solution)/shard_map/all_to_all | solution.py:36
  24.2 0.0 copy-done.2
  24.2 0.7 shard_map.146
  24.9 0.0 collective-permute-done.inner
  24.9 0.0 copy-start.7
  24.9 11.8 %all-to-all-start.1 = ((bf16[16,16,128]{2,1,0:T(8,128)(2,1)}), bf16[16,16,128]{2,1,0:T(8,128)(2,1)S(1)}, u32[]{:S(2)}, u32[]{:S(2)}) async-start(bf16[16,16,128]{2,1,0:T(8,128)(2,1)} %get-tuple-element.43), calls=%async_computation.1 | async-start | bytes 131072 | tf_op jit(solution)/shard_map/all_to_all | solution.py:36
  36.8 0.0 copy-start.4
  36.8 0.0 copy-done.7
  36.8 0.7 collective-permute-start.1
  37.5 0.0 copy-start.5
  37.5 0.0 copy-start.6
  37.5 0.0 copy-done
  37.5 0.0 copy-done.3
  37.5 0.0 copy-done.4
  37.5 0.6 copy-done.5
  38.1 0.0 copy-done.6
  38.1 0.0 copy-start.1
  38.1 0.8 shard_map.148
  38.9 0.0 collective-permute-done.1.outer
  38.9 0.1 copy-done.1
  39.1 4.4 %collective-permute-start.2 = (bf16[24,128]{1,0:T(8,128)(2,1)S(1)}, bf16[24,128]{1,0:T(8,128)(2,1)S(1)}, u32[]{:S(2)}, u32[]{:S(2)}) collective-permute-start(bf16[24,128]{1,0:T(8,128)(2,1)S(1)} %get-tuple-element.54), channel_id=1, source_target_pairs={{1,2},{3,4},{5,6},{7,8},{9,10},{11,12},{13,14},{15,16},{17,18},{19... | collective-permute-start | bytes 18440 | tf_op jit(solution)/shard_map/ppermute | solution.py:26
  43.4 2.3 %all-to-all-done.1.slots = bf16[16,16,128]{2,1,0:T(8,128)(2,1)S(1)} async-done(((bf16[16,16,128]{2,1,0:T(8,128)(2,1)}), bf16[16,16,128]{2,1,0:T(8,128)(2,1)S(1)}, u32[]{:S(2)}, u32[]{:S(2)}) %all-to-all-start.1) | async-done | bytes 65568 | tf_op jit(solution)/shard_map/all_to_all | solution.py:36
  45.7 1.2 %shard_map.149 = (f32[4,128]{1,0:T(4,128)S(1)}, f32[2,256,128]{2,1,0:T(8,128)S(1)}, bf16[33,40,128]{2,1,0:T(8,128)(2,1)S(1)}) custom-call(bf16[16,16,128]{2,1,0:T(8,128)(2,1)S(1)} %all-to-all-done.1.slots, bf16[2,8,32,128]{3,2,1,0:T(8,128)(2,1)S(1)} %copy-done.1, bf16[40,128]{1,0:T(8,128)(2,1)S(1)} %get-tuple-element.44.edges, ...), custom_call_target="tpu_custom_call" | custom-call | tf_op jit(solution)/shard_map/pallas_call | solution.py:516
  46.9 5.2 %all-gather = bf16[66,40,128]{2,1,0:T(8,128)(2,1)S(1)} all-gather(bf16[33,40,128]{2,1,0:T(8,128)(2,1)S(1)} %get-tuple-element.51), channel_id=2, replica_groups=mesh['zh'=4,'x'=4,'zl'=2,'y'=8,'c'=2] {'c'}, dimensions={0}, use_global_device_ids=true | all-gather | bytes 1013760 | tf_op jit(solution)/shard_map/all_gather | solution.py:536
  52.1 0.1 shard_map.150
  52.2 0.0 collective-permute-done.2.passed
  52.2 10.1 %all_to_all.25.slots = bf16[16,40,128]{2,1,0:T(8,128)(2,1)S(1)} all-to-all(bf16[16,40,128]{2,1,0:T(8,128)(2,1)S(1)} %get-tuple-element.58), channel_id=1, replica_groups=mesh['zh'=4,'x'=4,'zl'=2,'y'=8,'c'=2] {'zl','y'}, dimensions={0} | all-to-all | bytes 327680 | tf_op jit(solution)/shard_map/all_to_all | solution.py:36
  62.3 0.1 shard_map.152
  62.4 21.9 %all_to_all.26.slots = bf16[16,40,128]{2,1,0:T(8,128)(2,1)S(1)} all-to-all(bf16[16,40,128]{2,1,0:T(8,128)(2,1)S(1)} %shard_map.152), channel_id=1, replica_groups=mesh['zh'=4,'x'=4,'zl'=2,'y'=8,'c'=2] {'zh','x'}, dimensions={0} | all-to-all | bytes 327680 | tf_op jit(solution)/shard_map/all_to_all | solution.py:36
  84.3 0.8 shard_map.153
  85.1 4.5 %all-to-all-start.4 = ((bf16[16,40,128]{2,1,0:T(8,128)(2,1)}), bf16[16,40,128]{2,1,0:T(8,128)(2,1)S(1)}, u32[]{:S(2)}, u32[]{:S(2)}) async-start(bf16[16,40,128]{2,1,0:T(8,128)(2,1)} %shard_map.153), calls=%async_computation.4 | async-start | bytes 327680 | tf_op jit(solution)/shard_map/all_to_all | solution.py:36
  89.6 1.3 %shard_map.151 = bf16[2,8,32,128]{3,2,1,0:T(8,128)(2,1)} custom-call(bf16[2,8,32,128]{3,2,1,0:T(8,128)(2,1)S(1)} %copy-done.1, bf16[2,2,32,128]{3,2,1,0:T(8,128)(2,1)S(1)} %collective-permute-done.inner, bf16[2,2,32,128]{3,2,1,0:T(8,128)(2,1)S(1)} %collective-permute-done.1.outer, bf16[40,128]{1,0:T(8,128)(2,1)S(1)} %get-tuple-element.52.other, ...), custom_call_target="tpu_custom_call" | custom-call | tf_op jit(solution)/shard_map/pallas_call | solution.py:543
  90.9 6.2 %all-to-all-done.4 = bf16[16,40,128]{2,1,0:T(8,128)(2,1)S(1)} async-done(((bf16[16,40,128]{2,1,0:T(8,128)(2,1)}), bf16[16,40,128]{2,1,0:T(8,128)(2,1)S(1)}, u32[]{:S(2)}, u32[]{:S(2)}) %all-to-all-start.4) | async-done | bytes 163872 | tf_op jit(solution)/shard_map/all_to_all | solution.py:36
  97.1 5.6 %all-gather.1.gathered = bf16[32,40,128]{2,1,0:T(8,128)(2,1)S(1)} all-gather(bf16[16,40,128]{2,1,0:T(8,128)(2,1)S(1)} %all-to-all-done.4), channel_id=3, replica_groups=mesh['zh'=4,'x'=4,'zl'=2,'y'=8,'c'=2] {'c'}, dimensions={0}, use_global_device_ids=true | all-gather | bytes 491520 | tf_op jit(solution)/shard_map/all_gather | solution.py:542
  102.7 1.2 %shard_map.154 = (bf16[2,8,32,128]{3,2,1,0:T(8,128)(2,1)}, f32[9,128,128]{2,1,0:T(8,128)}, f32[512,128]{1,0:T(8,128)}, f32[1,128]{1,0:T(1,128)}, f32[1,128]{1,0:T(1,128)}) custom-call(bf16[32,40,128]{2,1,0:T(8,128)(2,1)S(1)} %all-gather.1.gathered, f32[4,128]{1,0:T(4,128)S(1)} %get-tuple-element.57.stats, bf16[2,8,32,128]{3,2,1,0:T(8,128)(2,1)S(1)} %copy-done.1, ...), custom_call_target="tpu_custom_call" | custom-call | tf_op jit(solution)/shard_map/pallas_call | solution.py:547
  (1 shorter events, 0.0 us)
Async XLA Ops:
  0.6 36.8 %copy-start = (f32[3,3,128,128]{3,2,1,0:T(8,128)S(1)}, f32[3,3,128,128]{3,2,1,0:T(8,128)}, u32[]{:S(2)}) copy-start(f32[3,3,128,128]{3,2,1,0:T(8,128)} %param.16) | copy-start | bytes 1769476
  3.2 10.8 %copy-start.8 = (bf16[2,2,32,128]{3,2,1,0:T(8,128)(2,1)S(1)}, bf16[2,2,32,128]{3,2,1,0:T(8,128)(2,1)}, u32[]{:S(2)}) copy-start(bf16[2,2,32,128]{3,2,1,0:T(8,128)(2,1)} %get-tuple-element.40) | copy-start | bytes 98308
  3.3 20.9 %copy-start.2 = (bf16[2,8,32,128]{3,2,1,0:T(8,128)(2,1)S(1)}, bf16[2,8,32,128]{3,2,1,0:T(8,128)(2,1)}, u32[]{:S(2)}) copy-start(bf16[2,8,32,128]{3,2,1,0:T(8,128)(2,1)} %cotangent.1) | copy-start | bytes 393220
  3.3 20.9 %all-to-all-start = ((bf16[32,24,128]{2,1,0:T(8,128)(2,1)}), bf16[32,24,128]{2,1,0:T(8,128)(2,1)S(1)}, u32[]{:S(2)}, u32[]{:S(2)}) async-start(bf16[32,24,128]{2,1,0:T(8,128)(2,1)} %get-tuple-element.38), calls=%async_computation | async-start | bytes 393216 | tf_op jit(solution)/shard_map/all_to_all | solution.py:36
  14.0 23.5 %copy-start.3 = (f32[512,128]{1,0:T(8,128)S(1)}, f32[512,128]{1,0:T(8,128)}, u32[]{:S(2)}) copy-start(f32[512,128]{1,0:T(8,128)} %style_weight.1) | copy-start | bytes 786436
  14.0 10.9 %collective-permute-start = (bf16[2,2,32,128]{3,2,1,0:T(8,128)(2,1)S(1)}, bf16[2,2,32,128]{3,2,1,0:T(8,128)(2,1)S(1)}, u32[]{:S(2)}, u32[]{:S(2)}) collective-permute-start(bf16[2,2,32,128]{3,2,1,0:T(8,128)(2,1)S(1)} %copy-done.8), channel_id=1, source_target_pairs={{0,32},{64,96},{128,160},{192,224},{256,288},{320,352},{384,416},{... | collective-permute-start | bytes 98312 | tf_op jit(solution)/shard_map/ppermute | solution.py:26
  24.9 11.8 %copy-start.7 = (bf16[2,2,32,128]{3,2,1,0:T(8,128)(2,1)S(1)}, bf16[2,2,32,128]{3,2,1,0:T(8,128)(2,1)}, u32[]{:S(2)}) copy-start(bf16[2,2,32,128]{3,2,1,0:T(8,128)(2,1)} %get-tuple-element.42) | copy-start | bytes 98308
  24.9 20.8 %all-to-all-start.1 = ((bf16[16,16,128]{2,1,0:T(8,128)(2,1)}), bf16[16,16,128]{2,1,0:T(8,128)(2,1)S(1)}, u32[]{:S(2)}, u32[]{:S(2)}) async-start(bf16[16,16,128]{2,1,0:T(8,128)(2,1)} %get-tuple-element.43), calls=%async_computation.1 | async-start | bytes 131072 | tf_op jit(solution)/shard_map/all_to_all | solution.py:36
  36.8 0.7 copy-start.4
  36.8 2.1 %collective-permute-start.1 = (bf16[2,2,32,128]{3,2,1,0:T(8,128)(2,1)S(1)}, bf16[2,2,32,128]{3,2,1,0:T(8,128)(2,1)S(1)}, u32[]{:S(2)}, u32[]{:S(2)}) collective-permute-start(bf16[2,2,32,128]{3,2,1,0:T(8,128)(2,1)S(1)} %copy-done.7), channel_id=1, source_target_pairs={{32,64},{96,128},{160,192},{224,256},{288,320},{352,384},{416,448}... | collective-permute-start | bytes 98312 | tf_op jit(solution)/shard_map/ppermute | solution.py:26
  37.5 0.7 copy-start.5
  37.5 0.7 copy-start.6
  38.1 0.9 copy-start.1
  39.1 13.1 %collective-permute-start.2 = (bf16[24,128]{1,0:T(8,128)(2,1)S(1)}, bf16[24,128]{1,0:T(8,128)(2,1)S(1)}, u32[]{:S(2)}, u32[]{:S(2)}) collective-permute-start(bf16[24,128]{1,0:T(8,128)(2,1)S(1)} %get-tuple-element.54), channel_id=1, source_target_pairs={{1,2},{3,4},{5,6},{7,8},{9,10},{11,12},{13,14},{15,16},{17,18},{19... | collective-permute-start | bytes 18440 | tf_op jit(solution)/shard_map/ppermute | solution.py:26
  85.1 12.1 %all-to-all-start.4 = ((bf16[16,40,128]{2,1,0:T(8,128)(2,1)}), bf16[16,40,128]{2,1,0:T(8,128)(2,1)S(1)}, u32[]{:S(2)}, u32[]{:S(2)}) async-start(bf16[16,40,128]{2,1,0:T(8,128)(2,1)} %shard_map.153), calls=%async_computation.4 | async-start | bytes 327680 | tf_op jit(solution)/shard_map/all_to_all | solution.py:36

commit v14 on v13

--- a/solution.py
+++ b/solution.py
@@ -479,7 +479,7 @@
         in_specs=[pl.BlockSpec(memory_space=pl.ANY)] * 5,
     )(feats, cond, null_field, cotangent, drop_flags)
     slots = exchange(slots, LON)
-    inner, outer = swap(inner, LAT, 0, False), swap(outer, LAT, 1, False)
+    outer, inner = swap(outer, LAT, 1, False), swap(inner, LAT, 0, False)
     wide_cot, slots = call(
         functools.partial(merge_body, cells_local),
         (
@@ -487,7 +487,7 @@
             array((lat_count, lat_slot, LANES), BF16),
         ),
     )(slots, cotangent)
-    slots, inner = lax.optimization_barrier((slots, inner))
+    slots, outer, inner = lax.optimization_barrier((slots, outer, inner))
     slots = exchange(slots, LAT)
     half = samples * (tile_rows + 2)
     edges, passed = call(

time: 105 us -> 97.6 us (0.930)
  blocking collectives: 42.8 us -> 35.8 us
  starting transfers between devices: 35.3 us -> 37.8 us
  waiting for transfers between devices: 15.4 us -> 13 us
    all_to_all x2, blocking collectives: 32 us -> 24.9 us  [exchange(): return lax.all_to_all(block, axes, 0, 0)]
    all_to_all x3, waiting for transfers between devices: 15.4 us -> 13 us  [exchange(): return lax.all_to_all(block, axes, 0, 0)]
    ppermute x3, starting transfers between devices: 8.27 us -> 10.7 us  [swap(): lax.ppermute(block, axes, pairs + [(target, source) for source, target in...]
where the time goes in v14:
time: 97.6 us; the launch traced here: 97 us
  starting transfers between devices  37.8 us (39%)
  blocking collectives  35.8 us (37%)
  waiting for transfers between devices  13 us (13%)
  Pallas kernels  8.81 us (9%)
    all_to_all x3, starting transfers between devices, exchange(): return lax.all_to_all(block, axes, 0, 0)  27.1 us
    all_to_all x2, blocking collectives, exchange(): return lax.all_to_all(block, axes, 0, 0)  24.9 us
    all_to_all x3, waiting for transfers between devices, exchange(): return lax.all_to_all(block, axes, 0, 0)  13 us
    ppermute x3, starting transfers between devices, swap(): lax.ppermute(block, axes, pairs + [(target, source) for source, target in...  10.7 us
    all_gather x1, blocking collectives, on_device(): payload = lax.all_gather(exchange(slots, NEAR), 'c')  5.69 us
    all_gather x1, blocking collectives, on_device(): lax.all_gather(payload, 'c')  5.21 us
    pallas_call x1, Pallas kernels, on_device(): call(mix_body, (array(feats.shape, BF16), array((lon_count, lon_slot, LAN...  2.59 us
  transfers between devices with their start and end apart: 6, of which 3 were waited for; matrix products, arithmetic and copies ran while one was open for 0% of the time, Pallas kernels for 4%

profile of v14, /device:TPU:1, one launch (start us, length us, event | category | flops | bytes accessed | tf_op | source)
XLA Modules:
  0.0 97.0 jit_solution(12189059697021214576)
XLA Ops:
  0.6 0.0 copy-start
  0.6 2.6 %shard_map.145 = (bf16[2,8,32,128]{3,2,1,0:T(8,128)(2,1)}, bf16[32,24,128]{2,1,0:T(8,128)(2,1)}, bf16[2,2,32,128]{3,2,1,0:T(8,128)(2,1)}, bf16[2,2,32,128]{3,2,1,0:T(8,128)(2,1)}) custom-call(bf16[2,8,32,128]{3,2,1,0:T(8,128)(2,1)} %feats_in.1, bf16[2,8,32,128]{3,2,1,0:T(8,128)(2,1)} %cond_in.1, bf16[8,32,128]{2,1,0:T(8,128)(2,1)} %null_in.1, ...), custom_call_target="tpu_custom_call" | custom-call | tf_op jit(solution)/shard_map/pallas_call | solution.py:467
  3.2 0.0 copy-start.8
  3.3 0.0 copy-start.7
  3.3 0.0 copy-start.2
  3.3 10.7 %all-to-all-start = ((bf16[32,24,128]{2,1,0:T(8,128)(2,1)}), bf16[32,24,128]{2,1,0:T(8,128)(2,1)S(1)}, u32[]{:S(2)}, u32[]{:S(2)}) async-start(bf16[32,24,128]{2,1,0:T(8,128)(2,1)} %get-tuple-element.39), calls=%async_computation | async-start | bytes 393216 | tf_op jit(solution)/shard_map/all_to_all | solution.py:36
  14.0 0.0 copy-start.3
  14.0 0.0 copy-done.8
  14.0 0.8 collective-permute-start
  14.8 0.0 copy-done.7
  14.8 5.6 %collective-permute-start.1 = (bf16[2,2,32,128]{3,2,1,0:T(8,128)(2,1)S(1)}, bf16[2,2,32,128]{3,2,1,0:T(8,128)(2,1)S(1)}, u32[]{:S(2)}, u32[]{:S(2)}) collective-permute-start(bf16[2,2,32,128]{3,2,1,0:T(8,128)(2,1)S(1)} %copy-done.7), channel_id=1, source_target_pairs={{0,32},{64,96},{128,160},{192,224},{256,288},{320,352},{384,416},{... | collective-permute-start | bytes 98312 | tf_op jit(solution)/shard_map/ppermute | solution.py:26
  20.4 3.8 %all-to-all-done.slots = bf16[32,24,128]{2,1,0:T(8,128)(2,1)S(1)} async-done(((bf16[32,24,128]{2,1,0:T(8,128)(2,1)}), bf16[32,24,128]{2,1,0:T(8,128)(2,1)S(1)}, u32[]{:S(2)}, u32[]{:S(2)}) %all-to-all-start) | async-done | bytes 196640 | tf_op jit(solution)/shard_map/all_to_all | solution.py:36
  24.2 0.0 copy-done.2
  24.2 0.7 shard_map.146
  24.9 0.0 collective-permute-done.outer
  24.9 0.0 collective-permute-done.1.inner
  24.9 11.7 %all-to-all-start.1 = ((bf16[16,16,128]{2,1,0:T(8,128)(2,1)}), bf16[16,16,128]{2,1,0:T(8,128)(2,1)S(1)}, u32[]{:S(2)}, u32[]{:S(2)}) async-start(bf16[16,16,128]{2,1,0:T(8,128)(2,1)} %get-tuple-element.45), calls=%async_computation.1 | async-start | bytes 131072 | tf_op jit(solution)/shard_map/all_to_all | solution.py:36
  36.6 0.0 copy-start.4
  36.7 0.0 copy-start.5
  36.7 0.0 copy-start.6
  36.7 0.0 copy-done
  36.7 0.0 copy-done.3
  36.7 0.6 copy-done.4
  37.3 0.0 copy-done.5
  37.3 0.0 copy-done.6
  37.3 0.0 copy-start.1
  37.3 0.8 shard_map.148
  38.1 0.1 copy-done.1
  38.3 4.4 %collective-permute-start.2 = (bf16[24,128]{1,0:T(8,128)(2,1)S(1)}, bf16[24,128]{1,0:T(8,128)(2,1)S(1)}, u32[]{:S(2)}, u32[]{:S(2)}) collective-permute-start(bf16[24,128]{1,0:T(8,128)(2,1)S(1)} %get-tuple-element.56), channel_id=1, source_target_pairs={{1,2},{3,4},{5,6},{7,8},{9,10},{11,12},{13,14},{15,16},{17,18},{19... | collective-permute-start | bytes 18440 | tf_op jit(solution)/shard_map/ppermute | solution.py:26
  42.6 3.0 %all-to-all-done.1.slots = bf16[16,16,128]{2,1,0:T(8,128)(2,1)S(1)} async-done(((bf16[16,16,128]{2,1,0:T(8,128)(2,1)}), bf16[16,16,128]{2,1,0:T(8,128)(2,1)S(1)}, u32[]{:S(2)}, u32[]{:S(2)}) %all-to-all-start.1) | async-done | bytes 65568 | tf_op jit(solution)/shard_map/all_to_all | solution.py:36
  45.6 1.2 %shard_map.149 = (f32[4,128]{1,0:T(4,128)S(1)}, f32[2,256,128]{2,1,0:T(8,128)S(1)}, bf16[33,40,128]{2,1,0:T(8,128)(2,1)S(1)}) custom-call(bf16[16,16,128]{2,1,0:T(8,128)(2,1)S(1)} %all-to-all-done.1.slots, bf16[2,8,32,128]{3,2,1,0:T(8,128)(2,1)S(1)} %copy-done.1, bf16[40,128]{1,0:T(8,128)(2,1)S(1)} %get-tuple-element.46.edges, ...), custom_call_target="tpu_custom_call" | custom-call | tf_op jit(solution)/shard_map/pallas_call | solution.py:516
  46.8 5.2 %all-gather = bf16[66,40,128]{2,1,0:T(8,128)(2,1)S(1)} all-gather(bf16[33,40,128]{2,1,0:T(8,128)(2,1)S(1)} %get-tuple-element.53), channel_id=2, replica_groups=mesh['zh'=4,'x'=4,'zl'=2,'y'=8,'c'=2] {'c'}, dimensions={0}, use_global_device_ids=true | all-gather | bytes 1013760 | tf_op jit(solution)/shard_map/all_gather | solution.py:536
  52.0 0.1 shard_map.150
  52.1 0.0 collective-permute-done.2.passed
  52.1 12.3 %all_to_all.25.slots = bf16[16,40,128]{2,1,0:T(8,128)(2,1)S(1)} all-to-all(bf16[16,40,128]{2,1,0:T(8,128)(2,1)S(1)} %get-tuple-element.60), channel_id=1, replica_groups=mesh['zh'=4,'x'=4,'zl'=2,'y'=8,'c'=2] {'zl','y'}, dimensions={0} | all-to-all | bytes 327680 | tf_op jit(solution)/shard_map/all_to_all | solution.py:36
  64.4 0.1 shard_map.152
  64.5 12.6 %all_to_all.26.slots = bf16[16,40,128]{2,1,0:T(8,128)(2,1)S(1)} all-to-all(bf16[16,40,128]{2,1,0:T(8,128)(2,1)S(1)} %shard_map.152), channel_id=1, replica_groups=mesh['zh'=4,'x'=4,'zl'=2,'y'=8,'c'=2] {'zh','x'}, dimensions={0} | all-to-all | bytes 327680 | tf_op jit(solution)/shard_map/all_to_all | solution.py:36
  77.1 0.8 shard_map.153
  77.9 4.7 %all-to-all-start.4 = ((bf16[16,40,128]{2,1,0:T(8,128)(2,1)}), bf16[16,40,128]{2,1,0:T(8,128)(2,1)S(1)}, u32[]{:S(2)}, u32[]{:S(2)}) async-start(bf16[16,40,128]{2,1,0:T(8,128)(2,1)} %shard_map.153), calls=%async_computation.4 | async-start | bytes 327680 | tf_op jit(solution)/shard_map/all_to_all | solution.py:36
  82.6 1.3 %shard_map.151 = bf16[2,8,32,128]{3,2,1,0:T(8,128)(2,1)} custom-call(bf16[2,8,32,128]{3,2,1,0:T(8,128)(2,1)S(1)} %copy-done.1, bf16[2,2,32,128]{3,2,1,0:T(8,128)(2,1)S(1)} %collective-permute-done.1.inner, bf16[2,2,32,128]{3,2,1,0:T(8,128)(2,1)S(1)} %collective-permute-done.outer, bf16[40,128]{1,0:T(8,128)(2,1)S(1)} %get-tuple-element.54.other, ...), custom_call_target="tpu_custom_call" | custom-call | tf_op jit(solution)/shard_map/pallas_call | solution.py:543
  83.9 6.2 %all-to-all-done.4 = bf16[16,40,128]{2,1,0:T(8,128)(2,1)S(1)} async-done(((bf16[16,40,128]{2,1,0:T(8,128)(2,1)}), bf16[16,40,128]{2,1,0:T(8,128)(2,1)S(1)}, u32[]{:S(2)}, u32[]{:S(2)}) %all-to-all-start.4) | async-done | bytes 163872 | tf_op jit(solution)/shard_map/all_to_all | solution.py:36
  90.1 5.7 %all-gather.1.gathered = bf16[32,40,128]{2,1,0:T(8,128)(2,1)S(1)} all-gather(bf16[16,40,128]{2,1,0:T(8,128)(2,1)S(1)} %all-to-all-done.4), channel_id=3, replica_groups=mesh['zh'=4,'x'=4,'zl'=2,'y'=8,'c'=2] {'c'}, dimensions={0}, use_global_device_ids=true | all-gather | bytes 491520 | tf_op jit(solution)/shard_map/all_gather | solution.py:542
  95.8 1.2 %shard_map.154 = (bf16[2,8,32,128]{3,2,1,0:T(8,128)(2,1)}, f32[9,128,128]{2,1,0:T(8,128)}, f32[512,128]{1,0:T(8,128)}, f32[1,128]{1,0:T(1,128)}, f32[1,128]{1,0:T(1,128)}) custom-call(bf16[32,40,128]{2,1,0:T(8,128)(2,1)S(1)} %all-gather.1.gathered, f32[4,128]{1,0:T(4,128)S(1)} %get-tuple-element.59.stats, bf16[2,8,32,128]{3,2,1,0:T(8,128)(2,1)S(1)} %copy-done.1, ...), custom_call_target="tpu_custom_call" | custom-call | tf_op jit(solution)/shard_map/pallas_call | solution.py:547
  (1 shorter events, 0.0 us)
Async XLA Ops:
  0.6 36.0 %copy-start = (f32[3,3,128,128]{3,2,1,0:T(8,128)S(1)}, f32[3,3,128,128]{3,2,1,0:T(8,128)}, u32[]{:S(2)}) copy-start(f32[3,3,128,128]{3,2,1,0:T(8,128)} %param.16) | copy-start | bytes 1769476
  3.2 10.8 %copy-start.8 = (bf16[2,2,32,128]{3,2,1,0:T(8,128)(2,1)S(1)}, bf16[2,2,32,128]{3,2,1,0:T(8,128)(2,1)}, u32[]{:S(2)}) copy-start(bf16[2,2,32,128]{3,2,1,0:T(8,128)(2,1)} %get-tuple-element.41) | copy-start | bytes 98308
  3.3 11.6 %copy-start.7 = (bf16[2,2,32,128]{3,2,1,0:T(8,128)(2,1)S(1)}, bf16[2,2,32,128]{3,2,1,0:T(8,128)(2,1)}, u32[]{:S(2)}) copy-start(bf16[2,2,32,128]{3,2,1,0:T(8,128)(2,1)} %get-tuple-element.42) | copy-start | bytes 98308
  3.3 20.9 %copy-start.2 = (bf16[2,8,32,128]{3,2,1,0:T(8,128)(2,1)S(1)}, bf16[2,8,32,128]{3,2,1,0:T(8,128)(2,1)}, u32[]{:S(2)}) copy-start(bf16[2,8,32,128]{3,2,1,0:T(8,128)(2,1)} %cotangent.1) | copy-start | bytes 393220
  3.3 20.9 %all-to-all-start = ((bf16[32,24,128]{2,1,0:T(8,128)(2,1)}), bf16[32,24,128]{2,1,0:T(8,128)(2,1)S(1)}, u32[]{:S(2)}, u32[]{:S(2)}) async-start(bf16[32,24,128]{2,1,0:T(8,128)(2,1)} %get-tuple-element.39), calls=%async_computation | async-start | bytes 393216 | tf_op jit(solution)/shard_map/all_to_all | solution.py:36
  14.0 22.7 %copy-start.3 = (f32[512,128]{1,0:T(8,128)S(1)}, f32[512,128]{1,0:T(8,128)}, u32[]{:S(2)}) copy-start(f32[512,128]{1,0:T(8,128)} %style_weight.1) | copy-start | bytes 786436
  14.0 10.9 %collective-permute-start = (bf16[2,2,32,128]{3,2,1,0:T(8,128)(2,1)S(1)}, bf16[2,2,32,128]{3,2,1,0:T(8,128)(2,1)S(1)}, u32[]{:S(2)}, u32[]{:S(2)}) collective-permute-start(bf16[2,2,32,128]{3,2,1,0:T(8,128)(2,1)S(1)} %copy-done.8), channel_id=1, source_target_pairs={{32,64},{96,128},{160,192},{224,256},{288,320},{352,384},{416,448}... | collective-permute-start | bytes 98312 | tf_op jit(solution)/shard_map/ppermute | solution.py:26
  14.8 10.1 %collective-permute-start.1 = (bf16[2,2,32,128]{3,2,1,0:T(8,128)(2,1)S(1)}, bf16[2,2,32,128]{3,2,1,0:T(8,128)(2,1)S(1)}, u32[]{:S(2)}, u32[]{:S(2)}) collective-permute-start(bf16[2,2,32,128]{3,2,1,0:T(8,128)(2,1)S(1)} %copy-done.7), channel_id=1, source_target_pairs={{0,32},{64,96},{128,160},{192,224},{256,288},{320,352},{384,416},{... | collective-permute-start | bytes 98312 | tf_op jit(solution)/shard_map/ppermute | solution.py:26
  24.9 20.6 %all-to-all-start.1 = ((bf16[16,16,128]{2,1,0:T(8,128)(2,1)}), bf16[16,16,128]{2,1,0:T(8,128)(2,1)S(1)}, u32[]{:S(2)}, u32[]{:S(2)}) async-start(bf16[16,16,128]{2,1,0:T(8,128)(2,1)} %get-tuple-element.45), calls=%async_computation.1 | async-start | bytes 131072 | tf_op jit(solution)/shard_map/all_to_all | solution.py:36
  36.6 0.7 copy-start.4
  36.7 0.7 copy-start.5
  36.7 0.7 copy-start.6
  37.3 0.9 copy-start.1
  38.3 13.8 %collective-permute-start.2 = (bf16[24,128]{1,0:T(8,128)(2,1)S(1)}, bf16[24,128]{1,0:T(8,128)(2,1)S(1)}, u32[]{:S(2)}, u32[]{:S(2)}) collective-permute-start(bf16[24,128]{1,0:T(8,128)(2,1)S(1)} %get-tuple-element.56), channel_id=1, source_target_pairs={{1,2},{3,4},{5,6},{7,8},{9,10},{11,12},{13,14},{15,16},{17,18},{19... | collective-permute-start | bytes 18440 | tf_op jit(solution)/shard_map/ppermute | solution.py:26
  77.9 12.2 %all-to-all-start.4 = ((bf16[16,40,128]{2,1,0:T(8,128)(2,1)}), bf16[16,40,128]{2,1,0:T(8,128)(2,1)S(1)}, u32[]{:S(2)}, u32[]{:S(2)}) async-start(bf16[16,40,128]{2,1,0:T(8,128)(2,1)} %shard_map.153), calls=%async_computation.4 | async-start | bytes 327680 | tf_op jit(solution)/shard_map/all_to_all | solution.py:36

commit v15 on v14

--- a/solution.py
+++ b/solution.py
@@ -135,7 +135,7 @@
         outer_out[field, sample] = jnp.where(even, top, bottom).astype(BF16)
 
     null32 = null[...].astype(F32)
-    means, spreads = [], []
+    fields, sums = [], []
     for sample in range(samples):
         for copy in field_copies[sample]:
             copy.wait()
@@ -145,11 +145,15 @@
         ).astype(BF16)
         mixed_out[sample] = mixed
         put_rims(0, sample, mixed[0], mixed[tile_rows - 1])
-        wide = mixed.astype(F32).reshape(cells, channels)
-        mean = group_total(jnp.sum(wide, axis=0, keepdims=True)) * (1.0 / size)
-        away = wide - mean
-        means.append(mean)
-        spreads.append(group_total(jnp.sum(away * away, axis=0, keepdims=True)))
+        fields.append(mixed.astype(F32).reshape(cells, channels))
+        sums.append(jnp.sum(fields[-1], axis=0, keepdims=True))
+    means = group_total(jnp.concatenate(sums, axis=0)) * (1.0 / size)
+    sums = []
+    for sample in range(samples):
+        away = fields[sample] - means[sample : sample + 1, :]
+        sums.append(jnp.sum(away * away, axis=0, keepdims=True))
+    spreads = group_total(jnp.concatenate(sums, axis=0))
+    means, spreads = (means[0:1, :], means[1:2, :]), (spreads[0:1, :], spreads[1:2, :])
     rows = header(weave(*means), weave(*spreads))
     cot_copy.wait()
     firsts, lasts = [], []
@@ -417,6 +421,7 @@
         small.append(whole)
     demod_sums, style_sums, gamma_sums, beta_sums = small[0:2], small[2:4], small[4:6], small[6:8]
     gain = gamma[...]
+    group_means = group_total(gain * jnp.concatenate(beta_sums + gamma_sums, axis=0)) * (1.0 / cells)
     gamma_out[...] = scale * (gamma_sums[0] + gamma_sums[1])
     beta_out[...] = scale * (beta_sums[0] + beta_sums[1])
     shrink = jnp.zeros((channels, channels), F32)
@@ -441,8 +446,8 @@
     style_out[...] = scale * (emb_full[0] * rows[0] + emb_full[1] * rows[1])
     for sample in range(samples):
         inverse = stats[samples + sample : samples + sample + 1, :]
-        product_mean = group_total(gain * beta_sums[sample]) * (1.0 / cells)
-        squared_mean = group_total(gain * gamma_sums[sample]) * (1.0 / cells)
+        product_mean = group_means[sample : sample + 1, :]
+        squared_mean = group_means[samples + sample : samples + sample + 1, :]
         flat = mixed[sample].astype(F32).reshape(size, channels)
         norm = (flat - stats[sample : sample + 1, :]) * inverse
         change = inverse * (gain * grad_pre[sample] - product_mean - norm * squared_mean)

time: 97.6 us -> 97.3 us (level)
  no operation moved by 1% of the time
where the time goes in v15:
time: 97.3 us; the launch traced here: 96.7 us
  starting transfers between devices  37.9 us (39%)
  blocking collectives  35.8 us (37%)
  waiting for transfers between devices  13 us (13%)
  Pallas kernels  8.51 us (9%)
    all_to_all x3, starting transfers between devices, exchange(): return lax.all_to_all(block, axes, 0, 0)  27.1 us
    all_to_all x2, blocking collectives, exchange(): return lax.all_to_all(block, axes, 0, 0)  24.9 us
    all_to_all x3, waiting for transfers between devices, exchange(): return lax.all_to_all(block, axes, 0, 0)  12.9 us
    ppermute x3, starting transfers between devices, swap(): lax.ppermute(block, axes, pairs + [(target, source) for source, target in...  10.7 us
    all_gather x1, blocking collectives, on_device(): payload = lax.all_gather(exchange(slots, NEAR), 'c')  5.68 us
    all_gather x1, blocking collectives, on_device(): lax.all_gather(payload, 'c')  5.19 us
    pallas_call x1, Pallas kernels, on_device(): call(mix_body, (array(feats.shape, BF16), array((lon_count, lon_slot, LAN...  2.27 us
  transfers between devices with their start and end apart: 6, of which 3 were waited for; matrix products, arithmetic and copies ran while one was open for 0% of the time, Pallas kernels for 4%

profile of v15, /device:TPU:1, one launch (start us, length us, event | category | flops | bytes accessed | tf_op | source)
XLA Modules:
  0.0 96.7 jit_solution(5555843629550743719)
XLA Ops:
  0.6 0.0 copy-start
  0.6 2.3 %shard_map.145 = (bf16[2,8,32,128]{3,2,1,0:T(8,128)(2,1)}, bf16[32,24,128]{2,1,0:T(8,128)(2,1)}, bf16[2,2,32,128]{3,2,1,0:T(8,128)(2,1)}, bf16[2,2,32,128]{3,2,1,0:T(8,128)(2,1)}) custom-call(bf16[2,8,32,128]{3,2,1,0:T(8,128)(2,1)} %feats_in.1, bf16[2,8,32,128]{3,2,1,0:T(8,128)(2,1)} %cond_in.1, bf16[8,32,128]{2,1,0:T(8,128)(2,1)} %null_in.1, ...), custom_call_target="tpu_custom_call" | custom-call | tf_op jit(solution)/shard_map/pallas_call | solution.py:472
  2.9 0.0 copy-start.8
  2.9 0.0 copy-start.7
  2.9 0.0 copy-start.2
  3.0 10.7 %all-to-all-start = ((bf16[32,24,128]{2,1,0:T(8,128)(2,1)}), bf16[32,24,128]{2,1,0:T(8,128)(2,1)S(1)}, u32[]{:S(2)}, u32[]{:S(2)}) async-start(bf16[32,24,128]{2,1,0:T(8,128)(2,1)} %get-tuple-element.39), calls=%async_computation | async-start | bytes 393216 | tf_op jit(solution)/shard_map/all_to_all | solution.py:36
  13.7 0.0 copy-start.3
  13.7 0.0 copy-done.8
  13.7 0.8 collective-permute-start
  14.5 0.0 copy-done.7
  14.5 5.6 %collective-permute-start.1 = (bf16[2,2,32,128]{3,2,1,0:T(8,128)(2,1)S(1)}, bf16[2,2,32,128]{3,2,1,0:T(8,128)(2,1)S(1)}, u32[]{:S(2)}, u32[]{:S(2)}) collective-permute-start(bf16[2,2,32,128]{3,2,1,0:T(8,128)(2,1)S(1)} %copy-done.7), channel_id=1, source_target_pairs={{0,32},{64,96},{128,160},{192,224},{256,288},{320,352},{384,416},{... | collective-permute-start | bytes 98312 | tf_op jit(solution)/shard_map/ppermute | solution.py:26
  20.1 3.8 %all-to-all-done.slots = bf16[32,24,128]{2,1,0:T(8,128)(2,1)S(1)} async-done(((bf16[32,24,128]{2,1,0:T(8,128)(2,1)}), bf16[32,24,128]{2,1,0:T(8,128)(2,1)S(1)}, u32[]{:S(2)}, u32[]{:S(2)}) %all-to-all-start) | async-done | bytes 196640 | tf_op jit(solution)/shard_map/all_to_all | solution.py:36
  23.9 0.0 copy-done.2
  23.9 0.7 shard_map.146
  24.6 0.0 collective-permute-done.outer
  24.6 0.0 collective-permute-done.1.inner
  24.6 11.7 %all-to-all-start.1 = ((bf16[16,16,128]{2,1,0:T(8,128)(2,1)}), bf16[16,16,128]{2,1,0:T(8,128)(2,1)S(1)}, u32[]{:S(2)}, u32[]{:S(2)}) async-start(bf16[16,16,128]{2,1,0:T(8,128)(2,1)} %get-tuple-element.45), calls=%async_computation.1 | async-start | bytes 131072 | tf_op jit(solution)/shard_map/all_to_all | solution.py:36
  36.3 0.0 copy-start.4
  36.3 0.0 copy-start.5
  36.3 0.0 copy-start.6
  36.4 0.0 copy-done
  36.4 0.0 copy-done.3
  36.4 0.6 copy-done.4
  37.0 0.0 copy-done.5
  37.0 0.0 copy-done.6
  37.0 0.0 copy-start.1
  37.0 0.8 shard_map.148
  37.8 0.1 copy-done.1
  38.0 4.4 %collective-permute-start.2 = (bf16[24,128]{1,0:T(8,128)(2,1)S(1)}, bf16[24,128]{1,0:T(8,128)(2,1)S(1)}, u32[]{:S(2)}, u32[]{:S(2)}) collective-permute-start(bf16[24,128]{1,0:T(8,128)(2,1)S(1)} %get-tuple-element.56), channel_id=1, source_target_pairs={{1,2},{3,4},{5,6},{7,8},{9,10},{11,12},{13,14},{15,16},{17,18},{19... | collective-permute-start | bytes 18440 | tf_op jit(solution)/shard_map/ppermute | solution.py:26
  42.3 3.0 %all-to-all-done.1.slots = bf16[16,16,128]{2,1,0:T(8,128)(2,1)S(1)} async-done(((bf16[16,16,128]{2,1,0:T(8,128)(2,1)}), bf16[16,16,128]{2,1,0:T(8,128)(2,1)S(1)}, u32[]{:S(2)}, u32[]{:S(2)}) %all-to-all-start.1) | async-done | bytes 65568 | tf_op jit(solution)/shard_map/all_to_all | solution.py:36
  45.3 1.2 %shard_map.149 = (f32[4,128]{1,0:T(4,128)S(1)}, f32[2,256,128]{2,1,0:T(8,128)S(1)}, bf16[33,40,128]{2,1,0:T(8,128)(2,1)S(1)}) custom-call(bf16[16,16,128]{2,1,0:T(8,128)(2,1)S(1)} %all-to-all-done.1.slots, bf16[2,8,32,128]{3,2,1,0:T(8,128)(2,1)S(1)} %copy-done.1, bf16[40,128]{1,0:T(8,128)(2,1)S(1)} %get-tuple-element.46.edges, ...), custom_call_target="tpu_custom_call" | custom-call | tf_op jit(solution)/shard_map/pallas_call | solution.py:521
  46.5 5.2 %all-gather = bf16[66,40,128]{2,1,0:T(8,128)(2,1)S(1)} all-gather(bf16[33,40,128]{2,1,0:T(8,128)(2,1)S(1)} %get-tuple-element.53), channel_id=2, replica_groups=mesh['zh'=4,'x'=4,'zl'=2,'y'=8,'c'=2] {'c'}, dimensions={0}, use_global_device_ids=true | all-gather | bytes 1013760 | tf_op jit(solution)/shard_map/all_gather | solution.py:541
  51.7 0.1 shard_map.150
  51.8 0.0 collective-permute-done.2.passed
  51.8 12.3 %all_to_all.25.slots = bf16[16,40,128]{2,1,0:T(8,128)(2,1)S(1)} all-to-all(bf16[16,40,128]{2,1,0:T(8,128)(2,1)S(1)} %get-tuple-element.60), channel_id=1, replica_groups=mesh['zh'=4,'x'=4,'zl'=2,'y'=8,'c'=2] {'zl','y'}, dimensions={0} | all-to-all | bytes 327680 | tf_op jit(solution)/shard_map/all_to_all | solution.py:36
  64.1 0.1 shard_map.152
  64.2 12.6 %all_to_all.26.slots = bf16[16,40,128]{2,1,0:T(8,128)(2,1)S(1)} all-to-all(bf16[16,40,128]{2,1,0:T(8,128)(2,1)S(1)} %shard_map.152), channel_id=1, replica_groups=mesh['zh'=4,'x'=4,'zl'=2,'y'=8,'c'=2] {'zh','x'}, dimensions={0} | all-to-all | bytes 327680 | tf_op jit(solution)/shard_map/all_to_all | solution.py:36
  76.8 0.8 shard_map.153
  77.6 4.7 %all-to-all-start.4 = ((bf16[16,40,128]{2,1,0:T(8,128)(2,1)}), bf16[16,40,128]{2,1,0:T(8,128)(2,1)S(1)}, u32[]{:S(2)}, u32[]{:S(2)}) async-start(bf16[16,40,128]{2,1,0:T(8,128)(2,1)} %shard_map.153), calls=%async_computation.4 | async-start | bytes 327680 | tf_op jit(solution)/shard_map/all_to_all | solution.py:36
  82.3 1.3 %shard_map.151 = bf16[2,8,32,128]{3,2,1,0:T(8,128)(2,1)} custom-call(bf16[2,8,32,128]{3,2,1,0:T(8,128)(2,1)S(1)} %copy-done.1, bf16[2,2,32,128]{3,2,1,0:T(8,128)(2,1)S(1)} %collective-permute-done.1.inner, bf16[2,2,32,128]{3,2,1,0:T(8,128)(2,1)S(1)} %collective-permute-done.outer, bf16[40,128]{1,0:T(8,128)(2,1)S(1)} %get-tuple-element.54.other, ...), custom_call_target="tpu_custom_call" | custom-call | tf_op jit(solution)/shard_map/pallas_call | solution.py:548
  83.6 6.2 %all-to-all-done.4 = bf16[16,40,128]{2,1,0:T(8,128)(2,1)S(1)} async-done(((bf16[16,40,128]{2,1,0:T(8,128)(2,1)}), bf16[16,40,128]{2,1,0:T(8,128)(2,1)S(1)}, u32[]{:S(2)}, u32[]{:S(2)}) %all-to-all-start.4) | async-done | bytes 163872 | tf_op jit(solution)/shard_map/all_to_all | solution.py:36
  89.8 5.7 %all-gather.1.gathered = bf16[32,40,128]{2,1,0:T(8,128)(2,1)S(1)} all-gather(bf16[16,40,128]{2,1,0:T(8,128)(2,1)S(1)} %all-to-all-done.4), channel_id=3, replica_groups=mesh['zh'=4,'x'=4,'zl'=2,'y'=8,'c'=2] {'c'}, dimensions={0}, use_global_device_ids=true | all-gather | bytes 491520 | tf_op jit(solution)/shard_map/all_gather | solution.py:547
  95.5 1.2 %shard_map.154 = (bf16[2,8,32,128]{3,2,1,0:T(8,128)(2,1)}, f32[9,128,128]{2,1,0:T(8,128)}, f32[512,128]{1,0:T(8,128)}, f32[1,128]{1,0:T(1,128)}, f32[1,128]{1,0:T(1,128)}) custom-call(bf16[32,40,128]{2,1,0:T(8,128)(2,1)S(1)} %all-gather.1.gathered, f32[4,128]{1,0:T(4,128)S(1)} %get-tuple-element.59.stats, bf16[2,8,32,128]{3,2,1,0:T(8,128)(2,1)S(1)} %copy-done.1, ...), custom_call_target="tpu_custom_call" | custom-call | tf_op jit(solution)/shard_map/pallas_call | solution.py:552
  (1 shorter events, 0.0 us)
Async XLA Ops:
  0.6 35.7 %copy-start = (f32[3,3,128,128]{3,2,1,0:T(8,128)S(1)}, f32[3,3,128,128]{3,2,1,0:T(8,128)}, u32[]{:S(2)}) copy-start(f32[3,3,128,128]{3,2,1,0:T(8,128)} %param.16) | copy-start | bytes 1769476
  2.9 10.8 %copy-start.8 = (bf16[2,2,32,128]{3,2,1,0:T(8,128)(2,1)S(1)}, bf16[2,2,32,128]{3,2,1,0:T(8,128)(2,1)}, u32[]{:S(2)}) copy-start(bf16[2,2,32,128]{3,2,1,0:T(8,128)(2,1)} %get-tuple-element.41) | copy-start | bytes 98308
  2.9 11.6 %copy-start.7 = (bf16[2,2,32,128]{3,2,1,0:T(8,128)(2,1)S(1)}, bf16[2,2,32,128]{3,2,1,0:T(8,128)(2,1)}, u32[]{:S(2)}) copy-start(bf16[2,2,32,128]{3,2,1,0:T(8,128)(2,1)} %get-tuple-element.42) | copy-start | bytes 98308
  2.9 20.9 %copy-start.2 = (bf16[2,8,32,128]{3,2,1,0:T(8,128)(2,1)S(1)}, bf16[2,8,32,128]{3,2,1,0:T(8,128)(2,1)}, u32[]{:S(2)}) copy-start(bf16[2,8,32,128]{3,2,1,0:T(8,128)(2,1)} %cotangent.1) | copy-start | bytes 393220
  3.0 20.9 %all-to-all-start = ((bf16[32,24,128]{2,1,0:T(8,128)(2,1)}), bf16[32,24,128]{2,1,0:T(8,128)(2,1)S(1)}, u32[]{:S(2)}, u32[]{:S(2)}) async-start(bf16[32,24,128]{2,1,0:T(8,128)(2,1)} %get-tuple-element.39), calls=%async_computation | async-start | bytes 393216 | tf_op jit(solution)/shard_map/all_to_all | solution.py:36
  13.7 22.7 %copy-start.3 = (f32[512,128]{1,0:T(8,128)S(1)}, f32[512,128]{1,0:T(8,128)}, u32[]{:S(2)}) copy-start(f32[512,128]{1,0:T(8,128)} %style_weight.1) | copy-start | bytes 786436
  13.7 10.9 %collective-permute-start = (bf16[2,2,32,128]{3,2,1,0:T(8,128)(2,1)S(1)}, bf16[2,2,32,128]{3,2,1,0:T(8,128)(2,1)S(1)}, u32[]{:S(2)}, u32[]{:S(2)}) collective-permute-start(bf16[2,2,32,128]{3,2,1,0:T(8,128)(2,1)S(1)} %copy-done.8), channel_id=1, source_target_pairs={{32,64},{96,128},{160,192},{224,256},{288,320},{352,384},{416,448}... | collective-permute-start | bytes 98312 | tf_op jit(solution)/shard_map/ppermute | solution.py:26
  14.5 10.1 %collective-permute-start.1 = (bf16[2,2,32,128]{3,2,1,0:T(8,128)(2,1)S(1)}, bf16[2,2,32,128]{3,2,1,0:T(8,128)(2,1)S(1)}, u32[]{:S(2)}, u32[]{:S(2)}) collective-permute-start(bf16[2,2,32,128]{3,2,1,0:T(8,128)(2,1)S(1)} %copy-done.7), channel_id=1, source_target_pairs={{0,32},{64,96},{128,160},{192,224},{256,288},{320,352},{384,416},{... | collective-permute-start | bytes 98312 | tf_op jit(solution)/shard_map/ppermute | solution.py:26
  24.6 20.6 %all-to-all-start.1 = ((bf16[16,16,128]{2,1,0:T(8,128)(2,1)}), bf16[16,16,128]{2,1,0:T(8,128)(2,1)S(1)}, u32[]{:S(2)}, u32[]{:S(2)}) async-start(bf16[16,16,128]{2,1,0:T(8,128)(2,1)} %get-tuple-element.45), calls=%async_computation.1 | async-start | bytes 131072 | tf_op jit(solution)/shard_map/all_to_all | solution.py:36
  36.3 0.7 copy-start.4
  36.3 0.7 copy-start.5
  36.3 0.7 copy-start.6
  37.0 0.9 copy-start.1
  38.0 13.8 %collective-permute-start.2 = (bf16[24,128]{1,0:T(8,128)(2,1)S(1)}, bf16[24,128]{1,0:T(8,128)(2,1)S(1)}, u32[]{:S(2)}, u32[]{:S(2)}) collective-permute-start(bf16[24,128]{1,0:T(8,128)(2,1)S(1)} %get-tuple-element.56), channel_id=1, source_target_pairs={{1,2},{3,4},{5,6},{7,8},{9,10},{11,12},{13,14},{15,16},{17,18},{19... | collective-permute-start | bytes 18440 | tf_op jit(solution)/shard_map/ppermute | solution.py:26
  77.6 12.2 %all-to-all-start.4 = ((bf16[16,40,128]{2,1,0:T(8,128)(2,1)}), bf16[16,40,128]{2,1,0:T(8,128)(2,1)S(1)}, u32[]{:S(2)}, u32[]{:S(2)}) async-start(bf16[16,40,128]{2,1,0:T(8,128)(2,1)} %shard_map.153), calls=%async_computation.4 | async-start | bytes 327680 | tf_op jit(solution)/shard_map/all_to_all | solution.py:36

commit v16 on v15

--- a/solution.py
+++ b/solution.py
@@ -398,8 +398,9 @@
 
 
 def last_body(
-    scale, cells, gathered, stats, mixed, cotangent, grad_pre, gamma, style, column, demod,
-    power, weight, emb_full, feats_out, weight_out, style_out, gamma_out, beta_out,
+    scale, cells, gathered, stats, mixed, cotangent, grad_pre, gamma, beta, style, column, demod,
+    power, weight, emb_full, inner, outer, other, passed, fore_taps,
+    feats_out, weight_out, style_out, gamma_out, beta_out, block_out, spread, shifted,
 ):
     samples, tile_rows, tile_cols, channels = cotangent.shape
     size = tile_rows * tile_cols
@@ -453,6 +454,9 @@
         change = inverse * (gain * grad_pre[sample] - product_mean - norm * squared_mean)
         out = cotangent[sample].reshape(size, channels).astype(F32) + change
         feats_out[sample] = out.astype(BF16).reshape(tile_rows, tile_cols, channels)
+    forward_body(
+        mixed, inner, outer, other, passed, fore_taps, stats, gamma, beta, block_out, spread, shifted
+    )
 
 
 def on_device(
@@ -545,11 +549,7 @@
     slots = call(sum_body, summed)(exchange(slots, NEAR))
     slots = call(sum_body, shard)(exchange(slots, LAT))
     payload = lax.all_gather(exchange(slots, NEAR), "c")
-    block_out = call(forward_body, array(feats.shape, BF16), (spread, shifted))(
-        mixed, inner, outer, other, passed, fore_taps, stats, gamma, beta
-    )
-
-    grad_feats, grad_weight, grad_style, grad_gamma, grad_beta = call(
+    grad_feats, grad_weight, grad_style, grad_gamma, grad_beta, block_out = call(
         functools.partial(last_body, scale_gradient, cells_per_group),
         (
             array(feats.shape, BF16),
@@ -557,10 +557,12 @@
             array(style_weight.shape),
             array((1, LANES)),
             array((1, LANES)),
+            array(feats.shape, BF16),
         ),
+        (spread, shifted),
     )(
-        payload.reshape(SHARDS, SLOT, LANES), stats, mixed, cotangent, grad_pre, gamma, style,
-        column, demod, power, taps, emb_full,
+        payload.reshape(SHARDS, SLOT, LANES), stats, mixed, cotangent, grad_pre, gamma, beta, style,
+        column, demod, power, taps, emb_full, inner, outer, other, passed, fore_taps,
     )
     return (
         block_out,

time: 97.3 us -> 96.7 us (level)
  blocking collectives: 35.8 us -> 47.8 us
  waiting for transfers between devices: 13 us -> 6.74 us
  starting transfers between devices: 37.9 us -> 33.1 us
  Pallas kernels: 8.51 us -> 6.92 us
    all_to_all x2 -> x3, blocking collectives: 24.9 us -> 36.9 us  [exchange(): return lax.all_to_all(block, axes, 0, 0)]
    all_to_all x3 -> x2, waiting for transfers between devices: 12.9 us -> 6.73 us  [exchange(): return lax.all_to_all(block, axes, 0, 0)]
    all_to_all x3 -> x2, starting transfers between devices: 27.1 us -> 22.4 us  [exchange(): return lax.all_to_all(block, axes, 0, 0)]
    pallas_call x1 -> x0, Pallas kernels: 1.3 us -> none  [on_device(): call(forward_body, array(feats.shape, BF16), (spread, shifted))]
  transfers between devices with their start and end apart: 6 -> 5, of which waited for: 3 -> 2; matrix products, arithmetic and copies ran while one was open for 0% -> 0% of each run, Pallas kernels for 4% -> 3%
where the time goes in v16:
time: 96.7 us; the launch traced here: 96.2 us
  blocking collectives  47.8 us (49%)
  starting transfers between devices  33.1 us (34%)
  Pallas kernels  6.92 us (7%)
  waiting for transfers between devices  6.74 us (7%)
    all_to_all x3, blocking collectives, exchange(): return lax.all_to_all(block, axes, 0, 0)  36.9 us
    all_to_all x2, starting transfers between devices, exchange(): return lax.all_to_all(block, axes, 0, 0)  22.4 us
    ppermute x3, starting transfers between devices, swap(): lax.ppermute(block, axes, pairs + [(target, source) for source, target in...  10.7 us
    all_to_all x2, waiting for transfers between devices, exchange(): return lax.all_to_all(block, axes, 0, 0)  6.73 us
    all_gather x1, blocking collectives, on_device(): payload = lax.all_gather(exchange(slots, NEAR), 'c')  5.69 us
    all_gather x1, blocking collectives, on_device(): lax.all_gather(payload, 'c')  5.2 us
    pallas_call x1, Pallas kernels, on_device(): call(mix_body, (array(feats.shape, BF16), array((lon_count, lon_slot, LAN...  2.27 us
  transfers between devices with their start and end apart: 5, of which 2 were waited for; matrix products, arithmetic and copies ran while one was open for 0% of the time, Pallas kernels for 3%

profile of v16, /device:TPU:1, one launch (start us, length us, event | category | flops | bytes accessed | tf_op | source)
XLA Modules:
  0.0 96.2 jit_solution(5092102314247749761)
XLA Ops:
  0.6 0.0 copy-start
  0.6 2.3 %shard_map.145 = (bf16[2,8,32,128]{3,2,1,0:T(8,128)(2,1)}, bf16[32,24,128]{2,1,0:T(8,128)(2,1)}, bf16[2,2,32,128]{3,2,1,0:T(8,128)(2,1)}, bf16[2,2,32,128]{3,2,1,0:T(8,128)(2,1)}) custom-call(bf16[2,8,32,128]{3,2,1,0:T(8,128)(2,1)} %feats_in.1, bf16[2,8,32,128]{3,2,1,0:T(8,128)(2,1)} %cond_in.1, bf16[8,32,128]{2,1,0:T(8,128)(2,1)} %null_in.1, ...), custom_call_target="tpu_custom_call" | custom-call | tf_op jit(solution)/shard_map/pallas_call | solution.py:476
  2.9 0.0 copy-start.8
  2.9 0.0 copy-start.7
  2.9 0.0 copy-start.1
  3.0 10.7 %all-to-all-start = ((bf16[32,24,128]{2,1,0:T(8,128)(2,1)}), bf16[32,24,128]{2,1,0:T(8,128)(2,1)S(1)}, u32[]{:S(2)}, u32[]{:S(2)}) async-start(bf16[32,24,128]{2,1,0:T(8,128)(2,1)} %get-tuple-element.39), calls=%async_computation | async-start | bytes 393216 | tf_op jit(solution)/shard_map/all_to_all | solution.py:36
  13.7 0.0 copy-start.3
  13.7 0.0 copy-done.8
  13.7 0.8 collective-permute-start
  14.5 0.0 copy-done.7
  14.5 5.6 %collective-permute-start.1 = (bf16[2,2,32,128]{3,2,1,0:T(8,128)(2,1)S(1)}, bf16[2,2,32,128]{3,2,1,0:T(8,128)(2,1)S(1)}, u32[]{:S(2)}, u32[]{:S(2)}) collective-permute-start(bf16[2,2,32,128]{3,2,1,0:T(8,128)(2,1)S(1)} %copy-done.7), channel_id=1, source_target_pairs={{0,32},{64,96},{128,160},{192,224},{256,288},{320,352},{384,416},{... | collective-permute-start | bytes 98312 | tf_op jit(solution)/shard_map/ppermute | solution.py:26
  20.1 3.8 %all-to-all-done.slots = bf16[32,24,128]{2,1,0:T(8,128)(2,1)S(1)} async-done(((bf16[32,24,128]{2,1,0:T(8,128)(2,1)}), bf16[32,24,128]{2,1,0:T(8,128)(2,1)S(1)}, u32[]{:S(2)}, u32[]{:S(2)}) %all-to-all-start) | async-done | bytes 196640 | tf_op jit(solution)/shard_map/all_to_all | solution.py:36
  23.9 0.0 copy-done.1
  23.9 0.7 shard_map.146
  24.6 0.0 collective-permute-done.outer
  24.6 0.0 collective-permute-done.1.inner
  24.6 11.7 %all-to-all-start.1 = ((bf16[16,16,128]{2,1,0:T(8,128)(2,1)}), bf16[16,16,128]{2,1,0:T(8,128)(2,1)S(1)}, u32[]{:S(2)}, u32[]{:S(2)}) async-start(bf16[16,16,128]{2,1,0:T(8,128)(2,1)} %get-tuple-element.43), calls=%async_computation.1 | async-start | bytes 131072 | tf_op jit(solution)/shard_map/all_to_all | solution.py:36
  36.3 0.0 copy-start.4
  36.3 0.0 copy-start.5
  36.3 0.0 copy-start.6
  36.4 0.0 copy-done
  36.4 0.0 copy-done.3
  36.4 0.6 copy-done.4
  37.0 0.0 copy-done.5
  37.0 0.0 copy-done.6
  37.0 0.0 copy-start.2
  37.0 0.8 shard_map.148
  37.8 0.1 copy-done.2
  38.0 4.4 %collective-permute-start.2 = (bf16[24,128]{1,0:T(8,128)(2,1)S(1)}, bf16[24,128]{1,0:T(8,128)(2,1)S(1)}, u32[]{:S(2)}, u32[]{:S(2)}) collective-permute-start(bf16[24,128]{1,0:T(8,128)(2,1)S(1)} %get-tuple-element.56), channel_id=1, source_target_pairs={{1,2},{3,4},{5,6},{7,8},{9,10},{11,12},{13,14},{15,16},{17,18},{19... | collective-permute-start | bytes 18440 | tf_op jit(solution)/shard_map/ppermute | solution.py:26
  42.3 3.0 %all-to-all-done.1.slots = bf16[16,16,128]{2,1,0:T(8,128)(2,1)S(1)} async-done(((bf16[16,16,128]{2,1,0:T(8,128)(2,1)}), bf16[16,16,128]{2,1,0:T(8,128)(2,1)S(1)}, u32[]{:S(2)}, u32[]{:S(2)}) %all-to-all-start.1) | async-done | bytes 65568 | tf_op jit(solution)/shard_map/all_to_all | solution.py:36
  45.3 1.2 %shard_map.149 = (f32[4,128]{1,0:T(4,128)S(1)}, f32[2,256,128]{2,1,0:T(8,128)S(1)}, bf16[33,40,128]{2,1,0:T(8,128)(2,1)S(1)}) custom-call(bf16[16,16,128]{2,1,0:T(8,128)(2,1)S(1)} %all-to-all-done.1.slots, bf16[2,8,32,128]{3,2,1,0:T(8,128)(2,1)S(1)} %copy-done.2, bf16[40,128]{1,0:T(8,128)(2,1)S(1)} %get-tuple-element.47.edges, ...), custom_call_target="tpu_custom_call" | custom-call | tf_op jit(solution)/shard_map/pallas_call | solution.py:525
  46.5 5.2 %all-gather = bf16[66,40,128]{2,1,0:T(8,128)(2,1)S(1)} all-gather(bf16[33,40,128]{2,1,0:T(8,128)(2,1)S(1)} %get-tuple-element.54), channel_id=2, replica_groups=mesh['zh'=4,'x'=4,'zl'=2,'y'=8,'c'=2] {'c'}, dimensions={0}, use_global_device_ids=true | all-gather | bytes 1013760 | tf_op jit(solution)/shard_map/all_gather | solution.py:545
  51.7 0.1 shard_map.150
  51.8 0.0 collective-permute-done.2.passed
  51.8 12.3 %all_to_all.25.slots = bf16[16,40,128]{2,1,0:T(8,128)(2,1)S(1)} all-to-all(bf16[16,40,128]{2,1,0:T(8,128)(2,1)S(1)} %get-tuple-element.57), channel_id=1, replica_groups=mesh['zh'=4,'x'=4,'zl'=2,'y'=8,'c'=2] {'zl','y'}, dimensions={0} | all-to-all | bytes 327680 | tf_op jit(solution)/shard_map/all_to_all | solution.py:36
  64.1 0.1 shard_map.151
  64.2 12.6 %all_to_all.26.slots = bf16[16,40,128]{2,1,0:T(8,128)(2,1)S(1)} all-to-all(bf16[16,40,128]{2,1,0:T(8,128)(2,1)S(1)} %shard_map.151), channel_id=1, replica_groups=mesh['zh'=4,'x'=4,'zl'=2,'y'=8,'c'=2] {'zh','x'}, dimensions={0} | all-to-all | bytes 327680 | tf_op jit(solution)/shard_map/all_to_all | solution.py:36
  76.8 0.1 shard_map.152
  76.9 12.0 %all_to_all.27 = bf16[16,40,128]{2,1,0:T(8,128)(2,1)S(1)} all-to-all(bf16[16,40,128]{2,1,0:T(8,128)(2,1)S(1)} %shard_map.152), channel_id=1, replica_groups=mesh['zh'=4,'x'=4,'zl'=2,'y'=8,'c'=2] {'zl','y'}, dimensions={0} | all-to-all | bytes 327680 | tf_op jit(solution)/shard_map/all_to_all | solution.py:36
  88.9 5.7 %all-gather.1.gathered = bf16[32,40,128]{2,1,0:T(8,128)(2,1)S(1)} all-gather(bf16[16,40,128]{2,1,0:T(8,128)(2,1)S(1)} %all_to_all.27), channel_id=3, replica_groups=mesh['zh'=4,'x'=4,'zl'=2,'y'=8,'c'=2] {'c'}, dimensions={0}, use_global_device_ids=true | all-gather | bytes 491520 | tf_op jit(solution)/shard_map/all_gather | solution.py:551
  94.6 1.6 %shard_map.153 = (bf16[2,8,32,128]{3,2,1,0:T(8,128)(2,1)}, f32[9,128,128]{2,1,0:T(8,128)}, f32[512,128]{1,0:T(8,128)}, f32[1,128]{1,0:T(1,128)}, f32[1,128]{1,0:T(1,128)}, /*index=5*/bf16[2,8,32,128]{3,2,1,0:T(8,128)(2,1)}) custom-call(bf16[32,40,128]{2,1,0:T(8,128)(2,1)S(1)} %all-gather.1.gathered, f32[4,128]{1,0:T(4,128)S(1)} %get-tuple-element.58.stats, ...), custom_call_target="tpu_custom_call" | custom-call | tf_op jit(solution)/shard_map/pallas_call | solution.py:552
  (1 shorter events, 0.0 us)
Async XLA Ops:
  0.6 35.7 %copy-start = (f32[3,3,128,128]{3,2,1,0:T(8,128)S(1)}, f32[3,3,128,128]{3,2,1,0:T(8,128)}, u32[]{:S(2)}) copy-start(f32[3,3,128,128]{3,2,1,0:T(8,128)} %param.16) | copy-start | bytes 1769476
  2.9 10.8 %copy-start.8 = (bf16[2,2,32,128]{3,2,1,0:T(8,128)(2,1)S(1)}, bf16[2,2,32,128]{3,2,1,0:T(8,128)(2,1)}, u32[]{:S(2)}) copy-start(bf16[2,2,32,128]{3,2,1,0:T(8,128)(2,1)} %get-tuple-element.41) | copy-start | bytes 98308
  2.9 11.6 %copy-start.7 = (bf16[2,2,32,128]{3,2,1,0:T(8,128)(2,1)S(1)}, bf16[2,2,32,128]{3,2,1,0:T(8,128)(2,1)}, u32[]{:S(2)}) copy-start(bf16[2,2,32,128]{3,2,1,0:T(8,128)(2,1)} %get-tuple-element.42) | copy-start | bytes 98308
  2.9 20.9 %copy-start.1 = (bf16[2,8,32,128]{3,2,1,0:T(8,128)(2,1)S(1)}, bf16[2,8,32,128]{3,2,1,0:T(8,128)(2,1)}, u32[]{:S(2)}) copy-start(bf16[2,8,32,128]{3,2,1,0:T(8,128)(2,1)} %cotangent.1) | copy-start | bytes 393220
  3.0 20.9 %all-to-all-start = ((bf16[32,24,128]{2,1,0:T(8,128)(2,1)}), bf16[32,24,128]{2,1,0:T(8,128)(2,1)S(1)}, u32[]{:S(2)}, u32[]{:S(2)}) async-start(bf16[32,24,128]{2,1,0:T(8,128)(2,1)} %get-tuple-element.39), calls=%async_computation | async-start | bytes 393216 | tf_op jit(solution)/shard_map/all_to_all | solution.py:36
  13.7 22.7 %copy-start.3 = (f32[512,128]{1,0:T(8,128)S(1)}, f32[512,128]{1,0:T(8,128)}, u32[]{:S(2)}) copy-start(f32[512,128]{1,0:T(8,128)} %style_weight.1) | copy-start | bytes 786436
  13.7 10.9 %collective-permute-start = (bf16[2,2,32,128]{3,2,1,0:T(8,128)(2,1)S(1)}, bf16[2,2,32,128]{3,2,1,0:T(8,128)(2,1)S(1)}, u32[]{:S(2)}, u32[]{:S(2)}) collective-permute-start(bf16[2,2,32,128]{3,2,1,0:T(8,128)(2,1)S(1)} %copy-done.8), channel_id=1, source_target_pairs={{32,64},{96,128},{160,192},{224,256},{288,320},{352,384},{416,448}... | collective-permute-start | bytes 98312 | tf_op jit(solution)/shard_map/ppermute | solution.py:26
  14.5 10.1 %collective-permute-start.1 = (bf16[2,2,32,128]{3,2,1,0:T(8,128)(2,1)S(1)}, bf16[2,2,32,128]{3,2,1,0:T(8,128)(2,1)S(1)}, u32[]{:S(2)}, u32[]{:S(2)}) collective-permute-start(bf16[2,2,32,128]{3,2,1,0:T(8,128)(2,1)S(1)} %copy-done.7), channel_id=1, source_target_pairs={{0,32},{64,96},{128,160},{192,224},{256,288},{320,352},{384,416},{... | collective-permute-start | bytes 98312 | tf_op jit(solution)/shard_map/ppermute | solution.py:26
  24.6 20.6 %all-to-all-start.1 = ((bf16[16,16,128]{2,1,0:T(8,128)(2,1)}), bf16[16,16,128]{2,1,0:T(8,128)(2,1)S(1)}, u32[]{:S(2)}, u32[]{:S(2)}) async-start(bf16[16,16,128]{2,1,0:T(8,128)(2,1)} %get-tuple-element.43), calls=%async_computation.1 | async-start | bytes 131072 | tf_op jit(solution)/shard_map/all_to_all | solution.py:36
  36.3 0.7 copy-start.4
  36.3 0.7 copy-start.5
  36.3 0.7 copy-start.6
  37.0 0.9 copy-start.2
  38.0 13.8 %collective-permute-start.2 = (bf16[24,128]{1,0:T(8,128)(2,1)S(1)}, bf16[24,128]{1,0:T(8,128)(2,1)S(1)}, u32[]{:S(2)}, u32[]{:S(2)}) collective-permute-start(bf16[24,128]{1,0:T(8,128)(2,1)S(1)} %get-tuple-element.56), channel_id=1, source_target_pairs={{1,2},{3,4},{5,6},{7,8},{9,10},{11,12},{13,14},{15,16},{17,18},{19... | collective-permute-start | bytes 18440 | tf_op jit(solution)/shard_map/ppermute | solution.py:26

commit v17 on v16

--- a/solution.py
+++ b/solution.py
@@ -400,7 +400,8 @@
 def last_body(
     scale, cells, gathered, stats, mixed, cotangent, grad_pre, gamma, beta, style, column, demod,
     power, weight, emb_full, inner, outer, other, passed, fore_taps,
-    feats_out, weight_out, style_out, gamma_out, beta_out, block_out, spread, shifted,
+    feats_far, weight_far, style_far, gamma_out, beta_out, block_out,
+    spread, shifted, feats_out, weight_out, style_out, arrivals,
 ):
     samples, tile_rows, tile_cols, channels = cotangent.shape
     size = tile_rows * tile_cols
@@ -444,7 +445,10 @@
         here = slice(8 * pair, 8 * pair + 8)
         block = jnp.where(sub < 4, tails[2 * pair], pltpu.roll(tails[2 * pair + 1], 4, 0))
         weight_out[8, here, :] = scale * (block - shrink[here, :] * weight[8, here, :])
+    fetch = fetcher(arrivals)
+    copies = [fetch(weight_out, weight_far)]
     style_out[...] = scale * (emb_full[0] * rows[0] + emb_full[1] * rows[1])
+    copies.append(fetch(style_out, style_far))
     for sample in range(samples):
         inverse = stats[samples + sample : samples + sample + 1, :]
         product_mean = group_means[sample : sample + 1, :]
@@ -454,9 +458,12 @@
         change = inverse * (gain * grad_pre[sample] - product_mean - norm * squared_mean)
         out = cotangent[sample].reshape(size, channels).astype(F32) + change
         feats_out[sample] = out.astype(BF16).reshape(tile_rows, tile_cols, channels)
+    copies.append(fetch(feats_out, feats_far))
     forward_body(
         mixed, inner, outer, other, passed, fore_taps, stats, gamma, beta, block_out, spread, shifted
     )
+    for copy in copies:
+        copy.wait()
 
 
 def on_device(
@@ -559,7 +566,16 @@
             array((1, LANES)),
             array(feats.shape, BF16),
         ),
-        (spread, shifted),
+        (
+            spread,
+            shifted,
+            pltpu.VMEM(feats.shape, BF16),
+            pltpu.VMEM(taps.shape, F32),
+            pltpu.VMEM(style_weight.shape, F32),
+            pltpu.SemaphoreType.DMA((3,)),
+        ),
+        out_specs=[pl.BlockSpec(memory_space=pl.ANY)] * 3
+        + [pl.BlockSpec(memory_space=pltpu.VMEM)] * 3,
     )(
         payload.reshape(SHARDS, SLOT, LANES), stats, mixed, cotangent, grad_pre, gamma, beta, style,
         column, demod, power, taps, emb_full, inner, outer, other, passed, fore_taps,

time: 96.7 us -> 97.3 us (level)
  no operation moved by 1% of the time
where the time goes in v17:
time: 97.3 us; the launch traced here: 96.8 us
  blocking collectives  47.8 us (49%)
  starting transfers between devices  33.1 us (34%)
  Pallas kernels  7.51 us (8%)
  waiting for transfers between devices  6.74 us (7%)
    all_to_all x3, blocking collectives, exchange(): return lax.all_to_all(block, axes, 0, 0)  36.9 us
    all_to_all x2, starting transfers between devices, exchange(): return lax.all_to_all(block, axes, 0, 0)  22.4 us
    ppermute x3, starting transfers between devices, swap(): lax.ppermute(block, axes, pairs + [(target, source) for source, target in...  10.7 us
    all_to_all x2, waiting for transfers between devices, exchange(): return lax.all_to_all(block, axes, 0, 0)  6.73 us
    all_gather x1, blocking collectives, on_device(): payload = lax.all_gather(exchange(slots, NEAR), 'c')  5.69 us
    all_gather x1, blocking collectives, on_device(): lax.all_gather(payload, 'c')  5.2 us
    pallas_call x1, Pallas kernels, on_device(): call(mix_body, (array(feats.shape, BF16), array((lon_count, lon_slot, LAN...  2.27 us
    pallas_call x1, Pallas kernels, on_device(): call(functools.partial(last_body, scale_gradient, cells_per_group), (arra...  2.2 us
  transfers between devices with their start and end apart: 5, of which 2 were waited for; matrix products, arithmetic and copies ran while one was open for 0% of the time, Pallas kernels for 3%

profile of v17, /device:TPU:1, one launch (start us, length us, event | category | flops | bytes accessed | tf_op | source)
XLA Modules:
  0.0 96.8 jit_solution(2116369270725342090)
XLA Ops:
  0.6 0.0 copy-start
  0.6 2.3 %shard_map.145 = (bf16[2,8,32,128]{3,2,1,0:T(8,128)(2,1)}, bf16[32,24,128]{2,1,0:T(8,128)(2,1)}, bf16[2,2,32,128]{3,2,1,0:T(8,128)(2,1)}, bf16[2,2,32,128]{3,2,1,0:T(8,128)(2,1)}) custom-call(bf16[2,8,32,128]{3,2,1,0:T(8,128)(2,1)} %feats_in.1, bf16[2,8,32,128]{3,2,1,0:T(8,128)(2,1)} %cond_in.1, bf16[8,32,128]{2,1,0:T(8,128)(2,1)} %null_in.1, ...), custom_call_target="tpu_custom_call" | custom-call | tf_op jit(solution)/shard_map/pallas_call | solution.py:483
  2.9 0.0 copy-start.8
  2.9 0.0 copy-start.7
  2.9 0.0 copy-start.1
  3.0 10.7 %all-to-all-start = ((bf16[32,24,128]{2,1,0:T(8,128)(2,1)}), bf16[32,24,128]{2,1,0:T(8,128)(2,1)S(1)}, u32[]{:S(2)}, u32[]{:S(2)}) async-start(bf16[32,24,128]{2,1,0:T(8,128)(2,1)} %get-tuple-element.39), calls=%async_computation | async-start | bytes 393216 | tf_op jit(solution)/shard_map/all_to_all | solution.py:36
  13.7 0.0 copy-start.3
  13.7 0.0 copy-done.8
  13.7 0.8 collective-permute-start
  14.5 0.0 copy-done.7
  14.5 5.6 %collective-permute-start.1 = (bf16[2,2,32,128]{3,2,1,0:T(8,128)(2,1)S(1)}, bf16[2,2,32,128]{3,2,1,0:T(8,128)(2,1)S(1)}, u32[]{:S(2)}, u32[]{:S(2)}) collective-permute-start(bf16[2,2,32,128]{3,2,1,0:T(8,128)(2,1)S(1)} %copy-done.7), channel_id=1, source_target_pairs={{0,32},{64,96},{128,160},{192,224},{256,288},{320,352},{384,416},{... | collective-permute-start | bytes 98312 | tf_op jit(solution)/shard_map/ppermute | solution.py:26
  20.1 3.8 %all-to-all-done.slots = bf16[32,24,128]{2,1,0:T(8,128)(2,1)S(1)} async-done(((bf16[32,24,128]{2,1,0:T(8,128)(2,1)}), bf16[32,24,128]{2,1,0:T(8,128)(2,1)S(1)}, u32[]{:S(2)}, u32[]{:S(2)}) %all-to-all-start) | async-done | bytes 196640 | tf_op jit(solution)/shard_map/all_to_all | solution.py:36
  23.9 0.0 copy-done.1
  23.9 0.7 shard_map.146
  24.6 0.0 collective-permute-done.outer
  24.6 0.0 collective-permute-done.1.inner
  24.6 11.7 %all-to-all-start.1 = ((bf16[16,16,128]{2,1,0:T(8,128)(2,1)}), bf16[16,16,128]{2,1,0:T(8,128)(2,1)S(1)}, u32[]{:S(2)}, u32[]{:S(2)}) async-start(bf16[16,16,128]{2,1,0:T(8,128)(2,1)} %get-tuple-element.43), calls=%async_computation.1 | async-start | bytes 131072 | tf_op jit(solution)/shard_map/all_to_all | solution.py:36
  36.3 0.0 copy-start.4
  36.3 0.0 copy-start.5
  36.3 0.0 copy-start.6
  36.4 0.0 copy-done
  36.4 0.0 copy-done.3
  36.4 0.6 copy-done.4
  37.0 0.0 copy-done.5
  37.0 0.0 copy-done.6
  37.0 0.0 copy-start.2
  37.0 0.8 shard_map.148
  37.8 0.1 copy-done.2
  38.0 4.4 %collective-permute-start.2 = (bf16[24,128]{1,0:T(8,128)(2,1)S(1)}, bf16[24,128]{1,0:T(8,128)(2,1)S(1)}, u32[]{:S(2)}, u32[]{:S(2)}) collective-permute-start(bf16[24,128]{1,0:T(8,128)(2,1)S(1)} %get-tuple-element.56), channel_id=1, source_target_pairs={{1,2},{3,4},{5,6},{7,8},{9,10},{11,12},{13,14},{15,16},{17,18},{19... | collective-permute-start | bytes 18440 | tf_op jit(solution)/shard_map/ppermute | solution.py:26
  42.3 3.0 %all-to-all-done.1.slots = bf16[16,16,128]{2,1,0:T(8,128)(2,1)S(1)} async-done(((bf16[16,16,128]{2,1,0:T(8,128)(2,1)}), bf16[16,16,128]{2,1,0:T(8,128)(2,1)S(1)}, u32[]{:S(2)}, u32[]{:S(2)}) %all-to-all-start.1) | async-done | bytes 65568 | tf_op jit(solution)/shard_map/all_to_all | solution.py:36
  45.3 1.2 %shard_map.149 = (f32[4,128]{1,0:T(4,128)S(1)}, f32[2,256,128]{2,1,0:T(8,128)S(1)}, bf16[33,40,128]{2,1,0:T(8,128)(2,1)S(1)}) custom-call(bf16[16,16,128]{2,1,0:T(8,128)(2,1)S(1)} %all-to-all-done.1.slots, bf16[2,8,32,128]{3,2,1,0:T(8,128)(2,1)S(1)} %copy-done.2, bf16[40,128]{1,0:T(8,128)(2,1)S(1)} %get-tuple-element.47.edges, ...), custom_call_target="tpu_custom_call" | custom-call | tf_op jit(solution)/shard_map/pallas_call | solution.py:532
  46.5 5.2 %all-gather = bf16[66,40,128]{2,1,0:T(8,128)(2,1)S(1)} all-gather(bf16[33,40,128]{2,1,0:T(8,128)(2,1)S(1)} %get-tuple-element.54), channel_id=2, replica_groups=mesh['zh'=4,'x'=4,'zl'=2,'y'=8,'c'=2] {'c'}, dimensions={0}, use_global_device_ids=true | all-gather | bytes 1013760 | tf_op jit(solution)/shard_map/all_gather | solution.py:552
  51.7 0.1 shard_map.150
  51.8 0.0 collective-permute-done.2.passed
  51.8 12.3 %all_to_all.25.slots = bf16[16,40,128]{2,1,0:T(8,128)(2,1)S(1)} all-to-all(bf16[16,40,128]{2,1,0:T(8,128)(2,1)S(1)} %get-tuple-element.57), channel_id=1, replica_groups=mesh['zh'=4,'x'=4,'zl'=2,'y'=8,'c'=2] {'zl','y'}, dimensions={0} | all-to-all | bytes 327680 | tf_op jit(solution)/shard_map/all_to_all | solution.py:36
  64.1 0.1 shard_map.151
  64.2 12.6 %all_to_all.26.slots = bf16[16,40,128]{2,1,0:T(8,128)(2,1)S(1)} all-to-all(bf16[16,40,128]{2,1,0:T(8,128)(2,1)S(1)} %shard_map.151), channel_id=1, replica_groups=mesh['zh'=4,'x'=4,'zl'=2,'y'=8,'c'=2] {'zh','x'}, dimensions={0} | all-to-all | bytes 327680 | tf_op jit(solution)/shard_map/all_to_all | solution.py:36
  76.8 0.1 shard_map.152
  76.9 12.0 %all_to_all.27 = bf16[16,40,128]{2,1,0:T(8,128)(2,1)S(1)} all-to-all(bf16[16,40,128]{2,1,0:T(8,128)(2,1)S(1)} %shard_map.152), channel_id=1, replica_groups=mesh['zh'=4,'x'=4,'zl'=2,'y'=8,'c'=2] {'zl','y'}, dimensions={0} | all-to-all | bytes 327680 | tf_op jit(solution)/shard_map/all_to_all | solution.py:36
  88.9 5.7 %all-gather.1.gathered = bf16[32,40,128]{2,1,0:T(8,128)(2,1)S(1)} all-gather(bf16[16,40,128]{2,1,0:T(8,128)(2,1)S(1)} %all_to_all.27), channel_id=3, replica_groups=mesh['zh'=4,'x'=4,'zl'=2,'y'=8,'c'=2] {'c'}, dimensions={0}, use_global_device_ids=true | all-gather | bytes 491520 | tf_op jit(solution)/shard_map/all_gather | solution.py:558
  94.6 2.2 %shard_map.153 = (bf16[2,8,32,128]{3,2,1,0:T(8,128)(2,1)}, f32[9,128,128]{2,1,0:T(8,128)}, f32[512,128]{1,0:T(8,128)}, f32[1,128]{1,0:T(1,128)}, f32[1,128]{1,0:T(1,128)}, /*index=5*/bf16[2,8,32,128]{3,2,1,0:T(8,128)(2,1)}) custom-call(bf16[32,40,128]{2,1,0:T(8,128)(2,1)S(1)} %all-gather.1.gathered, f32[4,128]{1,0:T(4,128)S(1)} %get-tuple-element.58.stats, ...), custom_call_target="tpu_custom_call" | custom-call | tf_op jit(solution)/shard_map/pallas_call | solution.py:559
  (1 shorter events, 0.0 us)
Async XLA Ops:
  0.6 35.7 %copy-start = (f32[3,3,128,128]{3,2,1,0:T(8,128)S(1)}, f32[3,3,128,128]{3,2,1,0:T(8,128)}, u32[]{:S(2)}) copy-start(f32[3,3,128,128]{3,2,1,0:T(8,128)} %param.16) | copy-start | bytes 1769476
  2.9 10.8 %copy-start.8 = (bf16[2,2,32,128]{3,2,1,0:T(8,128)(2,1)S(1)}, bf16[2,2,32,128]{3,2,1,0:T(8,128)(2,1)}, u32[]{:S(2)}) copy-start(bf16[2,2,32,128]{3,2,1,0:T(8,128)(2,1)} %get-tuple-element.41) | copy-start | bytes 98308
  2.9 11.6 %copy-start.7 = (bf16[2,2,32,128]{3,2,1,0:T(8,128)(2,1)S(1)}, bf16[2,2,32,128]{3,2,1,0:T(8,128)(2,1)}, u32[]{:S(2)}) copy-start(bf16[2,2,32,128]{3,2,1,0:T(8,128)(2,1)} %get-tuple-element.42) | copy-start | bytes 98308
  2.9 20.9 %copy-start.1 = (bf16[2,8,32,128]{3,2,1,0:T(8,128)(2,1)S(1)}, bf16[2,8,32,128]{3,2,1,0:T(8,128)(2,1)}, u32[]{:S(2)}) copy-start(bf16[2,8,32,128]{3,2,1,0:T(8,128)(2,1)} %cotangent.1) | copy-start | bytes 393220
  3.0 20.9 %all-to-all-start = ((bf16[32,24,128]{2,1,0:T(8,128)(2,1)}), bf16[32,24,128]{2,1,0:T(8,128)(2,1)S(1)}, u32[]{:S(2)}, u32[]{:S(2)}) async-start(bf16[32,24,128]{2,1,0:T(8,128)(2,1)} %get-tuple-element.39), calls=%async_computation | async-start | bytes 393216 | tf_op jit(solution)/shard_map/all_to_all | solution.py:36
  13.7 22.7 %copy-start.3 = (f32[512,128]{1,0:T(8,128)S(1)}, f32[512,128]{1,0:T(8,128)}, u32[]{:S(2)}) copy-start(f32[512,128]{1,0:T(8,128)} %style_weight.1) | copy-start | bytes 786436
  13.7 10.9 %collective-permute-start = (bf16[2,2,32,128]{3,2,1,0:T(8,128)(2,1)S(1)}, bf16[2,2,32,128]{3,2,1,0:T(8,128)(2,1)S(1)}, u32[]{:S(2)}, u32[]{:S(2)}) collective-permute-start(bf16[2,2,32,128]{3,2,1,0:T(8,128)(2,1)S(1)} %copy-done.8), channel_id=1, source_target_pairs={{32,64},{96,128},{160,192},{224,256},{288,320},{352,384},{416,448}... | collective-permute-start | bytes 98312 | tf_op jit(solution)/shard_map/ppermute | solution.py:26
  14.5 10.1 %collective-permute-start.1 = (bf16[2,2,32,128]{3,2,1,0:T(8,128)(2,1)S(1)}, bf16[2,2,32,128]{3,2,1,0:T(8,128)(2,1)S(1)}, u32[]{:S(2)}, u32[]{:S(2)}) collective-permute-start(bf16[2,2,32,128]{3,2,1,0:T(8,128)(2,1)S(1)} %copy-done.7), channel_id=1, source_target_pairs={{0,32},{64,96},{128,160},{192,224},{256,288},{320,352},{384,416},{... | collective-permute-start | bytes 98312 | tf_op jit(solution)/shard_map/ppermute | solution.py:26
  24.6 20.6 %all-to-all-start.1 = ((bf16[16,16,128]{2,1,0:T(8,128)(2,1)}), bf16[16,16,128]{2,1,0:T(8,128)(2,1)S(1)}, u32[]{:S(2)}, u32[]{:S(2)}) async-start(bf16[16,16,128]{2,1,0:T(8,128)(2,1)} %get-tuple-element.43), calls=%async_computation.1 | async-start | bytes 131072 | tf_op jit(solution)/shard_map/all_to_all | solution.py:36
  36.3 0.7 copy-start.4
  36.3 0.7 copy-start.5
  36.3 0.7 copy-start.6
  37.0 0.9 copy-start.2
  38.0 13.8 %collective-permute-start.2 = (bf16[24,128]{1,0:T(8,128)(2,1)S(1)}, bf16[24,128]{1,0:T(8,128)(2,1)S(1)}, u32[]{:S(2)}, u32[]{:S(2)}) collective-permute-start(bf16[24,128]{1,0:T(8,128)(2,1)S(1)} %get-tuple-element.56), channel_id=1, source_target_pairs={{1,2},{3,4},{5,6},{7,8},{9,10},{11,12},{13,14},{15,16},{17,18},{19... | collective-permute-start | bytes 18440 | tf_op jit(solution)/shard_map/ppermute | solution.py:26
